TPU v7x, 32 devices: a whole 2x2x4 slice. The times are simulated.
32 devices in a mesh: row: 8 (over z, y), snk: 4 (over x, core).
Axes of the slice: x: 2, y: 2, z: 4, core: 2. Of those that a mesh axis runs over, the one named last changes fastest.
Arguments:
- start_basis: bfloat16 [65536, 128], P(('row', 'snk')), may hold values from -6 to 6
- band_cols: int32 [65536, 3, 8], P(('row', 'snk')), may hold values from 0 to 127, as said below
- band_wts: float32 [65536, 3, 8], P(('row', 'snk')), may hold values from 0.02 to 1
- far_dst: int32 [8192], P(('row', 'snk')), may hold values from 0 to 2047
- far_src: int32 [8192], P(('row', 'snk')), may hold values from 0 to 2047
- far_wts: float32 [8192], P(('row', 'snk')), may hold values from 1 to 8
Outputs:
- embedding: float32 [65536, 128], P(('row', 'snk'))
Inputs may be any that keep to these rules, and one draw needn't show every extreme that they name: `band_cols`: in each row and each of its three band blocks the 8 columns are distinct.
All inputs are finite; a program needn't handle non-finite values.
Results may differ from a plain program's by a relative error of at most 0.0047.
Values may be sent and summed in bfloat16 or wider, within the bound.
No kernel may reach another device: no remote copies, remote signals or barrier semaphores. Data moves between devices by JAX's collectives and lax.ppermute only.
A program may use at most 64 MiB of HBM per device.

v0:
```python
import math

import jax
import jax.numpy as jnp
from jax import lax
from jax.experimental import pallas as pl
from jax.experimental.pallas import tpu as pltpu
from jax.sharding import PartitionSpec as P

VECS = 128
BLK = 128
KB = 8
PEERS = 4
CAP = 64
DEGREE = 8
HALF_WIDTH = 0.95
AXES = ("row", "snk")
FAR = (2, 4)
BF16 = jnp.bfloat16
F32 = jnp.float32
VMEM = pl.BlockSpec(memory_space=pltpu.VMEM)
SMEM = pl.BlockSpec(memory_space=pltpu.SMEM)
PARAMS = pltpu.CompilerParams(vmem_limit_bytes=24 * 1024 * 1024)


def swap_pairs(count, by, odd):
    pairs = []
    for low in range(count):
        if (low // by) % 2 == odd:
            high = (low + by) % count
            pairs += [(low, high), (high, low)]
    return pairs


def split3(value):
    high = value.astype(BF16)
    rest = value - high.astype(F32)
    mid = rest.astype(BF16)
    low = (rest - mid.astype(F32)).astype(BF16)
    return high, mid, low


def stacked(value, height):
    parts = split3(value)
    pad = jnp.zeros((height - 3, value.shape[1]), BF16)
    return jnp.concatenate([*parts, pad], axis=0)


def dot(a, b, dims, precision=None):
    return lax.dot_general(
        a, b, (dims, ((), ())), precision=precision, preferred_element_type=F32
    )


def prepare_kernel(cols_ref, wts_ref, dst_ref, far_ref, band_ref, far_mat_ref):
    rows = cols_ref.shape[2]
    edges = dst_ref.shape[1]
    dst = dst_ref[...]
    far = far_ref[...]
    for b in range(rows // BLK):
        ids = lax.broadcasted_iota(jnp.int32, (BLK, edges), 0) + b * BLK
        far_mat_ref[pl.ds(b * BLK, BLK), :] = jnp.where(ids == dst, 1.0, 0.0).astype(BF16)
    hot = far_mat_ref[...]
    far_sum = jnp.sum(dot(stacked(far, 16), hot, ((1,), (1,))), axis=0, keepdims=True)
    degree = far_sum
    for o in range(3):
        degree = degree + jnp.sum(wts_ref[o], axis=0, keepdims=True)
    at_edge = jnp.sum(dot(stacked(degree, 16), hot, ((1,), (0,))), axis=0, keepdims=True)
    far_coef = (far / at_edge).astype(BF16)
    for b in range(rows // BLK):
        block = pl.ds(b * BLK, BLK)
        far_mat_ref[block, :] = far_mat_ref[block, :] * far_coef
        degree_b = degree[:, b * BLK : (b + 1) * BLK]
        for o in range(3):
            cols = cols_ref[o, :, block]
            coef = (wts_ref[o, :, block] / degree_b).astype(BF16).astype(F32)
            ids = lax.broadcasted_iota(jnp.int32, (BLK, BLK), 0)
            dense = jnp.zeros((BLK, BLK), F32)
            for k in range(KB):
                dense = jnp.where(ids == cols[k : k + 1, :], coef[k : k + 1, :], dense)
            band_ref[block, pl.ds(o * BLK, BLK)] = dense.T.astype(BF16)


def prepare(cols, wts, dst, far):
    rows, edges = cols.shape[2], dst.shape[1]
    return pl.pallas_call(
        prepare_kernel,
        out_shape=(
            jax.ShapeDtypeStruct((rows, 3 * BLK), BF16),
            jax.ShapeDtypeStruct((rows, edges), BF16),
        ),
        in_specs=[VMEM] * 4,
        out_specs=(VMEM, VMEM),
        compiler_params=PARAMS,
        name="prepare",
    )(cols, wts, dst, far)


def send_out(even, first, last, picked, edge_refs, pick_refs):
    edge_refs[0][...] = jnp.where(even, last, first)
    edge_refs[1][...] = jnp.where(even, first, last)
    for g in range(PEERS):
        pick_refs[g][...] = picked[g * CAP : (g + 1) * CAP].astype(BF16)


def first_kernel(even_ref, field_ref, w0, w1, w2, w3, pick_mat_ref, e0, e1, p0, p1, p2, p3):
    rows = field_ref.shape[0]
    half = 2 * CAP
    for g, (a, b) in enumerate(((w0, w1), (w2, w3))):
        wanted = jnp.concatenate([a[...], b[...]], axis=1)
        column = jnp.broadcast_to(wanted.astype(F32), (half, half)).T
        for b in range(rows // BLK):
            ids = lax.broadcasted_iota(jnp.int32, (half, BLK), 1) + b * BLK
            hot = jnp.where(column == ids.astype(F32), 1.0, 0.0).astype(BF16)
            pick_mat_ref[pl.ds(g * half, half), pl.ds(b * BLK, BLK)] = hot
    field = field_ref[...]
    picked = dot(pick_mat_ref[...], field, ((1,), (0,)))
    send_out(even_ref[0] == 0, field[:BLK], field[rows - BLK :], picked, (e0, e1), (p0, p1, p2, p3))


SENT = (
    *(jax.ShapeDtypeStruct((BLK, VECS), BF16),) * 2,
    *(jax.ShapeDtypeStruct((CAP, VECS), BF16),) * PEERS,
)


def first(even, field, wanted):
    rows = field.shape[0]
    return pl.pallas_call(
        first_kernel,
        out_shape=(jax.ShapeDtypeStruct((PEERS * CAP, rows), BF16), *SENT),
        in_specs=[SMEM] + [VMEM] * 5,
        out_specs=(VMEM,) * 7,
        compiler_params=PARAMS,
        name="first",
    )(even, field, *wanted)


def advance(even_ref, band_ref, far_mat_ref, field_ref, prev_ref, got, scale, store):
    rows = field_ref.shape[0]
    count = rows // BLK
    even = even_ref[0] == 0
    low = jnp.where(even, got[1][...], got[0][...])
    high = jnp.where(even, got[0][...], got[1][...])
    far = jnp.concatenate([g[...] for g in got[2:]], axis=0)
    for b in range(count):
        block = pl.ds(b * BLK, BLK)
        total = dot(far_mat_ref[block, :], far, ((1,), (0,)))
        if b == 0:
            total += dot(band_ref[block, :BLK], low, ((1,), (0,)))
            total += dot(band_ref[block, BLK:], field_ref[: 2 * BLK, :], ((1,), (0,)))
        elif b == count - 1:
            total += dot(
                band_ref[block, : 2 * BLK], field_ref[rows - 2 * BLK :, :], ((1,), (0,))
            )
            total += dot(band_ref[block, 2 * BLK :], high, ((1,), (0,)))
        else:
            total += dot(
                band_ref[block, :], field_ref[pl.ds((b - 1) * BLK, 3 * BLK), :], ((1,), (0,))
            )
        value = total * scale
        if prev_ref is not None:
            value = value - prev_ref[block, :].astype(F32)
        store(block, value)
    return even


def step_kernel(scale, has_prev, *refs):
    even_ref, band_ref, far_mat_ref, pick_mat_ref, field_ref = refs[:5]
    refs = refs[5:]
    prev_ref = None
    if has_prev:
        prev_ref, refs = refs[0], refs[1:]
    got, refs = refs[:6], refs[6:]
    next_ref, packed_ref, sent = refs[0], refs[1], refs[2:]

    def store(block, value):
        next_ref[block, :] = value
        packed_ref[block, :] = value.astype(BF16)

    even = advance(even_ref, band_ref, far_mat_ref, field_ref, prev_ref, got, scale, store)
    rows = field_ref.shape[0]
    picked = dot(pick_mat_ref[...], packed_ref[...], ((1,), (0,)))
    send_out(
        even, packed_ref[:BLK, :], packed_ref[rows - BLK :, :], picked, sent[:2], sent[2:]
    )


def step(scale, even, mats, field, prev, got):
    rows = field.shape[0]
    has_prev = prev is not None
    before = (prev,) if has_prev else ()
    return pl.pallas_call(
        lambda *refs: step_kernel(scale, has_prev, *refs),
        out_shape=(
            jax.ShapeDtypeStruct((rows, VECS), F32),
            jax.ShapeDtypeStruct((rows, VECS), BF16),
            *SENT,
        ),
        in_specs=[SMEM] + [VMEM] * (10 + len(before)),
        out_specs=(VMEM,) * 8,
        compiler_params=PARAMS,
        name="step",
    )(even, *mats, field, *before, *got)


def last_kernel(scale, *refs):
    even_ref, band_ref, far_mat_ref, field_ref, prev_ref = refs[:5]
    got, (next_ref, gram_ref) = refs[5:11], refs[11:]

    def store(block, value):
        next_ref[block, :] = value

    advance(even_ref, band_ref, far_mat_ref, field_ref, prev_ref, got, scale, store)
    value = next_ref[...]
    gram_ref[...] = dot(value, value, ((0,), (0,)), lax.Precision.HIGHEST)


def last(scale, even, band, far_mat, field, prev, got):
    rows = field.shape[0]
    return pl.pallas_call(
        lambda *refs: last_kernel(scale, *refs),
        out_shape=(
            jax.ShapeDtypeStruct((rows, VECS), F32),
            jax.ShapeDtypeStruct((VECS, VECS), F32),
        ),
        in_specs=[SMEM] + [VMEM] * 10,
        out_specs=(VMEM, VMEM),
        compiler_params=PARAMS,
        name="last",
    )(even, band, far_mat, field, prev, *got)


def summed(value, count):
    bits = [1 << i for i in range(count.bit_length() - 1)]
    stages = [bits[:1]] + [bits[i : i + 2] for i in range(1, len(bits), 2)]
    for stage in stages:
        masks = [stage[0]] if len(stage) == 1 else [*stage, stage[0] ^ stage[1]]
        total = value
        for mask in masks:
            total = total + lax.ppermute(value, AXES, [(i, i ^ mask) for i in range(count)])
        value = total
    return value


def local(start_basis, band_cols, band_wts, far_dst, far_src, far_wts):
    count = lax.axis_size(AXES)
    place = lax.axis_index(AXES)
    total_rows = start_basis.shape[0] * count

    def swap(value, by, odd):
        return lax.ppermute(value, AXES, swap_pairs(count, by, odd))

    def by_swap(edges):
        groups = edges.reshape(PEERS, CAP)
        ordered = []
        for i, by in enumerate(FAR):
            even = (place // by) % 2 == 0
            ahead, back = groups[2 * i : 2 * i + 1], groups[2 * i + 1 : 2 * i + 2]
            ordered += [jnp.where(even, ahead, back), jnp.where(even, back, ahead)]
        return ordered

    swaps = [(by, odd) for by in FAR for odd in (0, 1)]
    wanted = [swap(g, *s) for g, s in zip(by_swap(far_src), swaps)]
    dst = jnp.concatenate(by_swap(far_dst), axis=1)
    far = jnp.concatenate(by_swap(far_wts), axis=1)
    band, far_mat = prepare(
        jnp.transpose(band_cols, (1, 2, 0)), jnp.transpose(band_wts, (1, 2, 0)), dst, far
    )
    even = (place % 2).astype(jnp.int32).reshape(1)
    pick_mat, *sent = first(even, start_basis, wanted)

    def exchange(sent):
        return [swap(v, *s) for v, s in zip(sent, [(1, 0), (1, 1), *swaps])]

    mats = (band, far_mat, pick_mat)
    got = exchange(sent)
    previous, packed = start_basis, start_basis
    current, packed, *sent = step(1.0 / HALF_WIDTH, even, mats, packed, None, got)
    for _ in range(DEGREE - 2):
        got = exchange(sent)
        following, packed, *sent = step(2.0 / HALF_WIDTH, even, mats, packed, previous, got)
        previous, current = current, following
    got = exchange(sent)
    filtered, gram = last(2.0 / HALF_WIDTH, even, band, far_mat, packed, previous, got)
    factor = jnp.linalg.cholesky(summed(gram, count))
    basis = jax.scipy.linalg.solve_triangular(factor, filtered.T, lower=True).T
    return basis * math.sqrt(total_rows)


def solution(mesh):
    placed = (
        P(AXES, None),
        P(AXES, None, None),
        P(AXES, None, None),
        P(AXES),
        P(AXES),
        P(AXES),
    )
    return jax.shard_map(
        local, mesh=mesh, in_specs=placed, out_specs=P(AXES, None), check_vma=False
    )
```

profile of v0, /device:TPU:0, one launch (start us, length us, event | category | flops | bytes accessed | tf_op | source)
XLA Modules:
  0.0 168.0 jit_solution(9467354521871270554)
XLA Ops:
  0.0 0.9 fusion.14
  0.9 6.0 %collective-permute-start.3 = (s32[1,64]{1,0:T(1,128)S(1)}, s32[1,64]{1,0:T(1,128)S(1)}, u32[]{:S(2)}, u32[]{:S(2)}) collective-permute-start(s32[1,64]{1,0:T(1,128)S(1)} %get-tuple-element.137), channel_id=1, source_target_pairs={{4,8},{8,4},{5,9},{9,5},{6,10},{10,6},{7,11},{11,7},{12,16},{16,12... | collective-permute-start | bytes 776 | tf_op jit(solution)/shard_map/ppermute | solution.py:252
  6.9 1.5 collective-permute-start
  8.4 2.0 %collective-permute-start.2 = (s32[1,64]{1,0:T(1,128)S(1)}, s32[1,64]{1,0:T(1,128)S(1)}, u32[]{:S(2)}, u32[]{:S(2)}) collective-permute-start(s32[1,64]{1,0:T(1,128)S(1)} %get-tuple-element.140), channel_id=1, source_target_pairs={{0,4},{4,0},{1,5},{5,1},{2,6},{6,2},{3,7},{7,3},{8,12},{12,8},{9,1... | collective-permute-start | bytes 776 | tf_op jit(solution)/shard_map/ppermute | solution.py:252
  10.4 0.9 fusion.3
  11.3 0.9 fusion.5
  12.2 3.3 %collective-permute-done.1.w1 = s32[1,64]{1,0:T(1,128)S(1)} collective-permute-done((s32[1,64]{1,0:T(1,128)S(1)}, s32[1,64]{1,0:T(1,128)S(1)}, u32[]{:S(2)}, u32[]{:S(2)}) %collective-permute-start.1) | collective-permute-done | bytes 288 | tf_op jit(solution)/shard_map/ppermute | solution.py:252
  15.5 1.0 copy-done
  17.4 2.0 %collective-permute-start.7 = (bf16[64,128]{1,0:T(8,128)(2,1)S(1)}, bf16[64,128]{1,0:T(8,128)(2,1)S(1)}, u32[]{:S(2)}, u32[]{:S(2)}) collective-permute-start(bf16[64,128]{1,0:T(8,128)(2,1)S(1)} %get-tuple-element.77), channel_id=1, source_target_pairs={{2,4},{4,2},{3,5},{5,3},{6,8},{8,6},{7,9},{9,7},{10,12},{12,10},{1... | collective-permute-start | bytes 49160 | tf_op jit(solution)/shard_map/ppermute | solution.py:252
  19.4 1.4 collective-permute-start.8
  21.1 2.8 %collective-permute-start.5 = (bf16[128,128]{1,0:T(8,128)(2,1)S(1)}, bf16[128,128]{1,0:T(8,128)(2,1)S(1)}, u32[]{:S(2)}, u32[]{:S(2)}) collective-permute-start(bf16[128,128]{1,0:T(8,128)(2,1)S(1)} %get-tuple-element.75), channel_id=1, source_target_pairs={{1,2},{2,1},{3,4},{4,3},{5,6},{6,5},{7,8},{8,7},{9,10},{10,9},{11,... | collective-permute-start | bytes 98312 | tf_op jit(solution)/shard_map/ppermute | solution.py:252
  23.9 0.9 copy-done.3
  24.9 0.9 copy-done.4
  25.8 3.4 %prepare.1 = (bf16[2048,384]{1,0:T(8,128)(2,1)S(1)}, bf16[2048,256]{1,0:T(8,128)(2,1)S(1)}) custom-call(s32[3,8,2048]{2,1,0:T(8,128)S(1)} %bitcast.37, f32[3,8,2048]{2,1,0:T(8,128)S(1)} %bitcast.38, s32[1,256]{1,0:T(1,128)S(1)} %pad_add_fusion.dst_ref, f32[1,256]{1,0:T(1,128)S(1)} %pad_maximum_fusion.far_ref), custom_call_target="tpu_custom_call" | custom-call | tf_op jit(solution)/shard_map/prepare/pallas_call | solution.py:86
  29.3 1.0 copy-done.1
  30.3 1.1 step.7
  31.6 3.4 %collective-permute-start.11 = (bf16[128,128]{1,0:T(8,128)(2,1)S(1)}, bf16[128,128]{1,0:T(8,128)(2,1)S(1)}, u32[]{:S(2)}, u32[]{:S(2)}) collective-permute-start(bf16[128,128]{1,0:T(8,128)(2,1)S(1)} %get-tuple-element.82), channel_id=1, source_target_pairs={{1,2},{2,1},{3,4},{4,3},{5,6},{6,5},{7,8},{8,7},{9,10},{10,9},{11,... | collective-permute-start | bytes 98312 | tf_op jit(solution)/shard_map/ppermute | solution.py:252
  35.0 1.9 %collective-permute-start.13 = (bf16[64,128]{1,0:T(8,128)(2,1)S(1)}, bf16[64,128]{1,0:T(8,128)(2,1)S(1)}, u32[]{:S(2)}, u32[]{:S(2)}) collective-permute-start(bf16[64,128]{1,0:T(8,128)(2,1)S(1)} %get-tuple-element.84), channel_id=1, source_target_pairs={{2,4},{4,2},{3,5},{5,3},{6,8},{8,6},{7,9},{9,7},{10,12},{12,10},{1... | collective-permute-start | bytes 49160 | tf_op jit(solution)/shard_map/ppermute | solution.py:252
  37.0 0.8 collective-permute-start.15
  37.8 4.6 %collective-permute-done.13.refs_9_ = bf16[64,128]{1,0:T(8,128)(2,1)S(1)} collective-permute-done((bf16[64,128]{1,0:T(8,128)(2,1)S(1)}, bf16[64,128]{1,0:T(8,128)(2,1)S(1)}, u32[]{:S(2)}, u32[]{:S(2)}) %collective-permute-start.13) | collective-permute-done | bytes 16416 | tf_op jit(solution)/shard_map/ppermute | solution.py:252
  42.4 1.1 collective-permute-done.15.refs_11_
  43.4 1.1 step.8
  44.6 1.9 %collective-permute-start.18 = (bf16[64,128]{1,0:T(8,128)(2,1)S(1)}, bf16[64,128]{1,0:T(8,128)(2,1)S(1)}, u32[]{:S(2)}, u32[]{:S(2)}) collective-permute-start(bf16[64,128]{1,0:T(8,128)(2,1)S(1)} %get-tuple-element.91), channel_id=1, source_target_pairs={{0,2},{2,0},{1,3},{3,1},{4,6},{6,4},{5,7},{7,5},{8,10},{10,8},{9,1... | collective-permute-start | bytes 49160 | tf_op jit(solution)/shard_map/ppermute | solution.py:252
  46.5 2.0 %collective-permute-start.17 = (bf16[128,128]{1,0:T(8,128)(2,1)S(1)}, bf16[128,128]{1,0:T(8,128)(2,1)S(1)}, u32[]{:S(2)}, u32[]{:S(2)}) collective-permute-start(bf16[128,128]{1,0:T(8,128)(2,1)S(1)} %get-tuple-element.90), channel_id=1, source_target_pairs={{1,2},{2,1},{3,4},{4,3},{5,6},{6,5},{7,8},{8,7},{9,10},{10,9},{11,... | collective-permute-start | bytes 98312 | tf_op jit(solution)/shard_map/ppermute | solution.py:252
  48.5 1.9 %collective-permute-start.19 = (bf16[64,128]{1,0:T(8,128)(2,1)S(1)}, bf16[64,128]{1,0:T(8,128)(2,1)S(1)}, u32[]{:S(2)}, u32[]{:S(2)}) collective-permute-start(bf16[64,128]{1,0:T(8,128)(2,1)S(1)} %get-tuple-element.92), channel_id=1, source_target_pairs={{2,4},{4,2},{3,5},{5,3},{6,8},{8,6},{7,9},{9,7},{10,12},{12,10},{1... | collective-permute-start | bytes 49160 | tf_op jit(solution)/shard_map/ppermute | solution.py:252
  50.7 5.1 %collective-permute-done.19.refs_9_ = bf16[64,128]{1,0:T(8,128)(2,1)S(1)} collective-permute-done((bf16[64,128]{1,0:T(8,128)(2,1)S(1)}, bf16[64,128]{1,0:T(8,128)(2,1)S(1)}, u32[]{:S(2)}, u32[]{:S(2)}) %collective-permute-start.19) | collective-permute-done | bytes 16416 | tf_op jit(solution)/shard_map/ppermute | solution.py:252
  55.9 1.1 collective-permute-done.21.refs_11_
  56.9 1.2 step.9
  58.5 3.5 %collective-permute-start.23 = (bf16[128,128]{1,0:T(8,128)(2,1)S(1)}, bf16[128,128]{1,0:T(8,128)(2,1)S(1)}, u32[]{:S(2)}, u32[]{:S(2)}) collective-permute-start(bf16[128,128]{1,0:T(8,128)(2,1)S(1)} %get-tuple-element.98), channel_id=1, source_target_pairs={{1,2},{2,1},{3,4},{4,3},{5,6},{6,5},{7,8},{8,7},{9,10},{10,9},{11,... | collective-permute-start | bytes 98312 | tf_op jit(solution)/shard_map/ppermute | solution.py:252
  62.0 1.9 %collective-permute-start.25 = (bf16[64,128]{1,0:T(8,128)(2,1)S(1)}, bf16[64,128]{1,0:T(8,128)(2,1)S(1)}, u32[]{:S(2)}, u32[]{:S(2)}) collective-permute-start(bf16[64,128]{1,0:T(8,128)(2,1)S(1)} %get-tuple-element.100), channel_id=1, source_target_pairs={{2,4},{4,2},{3,5},{5,3},{6,8},{8,6},{7,9},{9,7},{10,12},{12,10},{1... | collective-permute-start | bytes 49160 | tf_op jit(solution)/shard_map/ppermute | solution.py:252
  64.2 5.2 %collective-permute-done.25.refs_9_ = bf16[64,128]{1,0:T(8,128)(2,1)S(1)} collective-permute-done((bf16[64,128]{1,0:T(8,128)(2,1)S(1)}, bf16[64,128]{1,0:T(8,128)(2,1)S(1)}, u32[]{:S(2)}, u32[]{:S(2)}) %collective-permute-start.25) | collective-permute-done | bytes 16416 | tf_op jit(solution)/shard_map/ppermute | solution.py:252
  69.4 1.0 collective-permute-done.27.refs_11_
  70.4 1.2 step.10
  72.0 3.5 %collective-permute-start.29 = (bf16[128,128]{1,0:T(8,128)(2,1)S(1)}, bf16[128,128]{1,0:T(8,128)(2,1)S(1)}, u32[]{:S(2)}, u32[]{:S(2)}) collective-permute-start(bf16[128,128]{1,0:T(8,128)(2,1)S(1)} %get-tuple-element.106), channel_id=1, source_target_pairs={{1,2},{2,1},{3,4},{4,3},{5,6},{6,5},{7,8},{8,7},{9,10},{10,9},{11,... | collective-permute-start | bytes 98312 | tf_op jit(solution)/shard_map/ppermute | solution.py:252
  75.5 1.9 %collective-permute-start.31 = (bf16[64,128]{1,0:T(8,128)(2,1)S(1)}, bf16[64,128]{1,0:T(8,128)(2,1)S(1)}, u32[]{:S(2)}, u32[]{:S(2)}) collective-permute-start(bf16[64,128]{1,0:T(8,128)(2,1)S(1)} %get-tuple-element.108), channel_id=1, source_target_pairs={{2,4},{4,2},{3,5},{5,3},{6,8},{8,6},{7,9},{9,7},{10,12},{12,10},{1... | collective-permute-start | bytes 49160 | tf_op jit(solution)/shard_map/ppermute | solution.py:252
  77.7 5.2 %collective-permute-done.31.refs_9_ = bf16[64,128]{1,0:T(8,128)(2,1)S(1)} collective-permute-done((bf16[64,128]{1,0:T(8,128)(2,1)S(1)}, bf16[64,128]{1,0:T(8,128)(2,1)S(1)}, u32[]{:S(2)}, u32[]{:S(2)}) %collective-permute-start.31) | collective-permute-done | bytes 16416 | tf_op jit(solution)/shard_map/ppermute | solution.py:252
  82.9 1.0 collective-permute-done.33.refs_11_
  83.9 1.4 step.11
  85.7 3.5 %collective-permute-start.35 = (bf16[128,128]{1,0:T(8,128)(2,1)S(1)}, bf16[128,128]{1,0:T(8,128)(2,1)S(1)}, u32[]{:S(2)}, u32[]{:S(2)}) collective-permute-start(bf16[128,128]{1,0:T(8,128)(2,1)S(1)} %get-tuple-element.114), channel_id=1, source_target_pairs={{1,2},{2,1},{3,4},{4,3},{5,6},{6,5},{7,8},{8,7},{9,10},{10,9},{11,... | collective-permute-start | bytes 98312 | tf_op jit(solution)/shard_map/ppermute | solution.py:252
  89.2 1.9 %collective-permute-start.37 = (bf16[64,128]{1,0:T(8,128)(2,1)S(1)}, bf16[64,128]{1,0:T(8,128)(2,1)S(1)}, u32[]{:S(2)}, u32[]{:S(2)}) collective-permute-start(bf16[64,128]{1,0:T(8,128)(2,1)S(1)} %get-tuple-element.116), channel_id=1, source_target_pairs={{2,4},{4,2},{3,5},{5,3},{6,8},{8,6},{7,9},{9,7},{10,12},{12,10},{1... | collective-permute-start | bytes 49160 | tf_op jit(solution)/shard_map/ppermute | solution.py:252
  91.4 5.2 %collective-permute-done.37.refs_9_ = bf16[64,128]{1,0:T(8,128)(2,1)S(1)} collective-permute-done((bf16[64,128]{1,0:T(8,128)(2,1)S(1)}, bf16[64,128]{1,0:T(8,128)(2,1)S(1)}, u32[]{:S(2)}, u32[]{:S(2)}) %collective-permute-start.37) | collective-permute-done | bytes 16416 | tf_op jit(solution)/shard_map/ppermute | solution.py:252
  96.6 1.0 collective-permute-done.39.refs_11_
  97.6 1.2 step.12
  99.2 3.5 %collective-permute-start.41 = (bf16[128,128]{1,0:T(8,128)(2,1)S(1)}, bf16[128,128]{1,0:T(8,128)(2,1)S(1)}, u32[]{:S(2)}, u32[]{:S(2)}) collective-permute-start(bf16[128,128]{1,0:T(8,128)(2,1)S(1)} %get-tuple-element.122), channel_id=1, source_target_pairs={{1,2},{2,1},{3,4},{4,3},{5,6},{6,5},{7,8},{8,7},{9,10},{10,9},{11,... | collective-permute-start | bytes 98312 | tf_op jit(solution)/shard_map/ppermute | solution.py:252
  102.7 1.9 %collective-permute-start.43 = (bf16[64,128]{1,0:T(8,128)(2,1)S(1)}, bf16[64,128]{1,0:T(8,128)(2,1)S(1)}, u32[]{:S(2)}, u32[]{:S(2)}) collective-permute-start(bf16[64,128]{1,0:T(8,128)(2,1)S(1)} %get-tuple-element.124), channel_id=1, source_target_pairs={{2,4},{4,2},{3,5},{5,3},{6,8},{8,6},{7,9},{9,7},{10,12},{12,10},{1... | collective-permute-start | bytes 49160 | tf_op jit(solution)/shard_map/ppermute | solution.py:252
  104.9 5.2 %collective-permute-done.43.refs_9_ = bf16[64,128]{1,0:T(8,128)(2,1)S(1)} collective-permute-done((bf16[64,128]{1,0:T(8,128)(2,1)S(1)}, bf16[64,128]{1,0:T(8,128)(2,1)S(1)}, u32[]{:S(2)}, u32[]{:S(2)}) %collective-permute-start.43) | collective-permute-done | bytes 16416 | tf_op jit(solution)/shard_map/ppermute | solution.py:252
  110.1 1.0 collective-permute-done.45.refs_11_
  111.1 2.0 %step.13 = (f32[2048,128]{1,0:T(8,128)}, bf16[2048,128]{1,0:T(8,128)(2,1)S(1)}, bf16[128,128]{1,0:T(8,128)(2,1)S(1)}, bf16[128,128]{1,0:T(8,128)(2,1)S(1)}, bf16...) custom-call(s32[1]{0:T(128)} %bitcast.even_ref.refs_0_, ...), custom_call_target="tpu_custom_call" | custom-call | tf_op jit(solution)/shard_map/step/pallas_call | solution.py:193
  113.5 3.4 %collective-permute-start.47 = (bf16[128,128]{1,0:T(8,128)(2,1)S(1)}, bf16[128,128]{1,0:T(8,128)(2,1)S(1)}, u32[]{:S(2)}, u32[]{:S(2)}) collective-permute-start(bf16[128,128]{1,0:T(8,128)(2,1)S(1)} %get-tuple-element.130), channel_id=1, source_target_pairs={{1,2},{2,1},{3,4},{4,3},{5,6},{6,5},{7,8},{8,7},{9,10},{10,9},{11,... | collective-permute-start | bytes 98312 | tf_op jit(solution)/shard_map/ppermute | solution.py:252
  116.9 2.0 %collective-permute-start.49 = (bf16[64,128]{1,0:T(8,128)(2,1)S(1)}, bf16[64,128]{1,0:T(8,128)(2,1)S(1)}, u32[]{:S(2)}, u32[]{:S(2)}) collective-permute-start(bf16[64,128]{1,0:T(8,128)(2,1)S(1)} %get-tuple-element.132), channel_id=1, source_target_pairs={{2,4},{4,2},{3,5},{5,3},{6,8},{8,6},{7,9},{9,7},{10,12},{12,10},{1... | collective-permute-start | bytes 49160 | tf_op jit(solution)/shard_map/ppermute | solution.py:252
  119.2 5.1 %collective-permute-done.49.refs_8_ = bf16[64,128]{1,0:T(8,128)(2,1)S(1)} collective-permute-done((bf16[64,128]{1,0:T(8,128)(2,1)S(1)}, bf16[64,128]{1,0:T(8,128)(2,1)S(1)}, u32[]{:S(2)}, u32[]{:S(2)}) %collective-permute-start.49) | collective-permute-done | bytes 16416 | tf_op jit(solution)/shard_map/ppermute | solution.py:252
  124.3 1.1 collective-permute-done.51.refs_10_
  125.4 1.7 %last.1 = (f32[2048,128]{1,0:T(8,128)S(1)}, f32[128,128]{1,0:T(8,128)S(1)}) custom-call(s32[1]{0:T(128)} %bitcast.even_ref.refs_0_, bf16[2048,384]{1,0:T(8,128)(2,1)S(1)} %get-tuple-element.71.refs_1_, bf16[2048,256]{1,0:T(8,128)(2,1)S(1)} %get-tuple-element.72.refs_2_, bf16[2048,128]{1,0:T(8,128)(2,1)S(1)} %get-tuple-element.127.refs_3_, ...), custom_call_target="tpu_custom_call" | custom-call | tf_op jit(solution)/shard_map/last/pallas_call | solution.py:221
  127.3 1.2 collective-permute-done.52
  128.7 1.8 %collective-permute-start.54 = (f32[128,128]{0,1:T(8,128)S(1)}, f32[128,128]{0,1:T(8,128)S(1)}, u32[]{:S(2)}, u32[]{:S(2)}) collective-permute-start(f32[128,128]{0,1:T(8,128)S(1)} %add.56), channel_id=1, source_target_pairs={{0,4},{1,5},{2,6},{3,7},{4,0},{5,1},{6,2},{7,3},{8,12},{9,13},{10,... | collective-permute-start | bytes 196616 | tf_op jit(solution)/shard_map/ppermute | solution.py:241
  130.5 1.7 collective-permute-start.53
  132.1 2.3 %collective-permute-done.55 = f32[128,128]{0,1:T(8,128)S(1)} collective-permute-done((f32[128,128]{0,1:T(8,128)S(1)}, f32[128,128]{0,1:T(8,128)S(1)}, u32[]{:S(2)}, u32[]{:S(2)}) %collective-permute-start.55) | collective-permute-done | bytes 65568 | tf_op jit(solution)/shard_map/ppermute | solution.py:241
  134.8 2.6 %collective-permute-start.58 = (f32[128,128]{0,1:T(8,128)S(1)}, f32[128,128]{0,1:T(8,128)S(1)}, u32[]{:S(2)}, u32[]{:S(2)}) collective-permute-start(f32[128,128]{0,1:T(8,128)S(1)} %add_add_fusion.1), channel_id=1, source_target_pairs={{0,24},{1,25},{2,26},{3,27},{4,28},{5,29},{6,30},{7,31},{8,16},{9,... | collective-permute-start | bytes 196616 | tf_op jit(solution)/shard_map/ppermute | solution.py:241
  137.4 1.8 %collective-permute-start.56 = (f32[128,128]{0,1:T(8,128)S(1)}, f32[128,128]{0,1:T(8,128)S(1)}, u32[]{:S(2)}, u32[]{:S(2)}) collective-permute-start(f32[128,128]{0,1:T(8,128)S(1)} %add_add_fusion.1), channel_id=1, source_target_pairs={{0,8},{1,9},{2,10},{3,11},{4,12},{5,13},{6,14},{7,15},{8,0},{9,1},... | collective-permute-start | bytes 196616 | tf_op jit(solution)/shard_map/ppermute | solution.py:241
  139.2 2.3 %collective-permute-done.58 = f32[128,128]{0,1:T(8,128)S(1)} collective-permute-done((f32[128,128]{0,1:T(8,128)S(1)}, f32[128,128]{0,1:T(8,128)S(1)}, u32[]{:S(2)}, u32[]{:S(2)}) %collective-permute-start.58) | collective-permute-done | bytes 65568 | tf_op jit(solution)/shard_map/ppermute | solution.py:241
  141.5 1.5 collective-permute-done.57
  143.1 11.7 %cholesky.16 = f32[128,128]{1,0:T(8,128)S(1)} custom-call(f32[128,128]{1,0:T(8,128)S(1)} %fusion.2), custom_call_target="Cholesky" | custom-call | tf_op jit(solution)/shard_map/jit(cholesky)/cholesky | solution.py:286
  156.2 9.8 %custom-call.7 = f32[1,128,128]{1,2,0:T(8,128)S(1)} custom-call(f32[1,128,128]{2,1,0:T(8,128)S(1)} %fusion), custom_call_target="InvertDiagBlocksLowerTriangular" | custom-call | tf_op jit(solution)/shard_map/jit(_solve_triangular)/triangular_solve | solution.py:287
  166.0 1.9 %convolution_multiply_fusion = f32[2048,128]{1,0:T(8,128)} fusion(f32[2048,128]{1,0:T(8,128)S(1)} %get-tuple-element.135, f32[1,128,128]{1,2,0:T(8,128)S(1)} %custom-call.7), kind=kOutput, calls=%fused_computation | convolution fusion | flops 402915328 | bytes 2162688 | tf_op jit(solution)/shard_map/jit(_solve_triangular)/triangular_solve | solution.py:287
  (91 shorter events, 6.9 us)
Async XLA Ops:
  0.9 11.3 %collective-permute-start.3 = (s32[1,64]{1,0:T(1,128)S(1)}, s32[1,64]{1,0:T(1,128)S(1)}, u32[]{:S(2)}, u32[]{:S(2)}) collective-permute-start(s32[1,64]{1,0:T(1,128)S(1)} %get-tuple-element.137), channel_id=1, source_target_pairs={{4,8},{8,4},{5,9},{9,5},{6,10},{10,6},{7,11},{11,7},{12,16},{16,12... | collective-permute-start | bytes 776 | tf_op jit(solution)/shard_map/ppermute | solution.py:252
  6.9 5.3 %collective-permute-start = (s32[1,64]{1,0:T(1,128)S(1)}, s32[1,64]{1,0:T(1,128)S(1)}, u32[]{:S(2)}, u32[]{:S(2)}) collective-permute-start(s32[1,64]{1,0:T(1,128)S(1)} %get-tuple-element.138), channel_id=1, source_target_pairs={{0,2},{2,0},{1,3},{3,1},{4,6},{6,4},{5,7},{7,5},{8,10},{10,8},{9,1... | collective-permute-start | bytes 776 | tf_op jit(solution)/shard_map/ppermute | solution.py:252
  8.4 7.1 %collective-permute-start.1 = (s32[1,64]{1,0:T(1,128)S(1)}, s32[1,64]{1,0:T(1,128)S(1)}, u32[]{:S(2)}, u32[]{:S(2)}) collective-permute-start(s32[1,64]{1,0:T(1,128)S(1)} %get-tuple-element.139), channel_id=1, source_target_pairs={{2,4},{4,2},{3,5},{5,3},{6,8},{8,6},{7,9},{9,7},{10,12},{12,10},{1... | collective-permute-start | bytes 776 | tf_op jit(solution)/shard_map/ppermute | solution.py:252
  8.4 7.1 %collective-permute-start.2 = (s32[1,64]{1,0:T(1,128)S(1)}, s32[1,64]{1,0:T(1,128)S(1)}, u32[]{:S(2)}, u32[]{:S(2)}) collective-permute-start(s32[1,64]{1,0:T(1,128)S(1)} %get-tuple-element.140), channel_id=1, source_target_pairs={{0,4},{4,0},{1,5},{5,1},{2,6},{6,2},{3,7},{7,3},{8,12},{12,8},{9,1... | collective-permute-start | bytes 776 | tf_op jit(solution)/shard_map/ppermute | solution.py:252
  15.5 1.0 copy-start
  17.3 3.8 %collective-permute-start.6 = (bf16[64,128]{1,0:T(8,128)(2,1)S(1)}, bf16[64,128]{1,0:T(8,128)(2,1)S(1)}, u32[]{:S(2)}, u32[]{:S(2)}) collective-permute-start(bf16[64,128]{1,0:T(8,128)(2,1)S(1)} %get-tuple-element.76), channel_id=1, source_target_pairs={{0,2},{2,0},{1,3},{3,1},{4,6},{6,4},{5,7},{7,5},{8,10},{10,8},{9,1... | collective-permute-start | bytes 49160 | tf_op jit(solution)/shard_map/ppermute | solution.py:252
  17.4 11.8 %collective-permute-start.7 = (bf16[64,128]{1,0:T(8,128)(2,1)S(1)}, bf16[64,128]{1,0:T(8,128)(2,1)S(1)}, u32[]{:S(2)}, u32[]{:S(2)}) collective-permute-start(bf16[64,128]{1,0:T(8,128)(2,1)S(1)} %get-tuple-element.77), channel_id=1, source_target_pairs={{2,4},{4,2},{3,5},{5,3},{6,8},{8,6},{7,9},{9,7},{10,12},{12,10},{1... | collective-permute-start | bytes 49160 | tf_op jit(solution)/shard_map/ppermute | solution.py:252
  19.4 9.8 %collective-permute-start.8 = (bf16[64,128]{1,0:T(8,128)(2,1)S(1)}, bf16[64,128]{1,0:T(8,128)(2,1)S(1)}, u32[]{:S(2)}, u32[]{:S(2)}) collective-permute-start(bf16[64,128]{1,0:T(8,128)(2,1)S(1)} %get-tuple-element.78), channel_id=1, source_target_pairs={{0,4},{4,0},{1,5},{5,1},{2,6},{6,2},{3,7},{7,3},{8,12},{12,8},{9,1... | collective-permute-start | bytes 49160 | tf_op jit(solution)/shard_map/ppermute | solution.py:252
  20.9 8.3 %collective-permute-start.9 = (bf16[64,128]{1,0:T(8,128)(2,1)S(1)}, bf16[64,128]{1,0:T(8,128)(2,1)S(1)}, u32[]{:S(2)}, u32[]{:S(2)}) collective-permute-start(bf16[64,128]{1,0:T(8,128)(2,1)S(1)} %get-tuple-element.79), channel_id=1, source_target_pairs={{4,8},{8,4},{5,9},{9,5},{6,10},{10,6},{7,11},{11,7},{12,16},{16,12... | collective-permute-start | bytes 49160 | tf_op jit(solution)/shard_map/ppermute | solution.py:252
  20.9 8.4 %collective-permute-start.4 = (bf16[128,128]{1,0:T(8,128)(2,1)S(1)}, bf16[128,128]{1,0:T(8,128)(2,1)S(1)}, u32[]{:S(2)}, u32[]{:S(2)}) collective-permute-start(bf16[128,128]{1,0:T(8,128)(2,1)S(1)} %get-tuple-element.74), channel_id=1, source_target_pairs={{0,1},{1,0},{2,3},{3,2},{4,5},{5,4},{6,7},{7,6},{8,9},{9,8},{10,11... | collective-permute-start | bytes 98312 | tf_op jit(solution)/shard_map/ppermute | solution.py:252
  21.1 8.2 %collective-permute-start.5 = (bf16[128,128]{1,0:T(8,128)(2,1)S(1)}, bf16[128,128]{1,0:T(8,128)(2,1)S(1)}, u32[]{:S(2)}, u32[]{:S(2)}) collective-permute-start(bf16[128,128]{1,0:T(8,128)(2,1)S(1)} %get-tuple-element.75), channel_id=1, source_target_pairs={{1,2},{2,1},{3,4},{4,3},{5,6},{6,5},{7,8},{8,7},{9,10},{10,9},{11,... | collective-permute-start | bytes 98312 | tf_op jit(solution)/shard_map/ppermute | solution.py:252
  23.9 0.9 copy-start.3
  24.9 0.9 copy-start.4
  29.3 1.0 copy-start.1
  30.3 13.1 %copy-start.2 = (bf16[2048,128]{1,0:T(8,128)(2,1)S(1)}, bf16[2048,128]{1,0:T(8,128)(2,1)}, u32[]{:S(2)}) copy-start(bf16[2048,128]{1,0:T(8,128)(2,1)} %refs_5_.1) | copy-start | bytes 1572868
  31.4 5.5 %collective-permute-start.12 = (bf16[64,128]{1,0:T(8,128)(2,1)S(1)}, bf16[64,128]{1,0:T(8,128)(2,1)S(1)}, u32[]{:S(2)}, u32[]{:S(2)}) collective-permute-start(bf16[64,128]{1,0:T(8,128)(2,1)S(1)} %get-tuple-element.83), channel_id=1, source_target_pairs={{0,2},{2,0},{1,3},{3,1},{4,6},{6,4},{5,7},{7,5},{8,10},{10,8},{9,1... | collective-permute-start | bytes 49160 | tf_op jit(solution)/shard_map/ppermute | solution.py:252
  31.5 11.9 %collective-permute-start.10 = (bf16[128,128]{1,0:T(8,128)(2,1)S(1)}, bf16[128,128]{1,0:T(8,128)(2,1)S(1)}, u32[]{:S(2)}, u32[]{:S(2)}) collective-permute-start(bf16[128,128]{1,0:T(8,128)(2,1)S(1)} %get-tuple-element.81), channel_id=1, source_target_pairs={{0,1},{1,0},{2,3},{3,2},{4,5},{5,4},{6,7},{7,6},{8,9},{9,8},{10,11... | collective-permute-start | bytes 98312 | tf_op jit(solution)/shard_map/ppermute | solution.py:252
  31.6 11.8 %collective-permute-start.11 = (bf16[128,128]{1,0:T(8,128)(2,1)S(1)}, bf16[128,128]{1,0:T(8,128)(2,1)S(1)}, u32[]{:S(2)}, u32[]{:S(2)}) collective-permute-start(bf16[128,128]{1,0:T(8,128)(2,1)S(1)} %get-tuple-element.82), channel_id=1, source_target_pairs={{1,2},{2,1},{3,4},{4,3},{5,6},{6,5},{7,8},{8,7},{9,10},{10,9},{11,... | collective-permute-start | bytes 98312 | tf_op jit(solution)/shard_map/ppermute | solution.py:252
  35.0 7.3 %collective-permute-start.13 = (bf16[64,128]{1,0:T(8,128)(2,1)S(1)}, bf16[64,128]{1,0:T(8,128)(2,1)S(1)}, u32[]{:S(2)}, u32[]{:S(2)}) collective-permute-start(bf16[64,128]{1,0:T(8,128)(2,1)S(1)} %get-tuple-element.84), channel_id=1, source_target_pairs={{2,4},{4,2},{3,5},{5,3},{6,8},{8,6},{7,9},{9,7},{10,12},{12,10},{1... | collective-permute-start | bytes 49160 | tf_op jit(solution)/shard_map/ppermute | solution.py:252
  37.0 5.4 %collective-permute-start.14 = (bf16[64,128]{1,0:T(8,128)(2,1)S(1)}, bf16[64,128]{1,0:T(8,128)(2,1)S(1)}, u32[]{:S(2)}, u32[]{:S(2)}) collective-permute-start(bf16[64,128]{1,0:T(8,128)(2,1)S(1)} %get-tuple-element.85), channel_id=1, source_target_pairs={{0,4},{4,0},{1,5},{5,1},{2,6},{6,2},{3,7},{7,3},{8,12},{12,8},{9,1... | collective-permute-start | bytes 49160 | tf_op jit(solution)/shard_map/ppermute | solution.py:252
  37.0 6.4 %collective-permute-start.15 = (bf16[64,128]{1,0:T(8,128)(2,1)S(1)}, bf16[64,128]{1,0:T(8,128)(2,1)S(1)}, u32[]{:S(2)}, u32[]{:S(2)}) collective-permute-start(bf16[64,128]{1,0:T(8,128)(2,1)S(1)} %get-tuple-element.86), channel_id=1, source_target_pairs={{4,8},{8,4},{5,9},{9,5},{6,10},{10,6},{7,11},{11,7},{12,16},{16,12... | collective-permute-start | bytes 49160 | tf_op jit(solution)/shard_map/ppermute | solution.py:252
  44.6 5.9 %collective-permute-start.18 = (bf16[64,128]{1,0:T(8,128)(2,1)S(1)}, bf16[64,128]{1,0:T(8,128)(2,1)S(1)}, u32[]{:S(2)}, u32[]{:S(2)}) collective-permute-start(bf16[64,128]{1,0:T(8,128)(2,1)S(1)} %get-tuple-element.91), channel_id=1, source_target_pairs={{0,2},{2,0},{1,3},{3,1},{4,6},{6,4},{5,7},{7,5},{8,10},{10,8},{9,1... | collective-permute-start | bytes 49160 | tf_op jit(solution)/shard_map/ppermute | solution.py:252
  46.5 10.4 %collective-permute-start.16 = (bf16[128,128]{1,0:T(8,128)(2,1)S(1)}, bf16[128,128]{1,0:T(8,128)(2,1)S(1)}, u32[]{:S(2)}, u32[]{:S(2)}) collective-permute-start(bf16[128,128]{1,0:T(8,128)(2,1)S(1)} %get-tuple-element.89), channel_id=1, source_target_pairs={{0,1},{1,0},{2,3},{3,2},{4,5},{5,4},{6,7},{7,6},{8,9},{9,8},{10,11... | collective-permute-start | bytes 98312 | tf_op jit(solution)/shard_map/ppermute | solution.py:252
  46.5 10.4 %collective-permute-start.17 = (bf16[128,128]{1,0:T(8,128)(2,1)S(1)}, bf16[128,128]{1,0:T(8,128)(2,1)S(1)}, u32[]{:S(2)}, u32[]{:S(2)}) collective-permute-start(bf16[128,128]{1,0:T(8,128)(2,1)S(1)} %get-tuple-element.90), channel_id=1, source_target_pairs={{1,2},{2,1},{3,4},{4,3},{5,6},{6,5},{7,8},{8,7},{9,10},{10,9},{11,... | collective-permute-start | bytes 98312 | tf_op jit(solution)/shard_map/ppermute | solution.py:252
  48.5 7.3 %collective-permute-start.19 = (bf16[64,128]{1,0:T(8,128)(2,1)S(1)}, bf16[64,128]{1,0:T(8,128)(2,1)S(1)}, u32[]{:S(2)}, u32[]{:S(2)}) collective-permute-start(bf16[64,128]{1,0:T(8,128)(2,1)S(1)} %get-tuple-element.92), channel_id=1, source_target_pairs={{2,4},{4,2},{3,5},{5,3},{6,8},{8,6},{7,9},{9,7},{10,12},{12,10},{1... | collective-permute-start | bytes 49160 | tf_op jit(solution)/shard_map/ppermute | solution.py:252
  50.5 5.4 %collective-permute-start.20 = (bf16[64,128]{1,0:T(8,128)(2,1)S(1)}, bf16[64,128]{1,0:T(8,128)(2,1)S(1)}, u32[]{:S(2)}, u32[]{:S(2)}) collective-permute-start(bf16[64,128]{1,0:T(8,128)(2,1)S(1)} %get-tuple-element.93), channel_id=1, source_target_pairs={{0,4},{4,0},{1,5},{5,1},{2,6},{6,2},{3,7},{7,3},{8,12},{12,8},{9,1... | collective-permute-start | bytes 49160 | tf_op jit(solution)/shard_map/ppermute | solution.py:252
  50.5 6.4 %collective-permute-start.21 = (bf16[64,128]{1,0:T(8,128)(2,1)S(1)}, bf16[64,128]{1,0:T(8,128)(2,1)S(1)}, u32[]{:S(2)}, u32[]{:S(2)}) collective-permute-start(bf16[64,128]{1,0:T(8,128)(2,1)S(1)} %get-tuple-element.94), channel_id=1, source_target_pairs={{4,8},{8,4},{5,9},{9,5},{6,10},{10,6},{7,11},{11,7},{12,16},{16,12... | collective-permute-start | bytes 49160 | tf_op jit(solution)/shard_map/ppermute | solution.py:252
  58.1 5.9 %collective-permute-start.24 = (bf16[64,128]{1,0:T(8,128)(2,1)S(1)}, bf16[64,128]{1,0:T(8,128)(2,1)S(1)}, u32[]{:S(2)}, u32[]{:S(2)}) collective-permute-start(bf16[64,128]{1,0:T(8,128)(2,1)S(1)} %get-tuple-element.99), channel_id=1, source_target_pairs={{0,2},{2,0},{1,3},{3,1},{4,6},{6,4},{5,7},{7,5},{8,10},{10,8},{9,1... | collective-permute-start | bytes 49160 | tf_op jit(solution)/shard_map/ppermute | solution.py:252
  58.5 11.9 %collective-permute-start.22 = (bf16[128,128]{1,0:T(8,128)(2,1)S(1)}, bf16[128,128]{1,0:T(8,128)(2,1)S(1)}, u32[]{:S(2)}, u32[]{:S(2)}) collective-permute-start(bf16[128,128]{1,0:T(8,128)(2,1)S(1)} %get-tuple-element.97), channel_id=1, source_target_pairs={{0,1},{1,0},{2,3},{3,2},{4,5},{5,4},{6,7},{7,6},{8,9},{9,8},{10,11... | collective-permute-start | bytes 98312 | tf_op jit(solution)/shard_map/ppermute | solution.py:252
  58.5 11.9 %collective-permute-start.23 = (bf16[128,128]{1,0:T(8,128)(2,1)S(1)}, bf16[128,128]{1,0:T(8,128)(2,1)S(1)}, u32[]{:S(2)}, u32[]{:S(2)}) collective-permute-start(bf16[128,128]{1,0:T(8,128)(2,1)S(1)} %get-tuple-element.98), channel_id=1, source_target_pairs={{1,2},{2,1},{3,4},{4,3},{5,6},{6,5},{7,8},{8,7},{9,10},{10,9},{11,... | collective-permute-start | bytes 98312 | tf_op jit(solution)/shard_map/ppermute | solution.py:252
  62.0 7.4 %collective-permute-start.25 = (bf16[64,128]{1,0:T(8,128)(2,1)S(1)}, bf16[64,128]{1,0:T(8,128)(2,1)S(1)}, u32[]{:S(2)}, u32[]{:S(2)}) collective-permute-start(bf16[64,128]{1,0:T(8,128)(2,1)S(1)} %get-tuple-element.100), channel_id=1, source_target_pairs={{2,4},{4,2},{3,5},{5,3},{6,8},{8,6},{7,9},{9,7},{10,12},{12,10},{1... | collective-permute-start | bytes 49160 | tf_op jit(solution)/shard_map/ppermute | solution.py:252
  64.0 5.4 %collective-permute-start.26 = (bf16[64,128]{1,0:T(8,128)(2,1)S(1)}, bf16[64,128]{1,0:T(8,128)(2,1)S(1)}, u32[]{:S(2)}, u32[]{:S(2)}) collective-permute-start(bf16[64,128]{1,0:T(8,128)(2,1)S(1)} %get-tuple-element.101), channel_id=1, source_target_pairs={{0,4},{4,0},{1,5},{5,1},{2,6},{6,2},{3,7},{7,3},{8,12},{12,8},{9,1... | collective-permute-start | bytes 49160 | tf_op jit(solution)/shard_map/ppermute | solution.py:252
  64.0 6.4 %collective-permute-start.27 = (bf16[64,128]{1,0:T(8,128)(2,1)S(1)}, bf16[64,128]{1,0:T(8,128)(2,1)S(1)}, u32[]{:S(2)}, u32[]{:S(2)}) collective-permute-start(bf16[64,128]{1,0:T(8,128)(2,1)S(1)} %get-tuple-element.102), channel_id=1, source_target_pairs={{4,8},{8,4},{5,9},{9,5},{6,10},{10,6},{7,11},{11,7},{12,16},{16,12... | collective-permute-start | bytes 49160 | tf_op jit(solution)/shard_map/ppermute | solution.py:252
  71.6 5.9 %collective-permute-start.30 = (bf16[64,128]{1,0:T(8,128)(2,1)S(1)}, bf16[64,128]{1,0:T(8,128)(2,1)S(1)}, u32[]{:S(2)}, u32[]{:S(2)}) collective-permute-start(bf16[64,128]{1,0:T(8,128)(2,1)S(1)} %get-tuple-element.107), channel_id=1, source_target_pairs={{0,2},{2,0},{1,3},{3,1},{4,6},{6,4},{5,7},{7,5},{8,10},{10,8},{9,1... | collective-permute-start | bytes 49160 | tf_op jit(solution)/shard_map/ppermute | solution.py:252
  72.0 11.9 %collective-permute-start.28 = (bf16[128,128]{1,0:T(8,128)(2,1)S(1)}, bf16[128,128]{1,0:T(8,128)(2,1)S(1)}, u32[]{:S(2)}, u32[]{:S(2)}) collective-permute-start(bf16[128,128]{1,0:T(8,128)(2,1)S(1)} %get-tuple-element.105), channel_id=1, source_target_pairs={{0,1},{1,0},{2,3},{3,2},{4,5},{5,4},{6,7},{7,6},{8,9},{9,8},{10,11... | collective-permute-start | bytes 98312 | tf_op jit(solution)/shard_map/ppermute | solution.py:252
  72.0 11.9 %collective-permute-start.29 = (bf16[128,128]{1,0:T(8,128)(2,1)S(1)}, bf16[128,128]{1,0:T(8,128)(2,1)S(1)}, u32[]{:S(2)}, u32[]{:S(2)}) collective-permute-start(bf16[128,128]{1,0:T(8,128)(2,1)S(1)} %get-tuple-element.106), channel_id=1, source_target_pairs={{1,2},{2,1},{3,4},{4,3},{5,6},{6,5},{7,8},{8,7},{9,10},{10,9},{11,... | collective-permute-start | bytes 98312 | tf_op jit(solution)/shard_map/ppermute | solution.py:252
  75.5 7.4 %collective-permute-start.31 = (bf16[64,128]{1,0:T(8,128)(2,1)S(1)}, bf16[64,128]{1,0:T(8,128)(2,1)S(1)}, u32[]{:S(2)}, u32[]{:S(2)}) collective-permute-start(bf16[64,128]{1,0:T(8,128)(2,1)S(1)} %get-tuple-element.108), channel_id=1, source_target_pairs={{2,4},{4,2},{3,5},{5,3},{6,8},{8,6},{7,9},{9,7},{10,12},{12,10},{1... | collective-permute-start | bytes 49160 | tf_op jit(solution)/shard_map/ppermute | solution.py:252
  77.5 5.5 %collective-permute-start.32 = (bf16[64,128]{1,0:T(8,128)(2,1)S(1)}, bf16[64,128]{1,0:T(8,128)(2,1)S(1)}, u32[]{:S(2)}, u32[]{:S(2)}) collective-permute-start(bf16[64,128]{1,0:T(8,128)(2,1)S(1)} %get-tuple-element.109), channel_id=1, source_target_pairs={{0,4},{4,0},{1,5},{5,1},{2,6},{6,2},{3,7},{7,3},{8,12},{12,8},{9,1... | collective-permute-start | bytes 49160 | tf_op jit(solution)/shard_map/ppermute | solution.py:252
  77.5 6.4 %collective-permute-start.33 = (bf16[64,128]{1,0:T(8,128)(2,1)S(1)}, bf16[64,128]{1,0:T(8,128)(2,1)S(1)}, u32[]{:S(2)}, u32[]{:S(2)}) collective-permute-start(bf16[64,128]{1,0:T(8,128)(2,1)S(1)} %get-tuple-element.110), channel_id=1, source_target_pairs={{4,8},{8,4},{5,9},{9,5},{6,10},{10,6},{7,11},{11,7},{12,16},{16,12... | collective-permute-start | bytes 49160 | tf_op jit(solution)/shard_map/ppermute | solution.py:252
  85.3 5.9 %collective-permute-start.36 = (bf16[64,128]{1,0:T(8,128)(2,1)S(1)}, bf16[64,128]{1,0:T(8,128)(2,1)S(1)}, u32[]{:S(2)}, u32[]{:S(2)}) collective-permute-start(bf16[64,128]{1,0:T(8,128)(2,1)S(1)} %get-tuple-element.115), channel_id=1, source_target_pairs={{0,2},{2,0},{1,3},{3,1},{4,6},{6,4},{5,7},{7,5},{8,10},{10,8},{9,1... | collective-permute-start | bytes 49160 | tf_op jit(solution)/shard_map/ppermute | solution.py:252
  85.7 11.9 %collective-permute-start.34 = (bf16[128,128]{1,0:T(8,128)(2,1)S(1)}, bf16[128,128]{1,0:T(8,128)(2,1)S(1)}, u32[]{:S(2)}, u32[]{:S(2)}) collective-permute-start(bf16[128,128]{1,0:T(8,128)(2,1)S(1)} %get-tuple-element.113), channel_id=1, source_target_pairs={{0,1},{1,0},{2,3},{3,2},{4,5},{5,4},{6,7},{7,6},{8,9},{9,8},{10,11... | collective-permute-start | bytes 98312 | tf_op jit(solution)/shard_map/ppermute | solution.py:252
  85.7 11.9 %collective-permute-start.35 = (bf16[128,128]{1,0:T(8,128)(2,1)S(1)}, bf16[128,128]{1,0:T(8,128)(2,1)S(1)}, u32[]{:S(2)}, u32[]{:S(2)}) collective-permute-start(bf16[128,128]{1,0:T(8,128)(2,1)S(1)} %get-tuple-element.114), channel_id=1, source_target_pairs={{1,2},{2,1},{3,4},{4,3},{5,6},{6,5},{7,8},{8,7},{9,10},{10,9},{11,... | collective-permute-start | bytes 98312 | tf_op jit(solution)/shard_map/ppermute | solution.py:252
  89.2 7.4 %collective-permute-start.37 = (bf16[64,128]{1,0:T(8,128)(2,1)S(1)}, bf16[64,128]{1,0:T(8,128)(2,1)S(1)}, u32[]{:S(2)}, u32[]{:S(2)}) collective-permute-start(bf16[64,128]{1,0:T(8,128)(2,1)S(1)} %get-tuple-element.116), channel_id=1, source_target_pairs={{2,4},{4,2},{3,5},{5,3},{6,8},{8,6},{7,9},{9,7},{10,12},{12,10},{1... | collective-permute-start | bytes 49160 | tf_op jit(solution)/shard_map/ppermute | solution.py:252
  91.2 5.5 %collective-permute-start.38 = (bf16[64,128]{1,0:T(8,128)(2,1)S(1)}, bf16[64,128]{1,0:T(8,128)(2,1)S(1)}, u32[]{:S(2)}, u32[]{:S(2)}) collective-permute-start(bf16[64,128]{1,0:T(8,128)(2,1)S(1)} %get-tuple-element.117), channel_id=1, source_target_pairs={{0,4},{4,0},{1,5},{5,1},{2,6},{6,2},{3,7},{7,3},{8,12},{12,8},{9,1... | collective-permute-start | bytes 49160 | tf_op jit(solution)/shard_map/ppermute | solution.py:252
  91.2 6.4 %collective-permute-start.39 = (bf16[64,128]{1,0:T(8,128)(2,1)S(1)}, bf16[64,128]{1,0:T(8,128)(2,1)S(1)}, u32[]{:S(2)}, u32[]{:S(2)}) collective-permute-start(bf16[64,128]{1,0:T(8,128)(2,1)S(1)} %get-tuple-element.118), channel_id=1, source_target_pairs={{4,8},{8,4},{5,9},{9,5},{6,10},{10,6},{7,11},{11,7},{12,16},{16,12... | collective-permute-start | bytes 49160 | tf_op jit(solution)/shard_map/ppermute | solution.py:252
  98.8 5.9 %collective-permute-start.42 = (bf16[64,128]{1,0:T(8,128)(2,1)S(1)}, bf16[64,128]{1,0:T(8,128)(2,1)S(1)}, u32[]{:S(2)}, u32[]{:S(2)}) collective-permute-start(bf16[64,128]{1,0:T(8,128)(2,1)S(1)} %get-tuple-element.123), channel_id=1, source_target_pairs={{0,2},{2,0},{1,3},{3,1},{4,6},{6,4},{5,7},{7,5},{8,10},{10,8},{9,1... | collective-permute-start | bytes 49160 | tf_op jit(solution)/shard_map/ppermute | solution.py:252
  99.2 11.9 %collective-permute-start.40 = (bf16[128,128]{1,0:T(8,128)(2,1)S(1)}, bf16[128,128]{1,0:T(8,128)(2,1)S(1)}, u32[]{:S(2)}, u32[]{:S(2)}) collective-permute-start(bf16[128,128]{1,0:T(8,128)(2,1)S(1)} %get-tuple-element.121), channel_id=1, source_target_pairs={{0,1},{1,0},{2,3},{3,2},{4,5},{5,4},{6,7},{7,6},{8,9},{9,8},{10,11... | collective-permute-start | bytes 98312 | tf_op jit(solution)/shard_map/ppermute | solution.py:252
  99.2 11.9 %collective-permute-start.41 = (bf16[128,128]{1,0:T(8,128)(2,1)S(1)}, bf16[128,128]{1,0:T(8,128)(2,1)S(1)}, u32[]{:S(2)}, u32[]{:S(2)}) collective-permute-start(bf16[128,128]{1,0:T(8,128)(2,1)S(1)} %get-tuple-element.122), channel_id=1, source_target_pairs={{1,2},{2,1},{3,4},{4,3},{5,6},{6,5},{7,8},{8,7},{9,10},{10,9},{11,... | collective-permute-start | bytes 98312 | tf_op jit(solution)/shard_map/ppermute | solution.py:252
  102.7 7.4 %collective-permute-start.43 = (bf16[64,128]{1,0:T(8,128)(2,1)S(1)}, bf16[64,128]{1,0:T(8,128)(2,1)S(1)}, u32[]{:S(2)}, u32[]{:S(2)}) collective-permute-start(bf16[64,128]{1,0:T(8,128)(2,1)S(1)} %get-tuple-element.124), channel_id=1, source_target_pairs={{2,4},{4,2},{3,5},{5,3},{6,8},{8,6},{7,9},{9,7},{10,12},{12,10},{1... | collective-permute-start | bytes 49160 | tf_op jit(solution)/shard_map/ppermute | solution.py:252
  104.7 5.5 %collective-permute-start.44 = (bf16[64,128]{1,0:T(8,128)(2,1)S(1)}, bf16[64,128]{1,0:T(8,128)(2,1)S(1)}, u32[]{:S(2)}, u32[]{:S(2)}) collective-permute-start(bf16[64,128]{1,0:T(8,128)(2,1)S(1)} %get-tuple-element.125), channel_id=1, source_target_pairs={{0,4},{4,0},{1,5},{5,1},{2,6},{6,2},{3,7},{7,3},{8,12},{12,8},{9,1... | collective-permute-start | bytes 49160 | tf_op jit(solution)/shard_map/ppermute | solution.py:252
  104.7 6.4 %collective-permute-start.45 = (bf16[64,128]{1,0:T(8,128)(2,1)S(1)}, bf16[64,128]{1,0:T(8,128)(2,1)S(1)}, u32[]{:S(2)}, u32[]{:S(2)}) collective-permute-start(bf16[64,128]{1,0:T(8,128)(2,1)S(1)} %get-tuple-element.126), channel_id=1, source_target_pairs={{4,8},{8,4},{5,9},{9,5},{6,10},{10,6},{7,11},{11,7},{12,16},{16,12... | collective-permute-start | bytes 49160 | tf_op jit(solution)/shard_map/ppermute | solution.py:252
  113.1 5.8 %collective-permute-start.48 = (bf16[64,128]{1,0:T(8,128)(2,1)S(1)}, bf16[64,128]{1,0:T(8,128)(2,1)S(1)}, u32[]{:S(2)}, u32[]{:S(2)}) collective-permute-start(bf16[64,128]{1,0:T(8,128)(2,1)S(1)} %get-tuple-element.131), channel_id=1, source_target_pairs={{0,2},{2,0},{1,3},{3,1},{4,6},{6,4},{5,7},{7,5},{8,10},{10,8},{9,1... | collective-permute-start | bytes 49160 | tf_op jit(solution)/shard_map/ppermute | solution.py:252
  113.5 11.9 %collective-permute-start.46 = (bf16[128,128]{1,0:T(8,128)(2,1)S(1)}, bf16[128,128]{1,0:T(8,128)(2,1)S(1)}, u32[]{:S(2)}, u32[]{:S(2)}) collective-permute-start(bf16[128,128]{1,0:T(8,128)(2,1)S(1)} %get-tuple-element.129), channel_id=1, source_target_pairs={{0,1},{1,0},{2,3},{3,2},{4,5},{5,4},{6,7},{7,6},{8,9},{9,8},{10,11... | collective-permute-start | bytes 98312 | tf_op jit(solution)/shard_map/ppermute | solution.py:252
  113.5 11.9 %collective-permute-start.47 = (bf16[128,128]{1,0:T(8,128)(2,1)S(1)}, bf16[128,128]{1,0:T(8,128)(2,1)S(1)}, u32[]{:S(2)}, u32[]{:S(2)}) collective-permute-start(bf16[128,128]{1,0:T(8,128)(2,1)S(1)} %get-tuple-element.130), channel_id=1, source_target_pairs={{1,2},{2,1},{3,4},{4,3},{5,6},{6,5},{7,8},{8,7},{9,10},{10,9},{11,... | collective-permute-start | bytes 98312 | tf_op jit(solution)/shard_map/ppermute | solution.py:252
  116.9 7.3 %collective-permute-start.49 = (bf16[64,128]{1,0:T(8,128)(2,1)S(1)}, bf16[64,128]{1,0:T(8,128)(2,1)S(1)}, u32[]{:S(2)}, u32[]{:S(2)}) collective-permute-start(bf16[64,128]{1,0:T(8,128)(2,1)S(1)} %get-tuple-element.132), channel_id=1, source_target_pairs={{2,4},{4,2},{3,5},{5,3},{6,8},{8,6},{7,9},{9,7},{10,12},{12,10},{1... | collective-permute-start | bytes 49160 | tf_op jit(solution)/shard_map/ppermute | solution.py:252
  119.0 5.3 %collective-permute-start.50 = (bf16[64,128]{1,0:T(8,128)(2,1)S(1)}, bf16[64,128]{1,0:T(8,128)(2,1)S(1)}, u32[]{:S(2)}, u32[]{:S(2)}) collective-permute-start(bf16[64,128]{1,0:T(8,128)(2,1)S(1)} %get-tuple-element.133), channel_id=1, source_target_pairs={{0,4},{4,0},{1,5},{5,1},{2,6},{6,2},{3,7},{7,3},{8,12},{12,8},{9,1... | collective-permute-start | bytes 49160 | tf_op jit(solution)/shard_map/ppermute | solution.py:252
  119.0 6.4 %collective-permute-start.51 = (bf16[64,128]{1,0:T(8,128)(2,1)S(1)}, bf16[64,128]{1,0:T(8,128)(2,1)S(1)}, u32[]{:S(2)}, u32[]{:S(2)}) collective-permute-start(bf16[64,128]{1,0:T(8,128)(2,1)S(1)} %get-tuple-element.134), channel_id=1, source_target_pairs={{4,8},{8,4},{5,9},{9,5},{6,10},{10,6},{7,11},{11,7},{12,16},{16,12... | collective-permute-start | bytes 49160 | tf_op jit(solution)/shard_map/ppermute | solution.py:252
  127.3 1.3 collective-permute-start.52
  128.6 5.8 %collective-permute-start.55 = (f32[128,128]{0,1:T(8,128)S(1)}, f32[128,128]{0,1:T(8,128)S(1)}, u32[]{:S(2)}, u32[]{:S(2)}) collective-permute-start(f32[128,128]{0,1:T(8,128)S(1)} %add.56), channel_id=1, source_target_pairs={{0,6},{1,7},{2,4},{3,5},{4,2},{5,3},{6,0},{7,1},{8,14},{9,15},{10,... | collective-permute-start | bytes 196616 | tf_op jit(solution)/shard_map/ppermute | solution.py:241
  128.7 5.7 %collective-permute-start.54 = (f32[128,128]{0,1:T(8,128)S(1)}, f32[128,128]{0,1:T(8,128)S(1)}, u32[]{:S(2)}, u32[]{:S(2)}) collective-permute-start(f32[128,128]{0,1:T(8,128)S(1)} %add.56), channel_id=1, source_target_pairs={{0,4},{1,5},{2,6},{3,7},{4,0},{5,1},{6,2},{7,3},{8,12},{9,13},{10,... | collective-permute-start | bytes 196616 | tf_op jit(solution)/shard_map/ppermute | solution.py:241
  130.5 4.3 %collective-permute-start.53 = (f32[128,128]{0,1:T(8,128)S(1)}, f32[128,128]{0,1:T(8,128)S(1)}, u32[]{:S(2)}, u32[]{:S(2)}) collective-permute-start(f32[128,128]{0,1:T(8,128)S(1)} %add.56), channel_id=1, source_target_pairs={{0,2},{1,3},{2,0},{3,1},{4,6},{5,7},{6,4},{7,5},{8,10},{9,11},{10,... | collective-permute-start | bytes 196616 | tf_op jit(solution)/shard_map/ppermute | solution.py:241
  134.8 6.7 %collective-permute-start.58 = (f32[128,128]{0,1:T(8,128)S(1)}, f32[128,128]{0,1:T(8,128)S(1)}, u32[]{:S(2)}, u32[]{:S(2)}) collective-permute-start(f32[128,128]{0,1:T(8,128)S(1)} %add_add_fusion.1), channel_id=1, source_target_pairs={{0,24},{1,25},{2,26},{3,27},{4,28},{5,29},{6,30},{7,31},{8,16},{9,... | collective-permute-start | bytes 196616 | tf_op jit(solution)/shard_map/ppermute | solution.py:241
  137.4 5.6 %collective-permute-start.57 = (f32[128,128]{0,1:T(8,128)S(1)}, f32[128,128]{0,1:T(8,128)S(1)}, u32[]{:S(2)}, u32[]{:S(2)}) collective-permute-start(f32[128,128]{0,1:T(8,128)S(1)} %add_add_fusion.1), channel_id=1, source_target_pairs={{0,16},{1,17},{2,18},{3,19},{4,20},{5,21},{6,22},{7,23},{8,24},{9,... | collective-permute-start | bytes 196616 | tf_op jit(solution)/shard_map/ppermute | solution.py:241
  137.4 5.6 %collective-permute-start.56 = (f32[128,128]{0,1:T(8,128)S(1)}, f32[128,128]{0,1:T(8,128)S(1)}, u32[]{:S(2)}, u32[]{:S(2)}) collective-permute-start(f32[128,128]{0,1:T(8,128)S(1)} %add_add_fusion.1), channel_id=1, source_target_pairs={{0,8},{1,9},{2,10},{3,11},{4,12},{5,13},{6,14},{7,15},{8,0},{9,1},... | collective-permute-start | bytes 196616 | tf_op jit(solution)/shard_map/ppermute | solution.py:241
where the time goes:
time: 168 us
  starting transfers between devices  66.8 us (40%)
  waiting for transfers between devices  54.1 us (32%)
  other arithmetic  25.8 us (15%)
  Pallas kernels  15 us (9%)
  local copies, waits for them, and re-layouts  4.11 us (2%)
  matrix products  1.94 us (1%)
    ppermute x52, starting transfers between devices, swap(): return lax.ppermute(value, AXES, swap_pairs(count, by, odd))  58.8 us
    ppermute x52, waiting for transfers between devices, swap(): return lax.ppermute(value, AXES, swap_pairs(count, by, odd))  46.4 us
    another operation x3, other arithmetic, local(): factor = jnp.linalg.cholesky(summed(gram, count))  12.4 us
    another operation x2, other arithmetic, local(): basis = jax.scipy.linalg.solve_triangular(factor, filtered.T, lower=True).T  10.5 us
    pallas_call x7, Pallas kernels, step(): pl.pallas_call(lambda *refs: step_kernel(scale, has_prev, *refs), out_sha...  9.15 us
    ppermute x7, starting transfers between devices, summed(): lax.ppermute(value, AXES, [(i, i ^ mask) for i in range(count)])  8.07 us
    ppermute x7, waiting for transfers between devices, summed(): lax.ppermute(value, AXES, [(i, i ^ mask) for i in range(count)])  7.63 us
    unnamed x10, local copies, waits for them, and re-layouts  3.94 us
  transfers between devices with their start and end apart: 59, of which 21 were waited for; matrix products, arithmetic and copies ran while one was open for 1% of the time, Pallas kernels for 2%

commit v1 on v0

v1 whole, which is shorter than its diff:
```python
import math

import jax
import jax.numpy as jnp
from jax import lax
from jax.experimental import pallas as pl
from jax.experimental.pallas import tpu as pltpu
from jax.sharding import PartitionSpec as P

VECS = 128
BLK = 128
KB = 8
PEERS = 4
CAP = 64
DEGREE = 8
HALF_WIDTH = 0.95
AXES = ("row", "snk")
FAR = (2, 4)
LINKS = ((4, 1), (2, 1), (1, 1), (4, 0), (2, 0), (1, 0))
FAR_LINKS = tuple((by, odd) for by in FAR for odd in (0, 1))
BF16 = jnp.bfloat16
F32 = jnp.float32
VMEM = pl.BlockSpec(memory_space=pltpu.VMEM)
ANY = pl.BlockSpec(memory_space=pl.ANY)
SMEM = pl.BlockSpec(memory_space=pltpu.SMEM)
PARAMS = pltpu.CompilerParams(vmem_limit_bytes=24 * 1024 * 1024)


def swap_pairs(count, by, odd):
    pairs = []
    for low in range(count):
        if (low // by) % 2 == odd:
            high = (low + by) % count
            pairs += [(low, high), (high, low)]
    return pairs


def split3(value):
    high = value.astype(BF16)
    rest = value - high.astype(F32)
    mid = rest.astype(BF16)
    low = (rest - mid.astype(F32)).astype(BF16)
    return high, mid, low


def stacked(value, height):
    parts = split3(value)
    pad = jnp.zeros((height - 3, value.shape[1]), BF16)
    return jnp.concatenate([*parts, pad], axis=0)


def dot(a, b, dims, precision=None):
    return lax.dot_general(
        a, b, (dims, ((), ())), precision=precision, preferred_element_type=F32
    )


def is_low(place_ref, by):
    return lax.rem(lax.div(place_ref[0], by), 2) == 0


def turned(row):
    half = row.shape[1] // 2
    return jnp.concatenate([row[:, half:], row[:, :half]], axis=1)


def by_link(place_ref, row):
    parts = []
    for i, by in enumerate(FAR):
        pair = row[:, 2 * CAP * i : 2 * CAP * (i + 1)]
        parts.append(jnp.where(is_low(place_ref, by), pair, turned(pair)))
    return jnp.concatenate(parts, axis=1)


def as_columns(row):
    return jnp.broadcast_to(row, (row.shape[1], row.shape[1])).T


def prepare_kernel(
    place_ref, cols_any, wts_any, dst_ref, far_ref, band_ref, hot_ref, coef_ref, cols_ref, wts_ref, sems
):
    copies = [
        pltpu.make_async_copy(cols_any, cols_ref, sems.at[0]),
        pltpu.make_async_copy(wts_any, wts_ref, sems.at[1]),
    ]
    for copy in copies:
        copy.start()
    rows = cols_ref.shape[2]
    edges = dst_ref.shape[1]
    dst = by_link(place_ref, dst_ref[...])
    far = by_link(place_ref, far_ref[...])
    for b in range(rows // BLK):
        ids = lax.broadcasted_iota(jnp.int32, (BLK, edges), 0) + b * BLK
        hot_ref[pl.ds(b * BLK, BLK), :] = jnp.where(ids == dst, 1.0, 0.0).astype(BF16)
    hot = hot_ref[...]
    degree = jnp.sum(dot(stacked(far, 16), hot, ((1,), (1,))), axis=0, keepdims=True)
    for copy in copies:
        copy.wait()
    for o in range(3):
        degree = degree + jnp.sum(wts_ref[o], axis=0, keepdims=True)
    at_edge = jnp.sum(dot(stacked(degree, 16), hot, ((1,), (0,))), axis=0, keepdims=True)
    far_coef = far / at_edge
    for i in range(edges // BLK):
        coef_ref[pl.ds(i * BLK, BLK), :] = as_columns(far_coef[:, i * BLK : (i + 1) * BLK])
    ids = lax.broadcasted_iota(jnp.int32, (BLK, BLK), 0)
    for b in range(rows // BLK):
        block = pl.ds(b * BLK, BLK)
        degree_b = degree[:, b * BLK : (b + 1) * BLK]
        for o in range(3):
            cols = cols_ref[o, :, block]
            coef = (wts_ref[o, :, block] / degree_b).astype(BF16).astype(F32)
            dense = jnp.zeros((BLK, BLK), F32)
            for k in range(KB):
                dense = jnp.where(ids == cols[k : k + 1, :], coef[k : k + 1, :], dense)
            band_ref[block, pl.ds(o * BLK, BLK)] = dense.T.astype(BF16)


def prepare(place, cols, wts, dst, far):
    rows, edges = cols.shape[2], dst.shape[1]
    return pl.pallas_call(
        prepare_kernel,
        out_shape=(
            jax.ShapeDtypeStruct((rows, 3 * BLK), BF16),
            jax.ShapeDtypeStruct((rows, edges), BF16),
            jax.ShapeDtypeStruct((edges, VECS), F32),
        ),
        in_specs=[SMEM, ANY, ANY, VMEM, VMEM],
        out_specs=(VMEM,) * 3,
        scratch_shapes=[
            pltpu.VMEM(cols.shape, jnp.int32),
            pltpu.VMEM(wts.shape, F32),
            pltpu.SemaphoreType.DMA((2,)),
        ],
        compiler_params=PARAMS,
        name="prepare",
    )(place, cols, wts, dst, far)


def send_out(even, first, last, picked, sent):
    sent = dict(zip(LINKS, sent, strict=True))
    sent[1, 0][...] = jnp.where(even, last, first)
    sent[1, 1][...] = jnp.where(even, first, last)
    for g, link in enumerate(FAR_LINKS):
        sent[link][:CAP, :] = picked[g * CAP : (g + 1) * CAP].astype(BF16)


def first_kernel(place_ref, field_ref, w0, w1, w2, w3, pick_mat_ref, *sent):
    rows = field_ref.shape[0]
    half = 2 * CAP
    lanes = lax.broadcasted_iota(jnp.int32, (1, half), 1)
    for i, (by, pair) in enumerate(zip(FAR, ((w0, w1), (w2, w3)), strict=True)):
        ahead, back = (w[:, i * half : (i + 1) * half] for w in pair)
        low = is_low(place_ref, by)
        ahead = jnp.where(low, turned(ahead), ahead)
        back = jnp.where(low, turned(back), back)
        wanted = jnp.where(lanes < CAP, ahead, back)
        column = as_columns(wanted.astype(F32))
        for b in range(rows // BLK):
            ids = lax.broadcasted_iota(jnp.int32, (half, BLK), 1) + b * BLK
            hot = jnp.where(column == ids.astype(F32), 1.0, 0.0).astype(BF16)
            pick_mat_ref[pl.ds(i * half, half), pl.ds(b * BLK, BLK)] = hot
    field = field_ref[...]
    picked = dot(pick_mat_ref[...], field, ((1,), (0,)))
    send_out(is_low(place_ref, 1), field[:BLK], field[rows - BLK :], picked, sent)


SENT = tuple(jax.ShapeDtypeStruct((BLK, VECS), BF16) for _ in LINKS)


def first(place, field, wanted):
    rows = field.shape[0]
    return pl.pallas_call(
        first_kernel,
        out_shape=(jax.ShapeDtypeStruct((PEERS * CAP, rows), BF16), *SENT),
        in_specs=[SMEM] + [VMEM] * 5,
        out_specs=(VMEM,) * 7,
        compiler_params=PARAMS,
        name="first",
    )(place, field, *wanted)


def advance(place_ref, band_ref, hot_ref, coef_ref, field_ref, prev_ref, got, scale, store):
    rows = field_ref.shape[0]
    count = rows // BLK
    even = is_low(place_ref, 1)
    got = dict(zip(LINKS, got, strict=True))
    low = jnp.where(even, got[1, 1][...], got[1, 0][...])
    high = jnp.where(even, got[1, 0][...], got[1, 1][...])
    far = jnp.concatenate([got[link][:CAP, :] for link in FAR_LINKS], axis=0)
    far = far.astype(F32) * coef_ref[...]
    far_high = far.astype(BF16)
    far_low = (far - far_high.astype(F32)).astype(BF16)
    for b in range(count):
        block = pl.ds(b * BLK, BLK)
        total = dot(hot_ref[block, :], far_high, ((1,), (0,)))
        total += dot(hot_ref[block, :], far_low, ((1,), (0,)))
        if b == 0:
            total += dot(band_ref[block, :BLK], low, ((1,), (0,)))
            total += dot(band_ref[block, BLK:], field_ref[: 2 * BLK, :], ((1,), (0,)))
        elif b == count - 1:
            total += dot(
                band_ref[block, : 2 * BLK], field_ref[rows - 2 * BLK :, :], ((1,), (0,))
            )
            total += dot(band_ref[block, 2 * BLK :], high, ((1,), (0,)))
        else:
            total += dot(
                band_ref[block, :], field_ref[pl.ds((b - 1) * BLK, 3 * BLK), :], ((1,), (0,))
            )
        value = total * scale
        if prev_ref is not None:
            value = value - prev_ref[block, :].astype(F32)
        store(block, value)
    return even


def step_kernel(scale, has_prev, *refs):
    place_ref, band_ref, hot_ref, coef_ref, pick_mat_ref, field_ref = refs[:6]
    refs = refs[6:]
    prev_ref = None
    if has_prev:
        prev_ref, refs = refs[0], refs[1:]
    got, refs = refs[:6], refs[6:]
    next_ref, packed_ref, sent = refs[0], refs[1], refs[2:]

    def store(block, value):
        next_ref[block, :] = value
        packed_ref[block, :] = value.astype(BF16)

    even = advance(
        place_ref, band_ref, hot_ref, coef_ref, field_ref, prev_ref, got, scale, store
    )
    rows = field_ref.shape[0]
    picked = dot(pick_mat_ref[...], packed_ref[...], ((1,), (0,)))
    send_out(even, packed_ref[:BLK, :], packed_ref[rows - BLK :, :], picked, sent)


def step(scale, place, mats, field, prev, got):
    rows = field.shape[0]
    has_prev = prev is not None
    before = (prev,) if has_prev else ()
    return pl.pallas_call(
        lambda *refs: step_kernel(scale, has_prev, *refs),
        out_shape=(
            jax.ShapeDtypeStruct((rows, VECS), F32),
            jax.ShapeDtypeStruct((rows, VECS), BF16),
            *SENT,
        ),
        in_specs=[SMEM] + [VMEM] * (11 + len(before)),
        out_specs=(VMEM,) * 8,
        compiler_params=PARAMS,
        name="step",
    )(place, *mats, field, *before, *got)


def last_kernel(scale, *refs):
    place_ref, band_ref, hot_ref, coef_ref, field_ref, prev_ref = refs[:6]
    got, (next_ref, gram_ref) = refs[6:12], refs[12:]

    def store(block, value):
        next_ref[block, :] = value

    advance(
        place_ref, band_ref, hot_ref, coef_ref, field_ref, prev_ref, got, scale, store
    )
    value = next_ref[...]
    gram_ref[...] = dot(value, value, ((0,), (0,)), lax.Precision.HIGHEST)


def last(scale, place, mats, field, prev, got):
    rows = field.shape[0]
    return pl.pallas_call(
        lambda *refs: last_kernel(scale, *refs),
        out_shape=(
            jax.ShapeDtypeStruct((rows, VECS), F32),
            jax.ShapeDtypeStruct((VECS, VECS), F32),
        ),
        in_specs=[SMEM] + [VMEM] * 11,
        out_specs=(VMEM, VMEM),
        compiler_params=PARAMS,
        name="last",
    )(place, *mats, field, prev, *got)


def finish_kernel(scale, gram_ref, field_ref, out_ref, inverse_ref):
    height = 8
    count = VECS // height
    ids = lax.broadcasted_iota(jnp.int32, (height, VECS), 0)
    lanes = lax.broadcasted_iota(jnp.int32, (height, VECS), 1)
    left = [gram_ref[height * b : height * (b + 1), :] for b in range(count)]
    right = [jnp.where(ids + height * b == lanes, 1.0, 0.0) for b in range(count)]
    for j in range(VECS):
        own, at = divmod(j, height)
        row, row_right = left[own][at : at + 1, :], right[own][at : at + 1, :]
        pivot = row[:, j : j + 1]
        inverse_ref[j : j + 1, :] = row_right * (lax.rsqrt(pivot) * scale)
        by_pivot = 1.0 / pivot
        row, row_right = row * by_pivot, row_right * by_pivot
        for b in range(own + (at == height - 1), count):
            factor = left[b][:, j : j + 1]
            if b == own:
                factor = jnp.where(ids[:, :1] > at, factor, 0.0)
            left[b] = left[b] - factor * row
            right[b] = right[b] - factor * row_right
    out_ref[...] = dot(field_ref[...], inverse_ref[...], ((1,), (1,)), lax.Precision.HIGHEST)


def finish(scale, gram, field):
    return pl.pallas_call(
        lambda *refs: finish_kernel(scale, *refs),
        out_shape=jax.ShapeDtypeStruct(field.shape, F32),
        in_specs=[VMEM] * 2,
        out_specs=VMEM,
        scratch_shapes=[pltpu.VMEM((VECS, VECS), F32)],
        compiler_params=PARAMS,
        name="finish",
    )(gram, field)


def summed(value, count):
    bits = [1 << i for i in range(count.bit_length() - 1)]
    stages = [bits[:1]] + [bits[i : i + 2] for i in range(1, len(bits), 2)]
    for stage in stages:
        masks = [stage[0]] if len(stage) == 1 else [*stage, stage[0] ^ stage[1]]
        total = value
        for mask in masks:
            total = total + lax.ppermute(value, AXES, [(i, i ^ mask) for i in range(count)])
        value = total
    return value


def local(start_basis, band_cols, band_wts, far_dst, far_src, far_wts):
    count = lax.axis_size(AXES)
    place = lax.axis_index(AXES)
    total_rows = start_basis.shape[0] * count

    def swap(value, by, odd):
        return lax.ppermute(value, AXES, swap_pairs(count, by, odd))

    def as_row(value):
        return value.reshape(1, -1)

    asked = as_row(far_src)
    wanted = [swap(asked, *link) for link in FAR_LINKS]
    here = place.astype(jnp.int32).reshape(1)
    band, hot, coef = prepare(
        here,
        jnp.transpose(band_cols, (1, 2, 0)),
        jnp.transpose(band_wts, (1, 2, 0)),
        as_row(far_dst),
        as_row(far_wts),
    )
    wanted, band = lax.optimization_barrier((wanted, band))
    pick_mat, *sent = first(here, start_basis, wanted)

    def exchange(sent):
        return [swap(v, *link) for v, link in zip(sent, LINKS, strict=True)]

    previous, packed = start_basis, start_basis
    mats = (band, hot, coef, pick_mat)
    got = exchange(sent)
    current, packed, *sent = step(1.0 / HALF_WIDTH, here, mats, packed, None, got)
    for _ in range(DEGREE - 2):
        got = exchange(sent)
        following, packed, *sent = step(2.0 / HALF_WIDTH, here, mats, packed, previous, got)
        previous, current = current, following
    got = exchange(sent)
    filtered, gram = last(2.0 / HALF_WIDTH, here, mats[:3], packed, previous, got)
    return finish(math.sqrt(total_rows), summed(gram, count), filtered)


def solution(mesh):
    placed = (
        P(AXES, None),
        P(AXES, None, None),
        P(AXES, None, None),
        P(AXES),
        P(AXES),
        P(AXES),
    )
    return jax.shard_map(
        local, mesh=mesh, in_specs=placed, out_specs=P(AXES, None), check_vma=False
    )
```

time: 168 us -> 145 us (0.86)
  other arithmetic: 25.8 us -> 0.04 us
  Pallas kernels: 15 us -> 30.3 us
  waiting for transfers between devices: 54.1 us -> 44.8 us
  starting transfers between devices: 66.8 us -> 64.8 us
  matrix products: 1.94 us -> 0 us
    another operation x5 -> x0, other arithmetic: 22.9 us -> none  [the longest x3 12.4 us: local(): factor = jnp.linalg.cholesky(summed(gram, count))]
    pallas_call x0 -> x1, Pallas kernels: none -> 12.7 us  [finish(): pl.pallas_call(lambda *refs: finish_kernel(scale, *refs), out_shape=jax.S...]
    ppermute x52, waiting for transfers between devices: 46.4 us -> 37.3 us  [swap(): return lax.ppermute(value, AXES, swap_pairs(count, by, odd))]
    select_n x3 -> x0, other arithmetic: 2.7 us -> none  [by_swap(): ordered += [jnp.where(even, ahead, back), jnp.where(even, back, ahead)]]
    ppermute x52, starting transfers between devices: 58.8 us -> 56.7 us  [swap(): return lax.ppermute(value, AXES, swap_pairs(count, by, odd))]
    another operation x1 -> x0, matrix products: 1.94 us -> none  [local(): basis = jax.scipy.linalg.solve_triangular(factor, filtered.T, lower=True).T]
  transfers between devices with their start and end apart: 59 -> 59, of which waited for: 21 -> 30; matrix products, arithmetic and copies ran while one was open for 1% -> 0% of each run, Pallas kernels for 2% -> 3%
where the time goes in v1:
time: 145 us; the launch traced here: 144 us
  starting transfers between devices  64.8 us (45%)
  waiting for transfers between devices  44.8 us (31%)
  Pallas kernels  30.3 us (21%)
  local copies, waits for them, and re-layouts  4.25 us (3%)
    ppermute x52, starting transfers between devices, swap(): return lax.ppermute(value, AXES, swap_pairs(count, by, odd))  56.7 us
    ppermute x52, waiting for transfers between devices, swap(): return lax.ppermute(value, AXES, swap_pairs(count, by, odd))  37.3 us
    pallas_call x1, Pallas kernels, finish(): pl.pallas_call(lambda *refs: finish_kernel(scale, *refs), out_shape=jax.S...  12.7 us
    pallas_call x7, Pallas kernels, step(): pl.pallas_call(lambda *refs: step_kernel(scale, has_prev, *refs), out_sha...  10.8 us
    ppermute x7, starting transfers between devices, summed(): lax.ppermute(value, AXES, [(i, i ^ mask) for i in range(count)])  8.07 us
    ppermute x7, waiting for transfers between devices, summed(): lax.ppermute(value, AXES, [(i, i ^ mask) for i in range(count)])  7.42 us
    unnamed x10, local copies, waits for them, and re-layouts  4.25 us
    pallas_call x1, Pallas kernels, prepare(): pl.pallas_call(prepare_kernel, out_shape=(jax.ShapeDtypeStruct((rows, 3 *...  4.18 us
  transfers between devices with their start and end apart: 59, of which 30 were waited for; matrix products, arithmetic and copies ran while one was open for 0% of the time, Pallas kernels for 3%

profile of v1, /device:TPU:0, one launch (start us, length us, event | category | flops | bytes accessed | tf_op | source)
XLA Modules:
  0.0 144.3 jit_solution(7405156057387165353)
XLA Ops:
  0.0 6.0 %collective-permute-start.3 = (s32[1,256]{1,0:T(1,128)}, s32[1,256]{1,0:T(1,128)S(1)}, u32[]{:S(2)}, u32[]{:S(2)}) collective-permute-start(s32[1,256]{1,0:T(1,128)} %bitcast.10), channel_id=1, source_target_pairs={{4,8},{8,4},{5,9},{9,5},{6,10},{10,6},{7,11},{11,7},{12,16},{16,12... | collective-permute-start | bytes 3080 | tf_op jit(solution)/shard_map/ppermute | solution.py:337
  6.0 2.8 %collective-permute-start.1 = (s32[1,256]{1,0:T(1,128)}, s32[1,256]{1,0:T(1,128)S(1)}, u32[]{:S(2)}, u32[]{:S(2)}) collective-permute-start(s32[1,256]{1,0:T(1,128)} %bitcast.12), channel_id=1, source_target_pairs={{2,4},{4,2},{3,5},{5,3},{6,8},{8,6},{7,9},{9,7},{10,12},{12,10},{1... | collective-permute-start | bytes 3080 | tf_op jit(solution)/shard_map/ppermute | solution.py:337
  9.5 0.9 copy-done.1
  10.4 0.9 copy-done.2
  11.4 0.7 copy-done.3
  12.7 4.2 %prepare.1 = (bf16[2048,384]{1,0:T(8,128)(2,1)S(1)}, bf16[2048,256]{1,0:T(8,128)(2,1)S(1)}, f32[256,128]{1,0:T(8,128)S(1)}) custom-call(s32[1]{0:T(128)} %bitcast.place_ref.refs_0_, s32[3,8,2048]{2,1,0:T(8,128)S(1)} %bitcast.6, f32[3,8,2048]{2,1,0:T(8,128)S(1)} %bitcast.7, s32[1,256]{1,0:T(1,128)S(1)} %bitcast.8, f32[1,256]{1,0:T(1,128)S(1)} %bitcast.9), custom_call_target="tpu_custom_call" | custom-call | tf_op jit(solution)/shard_map/prepare/pallas_call | solution.py:120
  16.9 1.0 copy-done
  18.7 2.8 %collective-permute-start.4 = (bf16[128,128]{1,0:T(8,128)(2,1)S(1)}, bf16[128,128]{1,0:T(8,128)(2,1)S(1)}, u32[]{:S(2)}, u32[]{:S(2)}) collective-permute-start(bf16[128,128]{1,0:T(8,128)(2,1)S(1)} %get-tuple-element.86), channel_id=1, source_target_pairs={{4,8},{8,4},{5,9},{9,5},{6,10},{10,6},{7,11},{11,7},{12,16},{16,12... | collective-permute-start | bytes 98312 | tf_op jit(solution)/shard_map/ppermute | solution.py:337
  21.4 2.8 %collective-permute-start.5 = (bf16[128,128]{1,0:T(8,128)(2,1)S(1)}, bf16[128,128]{1,0:T(8,128)(2,1)S(1)}, u32[]{:S(2)}, u32[]{:S(2)}) collective-permute-start(bf16[128,128]{1,0:T(8,128)(2,1)S(1)} %get-tuple-element.87), channel_id=1, source_target_pairs={{2,4},{4,2},{3,5},{5,3},{6,8},{8,6},{7,9},{9,7},{10,12},{12,10},{1... | collective-permute-start | bytes 98312 | tf_op jit(solution)/shard_map/ppermute | solution.py:337
  24.3 0.8 collective-permute-start.6
  25.3 1.2 collective-permute-start.9
  26.5 2.4 %collective-permute-done.5.refs_7_ = bf16[128,128]{1,0:T(8,128)(2,1)S(1)} collective-permute-done((bf16[128,128]{1,0:T(8,128)(2,1)S(1)}, bf16[128,128]{1,0:T(8,128)(2,1)S(1)}, u32[]{:S(2)}, u32[]{:S(2)}) %collective-permute-start.5) | collective-permute-done | bytes 32800 | tf_op jit(solution)/shard_map/ppermute | solution.py:337
  29.0 2.2 %collective-permute-done.6.refs_8_ = bf16[128,128]{1,0:T(8,128)(2,1)S(1)} collective-permute-done((bf16[128,128]{1,0:T(8,128)(2,1)S(1)}, bf16[128,128]{1,0:T(8,128)(2,1)S(1)}, u32[]{:S(2)}, u32[]{:S(2)}) %collective-permute-start.6) | collective-permute-done | bytes 32800 | tf_op jit(solution)/shard_map/ppermute | solution.py:337
  31.2 1.4 step.7
  32.7 1.9 %collective-permute-start.11 = (bf16[128,128]{1,0:T(8,128)(2,1)S(1)}, bf16[128,128]{1,0:T(8,128)(2,1)S(1)}, u32[]{:S(2)}, u32[]{:S(2)}) collective-permute-start(bf16[128,128]{1,0:T(8,128)(2,1)S(1)} %get-tuple-element.94), channel_id=1, source_target_pairs={{2,4},{4,2},{3,5},{5,3},{6,8},{8,6},{7,9},{9,7},{10,12},{12,10},{1... | collective-permute-start | bytes 98312 | tf_op jit(solution)/shard_map/ppermute | solution.py:337
  34.6 3.1 %collective-permute-start.12 = (bf16[128,128]{1,0:T(8,128)(2,1)S(1)}, bf16[128,128]{1,0:T(8,128)(2,1)S(1)}, u32[]{:S(2)}, u32[]{:S(2)}) collective-permute-start(bf16[128,128]{1,0:T(8,128)(2,1)S(1)} %get-tuple-element.95), channel_id=1, source_target_pairs={{1,2},{2,1},{3,4},{4,3},{5,6},{6,5},{7,8},{8,7},{9,10},{10,9},{11,... | collective-permute-start | bytes 98312 | tf_op jit(solution)/shard_map/ppermute | solution.py:337
  37.7 1.9 %collective-permute-done.10.refs_7_ = bf16[128,128]{1,0:T(8,128)(2,1)S(1)} collective-permute-done((bf16[128,128]{1,0:T(8,128)(2,1)S(1)}, bf16[128,128]{1,0:T(8,128)(2,1)S(1)}, u32[]{:S(2)}, u32[]{:S(2)}) %collective-permute-start.10) | collective-permute-done | bytes 32800 | tf_op jit(solution)/shard_map/ppermute | solution.py:337
  40.3 1.3 collective-permute-done.12.refs_9_
  41.9 1.4 step.8
  43.4 0.9 collective-permute-start.16
  44.3 3.0 %collective-permute-start.17 = (bf16[128,128]{1,0:T(8,128)(2,1)S(1)}, bf16[128,128]{1,0:T(8,128)(2,1)S(1)}, u32[]{:S(2)}, u32[]{:S(2)}) collective-permute-start(bf16[128,128]{1,0:T(8,128)(2,1)S(1)} %get-tuple-element.102), channel_id=1, source_target_pairs={{2,4},{4,2},{3,5},{5,3},{6,8},{8,6},{7,9},{9,7},{10,12},{12,10},{1... | collective-permute-start | bytes 98312 | tf_op jit(solution)/shard_map/ppermute | solution.py:337
  47.3 2.4 %collective-permute-start.18 = (bf16[128,128]{1,0:T(8,128)(2,1)S(1)}, bf16[128,128]{1,0:T(8,128)(2,1)S(1)}, u32[]{:S(2)}, u32[]{:S(2)}) collective-permute-start(bf16[128,128]{1,0:T(8,128)(2,1)S(1)} %get-tuple-element.103), channel_id=1, source_target_pairs={{1,2},{2,1},{3,4},{4,3},{5,6},{6,5},{7,8},{8,7},{9,10},{10,9},{11,... | collective-permute-start | bytes 98312 | tf_op jit(solution)/shard_map/ppermute | solution.py:337
  50.0 1.8 %collective-permute-done.17.refs_8_ = bf16[128,128]{1,0:T(8,128)(2,1)S(1)} collective-permute-done((bf16[128,128]{1,0:T(8,128)(2,1)S(1)}, bf16[128,128]{1,0:T(8,128)(2,1)S(1)}, u32[]{:S(2)}, u32[]{:S(2)}) %collective-permute-start.17) | collective-permute-done | bytes 32800 | tf_op jit(solution)/shard_map/ppermute | solution.py:337
  51.8 2.4 %collective-permute-done.18.refs_9_ = bf16[128,128]{1,0:T(8,128)(2,1)S(1)} collective-permute-done((bf16[128,128]{1,0:T(8,128)(2,1)S(1)}, bf16[128,128]{1,0:T(8,128)(2,1)S(1)}, u32[]{:S(2)}, u32[]{:S(2)}) %collective-permute-start.18) | collective-permute-done | bytes 32800 | tf_op jit(solution)/shard_map/ppermute | solution.py:337
  54.2 1.4 step.9
  55.7 3.5 %collective-permute-start.23 = (bf16[128,128]{1,0:T(8,128)(2,1)S(1)}, bf16[128,128]{1,0:T(8,128)(2,1)S(1)}, u32[]{:S(2)}, u32[]{:S(2)}) collective-permute-start(bf16[128,128]{1,0:T(8,128)(2,1)S(1)} %get-tuple-element.110), channel_id=1, source_target_pairs={{2,4},{4,2},{3,5},{5,3},{6,8},{8,6},{7,9},{9,7},{10,12},{12,10},{1... | collective-permute-start | bytes 98312 | tf_op jit(solution)/shard_map/ppermute | solution.py:337
  59.2 1.5 %collective-permute-start.24 = (bf16[128,128]{1,0:T(8,128)(2,1)S(1)}, bf16[128,128]{1,0:T(8,128)(2,1)S(1)}, u32[]{:S(2)}, u32[]{:S(2)}) collective-permute-start(bf16[128,128]{1,0:T(8,128)(2,1)S(1)} %get-tuple-element.111), channel_id=1, source_target_pairs={{1,2},{2,1},{3,4},{4,3},{5,6},{6,5},{7,8},{8,7},{9,10},{10,9},{11,... | collective-permute-start | bytes 98312 | tf_op jit(solution)/shard_map/ppermute | solution.py:337
  60.8 0.9 collective-permute-start.26
  61.7 1.0 collective-permute-done.22.refs_7_
  62.7 0.7 collective-permute-done.23.refs_8_
  63.4 2.9 %collective-permute-done.24.refs_9_ = bf16[128,128]{1,0:T(8,128)(2,1)S(1)} collective-permute-done((bf16[128,128]{1,0:T(8,128)(2,1)S(1)}, bf16[128,128]{1,0:T(8,128)(2,1)S(1)}, u32[]{:S(2)}, u32[]{:S(2)}) %collective-permute-start.24) | collective-permute-done | bytes 32800 | tf_op jit(solution)/shard_map/ppermute | solution.py:337
  66.3 1.4 step.10
  67.8 3.5 %collective-permute-start.29 = (bf16[128,128]{1,0:T(8,128)(2,1)S(1)}, bf16[128,128]{1,0:T(8,128)(2,1)S(1)}, u32[]{:S(2)}, u32[]{:S(2)}) collective-permute-start(bf16[128,128]{1,0:T(8,128)(2,1)S(1)} %get-tuple-element.118), channel_id=1, source_target_pairs={{2,4},{4,2},{3,5},{5,3},{6,8},{8,6},{7,9},{9,7},{10,12},{12,10},{1... | collective-permute-start | bytes 98312 | tf_op jit(solution)/shard_map/ppermute | solution.py:337
  71.3 1.5 %collective-permute-start.30 = (bf16[128,128]{1,0:T(8,128)(2,1)S(1)}, bf16[128,128]{1,0:T(8,128)(2,1)S(1)}, u32[]{:S(2)}, u32[]{:S(2)}) collective-permute-start(bf16[128,128]{1,0:T(8,128)(2,1)S(1)} %get-tuple-element.119), channel_id=1, source_target_pairs={{1,2},{2,1},{3,4},{4,3},{5,6},{6,5},{7,8},{8,7},{9,10},{10,9},{11,... | collective-permute-start | bytes 98312 | tf_op jit(solution)/shard_map/ppermute | solution.py:337
  72.9 1.8 %collective-permute-done.28.refs_7_ = bf16[128,128]{1,0:T(8,128)(2,1)S(1)} collective-permute-done((bf16[128,128]{1,0:T(8,128)(2,1)S(1)}, bf16[128,128]{1,0:T(8,128)(2,1)S(1)}, u32[]{:S(2)}, u32[]{:S(2)}) %collective-permute-start.28) | collective-permute-done | bytes 32800 | tf_op jit(solution)/shard_map/ppermute | solution.py:337
  75.4 2.9 %collective-permute-done.30.refs_9_ = bf16[128,128]{1,0:T(8,128)(2,1)S(1)} collective-permute-done((bf16[128,128]{1,0:T(8,128)(2,1)S(1)}, bf16[128,128]{1,0:T(8,128)(2,1)S(1)}, u32[]{:S(2)}, u32[]{:S(2)}) %collective-permute-start.30) | collective-permute-done | bytes 32800 | tf_op jit(solution)/shard_map/ppermute | solution.py:337
  78.3 1.4 step.11
  79.8 2.7 %collective-permute-start.35 = (bf16[128,128]{1,0:T(8,128)(2,1)S(1)}, bf16[128,128]{1,0:T(8,128)(2,1)S(1)}, u32[]{:S(2)}, u32[]{:S(2)}) collective-permute-start(bf16[128,128]{1,0:T(8,128)(2,1)S(1)} %get-tuple-element.126), channel_id=1, source_target_pairs={{2,4},{4,2},{3,5},{5,3},{6,8},{8,6},{7,9},{9,7},{10,12},{12,10},{1... | collective-permute-start | bytes 98312 | tf_op jit(solution)/shard_map/ppermute | solution.py:337
  82.5 2.2 %collective-permute-start.36 = (bf16[128,128]{1,0:T(8,128)(2,1)S(1)}, bf16[128,128]{1,0:T(8,128)(2,1)S(1)}, u32[]{:S(2)}, u32[]{:S(2)}) collective-permute-start(bf16[128,128]{1,0:T(8,128)(2,1)S(1)} %get-tuple-element.127), channel_id=1, source_target_pairs={{1,2},{2,1},{3,4},{4,3},{5,6},{6,5},{7,8},{8,7},{9,10},{10,9},{11,... | collective-permute-start | bytes 98312 | tf_op jit(solution)/shard_map/ppermute | solution.py:337
  84.9 1.9 %collective-permute-done.34.refs_7_ = bf16[128,128]{1,0:T(8,128)(2,1)S(1)} collective-permute-done((bf16[128,128]{1,0:T(8,128)(2,1)S(1)}, bf16[128,128]{1,0:T(8,128)(2,1)S(1)}, u32[]{:S(2)}, u32[]{:S(2)}) %collective-permute-start.34) | collective-permute-done | bytes 32800 | tf_op jit(solution)/shard_map/ppermute | solution.py:337
  86.8 0.7 collective-permute-done.35.refs_8_
  87.5 1.9 %collective-permute-done.36.refs_9_ = bf16[128,128]{1,0:T(8,128)(2,1)S(1)} collective-permute-done((bf16[128,128]{1,0:T(8,128)(2,1)S(1)}, bf16[128,128]{1,0:T(8,128)(2,1)S(1)}, u32[]{:S(2)}, u32[]{:S(2)}) %collective-permute-start.36) | collective-permute-done | bytes 32800 | tf_op jit(solution)/shard_map/ppermute | solution.py:337
  89.4 1.4 step.12
  91.4 3.0 %collective-permute-start.41 = (bf16[128,128]{1,0:T(8,128)(2,1)S(1)}, bf16[128,128]{1,0:T(8,128)(2,1)S(1)}, u32[]{:S(2)}, u32[]{:S(2)}) collective-permute-start(bf16[128,128]{1,0:T(8,128)(2,1)S(1)} %get-tuple-element.134), channel_id=1, source_target_pairs={{2,4},{4,2},{3,5},{5,3},{6,8},{8,6},{7,9},{9,7},{10,12},{12,10},{1... | collective-permute-start | bytes 98312 | tf_op jit(solution)/shard_map/ppermute | solution.py:337
  94.4 2.3 %collective-permute-start.42 = (bf16[128,128]{1,0:T(8,128)(2,1)S(1)}, bf16[128,128]{1,0:T(8,128)(2,1)S(1)}, u32[]{:S(2)}, u32[]{:S(2)}) collective-permute-start(bf16[128,128]{1,0:T(8,128)(2,1)S(1)} %get-tuple-element.135), channel_id=1, source_target_pairs={{1,2},{2,1},{3,4},{4,3},{5,6},{6,5},{7,8},{8,7},{9,10},{10,9},{11,... | collective-permute-start | bytes 98312 | tf_op jit(solution)/shard_map/ppermute | solution.py:337
  96.8 0.8 collective-permute-done.40.refs_7_
  97.5 1.4 collective-permute-done.41.refs_8_
  98.9 2.5 %collective-permute-done.42.refs_9_ = bf16[128,128]{1,0:T(8,128)(2,1)S(1)} collective-permute-done((bf16[128,128]{1,0:T(8,128)(2,1)S(1)}, bf16[128,128]{1,0:T(8,128)(2,1)S(1)}, u32[]{:S(2)}, u32[]{:S(2)}) %collective-permute-start.42) | collective-permute-done | bytes 32800 | tf_op jit(solution)/shard_map/ppermute | solution.py:337
  101.4 2.3 %step.13 = (f32[2048,128]{1,0:T(8,128)}, bf16[2048,128]{1,0:T(8,128)(2,1)S(1)}, bf16[128,128]{1,0:T(8,128)(2,1)S(1)}, bf16[128,128]{1,0:T(8,128)(2,1)S(1)}, bf16...) custom-call(s32[1]{0:T(128)} %bitcast.place_ref.refs_0_, ...), custom_call_target="tpu_custom_call" | custom-call | tf_op jit(solution)/shard_map/step/pallas_call | solution.py:241
  103.7 3.5 %collective-permute-start.47 = (bf16[128,128]{1,0:T(8,128)(2,1)S(1)}, bf16[128,128]{1,0:T(8,128)(2,1)S(1)}, u32[]{:S(2)}, u32[]{:S(2)}) collective-permute-start(bf16[128,128]{1,0:T(8,128)(2,1)S(1)} %get-tuple-element.142), channel_id=1, source_target_pairs={{2,4},{4,2},{3,5},{5,3},{6,8},{8,6},{7,9},{9,7},{10,12},{12,10},{1... | collective-permute-start | bytes 98312 | tf_op jit(solution)/shard_map/ppermute | solution.py:337
  107.1 1.6 %collective-permute-start.48 = (bf16[128,128]{1,0:T(8,128)(2,1)S(1)}, bf16[128,128]{1,0:T(8,128)(2,1)S(1)}, u32[]{:S(2)}, u32[]{:S(2)}) collective-permute-start(bf16[128,128]{1,0:T(8,128)(2,1)S(1)} %get-tuple-element.143), channel_id=1, source_target_pairs={{1,2},{2,1},{3,4},{4,3},{5,6},{6,5},{7,8},{8,7},{9,10},{10,9},{11,... | collective-permute-start | bytes 98312 | tf_op jit(solution)/shard_map/ppermute | solution.py:337
  108.7 0.8 collective-permute-start.50
  109.5 1.1 collective-permute-done.46.refs_6_
  111.2 2.9 %collective-permute-done.48.refs_8_ = bf16[128,128]{1,0:T(8,128)(2,1)S(1)} collective-permute-done((bf16[128,128]{1,0:T(8,128)(2,1)S(1)}, bf16[128,128]{1,0:T(8,128)(2,1)S(1)}, u32[]{:S(2)}, u32[]{:S(2)}) %collective-permute-start.48) | collective-permute-done | bytes 32800 | tf_op jit(solution)/shard_map/ppermute | solution.py:337
  114.1 2.0 %last.1 = (f32[2048,128]{1,0:T(8,128)S(1)}, f32[128,128]{1,0:T(8,128)S(1)}) custom-call(s32[1]{0:T(128)} %bitcast.place_ref.refs_0_, bf16[2048,384]{1,0:T(8,128)(2,1)S(1)} %get-tuple-element.78.refs_1_, bf16[2048,256]{1,0:T(8,128)(2,1)S(1)} %get-tuple-element.79.refs_2_, f32[256,128]{1,0:T(8,128)S(1)} %get-tuple-element.80.refs_3_, ...), custom_call_target="tpu_custom_call" | custom-call | tf_op jit(solution)/shard_map/last/pallas_call | solution.py:271
  116.2 1.2 collective-permute-done.52
  117.5 0.9 collective-permute-start.54
  118.5 2.5 %collective-permute-start.53 = (f32[128,128]{1,0:T(8,128)S(1)}, f32[128,128]{1,0:T(8,128)S(1)}, u32[]{:S(2)}, u32[]{:S(2)}) collective-permute-start(f32[128,128]{1,0:T(8,128)S(1)} %add.25), channel_id=1, source_target_pairs={{0,2},{1,3},{2,0},{3,1},{4,6},{5,7},{6,4},{7,5},{8,10},{9,11},{10,... | collective-permute-start | bytes 196616 | tf_op jit(solution)/shard_map/ppermute | solution.py:326
  121.0 2.3 %collective-permute-done.55 = f32[128,128]{1,0:T(8,128)S(1)} collective-permute-done((f32[128,128]{1,0:T(8,128)S(1)}, f32[128,128]{1,0:T(8,128)S(1)}, u32[]{:S(2)}, u32[]{:S(2)}) %collective-permute-start.55) | collective-permute-done | bytes 65568 | tf_op jit(solution)/shard_map/ppermute | solution.py:326
  123.5 1.8 %collective-permute-start.58 = (f32[128,128]{1,0:T(8,128)S(1)}, f32[128,128]{1,0:T(8,128)S(1)}, u32[]{:S(2)}, u32[]{:S(2)}) collective-permute-start(f32[128,128]{1,0:T(8,128)S(1)} %add_add_fusion.1), channel_id=1, source_target_pairs={{0,24},{1,25},{2,26},{3,27},{4,28},{5,29},{6,30},{7,31},{8,16},{9,... | collective-permute-start | bytes 196616 | tf_op jit(solution)/shard_map/ppermute | solution.py:326
  125.3 2.6 %collective-permute-start.56 = (f32[128,128]{1,0:T(8,128)S(1)}, f32[128,128]{1,0:T(8,128)S(1)}, u32[]{:S(2)}, u32[]{:S(2)}) collective-permute-start(f32[128,128]{1,0:T(8,128)S(1)} %add_add_fusion.1), channel_id=1, source_target_pairs={{0,8},{1,9},{2,10},{3,11},{4,12},{5,13},{6,14},{7,15},{8,0},{9,1},... | collective-permute-start | bytes 196616 | tf_op jit(solution)/shard_map/ppermute | solution.py:326
  128.0 2.4 %collective-permute-done.58 = f32[128,128]{1,0:T(8,128)S(1)} collective-permute-done((f32[128,128]{1,0:T(8,128)S(1)}, f32[128,128]{1,0:T(8,128)S(1)}, u32[]{:S(2)}, u32[]{:S(2)}) %collective-permute-start.58) | collective-permute-done | bytes 65568 | tf_op jit(solution)/shard_map/ppermute | solution.py:326
  130.3 1.3 collective-permute-done.57
  131.7 12.7 %finish.1 = f32[2048,128]{1,0:T(8,128)} custom-call(f32[128,128]{1,0:T(8,128)S(1)} %add_add_fusion.refs_0_, f32[2048,128]{1,0:T(8,128)S(1)} %get-tuple-element.148.refs_1_), custom_call_target="tpu_custom_call" | custom-call | tf_op jit(solution)/shard_map/finish/pallas_call | solution.py:308
  (78 shorter events, 6.5 us)
Async XLA Ops:
  0.0 16.9 %collective-permute-start.3 = (s32[1,256]{1,0:T(1,128)}, s32[1,256]{1,0:T(1,128)S(1)}, u32[]{:S(2)}, u32[]{:S(2)}) collective-permute-start(s32[1,256]{1,0:T(1,128)} %bitcast.10), channel_id=1, source_target_pairs={{4,8},{8,4},{5,9},{9,5},{6,10},{10,6},{7,11},{11,7},{12,16},{16,12... | collective-permute-start | bytes 3080 | tf_op jit(solution)/shard_map/ppermute | solution.py:337
  6.0 10.9 %collective-permute-start.2 = (s32[1,256]{1,0:T(1,128)}, s32[1,256]{1,0:T(1,128)S(1)}, u32[]{:S(2)}, u32[]{:S(2)}) collective-permute-start(s32[1,256]{1,0:T(1,128)} %bitcast.11), channel_id=1, source_target_pairs={{0,4},{4,0},{1,5},{5,1},{2,6},{6,2},{3,7},{7,3},{8,12},{12,8},{9,1... | collective-permute-start | bytes 3080 | tf_op jit(solution)/shard_map/ppermute | solution.py:337
  6.0 10.9 %collective-permute-start.1 = (s32[1,256]{1,0:T(1,128)}, s32[1,256]{1,0:T(1,128)S(1)}, u32[]{:S(2)}, u32[]{:S(2)}) collective-permute-start(s32[1,256]{1,0:T(1,128)} %bitcast.12), channel_id=1, source_target_pairs={{2,4},{4,2},{3,5},{5,3},{6,8},{8,6},{7,9},{9,7},{10,12},{12,10},{1... | collective-permute-start | bytes 3080 | tf_op jit(solution)/shard_map/ppermute | solution.py:337
  8.8 8.1 %collective-permute-start = (s32[1,256]{1,0:T(1,128)}, s32[1,256]{1,0:T(1,128)S(1)}, u32[]{:S(2)}, u32[]{:S(2)}) collective-permute-start(s32[1,256]{1,0:T(1,128)} %bitcast.13), channel_id=1, source_target_pairs={{0,2},{2,0},{1,3},{3,1},{4,6},{6,4},{5,7},{7,5},{8,10},{10,8},{9,1... | collective-permute-start | bytes 3080 | tf_op jit(solution)/shard_map/ppermute | solution.py:337
  9.5 0.9 copy-start.1
  10.4 0.9 copy-start.2
  11.4 0.7 copy-start.3
  12.0 0.7 copy-start.4
  16.9 1.0 copy-start
  18.7 6.7 %collective-permute-start.4 = (bf16[128,128]{1,0:T(8,128)(2,1)S(1)}, bf16[128,128]{1,0:T(8,128)(2,1)S(1)}, u32[]{:S(2)}, u32[]{:S(2)}) collective-permute-start(bf16[128,128]{1,0:T(8,128)(2,1)S(1)} %get-tuple-element.86), channel_id=1, source_target_pairs={{4,8},{8,4},{5,9},{9,5},{6,10},{10,6},{7,11},{11,7},{12,16},{16,12... | collective-permute-start | bytes 98312 | tf_op jit(solution)/shard_map/ppermute | solution.py:337
  21.4 7.5 %collective-permute-start.5 = (bf16[128,128]{1,0:T(8,128)(2,1)S(1)}, bf16[128,128]{1,0:T(8,128)(2,1)S(1)}, u32[]{:S(2)}, u32[]{:S(2)}) collective-permute-start(bf16[128,128]{1,0:T(8,128)(2,1)S(1)} %get-tuple-element.87), channel_id=1, source_target_pairs={{2,4},{4,2},{3,5},{5,3},{6,8},{8,6},{7,9},{9,7},{10,12},{12,10},{1... | collective-permute-start | bytes 98312 | tf_op jit(solution)/shard_map/ppermute | solution.py:337
  24.3 6.9 %collective-permute-start.6 = (bf16[128,128]{1,0:T(8,128)(2,1)S(1)}, bf16[128,128]{1,0:T(8,128)(2,1)S(1)}, u32[]{:S(2)}, u32[]{:S(2)}) collective-permute-start(bf16[128,128]{1,0:T(8,128)(2,1)S(1)} %get-tuple-element.88), channel_id=1, source_target_pairs={{1,2},{2,1},{3,4},{4,3},{5,6},{6,5},{7,8},{8,7},{9,10},{10,9},{11,... | collective-permute-start | bytes 98312 | tf_op jit(solution)/shard_map/ppermute | solution.py:337
  25.1 6.1 %collective-permute-start.7 = (bf16[128,128]{1,0:T(8,128)(2,1)S(1)}, bf16[128,128]{1,0:T(8,128)(2,1)S(1)}, u32[]{:S(2)}, u32[]{:S(2)}) collective-permute-start(bf16[128,128]{1,0:T(8,128)(2,1)S(1)} %get-tuple-element.89), channel_id=1, source_target_pairs={{0,4},{4,0},{1,5},{5,1},{2,6},{6,2},{3,7},{7,3},{8,12},{12,8},{9,1... | collective-permute-start | bytes 98312 | tf_op jit(solution)/shard_map/ppermute | solution.py:337
  25.1 6.1 %collective-permute-start.8 = (bf16[128,128]{1,0:T(8,128)(2,1)S(1)}, bf16[128,128]{1,0:T(8,128)(2,1)S(1)}, u32[]{:S(2)}, u32[]{:S(2)}) collective-permute-start(bf16[128,128]{1,0:T(8,128)(2,1)S(1)} %get-tuple-element.90), channel_id=1, source_target_pairs={{0,2},{2,0},{1,3},{3,1},{4,6},{6,4},{5,7},{7,5},{8,10},{10,8},{9,1... | collective-permute-start | bytes 98312 | tf_op jit(solution)/shard_map/ppermute | solution.py:337
  25.3 5.9 %collective-permute-start.9 = (bf16[128,128]{1,0:T(8,128)(2,1)S(1)}, bf16[128,128]{1,0:T(8,128)(2,1)S(1)}, u32[]{:S(2)}, u32[]{:S(2)}) collective-permute-start(bf16[128,128]{1,0:T(8,128)(2,1)S(1)} %get-tuple-element.91), channel_id=1, source_target_pairs={{0,1},{1,0},{2,3},{3,2},{4,5},{5,4},{6,7},{7,6},{8,9},{9,8},{10,11... | collective-permute-start | bytes 98312 | tf_op jit(solution)/shard_map/ppermute | solution.py:337
  32.6 7.0 %collective-permute-start.10 = (bf16[128,128]{1,0:T(8,128)(2,1)S(1)}, bf16[128,128]{1,0:T(8,128)(2,1)S(1)}, u32[]{:S(2)}, u32[]{:S(2)}) collective-permute-start(bf16[128,128]{1,0:T(8,128)(2,1)S(1)} %get-tuple-element.93), channel_id=1, source_target_pairs={{4,8},{8,4},{5,9},{9,5},{6,10},{10,6},{7,11},{11,7},{12,16},{16,12... | collective-permute-start | bytes 98312 | tf_op jit(solution)/shard_map/ppermute | solution.py:337
  32.7 7.6 %collective-permute-start.11 = (bf16[128,128]{1,0:T(8,128)(2,1)S(1)}, bf16[128,128]{1,0:T(8,128)(2,1)S(1)}, u32[]{:S(2)}, u32[]{:S(2)}) collective-permute-start(bf16[128,128]{1,0:T(8,128)(2,1)S(1)} %get-tuple-element.94), channel_id=1, source_target_pairs={{2,4},{4,2},{3,5},{5,3},{6,8},{8,6},{7,9},{9,7},{10,12},{12,10},{1... | collective-permute-start | bytes 98312 | tf_op jit(solution)/shard_map/ppermute | solution.py:337
  34.6 7.0 %collective-permute-start.12 = (bf16[128,128]{1,0:T(8,128)(2,1)S(1)}, bf16[128,128]{1,0:T(8,128)(2,1)S(1)}, u32[]{:S(2)}, u32[]{:S(2)}) collective-permute-start(bf16[128,128]{1,0:T(8,128)(2,1)S(1)} %get-tuple-element.95), channel_id=1, source_target_pairs={{1,2},{2,1},{3,4},{4,3},{5,6},{6,5},{7,8},{8,7},{9,10},{10,9},{11,... | collective-permute-start | bytes 98312 | tf_op jit(solution)/shard_map/ppermute | solution.py:337
  37.7 4.2 %collective-permute-start.13 = (bf16[128,128]{1,0:T(8,128)(2,1)S(1)}, bf16[128,128]{1,0:T(8,128)(2,1)S(1)}, u32[]{:S(2)}, u32[]{:S(2)}) collective-permute-start(bf16[128,128]{1,0:T(8,128)(2,1)S(1)} %get-tuple-element.96), channel_id=1, source_target_pairs={{0,4},{4,0},{1,5},{5,1},{2,6},{6,2},{3,7},{7,3},{8,12},{12,8},{9,1... | collective-permute-start | bytes 98312 | tf_op jit(solution)/shard_map/ppermute | solution.py:337
  37.7 4.2 %collective-permute-start.14 = (bf16[128,128]{1,0:T(8,128)(2,1)S(1)}, bf16[128,128]{1,0:T(8,128)(2,1)S(1)}, u32[]{:S(2)}, u32[]{:S(2)}) collective-permute-start(bf16[128,128]{1,0:T(8,128)(2,1)S(1)} %get-tuple-element.97), channel_id=1, source_target_pairs={{0,2},{2,0},{1,3},{3,1},{4,6},{6,4},{5,7},{7,5},{8,10},{10,8},{9,1... | collective-permute-start | bytes 98312 | tf_op jit(solution)/shard_map/ppermute | solution.py:337
  39.6 2.3 %collective-permute-start.15 = (bf16[128,128]{1,0:T(8,128)(2,1)S(1)}, bf16[128,128]{1,0:T(8,128)(2,1)S(1)}, u32[]{:S(2)}, u32[]{:S(2)}) collective-permute-start(bf16[128,128]{1,0:T(8,128)(2,1)S(1)} %get-tuple-element.98), channel_id=1, source_target_pairs={{0,1},{1,0},{2,3},{3,2},{4,5},{5,4},{6,7},{7,6},{8,9},{9,8},{10,11... | collective-permute-start | bytes 98312 | tf_op jit(solution)/shard_map/ppermute | solution.py:337
  43.4 6.7 %collective-permute-start.16 = (bf16[128,128]{1,0:T(8,128)(2,1)S(1)}, bf16[128,128]{1,0:T(8,128)(2,1)S(1)}, u32[]{:S(2)}, u32[]{:S(2)}) collective-permute-start(bf16[128,128]{1,0:T(8,128)(2,1)S(1)} %get-tuple-element.101), channel_id=1, source_target_pairs={{4,8},{8,4},{5,9},{9,5},{6,10},{10,6},{7,11},{11,7},{12,16},{16,12... | collective-permute-start | bytes 98312 | tf_op jit(solution)/shard_map/ppermute | solution.py:337
  44.3 7.5 %collective-permute-start.17 = (bf16[128,128]{1,0:T(8,128)(2,1)S(1)}, bf16[128,128]{1,0:T(8,128)(2,1)S(1)}, u32[]{:S(2)}, u32[]{:S(2)}) collective-permute-start(bf16[128,128]{1,0:T(8,128)(2,1)S(1)} %get-tuple-element.102), channel_id=1, source_target_pairs={{2,4},{4,2},{3,5},{5,3},{6,8},{8,6},{7,9},{9,7},{10,12},{12,10},{1... | collective-permute-start | bytes 98312 | tf_op jit(solution)/shard_map/ppermute | solution.py:337
  47.3 6.9 %collective-permute-start.18 = (bf16[128,128]{1,0:T(8,128)(2,1)S(1)}, bf16[128,128]{1,0:T(8,128)(2,1)S(1)}, u32[]{:S(2)}, u32[]{:S(2)}) collective-permute-start(bf16[128,128]{1,0:T(8,128)(2,1)S(1)} %get-tuple-element.103), channel_id=1, source_target_pairs={{1,2},{2,1},{3,4},{4,3},{5,6},{6,5},{7,8},{8,7},{9,10},{10,9},{11,... | collective-permute-start | bytes 98312 | tf_op jit(solution)/shard_map/ppermute | solution.py:337
  49.7 4.6 %collective-permute-start.19 = (bf16[128,128]{1,0:T(8,128)(2,1)S(1)}, bf16[128,128]{1,0:T(8,128)(2,1)S(1)}, u32[]{:S(2)}, u32[]{:S(2)}) collective-permute-start(bf16[128,128]{1,0:T(8,128)(2,1)S(1)} %get-tuple-element.104), channel_id=1, source_target_pairs={{0,4},{4,0},{1,5},{5,1},{2,6},{6,2},{3,7},{7,3},{8,12},{12,8},{9,1... | collective-permute-start | bytes 98312 | tf_op jit(solution)/shard_map/ppermute | solution.py:337
  49.7 4.6 %collective-permute-start.20 = (bf16[128,128]{1,0:T(8,128)(2,1)S(1)}, bf16[128,128]{1,0:T(8,128)(2,1)S(1)}, u32[]{:S(2)}, u32[]{:S(2)}) collective-permute-start(bf16[128,128]{1,0:T(8,128)(2,1)S(1)} %get-tuple-element.105), channel_id=1, source_target_pairs={{0,2},{2,0},{1,3},{3,1},{4,6},{6,4},{5,7},{7,5},{8,10},{10,8},{9,1... | collective-permute-start | bytes 98312 | tf_op jit(solution)/shard_map/ppermute | solution.py:337
  50.0 4.2 %collective-permute-start.21 = (bf16[128,128]{1,0:T(8,128)(2,1)S(1)}, bf16[128,128]{1,0:T(8,128)(2,1)S(1)}, u32[]{:S(2)}, u32[]{:S(2)}) collective-permute-start(bf16[128,128]{1,0:T(8,128)(2,1)S(1)} %get-tuple-element.106), channel_id=1, source_target_pairs={{0,1},{1,0},{2,3},{3,2},{4,5},{5,4},{6,7},{7,6},{8,9},{9,8},{10,11... | collective-permute-start | bytes 98312 | tf_op jit(solution)/shard_map/ppermute | solution.py:337
  55.7 7.0 %collective-permute-start.22 = (bf16[128,128]{1,0:T(8,128)(2,1)S(1)}, bf16[128,128]{1,0:T(8,128)(2,1)S(1)}, u32[]{:S(2)}, u32[]{:S(2)}) collective-permute-start(bf16[128,128]{1,0:T(8,128)(2,1)S(1)} %get-tuple-element.109), channel_id=1, source_target_pairs={{4,8},{8,4},{5,9},{9,5},{6,10},{10,6},{7,11},{11,7},{12,16},{16,12... | collective-permute-start | bytes 98312 | tf_op jit(solution)/shard_map/ppermute | solution.py:337
  55.7 7.7 %collective-permute-start.23 = (bf16[128,128]{1,0:T(8,128)(2,1)S(1)}, bf16[128,128]{1,0:T(8,128)(2,1)S(1)}, u32[]{:S(2)}, u32[]{:S(2)}) collective-permute-start(bf16[128,128]{1,0:T(8,128)(2,1)S(1)} %get-tuple-element.110), channel_id=1, source_target_pairs={{2,4},{4,2},{3,5},{5,3},{6,8},{8,6},{7,9},{9,7},{10,12},{12,10},{1... | collective-permute-start | bytes 98312 | tf_op jit(solution)/shard_map/ppermute | solution.py:337
  59.2 7.0 %collective-permute-start.24 = (bf16[128,128]{1,0:T(8,128)(2,1)S(1)}, bf16[128,128]{1,0:T(8,128)(2,1)S(1)}, u32[]{:S(2)}, u32[]{:S(2)}) collective-permute-start(bf16[128,128]{1,0:T(8,128)(2,1)S(1)} %get-tuple-element.111), channel_id=1, source_target_pairs={{1,2},{2,1},{3,4},{4,3},{5,6},{6,5},{7,8},{8,7},{9,10},{10,9},{11,... | collective-permute-start | bytes 98312 | tf_op jit(solution)/shard_map/ppermute | solution.py:337
  60.8 5.5 %collective-permute-start.25 = (bf16[128,128]{1,0:T(8,128)(2,1)S(1)}, bf16[128,128]{1,0:T(8,128)(2,1)S(1)}, u32[]{:S(2)}, u32[]{:S(2)}) collective-permute-start(bf16[128,128]{1,0:T(8,128)(2,1)S(1)} %get-tuple-element.112), channel_id=1, source_target_pairs={{0,4},{4,0},{1,5},{5,1},{2,6},{6,2},{3,7},{7,3},{8,12},{12,8},{9,1... | collective-permute-start | bytes 98312 | tf_op jit(solution)/shard_map/ppermute | solution.py:337
  60.8 5.5 %collective-permute-start.26 = (bf16[128,128]{1,0:T(8,128)(2,1)S(1)}, bf16[128,128]{1,0:T(8,128)(2,1)S(1)}, u32[]{:S(2)}, u32[]{:S(2)}) collective-permute-start(bf16[128,128]{1,0:T(8,128)(2,1)S(1)} %get-tuple-element.113), channel_id=1, source_target_pairs={{0,2},{2,0},{1,3},{3,1},{4,6},{6,4},{5,7},{7,5},{8,10},{10,8},{9,1... | collective-permute-start | bytes 98312 | tf_op jit(solution)/shard_map/ppermute | solution.py:337
  62.7 3.6 %collective-permute-start.27 = (bf16[128,128]{1,0:T(8,128)(2,1)S(1)}, bf16[128,128]{1,0:T(8,128)(2,1)S(1)}, u32[]{:S(2)}, u32[]{:S(2)}) collective-permute-start(bf16[128,128]{1,0:T(8,128)(2,1)S(1)} %get-tuple-element.114), channel_id=1, source_target_pairs={{0,1},{1,0},{2,3},{3,2},{4,5},{5,4},{6,7},{7,6},{8,9},{9,8},{10,11... | collective-permute-start | bytes 98312 | tf_op jit(solution)/shard_map/ppermute | solution.py:337
  67.7 7.0 %collective-permute-start.28 = (bf16[128,128]{1,0:T(8,128)(2,1)S(1)}, bf16[128,128]{1,0:T(8,128)(2,1)S(1)}, u32[]{:S(2)}, u32[]{:S(2)}) collective-permute-start(bf16[128,128]{1,0:T(8,128)(2,1)S(1)} %get-tuple-element.117), channel_id=1, source_target_pairs={{4,8},{8,4},{5,9},{9,5},{6,10},{10,6},{7,11},{11,7},{12,16},{16,12... | collective-permute-start | bytes 98312 | tf_op jit(solution)/shard_map/ppermute | solution.py:337
  67.8 7.6 %collective-permute-start.29 = (bf16[128,128]{1,0:T(8,128)(2,1)S(1)}, bf16[128,128]{1,0:T(8,128)(2,1)S(1)}, u32[]{:S(2)}, u32[]{:S(2)}) collective-permute-start(bf16[128,128]{1,0:T(8,128)(2,1)S(1)} %get-tuple-element.118), channel_id=1, source_target_pairs={{2,4},{4,2},{3,5},{5,3},{6,8},{8,6},{7,9},{9,7},{10,12},{12,10},{1... | collective-permute-start | bytes 98312 | tf_op jit(solution)/shard_map/ppermute | solution.py:337
  71.3 7.0 %collective-permute-start.30 = (bf16[128,128]{1,0:T(8,128)(2,1)S(1)}, bf16[128,128]{1,0:T(8,128)(2,1)S(1)}, u32[]{:S(2)}, u32[]{:S(2)}) collective-permute-start(bf16[128,128]{1,0:T(8,128)(2,1)S(1)} %get-tuple-element.119), channel_id=1, source_target_pairs={{1,2},{2,1},{3,4},{4,3},{5,6},{6,5},{7,8},{8,7},{9,10},{10,9},{11,... | collective-permute-start | bytes 98312 | tf_op jit(solution)/shard_map/ppermute | solution.py:337
  72.7 5.6 %collective-permute-start.31 = (bf16[128,128]{1,0:T(8,128)(2,1)S(1)}, bf16[128,128]{1,0:T(8,128)(2,1)S(1)}, u32[]{:S(2)}, u32[]{:S(2)}) collective-permute-start(bf16[128,128]{1,0:T(8,128)(2,1)S(1)} %get-tuple-element.120), channel_id=1, source_target_pairs={{0,4},{4,0},{1,5},{5,1},{2,6},{6,2},{3,7},{7,3},{8,12},{12,8},{9,1... | collective-permute-start | bytes 98312 | tf_op jit(solution)/shard_map/ppermute | solution.py:337
  72.7 5.6 %collective-permute-start.32 = (bf16[128,128]{1,0:T(8,128)(2,1)S(1)}, bf16[128,128]{1,0:T(8,128)(2,1)S(1)}, u32[]{:S(2)}, u32[]{:S(2)}) collective-permute-start(bf16[128,128]{1,0:T(8,128)(2,1)S(1)} %get-tuple-element.121), channel_id=1, source_target_pairs={{0,2},{2,0},{1,3},{3,1},{4,6},{6,4},{5,7},{7,5},{8,10},{10,8},{9,1... | collective-permute-start | bytes 98312 | tf_op jit(solution)/shard_map/ppermute | solution.py:337
  74.8 3.5 %collective-permute-start.33 = (bf16[128,128]{1,0:T(8,128)(2,1)S(1)}, bf16[128,128]{1,0:T(8,128)(2,1)S(1)}, u32[]{:S(2)}, u32[]{:S(2)}) collective-permute-start(bf16[128,128]{1,0:T(8,128)(2,1)S(1)} %get-tuple-element.122), channel_id=1, source_target_pairs={{0,1},{1,0},{2,3},{3,2},{4,5},{5,4},{6,7},{7,6},{8,9},{9,8},{10,11... | collective-permute-start | bytes 98312 | tf_op jit(solution)/shard_map/ppermute | solution.py:337
  79.7 7.1 %collective-permute-start.34 = (bf16[128,128]{1,0:T(8,128)(2,1)S(1)}, bf16[128,128]{1,0:T(8,128)(2,1)S(1)}, u32[]{:S(2)}, u32[]{:S(2)}) collective-permute-start(bf16[128,128]{1,0:T(8,128)(2,1)S(1)} %get-tuple-element.125), channel_id=1, source_target_pairs={{4,8},{8,4},{5,9},{9,5},{6,10},{10,6},{7,11},{11,7},{12,16},{16,12... | collective-permute-start | bytes 98312 | tf_op jit(solution)/shard_map/ppermute | solution.py:337
  79.8 7.7 %collective-permute-start.35 = (bf16[128,128]{1,0:T(8,128)(2,1)S(1)}, bf16[128,128]{1,0:T(8,128)(2,1)S(1)}, u32[]{:S(2)}, u32[]{:S(2)}) collective-permute-start(bf16[128,128]{1,0:T(8,128)(2,1)S(1)} %get-tuple-element.126), channel_id=1, source_target_pairs={{2,4},{4,2},{3,5},{5,3},{6,8},{8,6},{7,9},{9,7},{10,12},{12,10},{1... | collective-permute-start | bytes 98312 | tf_op jit(solution)/shard_map/ppermute | solution.py:337
  82.5 6.9 %collective-permute-start.36 = (bf16[128,128]{1,0:T(8,128)(2,1)S(1)}, bf16[128,128]{1,0:T(8,128)(2,1)S(1)}, u32[]{:S(2)}, u32[]{:S(2)}) collective-permute-start(bf16[128,128]{1,0:T(8,128)(2,1)S(1)} %get-tuple-element.127), channel_id=1, source_target_pairs={{1,2},{2,1},{3,4},{4,3},{5,6},{6,5},{7,8},{8,7},{9,10},{10,9},{11,... | collective-permute-start | bytes 98312 | tf_op jit(solution)/shard_map/ppermute | solution.py:337
  84.7 4.7 %collective-permute-start.37 = (bf16[128,128]{1,0:T(8,128)(2,1)S(1)}, bf16[128,128]{1,0:T(8,128)(2,1)S(1)}, u32[]{:S(2)}, u32[]{:S(2)}) collective-permute-start(bf16[128,128]{1,0:T(8,128)(2,1)S(1)} %get-tuple-element.128), channel_id=1, source_target_pairs={{0,4},{4,0},{1,5},{5,1},{2,6},{6,2},{3,7},{7,3},{8,12},{12,8},{9,1... | collective-permute-start | bytes 98312 | tf_op jit(solution)/shard_map/ppermute | solution.py:337
  84.8 4.7 %collective-permute-start.38 = (bf16[128,128]{1,0:T(8,128)(2,1)S(1)}, bf16[128,128]{1,0:T(8,128)(2,1)S(1)}, u32[]{:S(2)}, u32[]{:S(2)}) collective-permute-start(bf16[128,128]{1,0:T(8,128)(2,1)S(1)} %get-tuple-element.129), channel_id=1, source_target_pairs={{0,2},{2,0},{1,3},{3,1},{4,6},{6,4},{5,7},{7,5},{8,10},{10,8},{9,1... | collective-permute-start | bytes 98312 | tf_op jit(solution)/shard_map/ppermute | solution.py:337
  86.8 2.6 %collective-permute-start.39 = (bf16[128,128]{1,0:T(8,128)(2,1)S(1)}, bf16[128,128]{1,0:T(8,128)(2,1)S(1)}, u32[]{:S(2)}, u32[]{:S(2)}) collective-permute-start(bf16[128,128]{1,0:T(8,128)(2,1)S(1)} %get-tuple-element.130), channel_id=1, source_target_pairs={{0,1},{1,0},{2,3},{3,2},{4,5},{5,4},{6,7},{7,6},{8,9},{9,8},{10,11... | collective-permute-start | bytes 98312 | tf_op jit(solution)/shard_map/ppermute | solution.py:337
  90.9 6.7 %collective-permute-start.40 = (bf16[128,128]{1,0:T(8,128)(2,1)S(1)}, bf16[128,128]{1,0:T(8,128)(2,1)S(1)}, u32[]{:S(2)}, u32[]{:S(2)}) collective-permute-start(bf16[128,128]{1,0:T(8,128)(2,1)S(1)} %get-tuple-element.133), channel_id=1, source_target_pairs={{4,8},{8,4},{5,9},{9,5},{6,10},{10,6},{7,11},{11,7},{12,16},{16,12... | collective-permute-start | bytes 98312 | tf_op jit(solution)/shard_map/ppermute | solution.py:337
  91.4 7.5 %collective-permute-start.41 = (bf16[128,128]{1,0:T(8,128)(2,1)S(1)}, bf16[128,128]{1,0:T(8,128)(2,1)S(1)}, u32[]{:S(2)}, u32[]{:S(2)}) collective-permute-start(bf16[128,128]{1,0:T(8,128)(2,1)S(1)} %get-tuple-element.134), channel_id=1, source_target_pairs={{2,4},{4,2},{3,5},{5,3},{6,8},{8,6},{7,9},{9,7},{10,12},{12,10},{1... | collective-permute-start | bytes 98312 | tf_op jit(solution)/shard_map/ppermute | solution.py:337
  94.4 6.9 %collective-permute-start.42 = (bf16[128,128]{1,0:T(8,128)(2,1)S(1)}, bf16[128,128]{1,0:T(8,128)(2,1)S(1)}, u32[]{:S(2)}, u32[]{:S(2)}) collective-permute-start(bf16[128,128]{1,0:T(8,128)(2,1)S(1)} %get-tuple-element.135), channel_id=1, source_target_pairs={{1,2},{2,1},{3,4},{4,3},{5,6},{6,5},{7,8},{8,7},{9,10},{10,9},{11,... | collective-permute-start | bytes 98312 | tf_op jit(solution)/shard_map/ppermute | solution.py:337
  96.8 4.6 %collective-permute-start.43 = (bf16[128,128]{1,0:T(8,128)(2,1)S(1)}, bf16[128,128]{1,0:T(8,128)(2,1)S(1)}, u32[]{:S(2)}, u32[]{:S(2)}) collective-permute-start(bf16[128,128]{1,0:T(8,128)(2,1)S(1)} %get-tuple-element.136), channel_id=1, source_target_pairs={{0,4},{4,0},{1,5},{5,1},{2,6},{6,2},{3,7},{7,3},{8,12},{12,8},{9,1... | collective-permute-start | bytes 98312 | tf_op jit(solution)/shard_map/ppermute | solution.py:337
  96.8 4.6 %collective-permute-start.44 = (bf16[128,128]{1,0:T(8,128)(2,1)S(1)}, bf16[128,128]{1,0:T(8,128)(2,1)S(1)}, u32[]{:S(2)}, u32[]{:S(2)}) collective-permute-start(bf16[128,128]{1,0:T(8,128)(2,1)S(1)} %get-tuple-element.137), channel_id=1, source_target_pairs={{0,2},{2,0},{1,3},{3,1},{4,6},{6,4},{5,7},{7,5},{8,10},{10,8},{9,1... | collective-permute-start | bytes 98312 | tf_op jit(solution)/shard_map/ppermute | solution.py:337
  97.5 3.8 %collective-permute-start.45 = (bf16[128,128]{1,0:T(8,128)(2,1)S(1)}, bf16[128,128]{1,0:T(8,128)(2,1)S(1)}, u32[]{:S(2)}, u32[]{:S(2)}) collective-permute-start(bf16[128,128]{1,0:T(8,128)(2,1)S(1)} %get-tuple-element.138), channel_id=1, source_target_pairs={{0,1},{1,0},{2,3},{3,2},{4,5},{5,4},{6,7},{7,6},{8,9},{9,8},{10,11... | collective-permute-start | bytes 98312 | tf_op jit(solution)/shard_map/ppermute | solution.py:337
  103.7 7.0 %collective-permute-start.46 = (bf16[128,128]{1,0:T(8,128)(2,1)S(1)}, bf16[128,128]{1,0:T(8,128)(2,1)S(1)}, u32[]{:S(2)}, u32[]{:S(2)}) collective-permute-start(bf16[128,128]{1,0:T(8,128)(2,1)S(1)} %get-tuple-element.141), channel_id=1, source_target_pairs={{4,8},{8,4},{5,9},{9,5},{6,10},{10,6},{7,11},{11,7},{12,16},{16,12... | collective-permute-start | bytes 98312 | tf_op jit(solution)/shard_map/ppermute | solution.py:337
  103.7 7.6 %collective-permute-start.47 = (bf16[128,128]{1,0:T(8,128)(2,1)S(1)}, bf16[128,128]{1,0:T(8,128)(2,1)S(1)}, u32[]{:S(2)}, u32[]{:S(2)}) collective-permute-start(bf16[128,128]{1,0:T(8,128)(2,1)S(1)} %get-tuple-element.142), channel_id=1, source_target_pairs={{2,4},{4,2},{3,5},{5,3},{6,8},{8,6},{7,9},{9,7},{10,12},{12,10},{1... | collective-permute-start | bytes 98312 | tf_op jit(solution)/shard_map/ppermute | solution.py:337
  107.1 7.0 %collective-permute-start.48 = (bf16[128,128]{1,0:T(8,128)(2,1)S(1)}, bf16[128,128]{1,0:T(8,128)(2,1)S(1)}, u32[]{:S(2)}, u32[]{:S(2)}) collective-permute-start(bf16[128,128]{1,0:T(8,128)(2,1)S(1)} %get-tuple-element.143), channel_id=1, source_target_pairs={{1,2},{2,1},{3,4},{4,3},{5,6},{6,5},{7,8},{8,7},{9,10},{10,9},{11,... | collective-permute-start | bytes 98312 | tf_op jit(solution)/shard_map/ppermute | solution.py:337
  108.7 5.4 %collective-permute-start.49 = (bf16[128,128]{1,0:T(8,128)(2,1)S(1)}, bf16[128,128]{1,0:T(8,128)(2,1)S(1)}, u32[]{:S(2)}, u32[]{:S(2)}) collective-permute-start(bf16[128,128]{1,0:T(8,128)(2,1)S(1)} %get-tuple-element.144), channel_id=1, source_target_pairs={{0,4},{4,0},{1,5},{5,1},{2,6},{6,2},{3,7},{7,3},{8,12},{12,8},{9,1... | collective-permute-start | bytes 98312 | tf_op jit(solution)/shard_map/ppermute | solution.py:337
  108.7 5.4 %collective-permute-start.50 = (bf16[128,128]{1,0:T(8,128)(2,1)S(1)}, bf16[128,128]{1,0:T(8,128)(2,1)S(1)}, u32[]{:S(2)}, u32[]{:S(2)}) collective-permute-start(bf16[128,128]{1,0:T(8,128)(2,1)S(1)} %get-tuple-element.145), channel_id=1, source_target_pairs={{0,2},{2,0},{1,3},{3,1},{4,6},{6,4},{5,7},{7,5},{8,10},{10,8},{9,1... | collective-permute-start | bytes 98312 | tf_op jit(solution)/shard_map/ppermute | solution.py:337
  110.6 3.5 %collective-permute-start.51 = (bf16[128,128]{1,0:T(8,128)(2,1)S(1)}, bf16[128,128]{1,0:T(8,128)(2,1)S(1)}, u32[]{:S(2)}, u32[]{:S(2)}) collective-permute-start(bf16[128,128]{1,0:T(8,128)(2,1)S(1)} %get-tuple-element.146), channel_id=1, source_target_pairs={{0,1},{1,0},{2,3},{3,2},{4,5},{5,4},{6,7},{7,6},{8,9},{9,8},{10,11... | collective-permute-start | bytes 98312 | tf_op jit(solution)/shard_map/ppermute | solution.py:337
  116.1 1.3 collective-permute-start.52
  117.4 5.8 %collective-permute-start.55 = (f32[128,128]{1,0:T(8,128)S(1)}, f32[128,128]{1,0:T(8,128)S(1)}, u32[]{:S(2)}, u32[]{:S(2)}) collective-permute-start(f32[128,128]{1,0:T(8,128)S(1)} %add.25), channel_id=1, source_target_pairs={{0,6},{1,7},{2,4},{3,5},{4,2},{5,3},{6,0},{7,1},{8,14},{9,15},{10,... | collective-permute-start | bytes 196616 | tf_op jit(solution)/shard_map/ppermute | solution.py:326
  117.5 5.7 %collective-permute-start.54 = (f32[128,128]{1,0:T(8,128)S(1)}, f32[128,128]{1,0:T(8,128)S(1)}, u32[]{:S(2)}, u32[]{:S(2)}) collective-permute-start(f32[128,128]{1,0:T(8,128)S(1)} %add.25), channel_id=1, source_target_pairs={{0,4},{1,5},{2,6},{3,7},{4,0},{5,1},{6,2},{7,3},{8,12},{9,13},{10,... | collective-permute-start | bytes 196616 | tf_op jit(solution)/shard_map/ppermute | solution.py:326
  118.5 5.0 %collective-permute-start.53 = (f32[128,128]{1,0:T(8,128)S(1)}, f32[128,128]{1,0:T(8,128)S(1)}, u32[]{:S(2)}, u32[]{:S(2)}) collective-permute-start(f32[128,128]{1,0:T(8,128)S(1)} %add.25), channel_id=1, source_target_pairs={{0,2},{1,3},{2,0},{3,1},{4,6},{5,7},{6,4},{7,5},{8,10},{9,11},{10,... | collective-permute-start | bytes 196616 | tf_op jit(solution)/shard_map/ppermute | solution.py:326
  123.5 6.8 %collective-permute-start.58 = (f32[128,128]{1,0:T(8,128)S(1)}, f32[128,128]{1,0:T(8,128)S(1)}, u32[]{:S(2)}, u32[]{:S(2)}) collective-permute-start(f32[128,128]{1,0:T(8,128)S(1)} %add_add_fusion.1), channel_id=1, source_target_pairs={{0,24},{1,25},{2,26},{3,27},{4,28},{5,29},{6,30},{7,31},{8,16},{9,... | collective-permute-start | bytes 196616 | tf_op jit(solution)/shard_map/ppermute | solution.py:326
  125.3 6.3 %collective-permute-start.57 = (f32[128,128]{1,0:T(8,128)S(1)}, f32[128,128]{1,0:T(8,128)S(1)}, u32[]{:S(2)}, u32[]{:S(2)}) collective-permute-start(f32[128,128]{1,0:T(8,128)S(1)} %add_add_fusion.1), channel_id=1, source_target_pairs={{0,16},{1,17},{2,18},{3,19},{4,20},{5,21},{6,22},{7,23},{8,24},{9,... | collective-permute-start | bytes 196616 | tf_op jit(solution)/shard_map/ppermute | solution.py:326
  125.3 6.3 %collective-permute-start.56 = (f32[128,128]{1,0:T(8,128)S(1)}, f32[128,128]{1,0:T(8,128)S(1)}, u32[]{:S(2)}, u32[]{:S(2)}) collective-permute-start(f32[128,128]{1,0:T(8,128)S(1)} %add_add_fusion.1), channel_id=1, source_target_pairs={{0,8},{1,9},{2,10},{3,11},{4,12},{5,13},{6,14},{7,15},{8,0},{9,1},... | collective-permute-start | bytes 196616 | tf_op jit(solution)/shard_map/ppermute | solution.py:326

commit v2 on v1

--- a/solution.py
+++ b/solution.py
@@ -21,7 +21,7 @@
 BF16 = jnp.bfloat16
 F32 = jnp.float32
 VMEM = pl.BlockSpec(memory_space=pltpu.VMEM)
-ANY = pl.BlockSpec(memory_space=pl.ANY)
+HBM = pl.BlockSpec(memory_space=pltpu.HBM)
 SMEM = pl.BlockSpec(memory_space=pltpu.SMEM)
 PARAMS = pltpu.CompilerParams(vmem_limit_bytes=24 * 1024 * 1024)
 
@@ -77,14 +77,38 @@
 
 
 def prepare_kernel(
-    place_ref, cols_any, wts_any, dst_ref, far_ref, band_ref, hot_ref, coef_ref, cols_ref, wts_ref, sems
+    place_ref,
+    dst_any,
+    far_any,
+    wts_any,
+    cols_any,
+    field_any,
+    band_ref,
+    hot_ref,
+    coef_ref,
+    field_ref,
+    dst_ref,
+    far_ref,
+    wts_ref,
+    cols_ref,
+    sems,
 ):
     copies = [
-        pltpu.make_async_copy(cols_any, cols_ref, sems.at[0]),
-        pltpu.make_async_copy(wts_any, wts_ref, sems.at[1]),
+        pltpu.make_async_copy(source, target, sems.at[i])
+        for i, (source, target) in enumerate(
+            (
+                (dst_any, dst_ref),
+                (far_any, far_ref),
+                (wts_any, wts_ref),
+                (cols_any, cols_ref),
+                (field_any, field_ref),
+            )
+        )
     ]
     for copy in copies:
         copy.start()
+    copies[0].wait()
+    copies[1].wait()
     rows = cols_ref.shape[2]
     edges = dst_ref.shape[1]
     dst = by_link(place_ref, dst_ref[...])
@@ -94,14 +118,14 @@
         hot_ref[pl.ds(b * BLK, BLK), :] = jnp.where(ids == dst, 1.0, 0.0).astype(BF16)
     hot = hot_ref[...]
     degree = jnp.sum(dot(stacked(far, 16), hot, ((1,), (1,))), axis=0, keepdims=True)
-    for copy in copies:
-        copy.wait()
+    copies[2].wait()
     for o in range(3):
         degree = degree + jnp.sum(wts_ref[o], axis=0, keepdims=True)
     at_edge = jnp.sum(dot(stacked(degree, 16), hot, ((1,), (0,))), axis=0, keepdims=True)
     far_coef = far / at_edge
     for i in range(edges // BLK):
         coef_ref[pl.ds(i * BLK, BLK), :] = as_columns(far_coef[:, i * BLK : (i + 1) * BLK])
+    copies[3].wait()
     ids = lax.broadcasted_iota(jnp.int32, (BLK, BLK), 0)
     for b in range(rows // BLK):
         block = pl.ds(b * BLK, BLK)
@@ -113,9 +137,10 @@
             for k in range(KB):
                 dense = jnp.where(ids == cols[k : k + 1, :], coef[k : k + 1, :], dense)
             band_ref[block, pl.ds(o * BLK, BLK)] = dense.T.astype(BF16)
-
-
-def prepare(place, cols, wts, dst, far):
+    copies[4].wait()
+
+
+def prepare(place, dst, far, wts, cols, field):
     rows, edges = cols.shape[2], dst.shape[1]
     return pl.pallas_call(
         prepare_kernel,
@@ -123,17 +148,20 @@
             jax.ShapeDtypeStruct((rows, 3 * BLK), BF16),
             jax.ShapeDtypeStruct((rows, edges), BF16),
             jax.ShapeDtypeStruct((edges, VECS), F32),
+            jax.ShapeDtypeStruct(field.shape, BF16),
         ),
-        in_specs=[SMEM, ANY, ANY, VMEM, VMEM],
-        out_specs=(VMEM,) * 3,
+        in_specs=[SMEM, *(HBM,) * 5],
+        out_specs=(VMEM,) * 4,
         scratch_shapes=[
+            pltpu.VMEM(dst.shape, jnp.int32),
+            pltpu.VMEM(far.shape, F32),
+            pltpu.VMEM(wts.shape, F32),
             pltpu.VMEM(cols.shape, jnp.int32),
-            pltpu.VMEM(wts.shape, F32),
-            pltpu.SemaphoreType.DMA((2,)),
+            pltpu.SemaphoreType.DMA((5,)),
         ],
         compiler_params=PARAMS,
         name="prepare",
-    )(place, cols, wts, dst, far)
+    )(place, dst, far, wts, cols, field)
 
 
 def send_out(even, first, last, picked, sent):
@@ -190,10 +218,11 @@
     far = far.astype(F32) * coef_ref[...]
     far_high = far.astype(BF16)
     far_low = (far - far_high.astype(F32)).astype(BF16)
+    far = jnp.concatenate([far_high, far_low], axis=1)
     for b in range(count):
         block = pl.ds(b * BLK, BLK)
-        total = dot(hot_ref[block, :], far_high, ((1,), (0,)))
-        total += dot(hot_ref[block, :], far_low, ((1,), (0,)))
+        both = dot(hot_ref[block, :], far, ((1,), (0,)))
+        total = both[:, :VECS] + both[:, VECS:]
         if b == 0:
             total += dot(band_ref[block, :BLK], low, ((1,), (0,)))
             total += dot(band_ref[block, BLK:], field_ref[: 2 * BLK, :], ((1,), (0,)))
@@ -213,17 +242,18 @@
     return even
 
 
-def step_kernel(scale, has_prev, *refs):
+def step_kernel(scale, has_prev, has_next, *refs):
     place_ref, band_ref, hot_ref, coef_ref, pick_mat_ref, field_ref = refs[:6]
     refs = refs[6:]
     prev_ref = None
     if has_prev:
         prev_ref, refs = refs[0], refs[1:]
     got, refs = refs[:6], refs[6:]
-    next_ref, packed_ref, sent = refs[0], refs[1], refs[2:]
+    packed_ref, sent, next_refs = refs[0], refs[1:7], refs[7:]
 
     def store(block, value):
-        next_ref[block, :] = value
+        if has_next:
+            next_refs[0][block, :] = value
         packed_ref[block, :] = value.astype(BF16)
 
     even = advance(
@@ -234,19 +264,19 @@
     send_out(even, packed_ref[:BLK, :], packed_ref[rows - BLK :, :], picked, sent)
 
 
-def step(scale, place, mats, field, prev, got):
+def step(scale, place, mats, field, prev, got, has_next=True):
     rows = field.shape[0]
     has_prev = prev is not None
     before = (prev,) if has_prev else ()
     return pl.pallas_call(
-        lambda *refs: step_kernel(scale, has_prev, *refs),
+        lambda *refs: step_kernel(scale, has_prev, has_next, *refs),
         out_shape=(
-            jax.ShapeDtypeStruct((rows, VECS), F32),
             jax.ShapeDtypeStruct((rows, VECS), BF16),
             *SENT,
+            *(jax.ShapeDtypeStruct((rows, VECS), F32),) * has_next,
         ),
         in_specs=[SMEM] + [VMEM] * (11 + len(before)),
-        out_specs=(VMEM,) * 8,
+        out_specs=(VMEM,) * (7 + has_next),
         compiler_params=PARAMS,
         name="step",
     )(place, *mats, field, *before, *got)
@@ -281,26 +311,62 @@
     )(place, *mats, field, prev, *got)
 
 
+def total_of(terms):
+    terms = list(terms)
+    while len(terms) > 1:
+        pairs = [terms[i] + terms[i + 1] for i in range(0, len(terms) - 1, 2)]
+        terms = pairs + terms[len(terms) - len(terms) % 2 :]
+    return terms[0]
+
+
 def finish_kernel(scale, gram_ref, field_ref, out_ref, inverse_ref):
-    height = 8
-    count = VECS // height
-    ids = lax.broadcasted_iota(jnp.int32, (height, VECS), 0)
-    lanes = lax.broadcasted_iota(jnp.int32, (height, VECS), 1)
-    left = [gram_ref[height * b : height * (b + 1), :] for b in range(count)]
-    right = [jnp.where(ids + height * b == lanes, 1.0, 0.0) for b in range(count)]
-    for j in range(VECS):
-        own, at = divmod(j, height)
-        row, row_right = left[own][at : at + 1, :], right[own][at : at + 1, :]
-        pivot = row[:, j : j + 1]
-        inverse_ref[j : j + 1, :] = row_right * (lax.rsqrt(pivot) * scale)
-        by_pivot = 1.0 / pivot
-        row, row_right = row * by_pivot, row_right * by_pivot
-        for b in range(own + (at == height - 1), count):
-            factor = left[b][:, j : j + 1]
-            if b == own:
-                factor = jnp.where(ids[:, :1] > at, factor, 0.0)
-            left[b] = left[b] - factor * row
-            right[b] = right[b] - factor * row_right
+    width = 8
+    shape = (width, VECS)
+    panels = VECS // width
+    ids = lax.broadcasted_iota(jnp.int32, shape, 0)
+    lanes = lax.broadcasted_iota(jnp.int32, shape, 1)
+
+    def spread(value):
+        return jnp.broadcast_to(value, shape)
+
+    left = [gram_ref[width * b : width * (b + 1), :] for b in range(panels)]
+    right = [jnp.where(ids + width * b == lanes, 1.0, 0.0) for b in range(panels)]
+    for p in range(panels):
+        base = width * p
+        columns = [spread(left[p][:, base + c : base + c + 1]) for c in range(width)]
+        entry = {
+            (i, c): spread(columns[c][i : i + 1, :]) for i in range(width) for c in range(i + 1)
+        }
+        inverse, l, n = [], {}, {}
+        for j in range(width):
+            inverse.append(1.0 / entry[j, j])
+            for i in range(j + 1, width):
+                l[i, j] = entry[i, j] * inverse[j]
+            for c in range(j + 1, width):
+                for i in range(c, width):
+                    entry[i, c] = entry[i, c] - l[i, j] * entry[c, j]
+        for j in range(width):
+            for i in range(j + 1, width):
+                n[i, j] = -total_of([l[i, j], *(l[i, m] * n[m, j] for m in range(j + 1, i))])
+        factors = []
+        for side in (left, right):
+            raw = [spread(side[p][i : i + 1, :]) for i in range(width)]
+            done = [total_of([raw[i], *(n[i, j] * raw[j] for j in range(i))]) for i in range(width)]
+            if side is right:
+                for i in range(width):
+                    row = done[i] * (lax.rsqrt(entry[i, i]) * scale)
+                    inverse_ref[base + i : base + i + 1, :] = row[:1, :]
+            done = [d * v for d, v in zip(done, inverse)]
+            factors.append(
+                [
+                    total_of([done[c], *(n[i, c] * done[i] for i in range(c + 1, width))])
+                    for c in range(width)
+                ]
+            )
+        for b in range(p + 1, panels):
+            columns = [spread(left[b][:, base + c : base + c + 1]) for c in range(width)]
+            for side, rows in zip((left, right), factors):
+                side[b] = side[b] - total_of(c * r for c, r in zip(columns, rows))
     out_ref[...] = dot(field_ref[...], inverse_ref[...], ((1,), (1,)), lax.Precision.HIGHEST)
 
 
@@ -342,27 +408,31 @@
     asked = as_row(far_src)
     wanted = [swap(asked, *link) for link in FAR_LINKS]
     here = place.astype(jnp.int32).reshape(1)
-    band, hot, coef = prepare(
+    band, hot, coef, field = prepare(
         here,
-        jnp.transpose(band_cols, (1, 2, 0)),
-        jnp.transpose(band_wts, (1, 2, 0)),
         as_row(far_dst),
         as_row(far_wts),
+        jnp.transpose(band_wts, (1, 2, 0)),
+        jnp.transpose(band_cols, (1, 2, 0)),
+        start_basis,
     )
     wanted, band = lax.optimization_barrier((wanted, band))
-    pick_mat, *sent = first(here, start_basis, wanted)
+    pick_mat, *sent = first(here, field, wanted)
 
     def exchange(sent):
         return [swap(v, *link) for v, link in zip(sent, LINKS, strict=True)]
 
-    previous, packed = start_basis, start_basis
+    previous, packed = field, field
     mats = (band, hot, coef, pick_mat)
     got = exchange(sent)
-    current, packed, *sent = step(1.0 / HALF_WIDTH, here, mats, packed, None, got)
-    for _ in range(DEGREE - 2):
+    packed, *sent, current = step(1.0 / HALF_WIDTH, here, mats, packed, None, got)
+    for _ in range(DEGREE - 3):
         got = exchange(sent)
-        following, packed, *sent = step(2.0 / HALF_WIDTH, here, mats, packed, previous, got)
+        packed, *sent, following = step(2.0 / HALF_WIDTH, here, mats, packed, previous, got)
         previous, current = current, following
+    got = exchange(sent)
+    packed, *sent = step(2.0 / HALF_WIDTH, here, mats, packed, previous, got, has_next=False)
+    previous = current
     got = exchange(sent)
     filtered, gram = last(2.0 / HALF_WIDTH, here, mats[:3], packed, previous, got)
     return finish(math.sqrt(total_rows), summed(gram, count), filtered)

time: 145 us -> 137 us (0.945)
  Pallas kernels: 30.3 us -> 22.4 us
    pallas_call x1, Pallas kernels: 12.7 us -> 7.14 us  [finish(): pl.pallas_call(lambda *refs: finish_kernel(scale, *refs), out_shape=jax.S...]
    pallas_call x7, Pallas kernels: 10.8 us -> 8.25 us  [step(): pl.pallas_call(lambda *refs: step_kernel(scale, has_prev, has_next, *refs...]
where the time goes in v2:
time: 137 us
  starting transfers between devices  64.9 us (47%)
  waiting for transfers between devices  44.8 us (33%)
  Pallas kernels  22.4 us (16%)
  local copies, waits for them, and re-layouts  4.25 us (3%)
    ppermute x52, starting transfers between devices, swap(): return lax.ppermute(value, AXES, swap_pairs(count, by, odd))  56.8 us
    ppermute x52, waiting for transfers between devices, swap(): return lax.ppermute(value, AXES, swap_pairs(count, by, odd))  37.4 us
    pallas_call x7, Pallas kernels, step(): pl.pallas_call(lambda *refs: step_kernel(scale, has_prev, has_next, *refs...  8.25 us
    ppermute x7, starting transfers between devices, summed(): lax.ppermute(value, AXES, [(i, i ^ mask) for i in range(count)])  8.07 us
    ppermute x7, waiting for transfers between devices, summed(): lax.ppermute(value, AXES, [(i, i ^ mask) for i in range(count)])  7.42 us
    pallas_call x1, Pallas kernels, finish(): pl.pallas_call(lambda *refs: finish_kernel(scale, *refs), out_shape=jax.S...  7.14 us
    pallas_call x1, Pallas kernels, prepare(): pl.pallas_call(prepare_kernel, out_shape=(jax.ShapeDtypeStruct((rows, 3 *...  4.56 us
    unnamed x10, local copies, waits for them, and re-layouts  4.25 us
  transfers between devices with their start and end apart: 59, of which 30 were waited for; matrix products, arithmetic and copies ran while one was open for 0% of the time, Pallas kernels for 3%

profile of v2, /device:TPU:0, one launch (start us, length us, event | category | flops | bytes accessed | tf_op | source)
XLA Modules:
  0.0 136.6 jit_solution(1709665698482997235)
XLA Ops:
  0.0 6.0 %collective-permute-start.3 = (s32[1,256]{1,0:T(1,128)}, s32[1,256]{1,0:T(1,128)S(1)}, u32[]{:S(2)}, u32[]{:S(2)}) collective-permute-start(s32[1,256]{1,0:T(1,128)} %bitcast.10), channel_id=1, source_target_pairs={{4,8},{8,4},{5,9},{9,5},{6,10},{10,6},{7,11},{11,7},{12,16},{16,12... | collective-permute-start | bytes 3080 | tf_op jit(solution)/shard_map/ppermute | solution.py:403
  6.0 2.8 %collective-permute-start.1 = (s32[1,256]{1,0:T(1,128)}, s32[1,256]{1,0:T(1,128)S(1)}, u32[]{:S(2)}, u32[]{:S(2)}) collective-permute-start(s32[1,256]{1,0:T(1,128)} %bitcast.12), channel_id=1, source_target_pairs={{2,4},{4,2},{3,5},{5,3},{6,8},{8,6},{7,9},{9,7},{10,12},{12,10},{1... | collective-permute-start | bytes 3080 | tf_op jit(solution)/shard_map/ppermute | solution.py:403
  9.5 1.0 copy-done
  10.5 0.9 copy-done.1
  11.5 0.9 copy-done.2
  13.8 4.6 %prepare.1 = (bf16[2048,384]{1,0:T(8,128)(2,1)S(1)}, bf16[2048,256]{1,0:T(8,128)(2,1)S(1)}, f32[256,128]{1,0:T(8,128)S(1)}, bf16[2048,128]{1,0:T(8,128)(2,1)S(1)}) custom-call(s32[1]{0:T(128)} %bitcast.place_ref.refs_0_, s32[1,256]{1,0:T(1,128)S(1)} %bitcast.8, f32[1,256]{1,0:T(1,128)S(1)} %bitcast.9, f32[3,8,2048]{2,1,0:T(8,128)S(1)} %bitcast.6, ...), custom_call_target="tpu_custom_call" | custom-call | tf_op jit(solution)/shard_map/prepare/pallas_call | solution.py:145
  18.4 0.7 first.1
  19.0 2.8 %collective-permute-start.4 = (bf16[128,128]{1,0:T(8,128)(2,1)S(1)}, bf16[128,128]{1,0:T(8,128)(2,1)S(1)}, u32[]{:S(2)}, u32[]{:S(2)}) collective-permute-start(bf16[128,128]{1,0:T(8,128)(2,1)S(1)} %get-tuple-element.88), channel_id=1, source_target_pairs={{4,8},{8,4},{5,9},{9,5},{6,10},{10,6},{7,11},{11,7},{12,16},{16,12... | collective-permute-start | bytes 98312 | tf_op jit(solution)/shard_map/ppermute | solution.py:403
  21.8 2.8 %collective-permute-start.5 = (bf16[128,128]{1,0:T(8,128)(2,1)S(1)}, bf16[128,128]{1,0:T(8,128)(2,1)S(1)}, u32[]{:S(2)}, u32[]{:S(2)}) collective-permute-start(bf16[128,128]{1,0:T(8,128)(2,1)S(1)} %get-tuple-element.89), channel_id=1, source_target_pairs={{2,4},{4,2},{3,5},{5,3},{6,8},{8,6},{7,9},{9,7},{10,12},{12,10},{1... | collective-permute-start | bytes 98312 | tf_op jit(solution)/shard_map/ppermute | solution.py:403
  24.6 0.8 collective-permute-start.6
  25.7 1.2 collective-permute-start.9
  26.9 2.4 %collective-permute-done.5.refs_7_ = bf16[128,128]{1,0:T(8,128)(2,1)S(1)} collective-permute-done((bf16[128,128]{1,0:T(8,128)(2,1)S(1)}, bf16[128,128]{1,0:T(8,128)(2,1)S(1)}, u32[]{:S(2)}, u32[]{:S(2)}) %collective-permute-start.5) | collective-permute-done | bytes 32800 | tf_op jit(solution)/shard_map/ppermute | solution.py:403
  29.3 2.2 %collective-permute-done.6.refs_8_ = bf16[128,128]{1,0:T(8,128)(2,1)S(1)} collective-permute-done((bf16[128,128]{1,0:T(8,128)(2,1)S(1)}, bf16[128,128]{1,0:T(8,128)(2,1)S(1)}, u32[]{:S(2)}, u32[]{:S(2)}) %collective-permute-start.6) | collective-permute-done | bytes 32800 | tf_op jit(solution)/shard_map/ppermute | solution.py:403
  31.6 1.2 step.7
  32.8 1.9 %collective-permute-start.11 = (bf16[128,128]{1,0:T(8,128)(2,1)S(1)}, bf16[128,128]{1,0:T(8,128)(2,1)S(1)}, u32[]{:S(2)}, u32[]{:S(2)}) collective-permute-start(bf16[128,128]{1,0:T(8,128)(2,1)S(1)} %get-tuple-element.96), channel_id=1, source_target_pairs={{2,4},{4,2},{3,5},{5,3},{6,8},{8,6},{7,9},{9,7},{10,12},{12,10},{1... | collective-permute-start | bytes 98312 | tf_op jit(solution)/shard_map/ppermute | solution.py:403
  34.8 3.1 %collective-permute-start.12 = (bf16[128,128]{1,0:T(8,128)(2,1)S(1)}, bf16[128,128]{1,0:T(8,128)(2,1)S(1)}, u32[]{:S(2)}, u32[]{:S(2)}) collective-permute-start(bf16[128,128]{1,0:T(8,128)(2,1)S(1)} %get-tuple-element.97), channel_id=1, source_target_pairs={{1,2},{2,1},{3,4},{4,3},{5,6},{6,5},{7,8},{8,7},{9,10},{10,9},{11,... | collective-permute-start | bytes 98312 | tf_op jit(solution)/shard_map/ppermute | solution.py:403
  37.9 1.9 %collective-permute-done.10.refs_7_ = bf16[128,128]{1,0:T(8,128)(2,1)S(1)} collective-permute-done((bf16[128,128]{1,0:T(8,128)(2,1)S(1)}, bf16[128,128]{1,0:T(8,128)(2,1)S(1)}, u32[]{:S(2)}, u32[]{:S(2)}) %collective-permute-start.10) | collective-permute-done | bytes 32800 | tf_op jit(solution)/shard_map/ppermute | solution.py:403
  40.4 1.3 collective-permute-done.12.refs_9_
  42.1 1.1 step.8
  43.2 0.9 collective-permute-start.16
  44.1 3.0 %collective-permute-start.17 = (bf16[128,128]{1,0:T(8,128)(2,1)S(1)}, bf16[128,128]{1,0:T(8,128)(2,1)S(1)}, u32[]{:S(2)}, u32[]{:S(2)}) collective-permute-start(bf16[128,128]{1,0:T(8,128)(2,1)S(1)} %get-tuple-element.104), channel_id=1, source_target_pairs={{2,4},{4,2},{3,5},{5,3},{6,8},{8,6},{7,9},{9,7},{10,12},{12,10},{1... | collective-permute-start | bytes 98312 | tf_op jit(solution)/shard_map/ppermute | solution.py:403
  47.2 2.4 %collective-permute-start.18 = (bf16[128,128]{1,0:T(8,128)(2,1)S(1)}, bf16[128,128]{1,0:T(8,128)(2,1)S(1)}, u32[]{:S(2)}, u32[]{:S(2)}) collective-permute-start(bf16[128,128]{1,0:T(8,128)(2,1)S(1)} %get-tuple-element.105), channel_id=1, source_target_pairs={{1,2},{2,1},{3,4},{4,3},{5,6},{6,5},{7,8},{8,7},{9,10},{10,9},{11,... | collective-permute-start | bytes 98312 | tf_op jit(solution)/shard_map/ppermute | solution.py:403
  49.9 1.8 %collective-permute-done.17.refs_8_ = bf16[128,128]{1,0:T(8,128)(2,1)S(1)} collective-permute-done((bf16[128,128]{1,0:T(8,128)(2,1)S(1)}, bf16[128,128]{1,0:T(8,128)(2,1)S(1)}, u32[]{:S(2)}, u32[]{:S(2)}) %collective-permute-start.17) | collective-permute-done | bytes 32800 | tf_op jit(solution)/shard_map/ppermute | solution.py:403
  51.7 2.4 %collective-permute-done.18.refs_9_ = bf16[128,128]{1,0:T(8,128)(2,1)S(1)} collective-permute-done((bf16[128,128]{1,0:T(8,128)(2,1)S(1)}, bf16[128,128]{1,0:T(8,128)(2,1)S(1)}, u32[]{:S(2)}, u32[]{:S(2)}) %collective-permute-start.18) | collective-permute-done | bytes 32800 | tf_op jit(solution)/shard_map/ppermute | solution.py:403
  54.1 1.2 step.9
  55.3 3.5 %collective-permute-start.23 = (bf16[128,128]{1,0:T(8,128)(2,1)S(1)}, bf16[128,128]{1,0:T(8,128)(2,1)S(1)}, u32[]{:S(2)}, u32[]{:S(2)}) collective-permute-start(bf16[128,128]{1,0:T(8,128)(2,1)S(1)} %get-tuple-element.112), channel_id=1, source_target_pairs={{2,4},{4,2},{3,5},{5,3},{6,8},{8,6},{7,9},{9,7},{10,12},{12,10},{1... | collective-permute-start | bytes 98312 | tf_op jit(solution)/shard_map/ppermute | solution.py:403
  58.8 1.5 %collective-permute-start.24 = (bf16[128,128]{1,0:T(8,128)(2,1)S(1)}, bf16[128,128]{1,0:T(8,128)(2,1)S(1)}, u32[]{:S(2)}, u32[]{:S(2)}) collective-permute-start(bf16[128,128]{1,0:T(8,128)(2,1)S(1)} %get-tuple-element.113), channel_id=1, source_target_pairs={{1,2},{2,1},{3,4},{4,3},{5,6},{6,5},{7,8},{8,7},{9,10},{10,9},{11,... | collective-permute-start | bytes 98312 | tf_op jit(solution)/shard_map/ppermute | solution.py:403
  60.4 0.9 collective-permute-start.26
  61.3 1.0 collective-permute-done.22.refs_7_
  62.3 0.7 collective-permute-done.23.refs_8_
  63.0 2.9 %collective-permute-done.24.refs_9_ = bf16[128,128]{1,0:T(8,128)(2,1)S(1)} collective-permute-done((bf16[128,128]{1,0:T(8,128)(2,1)S(1)}, bf16[128,128]{1,0:T(8,128)(2,1)S(1)}, u32[]{:S(2)}, u32[]{:S(2)}) %collective-permute-start.24) | collective-permute-done | bytes 32800 | tf_op jit(solution)/shard_map/ppermute | solution.py:403
  65.9 1.2 step.10
  67.1 3.5 %collective-permute-start.29 = (bf16[128,128]{1,0:T(8,128)(2,1)S(1)}, bf16[128,128]{1,0:T(8,128)(2,1)S(1)}, u32[]{:S(2)}, u32[]{:S(2)}) collective-permute-start(bf16[128,128]{1,0:T(8,128)(2,1)S(1)} %get-tuple-element.120), channel_id=1, source_target_pairs={{2,4},{4,2},{3,5},{5,3},{6,8},{8,6},{7,9},{9,7},{10,12},{12,10},{1... | collective-permute-start | bytes 98312 | tf_op jit(solution)/shard_map/ppermute | solution.py:403
  70.6 1.4 %collective-permute-start.30 = (bf16[128,128]{1,0:T(8,128)(2,1)S(1)}, bf16[128,128]{1,0:T(8,128)(2,1)S(1)}, u32[]{:S(2)}, u32[]{:S(2)}) collective-permute-start(bf16[128,128]{1,0:T(8,128)(2,1)S(1)} %get-tuple-element.121), channel_id=1, source_target_pairs={{1,2},{2,1},{3,4},{4,3},{5,6},{6,5},{7,8},{8,7},{9,10},{10,9},{11,... | collective-permute-start | bytes 98312 | tf_op jit(solution)/shard_map/ppermute | solution.py:403
  72.3 1.8 %collective-permute-done.28.refs_7_ = bf16[128,128]{1,0:T(8,128)(2,1)S(1)} collective-permute-done((bf16[128,128]{1,0:T(8,128)(2,1)S(1)}, bf16[128,128]{1,0:T(8,128)(2,1)S(1)}, u32[]{:S(2)}, u32[]{:S(2)}) %collective-permute-start.28) | collective-permute-done | bytes 32800 | tf_op jit(solution)/shard_map/ppermute | solution.py:403
  74.7 2.9 %collective-permute-done.30.refs_9_ = bf16[128,128]{1,0:T(8,128)(2,1)S(1)} collective-permute-done((bf16[128,128]{1,0:T(8,128)(2,1)S(1)}, bf16[128,128]{1,0:T(8,128)(2,1)S(1)}, u32[]{:S(2)}, u32[]{:S(2)}) %collective-permute-start.30) | collective-permute-done | bytes 32800 | tf_op jit(solution)/shard_map/ppermute | solution.py:403
  77.6 1.4 step.11
  79.1 2.7 %collective-permute-start.35 = (bf16[128,128]{1,0:T(8,128)(2,1)S(1)}, bf16[128,128]{1,0:T(8,128)(2,1)S(1)}, u32[]{:S(2)}, u32[]{:S(2)}) collective-permute-start(bf16[128,128]{1,0:T(8,128)(2,1)S(1)} %get-tuple-element.128), channel_id=1, source_target_pairs={{2,4},{4,2},{3,5},{5,3},{6,8},{8,6},{7,9},{9,7},{10,12},{12,10},{1... | collective-permute-start | bytes 98312 | tf_op jit(solution)/shard_map/ppermute | solution.py:403
  81.8 2.2 %collective-permute-start.36 = (bf16[128,128]{1,0:T(8,128)(2,1)S(1)}, bf16[128,128]{1,0:T(8,128)(2,1)S(1)}, u32[]{:S(2)}, u32[]{:S(2)}) collective-permute-start(bf16[128,128]{1,0:T(8,128)(2,1)S(1)} %get-tuple-element.129), channel_id=1, source_target_pairs={{1,2},{2,1},{3,4},{4,3},{5,6},{6,5},{7,8},{8,7},{9,10},{10,9},{11,... | collective-permute-start | bytes 98312 | tf_op jit(solution)/shard_map/ppermute | solution.py:403
  84.1 1.9 %collective-permute-done.34.refs_7_ = bf16[128,128]{1,0:T(8,128)(2,1)S(1)} collective-permute-done((bf16[128,128]{1,0:T(8,128)(2,1)S(1)}, bf16[128,128]{1,0:T(8,128)(2,1)S(1)}, u32[]{:S(2)}, u32[]{:S(2)}) %collective-permute-start.34) | collective-permute-done | bytes 32800 | tf_op jit(solution)/shard_map/ppermute | solution.py:403
  86.1 0.7 collective-permute-done.35.refs_8_
  86.8 1.9 %collective-permute-done.36.refs_9_ = bf16[128,128]{1,0:T(8,128)(2,1)S(1)} collective-permute-done((bf16[128,128]{1,0:T(8,128)(2,1)S(1)}, bf16[128,128]{1,0:T(8,128)(2,1)S(1)}, u32[]{:S(2)}, u32[]{:S(2)}) %collective-permute-start.36) | collective-permute-done | bytes 32800 | tf_op jit(solution)/shard_map/ppermute | solution.py:403
  88.7 1.1 step.12
  90.4 3.0 %collective-permute-start.41 = (bf16[128,128]{1,0:T(8,128)(2,1)S(1)}, bf16[128,128]{1,0:T(8,128)(2,1)S(1)}, u32[]{:S(2)}, u32[]{:S(2)}) collective-permute-start(bf16[128,128]{1,0:T(8,128)(2,1)S(1)} %get-tuple-element.136), channel_id=1, source_target_pairs={{2,4},{4,2},{3,5},{5,3},{6,8},{8,6},{7,9},{9,7},{10,12},{12,10},{1... | collective-permute-start | bytes 98312 | tf_op jit(solution)/shard_map/ppermute | solution.py:403
  93.4 2.4 %collective-permute-start.42 = (bf16[128,128]{1,0:T(8,128)(2,1)S(1)}, bf16[128,128]{1,0:T(8,128)(2,1)S(1)}, u32[]{:S(2)}, u32[]{:S(2)}) collective-permute-start(bf16[128,128]{1,0:T(8,128)(2,1)S(1)} %get-tuple-element.137), channel_id=1, source_target_pairs={{1,2},{2,1},{3,4},{4,3},{5,6},{6,5},{7,8},{8,7},{9,10},{10,9},{11,... | collective-permute-start | bytes 98312 | tf_op jit(solution)/shard_map/ppermute | solution.py:403
  95.8 0.8 collective-permute-done.40.refs_7_
  96.5 1.4 %collective-permute-done.41.refs_8_ = bf16[128,128]{1,0:T(8,128)(2,1)S(1)} collective-permute-done((bf16[128,128]{1,0:T(8,128)(2,1)S(1)}, bf16[128,128]{1,0:T(8,128)(2,1)S(1)}, u32[]{:S(2)}, u32[]{:S(2)}) %collective-permute-start.41) | collective-permute-done | bytes 32800 | tf_op jit(solution)/shard_map/ppermute | solution.py:403
  97.9 2.4 %collective-permute-done.42.refs_9_ = bf16[128,128]{1,0:T(8,128)(2,1)S(1)} collective-permute-done((bf16[128,128]{1,0:T(8,128)(2,1)S(1)}, bf16[128,128]{1,0:T(8,128)(2,1)S(1)}, u32[]{:S(2)}, u32[]{:S(2)}) %collective-permute-start.42) | collective-permute-done | bytes 32800 | tf_op jit(solution)/shard_map/ppermute | solution.py:403
  100.4 1.2 step.13
  101.6 3.5 %collective-permute-start.47 = (bf16[128,128]{1,0:T(8,128)(2,1)S(1)}, bf16[128,128]{1,0:T(8,128)(2,1)S(1)}, u32[]{:S(2)}, u32[]{:S(2)}) collective-permute-start(bf16[128,128]{1,0:T(8,128)(2,1)S(1)} %get-tuple-element.144), channel_id=1, source_target_pairs={{2,4},{4,2},{3,5},{5,3},{6,8},{8,6},{7,9},{9,7},{10,12},{12,10},{1... | collective-permute-start | bytes 98312 | tf_op jit(solution)/shard_map/ppermute | solution.py:403
  105.1 1.6 %collective-permute-start.48 = (bf16[128,128]{1,0:T(8,128)(2,1)S(1)}, bf16[128,128]{1,0:T(8,128)(2,1)S(1)}, u32[]{:S(2)}, u32[]{:S(2)}) collective-permute-start(bf16[128,128]{1,0:T(8,128)(2,1)S(1)} %get-tuple-element.145), channel_id=1, source_target_pairs={{1,2},{2,1},{3,4},{4,3},{5,6},{6,5},{7,8},{8,7},{9,10},{10,9},{11,... | collective-permute-start | bytes 98312 | tf_op jit(solution)/shard_map/ppermute | solution.py:403
  106.6 0.8 collective-permute-start.50
  107.5 1.1 collective-permute-done.46.refs_6_
  109.2 2.9 %collective-permute-done.48.refs_8_ = bf16[128,128]{1,0:T(8,128)(2,1)S(1)} collective-permute-done((bf16[128,128]{1,0:T(8,128)(2,1)S(1)}, bf16[128,128]{1,0:T(8,128)(2,1)S(1)}, u32[]{:S(2)}, u32[]{:S(2)}) %collective-permute-start.48) | collective-permute-done | bytes 32800 | tf_op jit(solution)/shard_map/ppermute | solution.py:403
  112.1 1.8 %last.1 = (f32[2048,128]{1,0:T(8,128)S(1)}, f32[128,128]{1,0:T(8,128)S(1)}) custom-call(s32[1]{0:T(128)} %bitcast.place_ref.refs_0_, bf16[2048,384]{1,0:T(8,128)(2,1)S(1)} %get-tuple-element.79.refs_1_, bf16[2048,256]{1,0:T(8,128)(2,1)S(1)} %get-tuple-element.80.refs_2_, f32[256,128]{1,0:T(8,128)S(1)} %get-tuple-element.81.refs_3_, ...), custom_call_target="tpu_custom_call" | custom-call | tf_op jit(solution)/shard_map/last/pallas_call | solution.py:301
  114.0 1.2 collective-permute-done.52
  115.3 0.9 collective-permute-start.54
  116.2 2.6 %collective-permute-start.53 = (f32[128,128]{1,0:T(8,128)S(1)}, f32[128,128]{1,0:T(8,128)S(1)}, u32[]{:S(2)}, u32[]{:S(2)}) collective-permute-start(f32[128,128]{1,0:T(8,128)S(1)} %add.25), channel_id=1, source_target_pairs={{0,2},{1,3},{2,0},{3,1},{4,6},{5,7},{6,4},{7,5},{8,10},{9,11},{10,... | collective-permute-start | bytes 196616 | tf_op jit(solution)/shard_map/ppermute | solution.py:392
  118.8 2.3 %collective-permute-done.55 = f32[128,128]{1,0:T(8,128)S(1)} collective-permute-done((f32[128,128]{1,0:T(8,128)S(1)}, f32[128,128]{1,0:T(8,128)S(1)}, u32[]{:S(2)}, u32[]{:S(2)}) %collective-permute-start.55) | collective-permute-done | bytes 65568 | tf_op jit(solution)/shard_map/ppermute | solution.py:392
  121.2 1.8 %collective-permute-start.58 = (f32[128,128]{1,0:T(8,128)S(1)}, f32[128,128]{1,0:T(8,128)S(1)}, u32[]{:S(2)}, u32[]{:S(2)}) collective-permute-start(f32[128,128]{1,0:T(8,128)S(1)} %add_add_fusion.1), channel_id=1, source_target_pairs={{0,24},{1,25},{2,26},{3,27},{4,28},{5,29},{6,30},{7,31},{8,16},{9,... | collective-permute-start | bytes 196616 | tf_op jit(solution)/shard_map/ppermute | solution.py:392
  123.1 2.6 %collective-permute-start.56 = (f32[128,128]{1,0:T(8,128)S(1)}, f32[128,128]{1,0:T(8,128)S(1)}, u32[]{:S(2)}, u32[]{:S(2)}) collective-permute-start(f32[128,128]{1,0:T(8,128)S(1)} %add_add_fusion.1), channel_id=1, source_target_pairs={{0,8},{1,9},{2,10},{3,11},{4,12},{5,13},{6,14},{7,15},{8,0},{9,1},... | collective-permute-start | bytes 196616 | tf_op jit(solution)/shard_map/ppermute | solution.py:392
  125.7 2.4 %collective-permute-done.58 = f32[128,128]{1,0:T(8,128)S(1)} collective-permute-done((f32[128,128]{1,0:T(8,128)S(1)}, f32[128,128]{1,0:T(8,128)S(1)}, u32[]{:S(2)}, u32[]{:S(2)}) %collective-permute-start.58) | collective-permute-done | bytes 65568 | tf_op jit(solution)/shard_map/ppermute | solution.py:392
  128.1 1.3 collective-permute-done.57
  129.5 7.1 %finish.1 = f32[2048,128]{1,0:T(8,128)} custom-call(f32[128,128]{1,0:T(8,128)S(1)} %add_add_fusion.refs_0_, f32[2048,128]{1,0:T(8,128)S(1)} %get-tuple-element.150.refs_1_), custom_call_target="tpu_custom_call" | custom-call | tf_op jit(solution)/shard_map/finish/pallas_call | solution.py:374
  (78 shorter events, 6.6 us)
Async XLA Ops:
  0.0 18.3 %collective-permute-start.3 = (s32[1,256]{1,0:T(1,128)}, s32[1,256]{1,0:T(1,128)S(1)}, u32[]{:S(2)}, u32[]{:S(2)}) collective-permute-start(s32[1,256]{1,0:T(1,128)} %bitcast.10), channel_id=1, source_target_pairs={{4,8},{8,4},{5,9},{9,5},{6,10},{10,6},{7,11},{11,7},{12,16},{16,12... | collective-permute-start | bytes 3080 | tf_op jit(solution)/shard_map/ppermute | solution.py:403
  6.0 12.3 %collective-permute-start.2 = (s32[1,256]{1,0:T(1,128)}, s32[1,256]{1,0:T(1,128)S(1)}, u32[]{:S(2)}, u32[]{:S(2)}) collective-permute-start(s32[1,256]{1,0:T(1,128)} %bitcast.11), channel_id=1, source_target_pairs={{0,4},{4,0},{1,5},{5,1},{2,6},{6,2},{3,7},{7,3},{8,12},{12,8},{9,1... | collective-permute-start | bytes 3080 | tf_op jit(solution)/shard_map/ppermute | solution.py:403
  6.0 12.3 %collective-permute-start.1 = (s32[1,256]{1,0:T(1,128)}, s32[1,256]{1,0:T(1,128)S(1)}, u32[]{:S(2)}, u32[]{:S(2)}) collective-permute-start(s32[1,256]{1,0:T(1,128)} %bitcast.12), channel_id=1, source_target_pairs={{2,4},{4,2},{3,5},{5,3},{6,8},{8,6},{7,9},{9,7},{10,12},{12,10},{1... | collective-permute-start | bytes 3080 | tf_op jit(solution)/shard_map/ppermute | solution.py:403
  8.8 9.5 %collective-permute-start = (s32[1,256]{1,0:T(1,128)}, s32[1,256]{1,0:T(1,128)S(1)}, u32[]{:S(2)}, u32[]{:S(2)}) collective-permute-start(s32[1,256]{1,0:T(1,128)} %bitcast.13), channel_id=1, source_target_pairs={{0,2},{2,0},{1,3},{3,1},{4,6},{6,4},{5,7},{7,5},{8,10},{10,8},{9,1... | collective-permute-start | bytes 3080 | tf_op jit(solution)/shard_map/ppermute | solution.py:403
  9.5 1.0 copy-start
  10.5 0.9 copy-start.1
  11.5 0.9 copy-start.2
  12.4 0.7 copy-start.3
  13.1 0.7 copy-start.4
  19.0 6.7 %collective-permute-start.4 = (bf16[128,128]{1,0:T(8,128)(2,1)S(1)}, bf16[128,128]{1,0:T(8,128)(2,1)S(1)}, u32[]{:S(2)}, u32[]{:S(2)}) collective-permute-start(bf16[128,128]{1,0:T(8,128)(2,1)S(1)} %get-tuple-element.88), channel_id=1, source_target_pairs={{4,8},{8,4},{5,9},{9,5},{6,10},{10,6},{7,11},{11,7},{12,16},{16,12... | collective-permute-start | bytes 98312 | tf_op jit(solution)/shard_map/ppermute | solution.py:403
  21.8 7.5 %collective-permute-start.5 = (bf16[128,128]{1,0:T(8,128)(2,1)S(1)}, bf16[128,128]{1,0:T(8,128)(2,1)S(1)}, u32[]{:S(2)}, u32[]{:S(2)}) collective-permute-start(bf16[128,128]{1,0:T(8,128)(2,1)S(1)} %get-tuple-element.89), channel_id=1, source_target_pairs={{2,4},{4,2},{3,5},{5,3},{6,8},{8,6},{7,9},{9,7},{10,12},{12,10},{1... | collective-permute-start | bytes 98312 | tf_op jit(solution)/shard_map/ppermute | solution.py:403
  24.6 6.9 %collective-permute-start.6 = (bf16[128,128]{1,0:T(8,128)(2,1)S(1)}, bf16[128,128]{1,0:T(8,128)(2,1)S(1)}, u32[]{:S(2)}, u32[]{:S(2)}) collective-permute-start(bf16[128,128]{1,0:T(8,128)(2,1)S(1)} %get-tuple-element.90), channel_id=1, source_target_pairs={{1,2},{2,1},{3,4},{4,3},{5,6},{6,5},{7,8},{8,7},{9,10},{10,9},{11,... | collective-permute-start | bytes 98312 | tf_op jit(solution)/shard_map/ppermute | solution.py:403
  25.5 6.1 %collective-permute-start.7 = (bf16[128,128]{1,0:T(8,128)(2,1)S(1)}, bf16[128,128]{1,0:T(8,128)(2,1)S(1)}, u32[]{:S(2)}, u32[]{:S(2)}) collective-permute-start(bf16[128,128]{1,0:T(8,128)(2,1)S(1)} %get-tuple-element.91), channel_id=1, source_target_pairs={{0,4},{4,0},{1,5},{5,1},{2,6},{6,2},{3,7},{7,3},{8,12},{12,8},{9,1... | collective-permute-start | bytes 98312 | tf_op jit(solution)/shard_map/ppermute | solution.py:403
  25.5 6.1 %collective-permute-start.8 = (bf16[128,128]{1,0:T(8,128)(2,1)S(1)}, bf16[128,128]{1,0:T(8,128)(2,1)S(1)}, u32[]{:S(2)}, u32[]{:S(2)}) collective-permute-start(bf16[128,128]{1,0:T(8,128)(2,1)S(1)} %get-tuple-element.92), channel_id=1, source_target_pairs={{0,2},{2,0},{1,3},{3,1},{4,6},{6,4},{5,7},{7,5},{8,10},{10,8},{9,1... | collective-permute-start | bytes 98312 | tf_op jit(solution)/shard_map/ppermute | solution.py:403
  25.7 5.9 %collective-permute-start.9 = (bf16[128,128]{1,0:T(8,128)(2,1)S(1)}, bf16[128,128]{1,0:T(8,128)(2,1)S(1)}, u32[]{:S(2)}, u32[]{:S(2)}) collective-permute-start(bf16[128,128]{1,0:T(8,128)(2,1)S(1)} %get-tuple-element.93), channel_id=1, source_target_pairs={{0,1},{1,0},{2,3},{3,2},{4,5},{5,4},{6,7},{7,6},{8,9},{9,8},{10,11... | collective-permute-start | bytes 98312 | tf_op jit(solution)/shard_map/ppermute | solution.py:403
  32.8 7.0 %collective-permute-start.10 = (bf16[128,128]{1,0:T(8,128)(2,1)S(1)}, bf16[128,128]{1,0:T(8,128)(2,1)S(1)}, u32[]{:S(2)}, u32[]{:S(2)}) collective-permute-start(bf16[128,128]{1,0:T(8,128)(2,1)S(1)} %get-tuple-element.95), channel_id=1, source_target_pairs={{4,8},{8,4},{5,9},{9,5},{6,10},{10,6},{7,11},{11,7},{12,16},{16,12... | collective-permute-start | bytes 98312 | tf_op jit(solution)/shard_map/ppermute | solution.py:403
  32.8 7.6 %collective-permute-start.11 = (bf16[128,128]{1,0:T(8,128)(2,1)S(1)}, bf16[128,128]{1,0:T(8,128)(2,1)S(1)}, u32[]{:S(2)}, u32[]{:S(2)}) collective-permute-start(bf16[128,128]{1,0:T(8,128)(2,1)S(1)} %get-tuple-element.96), channel_id=1, source_target_pairs={{2,4},{4,2},{3,5},{5,3},{6,8},{8,6},{7,9},{9,7},{10,12},{12,10},{1... | collective-permute-start | bytes 98312 | tf_op jit(solution)/shard_map/ppermute | solution.py:403
  34.8 7.0 %collective-permute-start.12 = (bf16[128,128]{1,0:T(8,128)(2,1)S(1)}, bf16[128,128]{1,0:T(8,128)(2,1)S(1)}, u32[]{:S(2)}, u32[]{:S(2)}) collective-permute-start(bf16[128,128]{1,0:T(8,128)(2,1)S(1)} %get-tuple-element.97), channel_id=1, source_target_pairs={{1,2},{2,1},{3,4},{4,3},{5,6},{6,5},{7,8},{8,7},{9,10},{10,9},{11,... | collective-permute-start | bytes 98312 | tf_op jit(solution)/shard_map/ppermute | solution.py:403
  37.9 4.2 %collective-permute-start.13 = (bf16[128,128]{1,0:T(8,128)(2,1)S(1)}, bf16[128,128]{1,0:T(8,128)(2,1)S(1)}, u32[]{:S(2)}, u32[]{:S(2)}) collective-permute-start(bf16[128,128]{1,0:T(8,128)(2,1)S(1)} %get-tuple-element.98), channel_id=1, source_target_pairs={{0,4},{4,0},{1,5},{5,1},{2,6},{6,2},{3,7},{7,3},{8,12},{12,8},{9,1... | collective-permute-start | bytes 98312 | tf_op jit(solution)/shard_map/ppermute | solution.py:403
  37.9 4.2 %collective-permute-start.14 = (bf16[128,128]{1,0:T(8,128)(2,1)S(1)}, bf16[128,128]{1,0:T(8,128)(2,1)S(1)}, u32[]{:S(2)}, u32[]{:S(2)}) collective-permute-start(bf16[128,128]{1,0:T(8,128)(2,1)S(1)} %get-tuple-element.99), channel_id=1, source_target_pairs={{0,2},{2,0},{1,3},{3,1},{4,6},{6,4},{5,7},{7,5},{8,10},{10,8},{9,1... | collective-permute-start | bytes 98312 | tf_op jit(solution)/shard_map/ppermute | solution.py:403
  39.7 2.3 %collective-permute-start.15 = (bf16[128,128]{1,0:T(8,128)(2,1)S(1)}, bf16[128,128]{1,0:T(8,128)(2,1)S(1)}, u32[]{:S(2)}, u32[]{:S(2)}) collective-permute-start(bf16[128,128]{1,0:T(8,128)(2,1)S(1)} %get-tuple-element.100), channel_id=1, source_target_pairs={{0,1},{1,0},{2,3},{3,2},{4,5},{5,4},{6,7},{7,6},{8,9},{9,8},{10,11... | collective-permute-start | bytes 98312 | tf_op jit(solution)/shard_map/ppermute | solution.py:403
  43.2 6.7 %collective-permute-start.16 = (bf16[128,128]{1,0:T(8,128)(2,1)S(1)}, bf16[128,128]{1,0:T(8,128)(2,1)S(1)}, u32[]{:S(2)}, u32[]{:S(2)}) collective-permute-start(bf16[128,128]{1,0:T(8,128)(2,1)S(1)} %get-tuple-element.103), channel_id=1, source_target_pairs={{4,8},{8,4},{5,9},{9,5},{6,10},{10,6},{7,11},{11,7},{12,16},{16,12... | collective-permute-start | bytes 98312 | tf_op jit(solution)/shard_map/ppermute | solution.py:403
  44.1 7.5 %collective-permute-start.17 = (bf16[128,128]{1,0:T(8,128)(2,1)S(1)}, bf16[128,128]{1,0:T(8,128)(2,1)S(1)}, u32[]{:S(2)}, u32[]{:S(2)}) collective-permute-start(bf16[128,128]{1,0:T(8,128)(2,1)S(1)} %get-tuple-element.104), channel_id=1, source_target_pairs={{2,4},{4,2},{3,5},{5,3},{6,8},{8,6},{7,9},{9,7},{10,12},{12,10},{1... | collective-permute-start | bytes 98312 | tf_op jit(solution)/shard_map/ppermute | solution.py:403
  47.2 6.9 %collective-permute-start.18 = (bf16[128,128]{1,0:T(8,128)(2,1)S(1)}, bf16[128,128]{1,0:T(8,128)(2,1)S(1)}, u32[]{:S(2)}, u32[]{:S(2)}) collective-permute-start(bf16[128,128]{1,0:T(8,128)(2,1)S(1)} %get-tuple-element.105), channel_id=1, source_target_pairs={{1,2},{2,1},{3,4},{4,3},{5,6},{6,5},{7,8},{8,7},{9,10},{10,9},{11,... | collective-permute-start | bytes 98312 | tf_op jit(solution)/shard_map/ppermute | solution.py:403
  49.5 4.6 %collective-permute-start.19 = (bf16[128,128]{1,0:T(8,128)(2,1)S(1)}, bf16[128,128]{1,0:T(8,128)(2,1)S(1)}, u32[]{:S(2)}, u32[]{:S(2)}) collective-permute-start(bf16[128,128]{1,0:T(8,128)(2,1)S(1)} %get-tuple-element.106), channel_id=1, source_target_pairs={{0,4},{4,0},{1,5},{5,1},{2,6},{6,2},{3,7},{7,3},{8,12},{12,8},{9,1... | collective-permute-start | bytes 98312 | tf_op jit(solution)/shard_map/ppermute | solution.py:403
  49.5 4.6 %collective-permute-start.20 = (bf16[128,128]{1,0:T(8,128)(2,1)S(1)}, bf16[128,128]{1,0:T(8,128)(2,1)S(1)}, u32[]{:S(2)}, u32[]{:S(2)}) collective-permute-start(bf16[128,128]{1,0:T(8,128)(2,1)S(1)} %get-tuple-element.107), channel_id=1, source_target_pairs={{0,2},{2,0},{1,3},{3,1},{4,6},{6,4},{5,7},{7,5},{8,10},{10,8},{9,1... | collective-permute-start | bytes 98312 | tf_op jit(solution)/shard_map/ppermute | solution.py:403
  49.9 4.2 %collective-permute-start.21 = (bf16[128,128]{1,0:T(8,128)(2,1)S(1)}, bf16[128,128]{1,0:T(8,128)(2,1)S(1)}, u32[]{:S(2)}, u32[]{:S(2)}) collective-permute-start(bf16[128,128]{1,0:T(8,128)(2,1)S(1)} %get-tuple-element.108), channel_id=1, source_target_pairs={{0,1},{1,0},{2,3},{3,2},{4,5},{5,4},{6,7},{7,6},{8,9},{9,8},{10,11... | collective-permute-start | bytes 98312 | tf_op jit(solution)/shard_map/ppermute | solution.py:403
  55.3 7.0 %collective-permute-start.22 = (bf16[128,128]{1,0:T(8,128)(2,1)S(1)}, bf16[128,128]{1,0:T(8,128)(2,1)S(1)}, u32[]{:S(2)}, u32[]{:S(2)}) collective-permute-start(bf16[128,128]{1,0:T(8,128)(2,1)S(1)} %get-tuple-element.111), channel_id=1, source_target_pairs={{4,8},{8,4},{5,9},{9,5},{6,10},{10,6},{7,11},{11,7},{12,16},{16,12... | collective-permute-start | bytes 98312 | tf_op jit(solution)/shard_map/ppermute | solution.py:403
  55.3 7.7 %collective-permute-start.23 = (bf16[128,128]{1,0:T(8,128)(2,1)S(1)}, bf16[128,128]{1,0:T(8,128)(2,1)S(1)}, u32[]{:S(2)}, u32[]{:S(2)}) collective-permute-start(bf16[128,128]{1,0:T(8,128)(2,1)S(1)} %get-tuple-element.112), channel_id=1, source_target_pairs={{2,4},{4,2},{3,5},{5,3},{6,8},{8,6},{7,9},{9,7},{10,12},{12,10},{1... | collective-permute-start | bytes 98312 | tf_op jit(solution)/shard_map/ppermute | solution.py:403
  58.8 7.0 %collective-permute-start.24 = (bf16[128,128]{1,0:T(8,128)(2,1)S(1)}, bf16[128,128]{1,0:T(8,128)(2,1)S(1)}, u32[]{:S(2)}, u32[]{:S(2)}) collective-permute-start(bf16[128,128]{1,0:T(8,128)(2,1)S(1)} %get-tuple-element.113), channel_id=1, source_target_pairs={{1,2},{2,1},{3,4},{4,3},{5,6},{6,5},{7,8},{8,7},{9,10},{10,9},{11,... | collective-permute-start | bytes 98312 | tf_op jit(solution)/shard_map/ppermute | solution.py:403
  60.4 5.5 %collective-permute-start.25 = (bf16[128,128]{1,0:T(8,128)(2,1)S(1)}, bf16[128,128]{1,0:T(8,128)(2,1)S(1)}, u32[]{:S(2)}, u32[]{:S(2)}) collective-permute-start(bf16[128,128]{1,0:T(8,128)(2,1)S(1)} %get-tuple-element.114), channel_id=1, source_target_pairs={{0,4},{4,0},{1,5},{5,1},{2,6},{6,2},{3,7},{7,3},{8,12},{12,8},{9,1... | collective-permute-start | bytes 98312 | tf_op jit(solution)/shard_map/ppermute | solution.py:403
  60.4 5.5 %collective-permute-start.26 = (bf16[128,128]{1,0:T(8,128)(2,1)S(1)}, bf16[128,128]{1,0:T(8,128)(2,1)S(1)}, u32[]{:S(2)}, u32[]{:S(2)}) collective-permute-start(bf16[128,128]{1,0:T(8,128)(2,1)S(1)} %get-tuple-element.115), channel_id=1, source_target_pairs={{0,2},{2,0},{1,3},{3,1},{4,6},{6,4},{5,7},{7,5},{8,10},{10,8},{9,1... | collective-permute-start | bytes 98312 | tf_op jit(solution)/shard_map/ppermute | solution.py:403
  62.3 3.6 %collective-permute-start.27 = (bf16[128,128]{1,0:T(8,128)(2,1)S(1)}, bf16[128,128]{1,0:T(8,128)(2,1)S(1)}, u32[]{:S(2)}, u32[]{:S(2)}) collective-permute-start(bf16[128,128]{1,0:T(8,128)(2,1)S(1)} %get-tuple-element.116), channel_id=1, source_target_pairs={{0,1},{1,0},{2,3},{3,2},{4,5},{5,4},{6,7},{7,6},{8,9},{9,8},{10,11... | collective-permute-start | bytes 98312 | tf_op jit(solution)/shard_map/ppermute | solution.py:403
  67.0 7.1 %collective-permute-start.28 = (bf16[128,128]{1,0:T(8,128)(2,1)S(1)}, bf16[128,128]{1,0:T(8,128)(2,1)S(1)}, u32[]{:S(2)}, u32[]{:S(2)}) collective-permute-start(bf16[128,128]{1,0:T(8,128)(2,1)S(1)} %get-tuple-element.119), channel_id=1, source_target_pairs={{4,8},{8,4},{5,9},{9,5},{6,10},{10,6},{7,11},{11,7},{12,16},{16,12... | collective-permute-start | bytes 98312 | tf_op jit(solution)/shard_map/ppermute | solution.py:403
  67.1 7.6 %collective-permute-start.29 = (bf16[128,128]{1,0:T(8,128)(2,1)S(1)}, bf16[128,128]{1,0:T(8,128)(2,1)S(1)}, u32[]{:S(2)}, u32[]{:S(2)}) collective-permute-start(bf16[128,128]{1,0:T(8,128)(2,1)S(1)} %get-tuple-element.120), channel_id=1, source_target_pairs={{2,4},{4,2},{3,5},{5,3},{6,8},{8,6},{7,9},{9,7},{10,12},{12,10},{1... | collective-permute-start | bytes 98312 | tf_op jit(solution)/shard_map/ppermute | solution.py:403
  70.6 7.0 %collective-permute-start.30 = (bf16[128,128]{1,0:T(8,128)(2,1)S(1)}, bf16[128,128]{1,0:T(8,128)(2,1)S(1)}, u32[]{:S(2)}, u32[]{:S(2)}) collective-permute-start(bf16[128,128]{1,0:T(8,128)(2,1)S(1)} %get-tuple-element.121), channel_id=1, source_target_pairs={{1,2},{2,1},{3,4},{4,3},{5,6},{6,5},{7,8},{8,7},{9,10},{10,9},{11,... | collective-permute-start | bytes 98312 | tf_op jit(solution)/shard_map/ppermute | solution.py:403
  72.0 5.6 %collective-permute-start.31 = (bf16[128,128]{1,0:T(8,128)(2,1)S(1)}, bf16[128,128]{1,0:T(8,128)(2,1)S(1)}, u32[]{:S(2)}, u32[]{:S(2)}) collective-permute-start(bf16[128,128]{1,0:T(8,128)(2,1)S(1)} %get-tuple-element.122), channel_id=1, source_target_pairs={{0,4},{4,0},{1,5},{5,1},{2,6},{6,2},{3,7},{7,3},{8,12},{12,8},{9,1... | collective-permute-start | bytes 98312 | tf_op jit(solution)/shard_map/ppermute | solution.py:403
  72.0 5.6 %collective-permute-start.32 = (bf16[128,128]{1,0:T(8,128)(2,1)S(1)}, bf16[128,128]{1,0:T(8,128)(2,1)S(1)}, u32[]{:S(2)}, u32[]{:S(2)}) collective-permute-start(bf16[128,128]{1,0:T(8,128)(2,1)S(1)} %get-tuple-element.123), channel_id=1, source_target_pairs={{0,2},{2,0},{1,3},{3,1},{4,6},{6,4},{5,7},{7,5},{8,10},{10,8},{9,1... | collective-permute-start | bytes 98312 | tf_op jit(solution)/shard_map/ppermute | solution.py:403
  74.1 3.6 %collective-permute-start.33 = (bf16[128,128]{1,0:T(8,128)(2,1)S(1)}, bf16[128,128]{1,0:T(8,128)(2,1)S(1)}, u32[]{:S(2)}, u32[]{:S(2)}) collective-permute-start(bf16[128,128]{1,0:T(8,128)(2,1)S(1)} %get-tuple-element.124), channel_id=1, source_target_pairs={{0,1},{1,0},{2,3},{3,2},{4,5},{5,4},{6,7},{7,6},{8,9},{9,8},{10,11... | collective-permute-start | bytes 98312 | tf_op jit(solution)/shard_map/ppermute | solution.py:403
  79.0 7.0 %collective-permute-start.34 = (bf16[128,128]{1,0:T(8,128)(2,1)S(1)}, bf16[128,128]{1,0:T(8,128)(2,1)S(1)}, u32[]{:S(2)}, u32[]{:S(2)}) collective-permute-start(bf16[128,128]{1,0:T(8,128)(2,1)S(1)} %get-tuple-element.127), channel_id=1, source_target_pairs={{4,8},{8,4},{5,9},{9,5},{6,10},{10,6},{7,11},{11,7},{12,16},{16,12... | collective-permute-start | bytes 98312 | tf_op jit(solution)/shard_map/ppermute | solution.py:403
  79.1 7.7 %collective-permute-start.35 = (bf16[128,128]{1,0:T(8,128)(2,1)S(1)}, bf16[128,128]{1,0:T(8,128)(2,1)S(1)}, u32[]{:S(2)}, u32[]{:S(2)}) collective-permute-start(bf16[128,128]{1,0:T(8,128)(2,1)S(1)} %get-tuple-element.128), channel_id=1, source_target_pairs={{2,4},{4,2},{3,5},{5,3},{6,8},{8,6},{7,9},{9,7},{10,12},{12,10},{1... | collective-permute-start | bytes 98312 | tf_op jit(solution)/shard_map/ppermute | solution.py:403
  81.8 6.9 %collective-permute-start.36 = (bf16[128,128]{1,0:T(8,128)(2,1)S(1)}, bf16[128,128]{1,0:T(8,128)(2,1)S(1)}, u32[]{:S(2)}, u32[]{:S(2)}) collective-permute-start(bf16[128,128]{1,0:T(8,128)(2,1)S(1)} %get-tuple-element.129), channel_id=1, source_target_pairs={{1,2},{2,1},{3,4},{4,3},{5,6},{6,5},{7,8},{8,7},{9,10},{10,9},{11,... | collective-permute-start | bytes 98312 | tf_op jit(solution)/shard_map/ppermute | solution.py:403
  84.0 4.7 %collective-permute-start.37 = (bf16[128,128]{1,0:T(8,128)(2,1)S(1)}, bf16[128,128]{1,0:T(8,128)(2,1)S(1)}, u32[]{:S(2)}, u32[]{:S(2)}) collective-permute-start(bf16[128,128]{1,0:T(8,128)(2,1)S(1)} %get-tuple-element.130), channel_id=1, source_target_pairs={{0,4},{4,0},{1,5},{5,1},{2,6},{6,2},{3,7},{7,3},{8,12},{12,8},{9,1... | collective-permute-start | bytes 98312 | tf_op jit(solution)/shard_map/ppermute | solution.py:403
  84.0 4.7 %collective-permute-start.38 = (bf16[128,128]{1,0:T(8,128)(2,1)S(1)}, bf16[128,128]{1,0:T(8,128)(2,1)S(1)}, u32[]{:S(2)}, u32[]{:S(2)}) collective-permute-start(bf16[128,128]{1,0:T(8,128)(2,1)S(1)} %get-tuple-element.131), channel_id=1, source_target_pairs={{0,2},{2,0},{1,3},{3,1},{4,6},{6,4},{5,7},{7,5},{8,10},{10,8},{9,1... | collective-permute-start | bytes 98312 | tf_op jit(solution)/shard_map/ppermute | solution.py:403
  86.1 2.7 %collective-permute-start.39 = (bf16[128,128]{1,0:T(8,128)(2,1)S(1)}, bf16[128,128]{1,0:T(8,128)(2,1)S(1)}, u32[]{:S(2)}, u32[]{:S(2)}) collective-permute-start(bf16[128,128]{1,0:T(8,128)(2,1)S(1)} %get-tuple-element.132), channel_id=1, source_target_pairs={{0,1},{1,0},{2,3},{3,2},{4,5},{5,4},{6,7},{7,6},{8,9},{9,8},{10,11... | collective-permute-start | bytes 98312 | tf_op jit(solution)/shard_map/ppermute | solution.py:403
  89.9 6.7 %collective-permute-start.40 = (bf16[128,128]{1,0:T(8,128)(2,1)S(1)}, bf16[128,128]{1,0:T(8,128)(2,1)S(1)}, u32[]{:S(2)}, u32[]{:S(2)}) collective-permute-start(bf16[128,128]{1,0:T(8,128)(2,1)S(1)} %get-tuple-element.135), channel_id=1, source_target_pairs={{4,8},{8,4},{5,9},{9,5},{6,10},{10,6},{7,11},{11,7},{12,16},{16,12... | collective-permute-start | bytes 98312 | tf_op jit(solution)/shard_map/ppermute | solution.py:403
  90.4 7.5 %collective-permute-start.41 = (bf16[128,128]{1,0:T(8,128)(2,1)S(1)}, bf16[128,128]{1,0:T(8,128)(2,1)S(1)}, u32[]{:S(2)}, u32[]{:S(2)}) collective-permute-start(bf16[128,128]{1,0:T(8,128)(2,1)S(1)} %get-tuple-element.136), channel_id=1, source_target_pairs={{2,4},{4,2},{3,5},{5,3},{6,8},{8,6},{7,9},{9,7},{10,12},{12,10},{1... | collective-permute-start | bytes 98312 | tf_op jit(solution)/shard_map/ppermute | solution.py:403
  93.4 6.9 %collective-permute-start.42 = (bf16[128,128]{1,0:T(8,128)(2,1)S(1)}, bf16[128,128]{1,0:T(8,128)(2,1)S(1)}, u32[]{:S(2)}, u32[]{:S(2)}) collective-permute-start(bf16[128,128]{1,0:T(8,128)(2,1)S(1)} %get-tuple-element.137), channel_id=1, source_target_pairs={{1,2},{2,1},{3,4},{4,3},{5,6},{6,5},{7,8},{8,7},{9,10},{10,9},{11,... | collective-permute-start | bytes 98312 | tf_op jit(solution)/shard_map/ppermute | solution.py:403
  95.8 4.6 %collective-permute-start.43 = (bf16[128,128]{1,0:T(8,128)(2,1)S(1)}, bf16[128,128]{1,0:T(8,128)(2,1)S(1)}, u32[]{:S(2)}, u32[]{:S(2)}) collective-permute-start(bf16[128,128]{1,0:T(8,128)(2,1)S(1)} %get-tuple-element.138), channel_id=1, source_target_pairs={{0,4},{4,0},{1,5},{5,1},{2,6},{6,2},{3,7},{7,3},{8,12},{12,8},{9,1... | collective-permute-start | bytes 98312 | tf_op jit(solution)/shard_map/ppermute | solution.py:403
  95.8 4.6 %collective-permute-start.44 = (bf16[128,128]{1,0:T(8,128)(2,1)S(1)}, bf16[128,128]{1,0:T(8,128)(2,1)S(1)}, u32[]{:S(2)}, u32[]{:S(2)}) collective-permute-start(bf16[128,128]{1,0:T(8,128)(2,1)S(1)} %get-tuple-element.139), channel_id=1, source_target_pairs={{0,2},{2,0},{1,3},{3,1},{4,6},{6,4},{5,7},{7,5},{8,10},{10,8},{9,1... | collective-permute-start | bytes 98312 | tf_op jit(solution)/shard_map/ppermute | solution.py:403
  96.5 3.8 %collective-permute-start.45 = (bf16[128,128]{1,0:T(8,128)(2,1)S(1)}, bf16[128,128]{1,0:T(8,128)(2,1)S(1)}, u32[]{:S(2)}, u32[]{:S(2)}) collective-permute-start(bf16[128,128]{1,0:T(8,128)(2,1)S(1)} %get-tuple-element.140), channel_id=1, source_target_pairs={{0,1},{1,0},{2,3},{3,2},{4,5},{5,4},{6,7},{7,6},{8,9},{9,8},{10,11... | collective-permute-start | bytes 98312 | tf_op jit(solution)/shard_map/ppermute | solution.py:403
  101.5 7.0 %collective-permute-start.46 = (bf16[128,128]{1,0:T(8,128)(2,1)S(1)}, bf16[128,128]{1,0:T(8,128)(2,1)S(1)}, u32[]{:S(2)}, u32[]{:S(2)}) collective-permute-start(bf16[128,128]{1,0:T(8,128)(2,1)S(1)} %get-tuple-element.143), channel_id=1, source_target_pairs={{4,8},{8,4},{5,9},{9,5},{6,10},{10,6},{7,11},{11,7},{12,16},{16,12... | collective-permute-start | bytes 98312 | tf_op jit(solution)/shard_map/ppermute | solution.py:403
  101.6 7.6 %collective-permute-start.47 = (bf16[128,128]{1,0:T(8,128)(2,1)S(1)}, bf16[128,128]{1,0:T(8,128)(2,1)S(1)}, u32[]{:S(2)}, u32[]{:S(2)}) collective-permute-start(bf16[128,128]{1,0:T(8,128)(2,1)S(1)} %get-tuple-element.144), channel_id=1, source_target_pairs={{2,4},{4,2},{3,5},{5,3},{6,8},{8,6},{7,9},{9,7},{10,12},{12,10},{1... | collective-permute-start | bytes 98312 | tf_op jit(solution)/shard_map/ppermute | solution.py:403
  105.1 7.0 %collective-permute-start.48 = (bf16[128,128]{1,0:T(8,128)(2,1)S(1)}, bf16[128,128]{1,0:T(8,128)(2,1)S(1)}, u32[]{:S(2)}, u32[]{:S(2)}) collective-permute-start(bf16[128,128]{1,0:T(8,128)(2,1)S(1)} %get-tuple-element.145), channel_id=1, source_target_pairs={{1,2},{2,1},{3,4},{4,3},{5,6},{6,5},{7,8},{8,7},{9,10},{10,9},{11,... | collective-permute-start | bytes 98312 | tf_op jit(solution)/shard_map/ppermute | solution.py:403
  106.6 5.5 %collective-permute-start.49 = (bf16[128,128]{1,0:T(8,128)(2,1)S(1)}, bf16[128,128]{1,0:T(8,128)(2,1)S(1)}, u32[]{:S(2)}, u32[]{:S(2)}) collective-permute-start(bf16[128,128]{1,0:T(8,128)(2,1)S(1)} %get-tuple-element.146), channel_id=1, source_target_pairs={{0,4},{4,0},{1,5},{5,1},{2,6},{6,2},{3,7},{7,3},{8,12},{12,8},{9,1... | collective-permute-start | bytes 98312 | tf_op jit(solution)/shard_map/ppermute | solution.py:403
  106.6 5.5 %collective-permute-start.50 = (bf16[128,128]{1,0:T(8,128)(2,1)S(1)}, bf16[128,128]{1,0:T(8,128)(2,1)S(1)}, u32[]{:S(2)}, u32[]{:S(2)}) collective-permute-start(bf16[128,128]{1,0:T(8,128)(2,1)S(1)} %get-tuple-element.147), channel_id=1, source_target_pairs={{0,2},{2,0},{1,3},{3,1},{4,6},{6,4},{5,7},{7,5},{8,10},{10,8},{9,1... | collective-permute-start | bytes 98312 | tf_op jit(solution)/shard_map/ppermute | solution.py:403
  108.6 3.6 %collective-permute-start.51 = (bf16[128,128]{1,0:T(8,128)(2,1)S(1)}, bf16[128,128]{1,0:T(8,128)(2,1)S(1)}, u32[]{:S(2)}, u32[]{:S(2)}) collective-permute-start(bf16[128,128]{1,0:T(8,128)(2,1)S(1)} %get-tuple-element.148), channel_id=1, source_target_pairs={{0,1},{1,0},{2,3},{3,2},{4,5},{5,4},{6,7},{7,6},{8,9},{9,8},{10,11... | collective-permute-start | bytes 98312 | tf_op jit(solution)/shard_map/ppermute | solution.py:403
  113.9 1.3 collective-permute-start.52
  115.3 5.8 %collective-permute-start.55 = (f32[128,128]{1,0:T(8,128)S(1)}, f32[128,128]{1,0:T(8,128)S(1)}, u32[]{:S(2)}, u32[]{:S(2)}) collective-permute-start(f32[128,128]{1,0:T(8,128)S(1)} %add.25), channel_id=1, source_target_pairs={{0,6},{1,7},{2,4},{3,5},{4,2},{5,3},{6,0},{7,1},{8,14},{9,15},{10,... | collective-permute-start | bytes 196616 | tf_op jit(solution)/shard_map/ppermute | solution.py:392
  115.3 5.7 %collective-permute-start.54 = (f32[128,128]{1,0:T(8,128)S(1)}, f32[128,128]{1,0:T(8,128)S(1)}, u32[]{:S(2)}, u32[]{:S(2)}) collective-permute-start(f32[128,128]{1,0:T(8,128)S(1)} %add.25), channel_id=1, source_target_pairs={{0,4},{1,5},{2,6},{3,7},{4,0},{5,1},{6,2},{7,3},{8,12},{9,13},{10,... | collective-permute-start | bytes 196616 | tf_op jit(solution)/shard_map/ppermute | solution.py:392
  116.2 5.0 %collective-permute-start.53 = (f32[128,128]{1,0:T(8,128)S(1)}, f32[128,128]{1,0:T(8,128)S(1)}, u32[]{:S(2)}, u32[]{:S(2)}) collective-permute-start(f32[128,128]{1,0:T(8,128)S(1)} %add.25), channel_id=1, source_target_pairs={{0,2},{1,3},{2,0},{3,1},{4,6},{5,7},{6,4},{7,5},{8,10},{9,11},{10,... | collective-permute-start | bytes 196616 | tf_op jit(solution)/shard_map/ppermute | solution.py:392
  121.2 6.9 %collective-permute-start.58 = (f32[128,128]{1,0:T(8,128)S(1)}, f32[128,128]{1,0:T(8,128)S(1)}, u32[]{:S(2)}, u32[]{:S(2)}) collective-permute-start(f32[128,128]{1,0:T(8,128)S(1)} %add_add_fusion.1), channel_id=1, source_target_pairs={{0,24},{1,25},{2,26},{3,27},{4,28},{5,29},{6,30},{7,31},{8,16},{9,... | collective-permute-start | bytes 196616 | tf_op jit(solution)/shard_map/ppermute | solution.py:392
  123.1 6.4 %collective-permute-start.57 = (f32[128,128]{1,0:T(8,128)S(1)}, f32[128,128]{1,0:T(8,128)S(1)}, u32[]{:S(2)}, u32[]{:S(2)}) collective-permute-start(f32[128,128]{1,0:T(8,128)S(1)} %add_add_fusion.1), channel_id=1, source_target_pairs={{0,16},{1,17},{2,18},{3,19},{4,20},{5,21},{6,22},{7,23},{8,24},{9,... | collective-permute-start | bytes 196616 | tf_op jit(solution)/shard_map/ppermute | solution.py:392
  123.1 6.4 %collective-permute-start.56 = (f32[128,128]{1,0:T(8,128)S(1)}, f32[128,128]{1,0:T(8,128)S(1)}, u32[]{:S(2)}, u32[]{:S(2)}) collective-permute-start(f32[128,128]{1,0:T(8,128)S(1)} %add_add_fusion.1), channel_id=1, source_target_pairs={{0,8},{1,9},{2,10},{3,11},{4,12},{5,13},{6,14},{7,15},{8,0},{9,1},... | collective-permute-start | bytes 196616 | tf_op jit(solution)/shard_map/ppermute | solution.py:392

commit v3 on v2

--- a/solution.py
+++ b/solution.py
@@ -70,6 +70,10 @@
         pair = row[:, 2 * CAP * i : 2 * CAP * (i + 1)]
         parts.append(jnp.where(is_low(place_ref, by), pair, turned(pair)))
     return jnp.concatenate(parts, axis=1)
+
+
+def as_rows(row):
+    return jnp.concatenate([jnp.broadcast_to(row, (16, row.shape[1])).astype(BF16)] * (BLK // 16), axis=0)
 
 
 def as_columns(row):
@@ -113,9 +117,12 @@
     edges = dst_ref.shape[1]
     dst = by_link(place_ref, dst_ref[...])
     far = by_link(place_ref, far_ref[...])
+    one, zero = jnp.ones((), BF16), jnp.zeros((), BF16)
+    ids = lax.broadcasted_iota(jnp.int32, (BLK, edges), 0).astype(F32).astype(BF16)
+    in_block = jnp.where(ids == as_rows(lax.rem(dst, BLK).astype(F32)), one, zero)
+    owner = lax.div(dst, BLK)
     for b in range(rows // BLK):
-        ids = lax.broadcasted_iota(jnp.int32, (BLK, edges), 0) + b * BLK
-        hot_ref[pl.ds(b * BLK, BLK), :] = jnp.where(ids == dst, 1.0, 0.0).astype(BF16)
+        hot_ref[pl.ds(b * BLK, BLK), :] = in_block * as_rows(jnp.where(owner == b, 1.0, 0.0))
     hot = hot_ref[...]
     degree = jnp.sum(dot(stacked(far, 16), hot, ((1,), (1,))), axis=0, keepdims=True)
     copies[2].wait()
@@ -126,17 +133,18 @@
     for i in range(edges // BLK):
         coef_ref[pl.ds(i * BLK, BLK), :] = as_columns(far_coef[:, i * BLK : (i + 1) * BLK])
     copies[3].wait()
-    ids = lax.broadcasted_iota(jnp.int32, (BLK, BLK), 0)
+    ids = ids[:, :BLK]
     for b in range(rows // BLK):
         block = pl.ds(b * BLK, BLK)
         degree_b = degree[:, b * BLK : (b + 1) * BLK]
         for o in range(3):
-            cols = cols_ref[o, :, block]
-            coef = (wts_ref[o, :, block] / degree_b).astype(BF16).astype(F32)
-            dense = jnp.zeros((BLK, BLK), F32)
+            cols = cols_ref[o, :, block].astype(F32)
+            coef = wts_ref[o, :, block] / degree_b
+            dense = jnp.zeros((BLK, BLK), BF16)
             for k in range(KB):
-                dense = jnp.where(ids == cols[k : k + 1, :], coef[k : k + 1, :], dense)
-            band_ref[block, pl.ds(o * BLK, BLK)] = dense.T.astype(BF16)
+                here = ids == as_rows(cols[k : k + 1, :])
+                dense = jnp.where(here, as_rows(coef[k : k + 1, :]), dense)
+            band_ref[block, pl.ds(o * BLK, BLK)] = dense.T
     copies[4].wait()
 
 
@@ -176,16 +184,19 @@
     rows = field_ref.shape[0]
     half = 2 * CAP
     lanes = lax.broadcasted_iota(jnp.int32, (1, half), 1)
+    one, zero = jnp.ones((), BF16), jnp.zeros((), BF16)
     for i, (by, pair) in enumerate(zip(FAR, ((w0, w1), (w2, w3)), strict=True)):
         ahead, back = (w[:, i * half : (i + 1) * half] for w in pair)
         low = is_low(place_ref, by)
         ahead = jnp.where(low, turned(ahead), ahead)
         back = jnp.where(low, turned(back), back)
         wanted = jnp.where(lanes < CAP, ahead, back)
-        column = as_columns(wanted.astype(F32))
+        column = as_columns(lax.rem(wanted, BLK).astype(F32)).astype(BF16)
+        owner = as_columns(lax.div(wanted, BLK).astype(F32)).astype(BF16)
+        ids = lax.broadcasted_iota(jnp.int32, (half, BLK), 1).astype(F32).astype(BF16)
+        in_block = jnp.where(column == ids, one, zero)
         for b in range(rows // BLK):
-            ids = lax.broadcasted_iota(jnp.int32, (half, BLK), 1) + b * BLK
-            hot = jnp.where(column == ids.astype(F32), 1.0, 0.0).astype(BF16)
+            hot = jnp.where(owner == jnp.full((), b, BF16), in_block, zero)
             pick_mat_ref[pl.ds(i * half, half), pl.ds(b * BLK, BLK)] = hot
     field = field_ref[...]
     picked = dot(pick_mat_ref[...], field, ((1,), (0,)))
@@ -410,11 +421,16 @@
     here = place.astype(jnp.int32).reshape(1)
     band, hot, coef, field = prepare(
         here,
-        as_row(far_dst),
-        as_row(far_wts),
-        jnp.transpose(band_wts, (1, 2, 0)),
-        jnp.transpose(band_cols, (1, 2, 0)),
-        start_basis,
+        *(
+            pltpu.with_memory_space_constraint(v, pltpu.HBM)
+            for v in (
+                as_row(far_dst),
+                as_row(far_wts),
+                jnp.transpose(band_wts, (1, 2, 0)),
+                jnp.transpose(band_cols, (1, 2, 0)),
+                start_basis,
+            )
+        ),
     )
     wanted, band = lax.optimization_barrier((wanted, band))
     pick_mat, *sent = first(here, field, wanted)

time: 137 us -> 131 us (0.956)
  local copies, waits for them, and re-layouts: 4.25 us -> 0 us
  starting transfers between devices: 64.9 us -> 63.3 us
  Pallas kernels: 22.4 us -> 20.8 us
  waiting for transfers between devices: 44.8 us -> 46.3 us
    unnamed x10 -> x0, local copies, waits for them, and re-layouts: 4.25 us -> none
    ppermute x52, starting transfers between devices: 56.8 us -> 55.3 us  [swap(): return lax.ppermute(value, AXES, swap_pairs(count, by, odd))]
    pallas_call x1, Pallas kernels: 4.56 us -> 3.08 us  [prepare(): pl.pallas_call(prepare_kernel, out_shape=(jax.ShapeDtypeStruct((rows, 3 *...]
    ppermute x52, waiting for transfers between devices: 37.4 us -> 38.9 us  [swap(): return lax.ppermute(value, AXES, swap_pairs(count, by, odd))]
  transfers between devices with their start and end apart: 59 -> 59, of which waited for: 30 -> 31; matrix products, arithmetic and copies ran while one was open for 0% -> 0% of each run, Pallas kernels for 3% -> 2%
where the time goes in v3:
time: 131 us
  starting transfers between devices  63.3 us (48%)
  waiting for transfers between devices  46.3 us (35%)
  Pallas kernels  20.8 us (16%)
    ppermute x52, starting transfers between devices, swap(): return lax.ppermute(value, AXES, swap_pairs(count, by, odd))  55.3 us
    ppermute x52, waiting for transfers between devices, swap(): return lax.ppermute(value, AXES, swap_pairs(count, by, odd))  38.9 us
    pallas_call x7, Pallas kernels, step(): pl.pallas_call(lambda *refs: step_kernel(scale, has_prev, has_next, *refs...  8.24 us
    ppermute x7, starting transfers between devices, summed(): lax.ppermute(value, AXES, [(i, i ^ mask) for i in range(count)])  8.07 us
    ppermute x7, waiting for transfers between devices, summed(): lax.ppermute(value, AXES, [(i, i ^ mask) for i in range(count)])  7.42 us
    pallas_call x1, Pallas kernels, finish(): pl.pallas_call(lambda *refs: finish_kernel(scale, *refs), out_shape=jax.S...  7.14 us
    pallas_call x1, Pallas kernels, prepare(): pl.pallas_call(prepare_kernel, out_shape=(jax.ShapeDtypeStruct((rows, 3 *...  3.08 us
  transfers between devices with their start and end apart: 59, of which 31 were waited for; matrix products, arithmetic and copies ran while one was open for 0% of the time, Pallas kernels for 2%

profile of v3, /device:TPU:0, one launch (start us, length us, event | category | flops | bytes accessed | tf_op | source)
XLA Modules:
  0.0 130.7 jit_solution(205918703148766438)
XLA Ops:
  0.0 6.0 %collective-permute-start.3 = (s32[1,256]{1,0:T(1,128)}, s32[1,256]{1,0:T(1,128)S(1)}, u32[]{:S(2)}, u32[]{:S(2)}) collective-permute-start(s32[1,256]{1,0:T(1,128)} %bitcast.10), channel_id=1, source_target_pairs={{4,8},{8,4},{5,9},{9,5},{6,10},{10,6},{7,11},{11,7},{12,16},{16,12... | collective-permute-start | bytes 3080 | tf_op jit(solution)/shard_map/ppermute | solution.py:414
  6.0 2.8 %collective-permute-start.1 = (s32[1,256]{1,0:T(1,128)}, s32[1,256]{1,0:T(1,128)S(1)}, u32[]{:S(2)}, u32[]{:S(2)}) collective-permute-start(s32[1,256]{1,0:T(1,128)} %bitcast.12), channel_id=1, source_target_pairs={{2,4},{4,2},{3,5},{5,3},{6,8},{8,6},{7,9},{9,7},{10,12},{12,10},{1... | collective-permute-start | bytes 3080 | tf_op jit(solution)/shard_map/ppermute | solution.py:414
  8.8 0.6 collective-permute-start
  9.5 3.1 %prepare.1 = (bf16[2048,384]{1,0:T(8,128)(2,1)S(1)}, bf16[2048,256]{1,0:T(8,128)(2,1)S(1)}, f32[256,128]{1,0:T(8,128)S(1)}, bf16[2048,128]{1,0:T(8,128)(2,1)S(1)}) custom-call(s32[1]{0:T(128)} %bitcast.place_ref.refs_0_, s32[1,256]{1,0:T(1,128)} %bitcast.8, f32[1,256]{1,0:T(1,128)} %bitcast.9, f32[3,8,2048]{2,1,0:T(8,128)} %bitcast.6, ...), custom_call_target="tpu_custom_call" | custom-call | tf_op jit(solution)/shard_map/prepare/pallas_call | solution.py:153
  12.6 0.8 collective-permute-done.1.w1
  14.0 2.0 %collective-permute-start.4 = (bf16[128,128]{1,0:T(8,128)(2,1)S(1)}, bf16[128,128]{1,0:T(8,128)(2,1)S(1)}, u32[]{:S(2)}, u32[]{:S(2)}) collective-permute-start(bf16[128,128]{1,0:T(8,128)(2,1)S(1)} %get-tuple-element.88), channel_id=1, source_target_pairs={{4,8},{8,4},{5,9},{9,5},{6,10},{10,6},{7,11},{11,7},{12,16},{16,12... | collective-permute-start | bytes 98312 | tf_op jit(solution)/shard_map/ppermute | solution.py:414
  16.0 2.8 %collective-permute-start.5 = (bf16[128,128]{1,0:T(8,128)(2,1)S(1)}, bf16[128,128]{1,0:T(8,128)(2,1)S(1)}, u32[]{:S(2)}, u32[]{:S(2)}) collective-permute-start(bf16[128,128]{1,0:T(8,128)(2,1)S(1)} %get-tuple-element.89), channel_id=1, source_target_pairs={{2,4},{4,2},{3,5},{5,3},{6,8},{8,6},{7,9},{9,7},{10,12},{12,10},{1... | collective-permute-start | bytes 98312 | tf_op jit(solution)/shard_map/ppermute | solution.py:414
  18.8 0.8 collective-permute-start.6
  19.7 1.0 collective-permute-done.4.refs_6_
  21.1 2.4 %collective-permute-done.5.refs_7_ = bf16[128,128]{1,0:T(8,128)(2,1)S(1)} collective-permute-done((bf16[128,128]{1,0:T(8,128)(2,1)S(1)}, bf16[128,128]{1,0:T(8,128)(2,1)S(1)}, u32[]{:S(2)}, u32[]{:S(2)}) %collective-permute-start.5) | collective-permute-done | bytes 32800 | tf_op jit(solution)/shard_map/ppermute | solution.py:414
  23.5 2.2 %collective-permute-done.6.refs_8_ = bf16[128,128]{1,0:T(8,128)(2,1)S(1)} collective-permute-done((bf16[128,128]{1,0:T(8,128)(2,1)S(1)}, bf16[128,128]{1,0:T(8,128)(2,1)S(1)}, u32[]{:S(2)}, u32[]{:S(2)}) %collective-permute-start.6) | collective-permute-done | bytes 32800 | tf_op jit(solution)/shard_map/ppermute | solution.py:414
  25.8 1.1 step.7
  27.0 1.9 %collective-permute-start.11 = (bf16[128,128]{1,0:T(8,128)(2,1)S(1)}, bf16[128,128]{1,0:T(8,128)(2,1)S(1)}, u32[]{:S(2)}, u32[]{:S(2)}) collective-permute-start(bf16[128,128]{1,0:T(8,128)(2,1)S(1)} %get-tuple-element.96), channel_id=1, source_target_pairs={{2,4},{4,2},{3,5},{5,3},{6,8},{8,6},{7,9},{9,7},{10,12},{12,10},{1... | collective-permute-start | bytes 98312 | tf_op jit(solution)/shard_map/ppermute | solution.py:414
  29.0 3.1 %collective-permute-start.12 = (bf16[128,128]{1,0:T(8,128)(2,1)S(1)}, bf16[128,128]{1,0:T(8,128)(2,1)S(1)}, u32[]{:S(2)}, u32[]{:S(2)}) collective-permute-start(bf16[128,128]{1,0:T(8,128)(2,1)S(1)} %get-tuple-element.97), channel_id=1, source_target_pairs={{1,2},{2,1},{3,4},{4,3},{5,6},{6,5},{7,8},{8,7},{9,10},{10,9},{11,... | collective-permute-start | bytes 98312 | tf_op jit(solution)/shard_map/ppermute | solution.py:414
  32.1 1.9 %collective-permute-done.10.refs_7_ = bf16[128,128]{1,0:T(8,128)(2,1)S(1)} collective-permute-done((bf16[128,128]{1,0:T(8,128)(2,1)S(1)}, bf16[128,128]{1,0:T(8,128)(2,1)S(1)}, u32[]{:S(2)}, u32[]{:S(2)}) %collective-permute-start.10) | collective-permute-done | bytes 32800 | tf_op jit(solution)/shard_map/ppermute | solution.py:414
  33.9 0.7 collective-permute-done.11.refs_8_
  34.6 1.3 %collective-permute-done.12.refs_9_ = bf16[128,128]{1,0:T(8,128)(2,1)S(1)} collective-permute-done((bf16[128,128]{1,0:T(8,128)(2,1)S(1)}, bf16[128,128]{1,0:T(8,128)(2,1)S(1)}, u32[]{:S(2)}, u32[]{:S(2)}) %collective-permute-start.12) | collective-permute-done | bytes 32800 | tf_op jit(solution)/shard_map/ppermute | solution.py:414
  36.3 1.1 step.8
  37.4 0.9 collective-permute-start.16
  38.3 3.0 %collective-permute-start.17 = (bf16[128,128]{1,0:T(8,128)(2,1)S(1)}, bf16[128,128]{1,0:T(8,128)(2,1)S(1)}, u32[]{:S(2)}, u32[]{:S(2)}) collective-permute-start(bf16[128,128]{1,0:T(8,128)(2,1)S(1)} %get-tuple-element.104), channel_id=1, source_target_pairs={{2,4},{4,2},{3,5},{5,3},{6,8},{8,6},{7,9},{9,7},{10,12},{12,10},{1... | collective-permute-start | bytes 98312 | tf_op jit(solution)/shard_map/ppermute | solution.py:414
  41.3 2.4 %collective-permute-start.18 = (bf16[128,128]{1,0:T(8,128)(2,1)S(1)}, bf16[128,128]{1,0:T(8,128)(2,1)S(1)}, u32[]{:S(2)}, u32[]{:S(2)}) collective-permute-start(bf16[128,128]{1,0:T(8,128)(2,1)S(1)} %get-tuple-element.105), channel_id=1, source_target_pairs={{1,2},{2,1},{3,4},{4,3},{5,6},{6,5},{7,8},{8,7},{9,10},{10,9},{11,... | collective-permute-start | bytes 98312 | tf_op jit(solution)/shard_map/ppermute | solution.py:414
  44.1 1.8 %collective-permute-done.17.refs_8_ = bf16[128,128]{1,0:T(8,128)(2,1)S(1)} collective-permute-done((bf16[128,128]{1,0:T(8,128)(2,1)S(1)}, bf16[128,128]{1,0:T(8,128)(2,1)S(1)}, u32[]{:S(2)}, u32[]{:S(2)}) %collective-permute-start.17) | collective-permute-done | bytes 32800 | tf_op jit(solution)/shard_map/ppermute | solution.py:414
  45.8 2.4 %collective-permute-done.18.refs_9_ = bf16[128,128]{1,0:T(8,128)(2,1)S(1)} collective-permute-done((bf16[128,128]{1,0:T(8,128)(2,1)S(1)}, bf16[128,128]{1,0:T(8,128)(2,1)S(1)}, u32[]{:S(2)}, u32[]{:S(2)}) %collective-permute-start.18) | collective-permute-done | bytes 32800 | tf_op jit(solution)/shard_map/ppermute | solution.py:414
  48.3 1.1 step.9
  49.5 3.5 %collective-permute-start.23 = (bf16[128,128]{1,0:T(8,128)(2,1)S(1)}, bf16[128,128]{1,0:T(8,128)(2,1)S(1)}, u32[]{:S(2)}, u32[]{:S(2)}) collective-permute-start(bf16[128,128]{1,0:T(8,128)(2,1)S(1)} %get-tuple-element.112), channel_id=1, source_target_pairs={{2,4},{4,2},{3,5},{5,3},{6,8},{8,6},{7,9},{9,7},{10,12},{12,10},{1... | collective-permute-start | bytes 98312 | tf_op jit(solution)/shard_map/ppermute | solution.py:414
  53.0 1.5 %collective-permute-start.24 = (bf16[128,128]{1,0:T(8,128)(2,1)S(1)}, bf16[128,128]{1,0:T(8,128)(2,1)S(1)}, u32[]{:S(2)}, u32[]{:S(2)}) collective-permute-start(bf16[128,128]{1,0:T(8,128)(2,1)S(1)} %get-tuple-element.113), channel_id=1, source_target_pairs={{1,2},{2,1},{3,4},{4,3},{5,6},{6,5},{7,8},{8,7},{9,10},{10,9},{11,... | collective-permute-start | bytes 98312 | tf_op jit(solution)/shard_map/ppermute | solution.py:414
  54.6 0.9 collective-permute-start.26
  55.5 1.0 collective-permute-done.22.refs_7_
  56.5 0.7 collective-permute-done.23.refs_8_
  57.2 2.9 %collective-permute-done.24.refs_9_ = bf16[128,128]{1,0:T(8,128)(2,1)S(1)} collective-permute-done((bf16[128,128]{1,0:T(8,128)(2,1)S(1)}, bf16[128,128]{1,0:T(8,128)(2,1)S(1)}, u32[]{:S(2)}, u32[]{:S(2)}) %collective-permute-start.24) | collective-permute-done | bytes 32800 | tf_op jit(solution)/shard_map/ppermute | solution.py:414
  60.1 1.2 step.10
  61.3 3.5 %collective-permute-start.29 = (bf16[128,128]{1,0:T(8,128)(2,1)S(1)}, bf16[128,128]{1,0:T(8,128)(2,1)S(1)}, u32[]{:S(2)}, u32[]{:S(2)}) collective-permute-start(bf16[128,128]{1,0:T(8,128)(2,1)S(1)} %get-tuple-element.120), channel_id=1, source_target_pairs={{2,4},{4,2},{3,5},{5,3},{6,8},{8,6},{7,9},{9,7},{10,12},{12,10},{1... | collective-permute-start | bytes 98312 | tf_op jit(solution)/shard_map/ppermute | solution.py:414
  64.8 1.4 %collective-permute-start.30 = (bf16[128,128]{1,0:T(8,128)(2,1)S(1)}, bf16[128,128]{1,0:T(8,128)(2,1)S(1)}, u32[]{:S(2)}, u32[]{:S(2)}) collective-permute-start(bf16[128,128]{1,0:T(8,128)(2,1)S(1)} %get-tuple-element.121), channel_id=1, source_target_pairs={{1,2},{2,1},{3,4},{4,3},{5,6},{6,5},{7,8},{8,7},{9,10},{10,9},{11,... | collective-permute-start | bytes 98312 | tf_op jit(solution)/shard_map/ppermute | solution.py:414
  66.5 1.8 %collective-permute-done.28.refs_7_ = bf16[128,128]{1,0:T(8,128)(2,1)S(1)} collective-permute-done((bf16[128,128]{1,0:T(8,128)(2,1)S(1)}, bf16[128,128]{1,0:T(8,128)(2,1)S(1)}, u32[]{:S(2)}, u32[]{:S(2)}) %collective-permute-start.28) | collective-permute-done | bytes 32800 | tf_op jit(solution)/shard_map/ppermute | solution.py:414
  68.9 2.9 %collective-permute-done.30.refs_9_ = bf16[128,128]{1,0:T(8,128)(2,1)S(1)} collective-permute-done((bf16[128,128]{1,0:T(8,128)(2,1)S(1)}, bf16[128,128]{1,0:T(8,128)(2,1)S(1)}, u32[]{:S(2)}, u32[]{:S(2)}) %collective-permute-start.30) | collective-permute-done | bytes 32800 | tf_op jit(solution)/shard_map/ppermute | solution.py:414
  71.8 1.2 step.11
  73.1 2.7 %collective-permute-start.35 = (bf16[128,128]{1,0:T(8,128)(2,1)S(1)}, bf16[128,128]{1,0:T(8,128)(2,1)S(1)}, u32[]{:S(2)}, u32[]{:S(2)}) collective-permute-start(bf16[128,128]{1,0:T(8,128)(2,1)S(1)} %get-tuple-element.128), channel_id=1, source_target_pairs={{2,4},{4,2},{3,5},{5,3},{6,8},{8,6},{7,9},{9,7},{10,12},{12,10},{1... | collective-permute-start | bytes 98312 | tf_op jit(solution)/shard_map/ppermute | solution.py:414
  75.7 2.2 %collective-permute-start.36 = (bf16[128,128]{1,0:T(8,128)(2,1)S(1)}, bf16[128,128]{1,0:T(8,128)(2,1)S(1)}, u32[]{:S(2)}, u32[]{:S(2)}) collective-permute-start(bf16[128,128]{1,0:T(8,128)(2,1)S(1)} %get-tuple-element.129), channel_id=1, source_target_pairs={{1,2},{2,1},{3,4},{4,3},{5,6},{6,5},{7,8},{8,7},{9,10},{10,9},{11,... | collective-permute-start | bytes 98312 | tf_op jit(solution)/shard_map/ppermute | solution.py:414
  78.1 1.9 %collective-permute-done.34.refs_7_ = bf16[128,128]{1,0:T(8,128)(2,1)S(1)} collective-permute-done((bf16[128,128]{1,0:T(8,128)(2,1)S(1)}, bf16[128,128]{1,0:T(8,128)(2,1)S(1)}, u32[]{:S(2)}, u32[]{:S(2)}) %collective-permute-start.34) | collective-permute-done | bytes 32800 | tf_op jit(solution)/shard_map/ppermute | solution.py:414
  80.0 0.7 collective-permute-done.35.refs_8_
  80.8 1.9 %collective-permute-done.36.refs_9_ = bf16[128,128]{1,0:T(8,128)(2,1)S(1)} collective-permute-done((bf16[128,128]{1,0:T(8,128)(2,1)S(1)}, bf16[128,128]{1,0:T(8,128)(2,1)S(1)}, u32[]{:S(2)}, u32[]{:S(2)}) %collective-permute-start.36) | collective-permute-done | bytes 32800 | tf_op jit(solution)/shard_map/ppermute | solution.py:414
  82.7 1.3 %step.12 = (bf16[2048,128]{1,0:T(8,128)(2,1)S(1)}, bf16[128,128]{1,0:T(8,128)(2,1)S(1)}, bf16[128,128]{1,0:T(8,128)(2,1)S(1)}, bf16[128,128]{1,0:T(8,128)(2,1)S(...) custom-call(s32[1]{0:T(128)} %bitcast.place_ref.refs_0_, ...), custom_call_target="tpu_custom_call" | custom-call | tf_op jit(solution)/shard_map/step/pallas_call | solution.py:282
  84.6 3.0 %collective-permute-start.41 = (bf16[128,128]{1,0:T(8,128)(2,1)S(1)}, bf16[128,128]{1,0:T(8,128)(2,1)S(1)}, u32[]{:S(2)}, u32[]{:S(2)}) collective-permute-start(bf16[128,128]{1,0:T(8,128)(2,1)S(1)} %get-tuple-element.136), channel_id=1, source_target_pairs={{2,4},{4,2},{3,5},{5,3},{6,8},{8,6},{7,9},{9,7},{10,12},{12,10},{1... | collective-permute-start | bytes 98312 | tf_op jit(solution)/shard_map/ppermute | solution.py:414
  87.6 2.4 %collective-permute-start.42 = (bf16[128,128]{1,0:T(8,128)(2,1)S(1)}, bf16[128,128]{1,0:T(8,128)(2,1)S(1)}, u32[]{:S(2)}, u32[]{:S(2)}) collective-permute-start(bf16[128,128]{1,0:T(8,128)(2,1)S(1)} %get-tuple-element.137), channel_id=1, source_target_pairs={{1,2},{2,1},{3,4},{4,3},{5,6},{6,5},{7,8},{8,7},{9,10},{10,9},{11,... | collective-permute-start | bytes 98312 | tf_op jit(solution)/shard_map/ppermute | solution.py:414
  90.0 0.8 collective-permute-done.40.refs_7_
  90.7 1.4 %collective-permute-done.41.refs_8_ = bf16[128,128]{1,0:T(8,128)(2,1)S(1)} collective-permute-done((bf16[128,128]{1,0:T(8,128)(2,1)S(1)}, bf16[128,128]{1,0:T(8,128)(2,1)S(1)}, u32[]{:S(2)}, u32[]{:S(2)}) %collective-permute-start.41) | collective-permute-done | bytes 32800 | tf_op jit(solution)/shard_map/ppermute | solution.py:414
  92.1 2.4 %collective-permute-done.42.refs_9_ = bf16[128,128]{1,0:T(8,128)(2,1)S(1)} collective-permute-done((bf16[128,128]{1,0:T(8,128)(2,1)S(1)}, bf16[128,128]{1,0:T(8,128)(2,1)S(1)}, u32[]{:S(2)}, u32[]{:S(2)}) %collective-permute-start.42) | collective-permute-done | bytes 32800 | tf_op jit(solution)/shard_map/ppermute | solution.py:414
  94.6 1.2 step.13
  95.8 3.5 %collective-permute-start.47 = (bf16[128,128]{1,0:T(8,128)(2,1)S(1)}, bf16[128,128]{1,0:T(8,128)(2,1)S(1)}, u32[]{:S(2)}, u32[]{:S(2)}) collective-permute-start(bf16[128,128]{1,0:T(8,128)(2,1)S(1)} %get-tuple-element.144), channel_id=1, source_target_pairs={{2,4},{4,2},{3,5},{5,3},{6,8},{8,6},{7,9},{9,7},{10,12},{12,10},{1... | collective-permute-start | bytes 98312 | tf_op jit(solution)/shard_map/ppermute | solution.py:414
  99.3 1.6 %collective-permute-start.48 = (bf16[128,128]{1,0:T(8,128)(2,1)S(1)}, bf16[128,128]{1,0:T(8,128)(2,1)S(1)}, u32[]{:S(2)}, u32[]{:S(2)}) collective-permute-start(bf16[128,128]{1,0:T(8,128)(2,1)S(1)} %get-tuple-element.145), channel_id=1, source_target_pairs={{1,2},{2,1},{3,4},{4,3},{5,6},{6,5},{7,8},{8,7},{9,10},{10,9},{11,... | collective-permute-start | bytes 98312 | tf_op jit(solution)/shard_map/ppermute | solution.py:414
  100.8 0.8 collective-permute-start.50
  101.7 1.1 collective-permute-done.46.refs_6_
  102.7 0.7 collective-permute-done.47.refs_7_
  103.4 2.8 %collective-permute-done.48.refs_8_ = bf16[128,128]{1,0:T(8,128)(2,1)S(1)} collective-permute-done((bf16[128,128]{1,0:T(8,128)(2,1)S(1)}, bf16[128,128]{1,0:T(8,128)(2,1)S(1)}, u32[]{:S(2)}, u32[]{:S(2)}) %collective-permute-start.48) | collective-permute-done | bytes 32800 | tf_op jit(solution)/shard_map/ppermute | solution.py:414
  106.2 1.8 %last.1 = (f32[2048,128]{1,0:T(8,128)S(1)}, f32[128,128]{1,0:T(8,128)S(1)}) custom-call(s32[1]{0:T(128)} %bitcast.place_ref.refs_0_, bf16[2048,384]{1,0:T(8,128)(2,1)S(1)} %get-tuple-element.79.refs_1_, bf16[2048,256]{1,0:T(8,128)(2,1)S(1)} %get-tuple-element.80.refs_2_, f32[256,128]{1,0:T(8,128)S(1)} %get-tuple-element.81.refs_3_, ...), custom_call_target="tpu_custom_call" | custom-call | tf_op jit(solution)/shard_map/last/pallas_call | solution.py:312
  108.1 1.2 collective-permute-done.52
  109.4 0.9 collective-permute-start.54
  110.4 2.5 %collective-permute-start.53 = (f32[128,128]{1,0:T(8,128)S(1)}, f32[128,128]{1,0:T(8,128)S(1)}, u32[]{:S(2)}, u32[]{:S(2)}) collective-permute-start(f32[128,128]{1,0:T(8,128)S(1)} %add.25), channel_id=1, source_target_pairs={{0,2},{1,3},{2,0},{3,1},{4,6},{5,7},{6,4},{7,5},{8,10},{9,11},{10,... | collective-permute-start | bytes 196616 | tf_op jit(solution)/shard_map/ppermute | solution.py:403
  112.9 2.3 %collective-permute-done.55 = f32[128,128]{1,0:T(8,128)S(1)} collective-permute-done((f32[128,128]{1,0:T(8,128)S(1)}, f32[128,128]{1,0:T(8,128)S(1)}, u32[]{:S(2)}, u32[]{:S(2)}) %collective-permute-start.55) | collective-permute-done | bytes 65568 | tf_op jit(solution)/shard_map/ppermute | solution.py:403
  115.4 1.8 %collective-permute-start.58 = (f32[128,128]{1,0:T(8,128)S(1)}, f32[128,128]{1,0:T(8,128)S(1)}, u32[]{:S(2)}, u32[]{:S(2)}) collective-permute-start(f32[128,128]{1,0:T(8,128)S(1)} %add_add_fusion.1), channel_id=1, source_target_pairs={{0,24},{1,25},{2,26},{3,27},{4,28},{5,29},{6,30},{7,31},{8,16},{9,... | collective-permute-start | bytes 196616 | tf_op jit(solution)/shard_map/ppermute | solution.py:403
  117.3 2.6 %collective-permute-start.56 = (f32[128,128]{1,0:T(8,128)S(1)}, f32[128,128]{1,0:T(8,128)S(1)}, u32[]{:S(2)}, u32[]{:S(2)}) collective-permute-start(f32[128,128]{1,0:T(8,128)S(1)} %add_add_fusion.1), channel_id=1, source_target_pairs={{0,8},{1,9},{2,10},{3,11},{4,12},{5,13},{6,14},{7,15},{8,0},{9,1},... | collective-permute-start | bytes 196616 | tf_op jit(solution)/shard_map/ppermute | solution.py:403
  119.9 2.4 %collective-permute-done.58 = f32[128,128]{1,0:T(8,128)S(1)} collective-permute-done((f32[128,128]{1,0:T(8,128)S(1)}, f32[128,128]{1,0:T(8,128)S(1)}, u32[]{:S(2)}, u32[]{:S(2)}) %collective-permute-start.58) | collective-permute-done | bytes 65568 | tf_op jit(solution)/shard_map/ppermute | solution.py:403
  122.2 1.3 %collective-permute-done.57 = f32[128,128]{1,0:T(8,128)S(1)} collective-permute-done((f32[128,128]{1,0:T(8,128)S(1)}, f32[128,128]{1,0:T(8,128)S(1)}, u32[]{:S(2)}, u32[]{:S(2)}) %collective-permute-start.57) | collective-permute-done | bytes 65568 | tf_op jit(solution)/shard_map/ppermute | solution.py:403
  123.6 7.1 %finish.1 = f32[2048,128]{1,0:T(8,128)} custom-call(f32[128,128]{1,0:T(8,128)S(1)} %add_add_fusion.refs_0_, f32[2048,128]{1,0:T(8,128)S(1)} %get-tuple-element.150.refs_1_), custom_call_target="tpu_custom_call" | custom-call | tf_op jit(solution)/shard_map/finish/pallas_call | solution.py:385
  (68 shorter events, 4.1 us)
Async XLA Ops:
  0.0 12.6 %collective-permute-start.3 = (s32[1,256]{1,0:T(1,128)}, s32[1,256]{1,0:T(1,128)S(1)}, u32[]{:S(2)}, u32[]{:S(2)}) collective-permute-start(s32[1,256]{1,0:T(1,128)} %bitcast.10), channel_id=1, source_target_pairs={{4,8},{8,4},{5,9},{9,5},{6,10},{10,6},{7,11},{11,7},{12,16},{16,12... | collective-permute-start | bytes 3080 | tf_op jit(solution)/shard_map/ppermute | solution.py:414
  6.0 6.6 %collective-permute-start.2 = (s32[1,256]{1,0:T(1,128)}, s32[1,256]{1,0:T(1,128)S(1)}, u32[]{:S(2)}, u32[]{:S(2)}) collective-permute-start(s32[1,256]{1,0:T(1,128)} %bitcast.11), channel_id=1, source_target_pairs={{0,4},{4,0},{1,5},{5,1},{2,6},{6,2},{3,7},{7,3},{8,12},{12,8},{9,1... | collective-permute-start | bytes 3080 | tf_op jit(solution)/shard_map/ppermute | solution.py:414
  6.0 7.4 %collective-permute-start.1 = (s32[1,256]{1,0:T(1,128)}, s32[1,256]{1,0:T(1,128)S(1)}, u32[]{:S(2)}, u32[]{:S(2)}) collective-permute-start(s32[1,256]{1,0:T(1,128)} %bitcast.12), channel_id=1, source_target_pairs={{2,4},{4,2},{3,5},{5,3},{6,8},{8,6},{7,9},{9,7},{10,12},{12,10},{1... | collective-permute-start | bytes 3080 | tf_op jit(solution)/shard_map/ppermute | solution.py:414
  8.8 4.5 %collective-permute-start = (s32[1,256]{1,0:T(1,128)}, s32[1,256]{1,0:T(1,128)S(1)}, u32[]{:S(2)}, u32[]{:S(2)}) collective-permute-start(s32[1,256]{1,0:T(1,128)} %bitcast.13), channel_id=1, source_target_pairs={{0,2},{2,0},{1,3},{3,1},{4,6},{6,4},{5,7},{7,5},{8,10},{10,8},{9,1... | collective-permute-start | bytes 3080 | tf_op jit(solution)/shard_map/ppermute | solution.py:414
  14.0 6.7 %collective-permute-start.4 = (bf16[128,128]{1,0:T(8,128)(2,1)S(1)}, bf16[128,128]{1,0:T(8,128)(2,1)S(1)}, u32[]{:S(2)}, u32[]{:S(2)}) collective-permute-start(bf16[128,128]{1,0:T(8,128)(2,1)S(1)} %get-tuple-element.88), channel_id=1, source_target_pairs={{4,8},{8,4},{5,9},{9,5},{6,10},{10,6},{7,11},{11,7},{12,16},{16,12... | collective-permute-start | bytes 98312 | tf_op jit(solution)/shard_map/ppermute | solution.py:414
  16.0 7.5 %collective-permute-start.5 = (bf16[128,128]{1,0:T(8,128)(2,1)S(1)}, bf16[128,128]{1,0:T(8,128)(2,1)S(1)}, u32[]{:S(2)}, u32[]{:S(2)}) collective-permute-start(bf16[128,128]{1,0:T(8,128)(2,1)S(1)} %get-tuple-element.89), channel_id=1, source_target_pairs={{2,4},{4,2},{3,5},{5,3},{6,8},{8,6},{7,9},{9,7},{10,12},{12,10},{1... | collective-permute-start | bytes 98312 | tf_op jit(solution)/shard_map/ppermute | solution.py:414
  18.8 6.9 %collective-permute-start.6 = (bf16[128,128]{1,0:T(8,128)(2,1)S(1)}, bf16[128,128]{1,0:T(8,128)(2,1)S(1)}, u32[]{:S(2)}, u32[]{:S(2)}) collective-permute-start(bf16[128,128]{1,0:T(8,128)(2,1)S(1)} %get-tuple-element.90), channel_id=1, source_target_pairs={{1,2},{2,1},{3,4},{4,3},{5,6},{6,5},{7,8},{8,7},{9,10},{10,9},{11,... | collective-permute-start | bytes 98312 | tf_op jit(solution)/shard_map/ppermute | solution.py:414
  19.7 6.1 %collective-permute-start.7 = (bf16[128,128]{1,0:T(8,128)(2,1)S(1)}, bf16[128,128]{1,0:T(8,128)(2,1)S(1)}, u32[]{:S(2)}, u32[]{:S(2)}) collective-permute-start(bf16[128,128]{1,0:T(8,128)(2,1)S(1)} %get-tuple-element.91), channel_id=1, source_target_pairs={{0,4},{4,0},{1,5},{5,1},{2,6},{6,2},{3,7},{7,3},{8,12},{12,8},{9,1... | collective-permute-start | bytes 98312 | tf_op jit(solution)/shard_map/ppermute | solution.py:414
  19.7 6.1 %collective-permute-start.8 = (bf16[128,128]{1,0:T(8,128)(2,1)S(1)}, bf16[128,128]{1,0:T(8,128)(2,1)S(1)}, u32[]{:S(2)}, u32[]{:S(2)}) collective-permute-start(bf16[128,128]{1,0:T(8,128)(2,1)S(1)} %get-tuple-element.92), channel_id=1, source_target_pairs={{0,2},{2,0},{1,3},{3,1},{4,6},{6,4},{5,7},{7,5},{8,10},{10,8},{9,1... | collective-permute-start | bytes 98312 | tf_op jit(solution)/shard_map/ppermute | solution.py:414
  20.7 5.1 %collective-permute-start.9 = (bf16[128,128]{1,0:T(8,128)(2,1)S(1)}, bf16[128,128]{1,0:T(8,128)(2,1)S(1)}, u32[]{:S(2)}, u32[]{:S(2)}) collective-permute-start(bf16[128,128]{1,0:T(8,128)(2,1)S(1)} %get-tuple-element.93), channel_id=1, source_target_pairs={{0,1},{1,0},{2,3},{3,2},{4,5},{5,4},{6,7},{7,6},{8,9},{9,8},{10,11... | collective-permute-start | bytes 98312 | tf_op jit(solution)/shard_map/ppermute | solution.py:414
  26.9 7.0 %collective-permute-start.10 = (bf16[128,128]{1,0:T(8,128)(2,1)S(1)}, bf16[128,128]{1,0:T(8,128)(2,1)S(1)}, u32[]{:S(2)}, u32[]{:S(2)}) collective-permute-start(bf16[128,128]{1,0:T(8,128)(2,1)S(1)} %get-tuple-element.95), channel_id=1, source_target_pairs={{4,8},{8,4},{5,9},{9,5},{6,10},{10,6},{7,11},{11,7},{12,16},{16,12... | collective-permute-start | bytes 98312 | tf_op jit(solution)/shard_map/ppermute | solution.py:414
  27.0 7.6 %collective-permute-start.11 = (bf16[128,128]{1,0:T(8,128)(2,1)S(1)}, bf16[128,128]{1,0:T(8,128)(2,1)S(1)}, u32[]{:S(2)}, u32[]{:S(2)}) collective-permute-start(bf16[128,128]{1,0:T(8,128)(2,1)S(1)} %get-tuple-element.96), channel_id=1, source_target_pairs={{2,4},{4,2},{3,5},{5,3},{6,8},{8,6},{7,9},{9,7},{10,12},{12,10},{1... | collective-permute-start | bytes 98312 | tf_op jit(solution)/shard_map/ppermute | solution.py:414
  29.0 7.0 %collective-permute-start.12 = (bf16[128,128]{1,0:T(8,128)(2,1)S(1)}, bf16[128,128]{1,0:T(8,128)(2,1)S(1)}, u32[]{:S(2)}, u32[]{:S(2)}) collective-permute-start(bf16[128,128]{1,0:T(8,128)(2,1)S(1)} %get-tuple-element.97), channel_id=1, source_target_pairs={{1,2},{2,1},{3,4},{4,3},{5,6},{6,5},{7,8},{8,7},{9,10},{10,9},{11,... | collective-permute-start | bytes 98312 | tf_op jit(solution)/shard_map/ppermute | solution.py:414
  32.0 4.2 %collective-permute-start.13 = (bf16[128,128]{1,0:T(8,128)(2,1)S(1)}, bf16[128,128]{1,0:T(8,128)(2,1)S(1)}, u32[]{:S(2)}, u32[]{:S(2)}) collective-permute-start(bf16[128,128]{1,0:T(8,128)(2,1)S(1)} %get-tuple-element.98), channel_id=1, source_target_pairs={{0,4},{4,0},{1,5},{5,1},{2,6},{6,2},{3,7},{7,3},{8,12},{12,8},{9,1... | collective-permute-start | bytes 98312 | tf_op jit(solution)/shard_map/ppermute | solution.py:414
  32.1 4.2 %collective-permute-start.14 = (bf16[128,128]{1,0:T(8,128)(2,1)S(1)}, bf16[128,128]{1,0:T(8,128)(2,1)S(1)}, u32[]{:S(2)}, u32[]{:S(2)}) collective-permute-start(bf16[128,128]{1,0:T(8,128)(2,1)S(1)} %get-tuple-element.99), channel_id=1, source_target_pairs={{0,2},{2,0},{1,3},{3,1},{4,6},{6,4},{5,7},{7,5},{8,10},{10,8},{9,1... | collective-permute-start | bytes 98312 | tf_op jit(solution)/shard_map/ppermute | solution.py:414
  33.9 2.3 %collective-permute-start.15 = (bf16[128,128]{1,0:T(8,128)(2,1)S(1)}, bf16[128,128]{1,0:T(8,128)(2,1)S(1)}, u32[]{:S(2)}, u32[]{:S(2)}) collective-permute-start(bf16[128,128]{1,0:T(8,128)(2,1)S(1)} %get-tuple-element.100), channel_id=1, source_target_pairs={{0,1},{1,0},{2,3},{3,2},{4,5},{5,4},{6,7},{7,6},{8,9},{9,8},{10,11... | collective-permute-start | bytes 98312 | tf_op jit(solution)/shard_map/ppermute | solution.py:414
  37.4 6.7 %collective-permute-start.16 = (bf16[128,128]{1,0:T(8,128)(2,1)S(1)}, bf16[128,128]{1,0:T(8,128)(2,1)S(1)}, u32[]{:S(2)}, u32[]{:S(2)}) collective-permute-start(bf16[128,128]{1,0:T(8,128)(2,1)S(1)} %get-tuple-element.103), channel_id=1, source_target_pairs={{4,8},{8,4},{5,9},{9,5},{6,10},{10,6},{7,11},{11,7},{12,16},{16,12... | collective-permute-start | bytes 98312 | tf_op jit(solution)/shard_map/ppermute | solution.py:414
  38.3 7.5 %collective-permute-start.17 = (bf16[128,128]{1,0:T(8,128)(2,1)S(1)}, bf16[128,128]{1,0:T(8,128)(2,1)S(1)}, u32[]{:S(2)}, u32[]{:S(2)}) collective-permute-start(bf16[128,128]{1,0:T(8,128)(2,1)S(1)} %get-tuple-element.104), channel_id=1, source_target_pairs={{2,4},{4,2},{3,5},{5,3},{6,8},{8,6},{7,9},{9,7},{10,12},{12,10},{1... | collective-permute-start | bytes 98312 | tf_op jit(solution)/shard_map/ppermute | solution.py:414
  41.3 6.9 %collective-permute-start.18 = (bf16[128,128]{1,0:T(8,128)(2,1)S(1)}, bf16[128,128]{1,0:T(8,128)(2,1)S(1)}, u32[]{:S(2)}, u32[]{:S(2)}) collective-permute-start(bf16[128,128]{1,0:T(8,128)(2,1)S(1)} %get-tuple-element.105), channel_id=1, source_target_pairs={{1,2},{2,1},{3,4},{4,3},{5,6},{6,5},{7,8},{8,7},{9,10},{10,9},{11,... | collective-permute-start | bytes 98312 | tf_op jit(solution)/shard_map/ppermute | solution.py:414
  43.7 4.6 %collective-permute-start.19 = (bf16[128,128]{1,0:T(8,128)(2,1)S(1)}, bf16[128,128]{1,0:T(8,128)(2,1)S(1)}, u32[]{:S(2)}, u32[]{:S(2)}) collective-permute-start(bf16[128,128]{1,0:T(8,128)(2,1)S(1)} %get-tuple-element.106), channel_id=1, source_target_pairs={{0,4},{4,0},{1,5},{5,1},{2,6},{6,2},{3,7},{7,3},{8,12},{12,8},{9,1... | collective-permute-start | bytes 98312 | tf_op jit(solution)/shard_map/ppermute | solution.py:414
  43.7 4.6 %collective-permute-start.20 = (bf16[128,128]{1,0:T(8,128)(2,1)S(1)}, bf16[128,128]{1,0:T(8,128)(2,1)S(1)}, u32[]{:S(2)}, u32[]{:S(2)}) collective-permute-start(bf16[128,128]{1,0:T(8,128)(2,1)S(1)} %get-tuple-element.107), channel_id=1, source_target_pairs={{0,2},{2,0},{1,3},{3,1},{4,6},{6,4},{5,7},{7,5},{8,10},{10,8},{9,1... | collective-permute-start | bytes 98312 | tf_op jit(solution)/shard_map/ppermute | solution.py:414
  44.1 4.2 %collective-permute-start.21 = (bf16[128,128]{1,0:T(8,128)(2,1)S(1)}, bf16[128,128]{1,0:T(8,128)(2,1)S(1)}, u32[]{:S(2)}, u32[]{:S(2)}) collective-permute-start(bf16[128,128]{1,0:T(8,128)(2,1)S(1)} %get-tuple-element.108), channel_id=1, source_target_pairs={{0,1},{1,0},{2,3},{3,2},{4,5},{5,4},{6,7},{7,6},{8,9},{9,8},{10,11... | collective-permute-start | bytes 98312 | tf_op jit(solution)/shard_map/ppermute | solution.py:414
  49.5 7.0 %collective-permute-start.22 = (bf16[128,128]{1,0:T(8,128)(2,1)S(1)}, bf16[128,128]{1,0:T(8,128)(2,1)S(1)}, u32[]{:S(2)}, u32[]{:S(2)}) collective-permute-start(bf16[128,128]{1,0:T(8,128)(2,1)S(1)} %get-tuple-element.111), channel_id=1, source_target_pairs={{4,8},{8,4},{5,9},{9,5},{6,10},{10,6},{7,11},{11,7},{12,16},{16,12... | collective-permute-start | bytes 98312 | tf_op jit(solution)/shard_map/ppermute | solution.py:414
  49.5 7.7 %collective-permute-start.23 = (bf16[128,128]{1,0:T(8,128)(2,1)S(1)}, bf16[128,128]{1,0:T(8,128)(2,1)S(1)}, u32[]{:S(2)}, u32[]{:S(2)}) collective-permute-start(bf16[128,128]{1,0:T(8,128)(2,1)S(1)} %get-tuple-element.112), channel_id=1, source_target_pairs={{2,4},{4,2},{3,5},{5,3},{6,8},{8,6},{7,9},{9,7},{10,12},{12,10},{1... | collective-permute-start | bytes 98312 | tf_op jit(solution)/shard_map/ppermute | solution.py:414
  53.0 7.0 %collective-permute-start.24 = (bf16[128,128]{1,0:T(8,128)(2,1)S(1)}, bf16[128,128]{1,0:T(8,128)(2,1)S(1)}, u32[]{:S(2)}, u32[]{:S(2)}) collective-permute-start(bf16[128,128]{1,0:T(8,128)(2,1)S(1)} %get-tuple-element.113), channel_id=1, source_target_pairs={{1,2},{2,1},{3,4},{4,3},{5,6},{6,5},{7,8},{8,7},{9,10},{10,9},{11,... | collective-permute-start | bytes 98312 | tf_op jit(solution)/shard_map/ppermute | solution.py:414
  54.6 5.5 %collective-permute-start.25 = (bf16[128,128]{1,0:T(8,128)(2,1)S(1)}, bf16[128,128]{1,0:T(8,128)(2,1)S(1)}, u32[]{:S(2)}, u32[]{:S(2)}) collective-permute-start(bf16[128,128]{1,0:T(8,128)(2,1)S(1)} %get-tuple-element.114), channel_id=1, source_target_pairs={{0,4},{4,0},{1,5},{5,1},{2,6},{6,2},{3,7},{7,3},{8,12},{12,8},{9,1... | collective-permute-start | bytes 98312 | tf_op jit(solution)/shard_map/ppermute | solution.py:414
  54.6 5.5 %collective-permute-start.26 = (bf16[128,128]{1,0:T(8,128)(2,1)S(1)}, bf16[128,128]{1,0:T(8,128)(2,1)S(1)}, u32[]{:S(2)}, u32[]{:S(2)}) collective-permute-start(bf16[128,128]{1,0:T(8,128)(2,1)S(1)} %get-tuple-element.115), channel_id=1, source_target_pairs={{0,2},{2,0},{1,3},{3,1},{4,6},{6,4},{5,7},{7,5},{8,10},{10,8},{9,1... | collective-permute-start | bytes 98312 | tf_op jit(solution)/shard_map/ppermute | solution.py:414
  56.5 3.6 %collective-permute-start.27 = (bf16[128,128]{1,0:T(8,128)(2,1)S(1)}, bf16[128,128]{1,0:T(8,128)(2,1)S(1)}, u32[]{:S(2)}, u32[]{:S(2)}) collective-permute-start(bf16[128,128]{1,0:T(8,128)(2,1)S(1)} %get-tuple-element.116), channel_id=1, source_target_pairs={{0,1},{1,0},{2,3},{3,2},{4,5},{5,4},{6,7},{7,6},{8,9},{9,8},{10,11... | collective-permute-start | bytes 98312 | tf_op jit(solution)/shard_map/ppermute | solution.py:414
  61.2 7.0 %collective-permute-start.28 = (bf16[128,128]{1,0:T(8,128)(2,1)S(1)}, bf16[128,128]{1,0:T(8,128)(2,1)S(1)}, u32[]{:S(2)}, u32[]{:S(2)}) collective-permute-start(bf16[128,128]{1,0:T(8,128)(2,1)S(1)} %get-tuple-element.119), channel_id=1, source_target_pairs={{4,8},{8,4},{5,9},{9,5},{6,10},{10,6},{7,11},{11,7},{12,16},{16,12... | collective-permute-start | bytes 98312 | tf_op jit(solution)/shard_map/ppermute | solution.py:414
  61.3 7.6 %collective-permute-start.29 = (bf16[128,128]{1,0:T(8,128)(2,1)S(1)}, bf16[128,128]{1,0:T(8,128)(2,1)S(1)}, u32[]{:S(2)}, u32[]{:S(2)}) collective-permute-start(bf16[128,128]{1,0:T(8,128)(2,1)S(1)} %get-tuple-element.120), channel_id=1, source_target_pairs={{2,4},{4,2},{3,5},{5,3},{6,8},{8,6},{7,9},{9,7},{10,12},{12,10},{1... | collective-permute-start | bytes 98312 | tf_op jit(solution)/shard_map/ppermute | solution.py:414
  64.8 7.0 %collective-permute-start.30 = (bf16[128,128]{1,0:T(8,128)(2,1)S(1)}, bf16[128,128]{1,0:T(8,128)(2,1)S(1)}, u32[]{:S(2)}, u32[]{:S(2)}) collective-permute-start(bf16[128,128]{1,0:T(8,128)(2,1)S(1)} %get-tuple-element.121), channel_id=1, source_target_pairs={{1,2},{2,1},{3,4},{4,3},{5,6},{6,5},{7,8},{8,7},{9,10},{10,9},{11,... | collective-permute-start | bytes 98312 | tf_op jit(solution)/shard_map/ppermute | solution.py:414
  66.2 5.6 %collective-permute-start.31 = (bf16[128,128]{1,0:T(8,128)(2,1)S(1)}, bf16[128,128]{1,0:T(8,128)(2,1)S(1)}, u32[]{:S(2)}, u32[]{:S(2)}) collective-permute-start(bf16[128,128]{1,0:T(8,128)(2,1)S(1)} %get-tuple-element.122), channel_id=1, source_target_pairs={{0,4},{4,0},{1,5},{5,1},{2,6},{6,2},{3,7},{7,3},{8,12},{12,8},{9,1... | collective-permute-start | bytes 98312 | tf_op jit(solution)/shard_map/ppermute | solution.py:414
  66.2 5.6 %collective-permute-start.32 = (bf16[128,128]{1,0:T(8,128)(2,1)S(1)}, bf16[128,128]{1,0:T(8,128)(2,1)S(1)}, u32[]{:S(2)}, u32[]{:S(2)}) collective-permute-start(bf16[128,128]{1,0:T(8,128)(2,1)S(1)} %get-tuple-element.123), channel_id=1, source_target_pairs={{0,2},{2,0},{1,3},{3,1},{4,6},{6,4},{5,7},{7,5},{8,10},{10,8},{9,1... | collective-permute-start | bytes 98312 | tf_op jit(solution)/shard_map/ppermute | solution.py:414
  68.3 3.6 %collective-permute-start.33 = (bf16[128,128]{1,0:T(8,128)(2,1)S(1)}, bf16[128,128]{1,0:T(8,128)(2,1)S(1)}, u32[]{:S(2)}, u32[]{:S(2)}) collective-permute-start(bf16[128,128]{1,0:T(8,128)(2,1)S(1)} %get-tuple-element.124), channel_id=1, source_target_pairs={{0,1},{1,0},{2,3},{3,2},{4,5},{5,4},{6,7},{7,6},{8,9},{9,8},{10,11... | collective-permute-start | bytes 98312 | tf_op jit(solution)/shard_map/ppermute | solution.py:414
  73.0 7.0 %collective-permute-start.34 = (bf16[128,128]{1,0:T(8,128)(2,1)S(1)}, bf16[128,128]{1,0:T(8,128)(2,1)S(1)}, u32[]{:S(2)}, u32[]{:S(2)}) collective-permute-start(bf16[128,128]{1,0:T(8,128)(2,1)S(1)} %get-tuple-element.127), channel_id=1, source_target_pairs={{4,8},{8,4},{5,9},{9,5},{6,10},{10,6},{7,11},{11,7},{12,16},{16,12... | collective-permute-start | bytes 98312 | tf_op jit(solution)/shard_map/ppermute | solution.py:414
  73.1 7.7 %collective-permute-start.35 = (bf16[128,128]{1,0:T(8,128)(2,1)S(1)}, bf16[128,128]{1,0:T(8,128)(2,1)S(1)}, u32[]{:S(2)}, u32[]{:S(2)}) collective-permute-start(bf16[128,128]{1,0:T(8,128)(2,1)S(1)} %get-tuple-element.128), channel_id=1, source_target_pairs={{2,4},{4,2},{3,5},{5,3},{6,8},{8,6},{7,9},{9,7},{10,12},{12,10},{1... | collective-permute-start | bytes 98312 | tf_op jit(solution)/shard_map/ppermute | solution.py:414
  75.7 6.9 %collective-permute-start.36 = (bf16[128,128]{1,0:T(8,128)(2,1)S(1)}, bf16[128,128]{1,0:T(8,128)(2,1)S(1)}, u32[]{:S(2)}, u32[]{:S(2)}) collective-permute-start(bf16[128,128]{1,0:T(8,128)(2,1)S(1)} %get-tuple-element.129), channel_id=1, source_target_pairs={{1,2},{2,1},{3,4},{4,3},{5,6},{6,5},{7,8},{8,7},{9,10},{10,9},{11,... | collective-permute-start | bytes 98312 | tf_op jit(solution)/shard_map/ppermute | solution.py:414
  78.0 4.7 %collective-permute-start.37 = (bf16[128,128]{1,0:T(8,128)(2,1)S(1)}, bf16[128,128]{1,0:T(8,128)(2,1)S(1)}, u32[]{:S(2)}, u32[]{:S(2)}) collective-permute-start(bf16[128,128]{1,0:T(8,128)(2,1)S(1)} %get-tuple-element.130), channel_id=1, source_target_pairs={{0,4},{4,0},{1,5},{5,1},{2,6},{6,2},{3,7},{7,3},{8,12},{12,8},{9,1... | collective-permute-start | bytes 98312 | tf_op jit(solution)/shard_map/ppermute | solution.py:414
  78.0 4.7 %collective-permute-start.38 = (bf16[128,128]{1,0:T(8,128)(2,1)S(1)}, bf16[128,128]{1,0:T(8,128)(2,1)S(1)}, u32[]{:S(2)}, u32[]{:S(2)}) collective-permute-start(bf16[128,128]{1,0:T(8,128)(2,1)S(1)} %get-tuple-element.131), channel_id=1, source_target_pairs={{0,2},{2,0},{1,3},{3,1},{4,6},{6,4},{5,7},{7,5},{8,10},{10,8},{9,1... | collective-permute-start | bytes 98312 | tf_op jit(solution)/shard_map/ppermute | solution.py:414
  80.0 2.6 %collective-permute-start.39 = (bf16[128,128]{1,0:T(8,128)(2,1)S(1)}, bf16[128,128]{1,0:T(8,128)(2,1)S(1)}, u32[]{:S(2)}, u32[]{:S(2)}) collective-permute-start(bf16[128,128]{1,0:T(8,128)(2,1)S(1)} %get-tuple-element.132), channel_id=1, source_target_pairs={{0,1},{1,0},{2,3},{3,2},{4,5},{5,4},{6,7},{7,6},{8,9},{9,8},{10,11... | collective-permute-start | bytes 98312 | tf_op jit(solution)/shard_map/ppermute | solution.py:414
  84.0 6.7 %collective-permute-start.40 = (bf16[128,128]{1,0:T(8,128)(2,1)S(1)}, bf16[128,128]{1,0:T(8,128)(2,1)S(1)}, u32[]{:S(2)}, u32[]{:S(2)}) collective-permute-start(bf16[128,128]{1,0:T(8,128)(2,1)S(1)} %get-tuple-element.135), channel_id=1, source_target_pairs={{4,8},{8,4},{5,9},{9,5},{6,10},{10,6},{7,11},{11,7},{12,16},{16,12... | collective-permute-start | bytes 98312 | tf_op jit(solution)/shard_map/ppermute | solution.py:414
  84.6 7.5 %collective-permute-start.41 = (bf16[128,128]{1,0:T(8,128)(2,1)S(1)}, bf16[128,128]{1,0:T(8,128)(2,1)S(1)}, u32[]{:S(2)}, u32[]{:S(2)}) collective-permute-start(bf16[128,128]{1,0:T(8,128)(2,1)S(1)} %get-tuple-element.136), channel_id=1, source_target_pairs={{2,4},{4,2},{3,5},{5,3},{6,8},{8,6},{7,9},{9,7},{10,12},{12,10},{1... | collective-permute-start | bytes 98312 | tf_op jit(solution)/shard_map/ppermute | solution.py:414
  87.6 6.9 %collective-permute-start.42 = (bf16[128,128]{1,0:T(8,128)(2,1)S(1)}, bf16[128,128]{1,0:T(8,128)(2,1)S(1)}, u32[]{:S(2)}, u32[]{:S(2)}) collective-permute-start(bf16[128,128]{1,0:T(8,128)(2,1)S(1)} %get-tuple-element.137), channel_id=1, source_target_pairs={{1,2},{2,1},{3,4},{4,3},{5,6},{6,5},{7,8},{8,7},{9,10},{10,9},{11,... | collective-permute-start | bytes 98312 | tf_op jit(solution)/shard_map/ppermute | solution.py:414
  90.0 4.6 %collective-permute-start.43 = (bf16[128,128]{1,0:T(8,128)(2,1)S(1)}, bf16[128,128]{1,0:T(8,128)(2,1)S(1)}, u32[]{:S(2)}, u32[]{:S(2)}) collective-permute-start(bf16[128,128]{1,0:T(8,128)(2,1)S(1)} %get-tuple-element.138), channel_id=1, source_target_pairs={{0,4},{4,0},{1,5},{5,1},{2,6},{6,2},{3,7},{7,3},{8,12},{12,8},{9,1... | collective-permute-start | bytes 98312 | tf_op jit(solution)/shard_map/ppermute | solution.py:414
  90.0 4.6 %collective-permute-start.44 = (bf16[128,128]{1,0:T(8,128)(2,1)S(1)}, bf16[128,128]{1,0:T(8,128)(2,1)S(1)}, u32[]{:S(2)}, u32[]{:S(2)}) collective-permute-start(bf16[128,128]{1,0:T(8,128)(2,1)S(1)} %get-tuple-element.139), channel_id=1, source_target_pairs={{0,2},{2,0},{1,3},{3,1},{4,6},{6,4},{5,7},{7,5},{8,10},{10,8},{9,1... | collective-permute-start | bytes 98312 | tf_op jit(solution)/shard_map/ppermute | solution.py:414
  90.7 3.8 %collective-permute-start.45 = (bf16[128,128]{1,0:T(8,128)(2,1)S(1)}, bf16[128,128]{1,0:T(8,128)(2,1)S(1)}, u32[]{:S(2)}, u32[]{:S(2)}) collective-permute-start(bf16[128,128]{1,0:T(8,128)(2,1)S(1)} %get-tuple-element.140), channel_id=1, source_target_pairs={{0,1},{1,0},{2,3},{3,2},{4,5},{5,4},{6,7},{7,6},{8,9},{9,8},{10,11... | collective-permute-start | bytes 98312 | tf_op jit(solution)/shard_map/ppermute | solution.py:414
  95.7 7.0 %collective-permute-start.46 = (bf16[128,128]{1,0:T(8,128)(2,1)S(1)}, bf16[128,128]{1,0:T(8,128)(2,1)S(1)}, u32[]{:S(2)}, u32[]{:S(2)}) collective-permute-start(bf16[128,128]{1,0:T(8,128)(2,1)S(1)} %get-tuple-element.143), channel_id=1, source_target_pairs={{4,8},{8,4},{5,9},{9,5},{6,10},{10,6},{7,11},{11,7},{12,16},{16,12... | collective-permute-start | bytes 98312 | tf_op jit(solution)/shard_map/ppermute | solution.py:414
  95.8 7.6 %collective-permute-start.47 = (bf16[128,128]{1,0:T(8,128)(2,1)S(1)}, bf16[128,128]{1,0:T(8,128)(2,1)S(1)}, u32[]{:S(2)}, u32[]{:S(2)}) collective-permute-start(bf16[128,128]{1,0:T(8,128)(2,1)S(1)} %get-tuple-element.144), channel_id=1, source_target_pairs={{2,4},{4,2},{3,5},{5,3},{6,8},{8,6},{7,9},{9,7},{10,12},{12,10},{1... | collective-permute-start | bytes 98312 | tf_op jit(solution)/shard_map/ppermute | solution.py:414
  99.3 7.0 %collective-permute-start.48 = (bf16[128,128]{1,0:T(8,128)(2,1)S(1)}, bf16[128,128]{1,0:T(8,128)(2,1)S(1)}, u32[]{:S(2)}, u32[]{:S(2)}) collective-permute-start(bf16[128,128]{1,0:T(8,128)(2,1)S(1)} %get-tuple-element.145), channel_id=1, source_target_pairs={{1,2},{2,1},{3,4},{4,3},{5,6},{6,5},{7,8},{8,7},{9,10},{10,9},{11,... | collective-permute-start | bytes 98312 | tf_op jit(solution)/shard_map/ppermute | solution.py:414
  100.8 5.4 %collective-permute-start.49 = (bf16[128,128]{1,0:T(8,128)(2,1)S(1)}, bf16[128,128]{1,0:T(8,128)(2,1)S(1)}, u32[]{:S(2)}, u32[]{:S(2)}) collective-permute-start(bf16[128,128]{1,0:T(8,128)(2,1)S(1)} %get-tuple-element.146), channel_id=1, source_target_pairs={{0,4},{4,0},{1,5},{5,1},{2,6},{6,2},{3,7},{7,3},{8,12},{12,8},{9,1... | collective-permute-start | bytes 98312 | tf_op jit(solution)/shard_map/ppermute | solution.py:414
  100.8 5.4 %collective-permute-start.50 = (bf16[128,128]{1,0:T(8,128)(2,1)S(1)}, bf16[128,128]{1,0:T(8,128)(2,1)S(1)}, u32[]{:S(2)}, u32[]{:S(2)}) collective-permute-start(bf16[128,128]{1,0:T(8,128)(2,1)S(1)} %get-tuple-element.147), channel_id=1, source_target_pairs={{0,2},{2,0},{1,3},{3,1},{4,6},{6,4},{5,7},{7,5},{8,10},{10,8},{9,1... | collective-permute-start | bytes 98312 | tf_op jit(solution)/shard_map/ppermute | solution.py:414
  102.7 3.5 %collective-permute-start.51 = (bf16[128,128]{1,0:T(8,128)(2,1)S(1)}, bf16[128,128]{1,0:T(8,128)(2,1)S(1)}, u32[]{:S(2)}, u32[]{:S(2)}) collective-permute-start(bf16[128,128]{1,0:T(8,128)(2,1)S(1)} %get-tuple-element.148), channel_id=1, source_target_pairs={{0,1},{1,0},{2,3},{3,2},{4,5},{5,4},{6,7},{7,6},{8,9},{9,8},{10,11... | collective-permute-start | bytes 98312 | tf_op jit(solution)/shard_map/ppermute | solution.py:414
  108.0 1.3 %collective-permute-start.52 = (f32[128,128]{1,0:T(8,128)S(1)}, f32[128,128]{1,0:T(8,128)S(1)}, u32[]{:S(2)}, u32[]{:S(2)}) collective-permute-start(f32[128,128]{1,0:T(8,128)S(1)} %get-tuple-element.149), channel_id=1, source_target_pairs={{0,1},{1,0},{2,3},{3,2},{4,5},{5,4},{6,7},{7,6},{8,9},{9,8},{10,11... | collective-permute-start | bytes 196616 | tf_op jit(solution)/shard_map/ppermute | solution.py:403
  109.4 5.8 %collective-permute-start.55 = (f32[128,128]{1,0:T(8,128)S(1)}, f32[128,128]{1,0:T(8,128)S(1)}, u32[]{:S(2)}, u32[]{:S(2)}) collective-permute-start(f32[128,128]{1,0:T(8,128)S(1)} %add.25), channel_id=1, source_target_pairs={{0,6},{1,7},{2,4},{3,5},{4,2},{5,3},{6,0},{7,1},{8,14},{9,15},{10,... | collective-permute-start | bytes 196616 | tf_op jit(solution)/shard_map/ppermute | solution.py:403
  109.4 5.7 %collective-permute-start.54 = (f32[128,128]{1,0:T(8,128)S(1)}, f32[128,128]{1,0:T(8,128)S(1)}, u32[]{:S(2)}, u32[]{:S(2)}) collective-permute-start(f32[128,128]{1,0:T(8,128)S(1)} %add.25), channel_id=1, source_target_pairs={{0,4},{1,5},{2,6},{3,7},{4,0},{5,1},{6,2},{7,3},{8,12},{9,13},{10,... | collective-permute-start | bytes 196616 | tf_op jit(solution)/shard_map/ppermute | solution.py:403
  110.4 5.0 %collective-permute-start.53 = (f32[128,128]{1,0:T(8,128)S(1)}, f32[128,128]{1,0:T(8,128)S(1)}, u32[]{:S(2)}, u32[]{:S(2)}) collective-permute-start(f32[128,128]{1,0:T(8,128)S(1)} %add.25), channel_id=1, source_target_pairs={{0,2},{1,3},{2,0},{3,1},{4,6},{5,7},{6,4},{7,5},{8,10},{9,11},{10,... | collective-permute-start | bytes 196616 | tf_op jit(solution)/shard_map/ppermute | solution.py:403
  115.4 6.8 %collective-permute-start.58 = (f32[128,128]{1,0:T(8,128)S(1)}, f32[128,128]{1,0:T(8,128)S(1)}, u32[]{:S(2)}, u32[]{:S(2)}) collective-permute-start(f32[128,128]{1,0:T(8,128)S(1)} %add_add_fusion.1), channel_id=1, source_target_pairs={{0,24},{1,25},{2,26},{3,27},{4,28},{5,29},{6,30},{7,31},{8,16},{9,... | collective-permute-start | bytes 196616 | tf_op jit(solution)/shard_map/ppermute | solution.py:403
  117.2 6.3 %collective-permute-start.57 = (f32[128,128]{1,0:T(8,128)S(1)}, f32[128,128]{1,0:T(8,128)S(1)}, u32[]{:S(2)}, u32[]{:S(2)}) collective-permute-start(f32[128,128]{1,0:T(8,128)S(1)} %add_add_fusion.1), channel_id=1, source_target_pairs={{0,16},{1,17},{2,18},{3,19},{4,20},{5,21},{6,22},{7,23},{8,24},{9,... | collective-permute-start | bytes 196616 | tf_op jit(solution)/shard_map/ppermute | solution.py:403
  117.3 6.3 %collective-permute-start.56 = (f32[128,128]{1,0:T(8,128)S(1)}, f32[128,128]{1,0:T(8,128)S(1)}, u32[]{:S(2)}, u32[]{:S(2)}) collective-permute-start(f32[128,128]{1,0:T(8,128)S(1)} %add_add_fusion.1), channel_id=1, source_target_pairs={{0,8},{1,9},{2,10},{3,11},{4,12},{5,13},{6,14},{7,15},{8,0},{9,1},... | collective-permute-start | bytes 196616 | tf_op jit(solution)/shard_map/ppermute | solution.py:403

commit v4 on v3

--- a/solution.py
+++ b/solution.py
@@ -295,7 +295,7 @@
 
 def last_kernel(scale, *refs):
     place_ref, band_ref, hot_ref, coef_ref, field_ref, prev_ref = refs[:6]
-    got, (next_ref, gram_ref) = refs[6:12], refs[12:]
+    got, (next_ref, kept_ref, sent_ref) = refs[6:12], refs[12:]
 
     def store(block, value):
         next_ref[block, :] = value
@@ -304,7 +304,11 @@
         place_ref, band_ref, hot_ref, coef_ref, field_ref, prev_ref, got, scale, store
     )
     value = next_ref[...]
-    gram_ref[...] = dot(value, value, ((0,), (0,)), lax.Precision.HIGHEST)
+    gram = dot(value, value, ((0,), (0,)), lax.Precision.HIGHEST)
+    half = VECS // 2
+    low = is_low(place_ref, 1)
+    kept_ref[...] = jnp.where(low, gram[:half], gram[half:])
+    sent_ref[...] = jnp.where(low, gram[half:], gram[:half])
 
 
 def last(scale, place, mats, field, prev, got):
@@ -313,10 +317,10 @@
         lambda *refs: last_kernel(scale, *refs),
         out_shape=(
             jax.ShapeDtypeStruct((rows, VECS), F32),
-            jax.ShapeDtypeStruct((VECS, VECS), F32),
+            *(jax.ShapeDtypeStruct((VECS // 2, VECS), F32),) * 2,
         ),
         in_specs=[SMEM] + [VMEM] * 11,
-        out_specs=(VMEM, VMEM),
+        out_specs=(VMEM,) * 3,
         compiler_params=PARAMS,
         name="last",
     )(place, *mats, field, prev, *got)
@@ -330,7 +334,7 @@
     return terms[0]
 
 
-def finish_kernel(scale, gram_ref, field_ref, out_ref, inverse_ref):
+def finish_kernel(scale, place_ref, own_ref, other_ref, field_ref, out_ref, inverse_ref):
     width = 8
     shape = (width, VECS)
     panels = VECS // width
@@ -340,7 +344,15 @@
     def spread(value):
         return jnp.broadcast_to(value, shape)
 
-    left = [gram_ref[width * b : width * (b + 1), :] for b in range(panels)]
+    low = is_low(place_ref, 1)
+    gram = jnp.concatenate(
+        [
+            jnp.where(low, own_ref[...], other_ref[...]),
+            jnp.where(low, other_ref[...], own_ref[...]),
+        ],
+        axis=0,
+    )
+    left = [gram[width * b : width * (b + 1), :] for b in range(panels)]
     right = [jnp.where(ids + width * b == lanes, 1.0, 0.0) for b in range(panels)]
     for p in range(panels):
         base = width * p
@@ -381,28 +393,29 @@
     out_ref[...] = dot(field_ref[...], inverse_ref[...], ((1,), (1,)), lax.Precision.HIGHEST)
 
 
-def finish(scale, gram, field):
+def finish(scale, place, halves, field):
     return pl.pallas_call(
         lambda *refs: finish_kernel(scale, *refs),
         out_shape=jax.ShapeDtypeStruct(field.shape, F32),
-        in_specs=[VMEM] * 2,
+        in_specs=[SMEM] + [VMEM] * 3,
         out_specs=VMEM,
         scratch_shapes=[pltpu.VMEM((VECS, VECS), F32)],
         compiler_params=PARAMS,
         name="finish",
-    )(gram, field)
-
-
-def summed(value, count):
-    bits = [1 << i for i in range(count.bit_length() - 1)]
-    stages = [bits[:1]] + [bits[i : i + 2] for i in range(1, len(bits), 2)]
-    for stage in stages:
-        masks = [stage[0]] if len(stage) == 1 else [*stage, stage[0] ^ stage[1]]
-        total = value
-        for mask in masks:
-            total = total + lax.ppermute(value, AXES, [(i, i ^ mask) for i in range(count)])
-        value = total
-    return value
+    )(place, *halves, field)
+
+
+def summed(kept, sent, count):
+    def swapped(value, mask):
+        return lax.ppermute(value, AXES, [(i, i ^ mask) for i in range(count)])
+
+    bits = [1 << i for i in range(1, count.bit_length() - 1)]
+    half = kept + swapped(sent, 1)
+    for i in range(0, len(bits), 2):
+        stage = bits[i : i + 2]
+        masks = stage if len(stage) == 1 else [*stage, stage[0] ^ stage[1]]
+        half = sum((swapped(half, mask) for mask in masks), half)
+    return half, swapped(half, 1)
 
 
 def local(start_basis, band_cols, band_wts, far_dst, far_src, far_wts):
@@ -450,8 +463,8 @@
     packed, *sent = step(2.0 / HALF_WIDTH, here, mats, packed, previous, got, has_next=False)
     previous = current
     got = exchange(sent)
-    filtered, gram = last(2.0 / HALF_WIDTH, here, mats[:3], packed, previous, got)
-    return finish(math.sqrt(total_rows), summed(gram, count), filtered)
+    filtered, kept, sent = last(2.0 / HALF_WIDTH, here, mats[:3], packed, previous, got)
+    return finish(math.sqrt(total_rows), here, summed(kept, sent, count), filtered)
 
 
 def solution(mesh):

time: 131 us -> 130 us (level)
    ppermute x7 -> x8, waiting for transfers between devices: 7.42 us -> 6.72 us  [swapped(): return lax.ppermute(value, AXES, [(i, i ^ mask) for i in range(count)])]
    ppermute x7 -> x8, starting transfers between devices: 8.07 us -> 8.08 us  [swapped(): return lax.ppermute(value, AXES, [(i, i ^ mask) for i in range(count)])]
  transfers between devices with their start and end apart: 59 -> 60, of which waited for: 31 -> 32; matrix products, arithmetic and copies ran while one was open for 0% -> 0% of each run, Pallas kernels for 2% -> 2%
where the time goes in v4:
time: 130 us
  starting transfers between devices  63.3 us (49%)
  waiting for transfers between devices  45.6 us (35%)
  Pallas kernels  20.8 us (16%)
    ppermute x52, starting transfers between devices, swap(): return lax.ppermute(value, AXES, swap_pairs(count, by, odd))  55.3 us
    ppermute x52, waiting for transfers between devices, swap(): return lax.ppermute(value, AXES, swap_pairs(count, by, odd))  38.9 us
    pallas_call x7, Pallas kernels, step(): pl.pallas_call(lambda *refs: step_kernel(scale, has_prev, has_next, *refs...  8.24 us
    ppermute x8, starting transfers between devices, swapped(): return lax.ppermute(value, AXES, [(i, i ^ mask) for i in range(count)])  8.08 us
    pallas_call x1, Pallas kernels, finish(): pl.pallas_call(lambda *refs: finish_kernel(scale, *refs), out_shape=jax.S...  7.14 us
    ppermute x8, waiting for transfers between devices, swapped(): return lax.ppermute(value, AXES, [(i, i ^ mask) for i in range(count)])  6.72 us
    pallas_call x1, Pallas kernels, prepare(): pl.pallas_call(prepare_kernel, out_shape=(jax.ShapeDtypeStruct((rows, 3 *...  3.08 us
  transfers between devices with their start and end apart: 60, of which 32 were waited for; matrix products, arithmetic and copies ran while one was open for 0% of the time, Pallas kernels for 2%

profile of v4, /device:TPU:0, one launch (start us, length us, event | category | flops | bytes accessed | tf_op | source)
XLA Modules:
  0.0 130.0 jit_solution(3266270200185614477)
XLA Ops:
  0.0 6.0 %collective-permute-start.3 = (s32[1,256]{1,0:T(1,128)}, s32[1,256]{1,0:T(1,128)S(1)}, u32[]{:S(2)}, u32[]{:S(2)}) collective-permute-start(s32[1,256]{1,0:T(1,128)} %bitcast.10), channel_id=1, source_target_pairs={{4,8},{8,4},{5,9},{9,5},{6,10},{10,6},{7,11},{11,7},{12,16},{16,12... | collective-permute-start | bytes 3080 | tf_op jit(solution)/shard_map/ppermute | solution.py:427
  6.0 2.8 %collective-permute-start.1 = (s32[1,256]{1,0:T(1,128)}, s32[1,256]{1,0:T(1,128)S(1)}, u32[]{:S(2)}, u32[]{:S(2)}) collective-permute-start(s32[1,256]{1,0:T(1,128)} %bitcast.12), channel_id=1, source_target_pairs={{2,4},{4,2},{3,5},{5,3},{6,8},{8,6},{7,9},{9,7},{10,12},{12,10},{1... | collective-permute-start | bytes 3080 | tf_op jit(solution)/shard_map/ppermute | solution.py:427
  9.5 3.1 %prepare.1 = (bf16[2048,384]{1,0:T(8,128)(2,1)S(1)}, bf16[2048,256]{1,0:T(8,128)(2,1)S(1)}, f32[256,128]{1,0:T(8,128)S(1)}, bf16[2048,128]{1,0:T(8,128)(2,1)S(1)}) custom-call(s32[1]{0:T(128)} %bitcast.place_ref.refs_0_, s32[1,256]{1,0:T(1,128)} %bitcast.8, f32[1,256]{1,0:T(1,128)} %bitcast.9, f32[3,8,2048]{2,1,0:T(8,128)} %bitcast.6, ...), custom_call_target="tpu_custom_call" | custom-call | tf_op jit(solution)/shard_map/prepare/pallas_call | solution.py:153
  12.6 0.8 collective-permute-done.1.w1
  14.0 2.0 %collective-permute-start.4 = (bf16[128,128]{1,0:T(8,128)(2,1)S(1)}, bf16[128,128]{1,0:T(8,128)(2,1)S(1)}, u32[]{:S(2)}, u32[]{:S(2)}) collective-permute-start(bf16[128,128]{1,0:T(8,128)(2,1)S(1)} %get-tuple-element.89), channel_id=1, source_target_pairs={{4,8},{8,4},{5,9},{9,5},{6,10},{10,6},{7,11},{11,7},{12,16},{16,12... | collective-permute-start | bytes 98312 | tf_op jit(solution)/shard_map/ppermute | solution.py:427
  16.0 2.8 %collective-permute-start.5 = (bf16[128,128]{1,0:T(8,128)(2,1)S(1)}, bf16[128,128]{1,0:T(8,128)(2,1)S(1)}, u32[]{:S(2)}, u32[]{:S(2)}) collective-permute-start(bf16[128,128]{1,0:T(8,128)(2,1)S(1)} %get-tuple-element.90), channel_id=1, source_target_pairs={{2,4},{4,2},{3,5},{5,3},{6,8},{8,6},{7,9},{9,7},{10,12},{12,10},{1... | collective-permute-start | bytes 98312 | tf_op jit(solution)/shard_map/ppermute | solution.py:427
  18.8 0.8 collective-permute-start.6
  19.7 1.0 collective-permute-done.4.refs_6_
  21.1 2.4 %collective-permute-done.5.refs_7_ = bf16[128,128]{1,0:T(8,128)(2,1)S(1)} collective-permute-done((bf16[128,128]{1,0:T(8,128)(2,1)S(1)}, bf16[128,128]{1,0:T(8,128)(2,1)S(1)}, u32[]{:S(2)}, u32[]{:S(2)}) %collective-permute-start.5) | collective-permute-done | bytes 32800 | tf_op jit(solution)/shard_map/ppermute | solution.py:427
  23.5 2.2 %collective-permute-done.6.refs_8_ = bf16[128,128]{1,0:T(8,128)(2,1)S(1)} collective-permute-done((bf16[128,128]{1,0:T(8,128)(2,1)S(1)}, bf16[128,128]{1,0:T(8,128)(2,1)S(1)}, u32[]{:S(2)}, u32[]{:S(2)}) %collective-permute-start.6) | collective-permute-done | bytes 32800 | tf_op jit(solution)/shard_map/ppermute | solution.py:427
  25.8 1.1 step.7
  27.0 1.9 %collective-permute-start.11 = (bf16[128,128]{1,0:T(8,128)(2,1)S(1)}, bf16[128,128]{1,0:T(8,128)(2,1)S(1)}, u32[]{:S(2)}, u32[]{:S(2)}) collective-permute-start(bf16[128,128]{1,0:T(8,128)(2,1)S(1)} %get-tuple-element.97), channel_id=1, source_target_pairs={{2,4},{4,2},{3,5},{5,3},{6,8},{8,6},{7,9},{9,7},{10,12},{12,10},{1... | collective-permute-start | bytes 98312 | tf_op jit(solution)/shard_map/ppermute | solution.py:427
  29.0 3.1 %collective-permute-start.12 = (bf16[128,128]{1,0:T(8,128)(2,1)S(1)}, bf16[128,128]{1,0:T(8,128)(2,1)S(1)}, u32[]{:S(2)}, u32[]{:S(2)}) collective-permute-start(bf16[128,128]{1,0:T(8,128)(2,1)S(1)} %get-tuple-element.98), channel_id=1, source_target_pairs={{1,2},{2,1},{3,4},{4,3},{5,6},{6,5},{7,8},{8,7},{9,10},{10,9},{11,... | collective-permute-start | bytes 98312 | tf_op jit(solution)/shard_map/ppermute | solution.py:427
  32.1 1.9 %collective-permute-done.10.refs_7_ = bf16[128,128]{1,0:T(8,128)(2,1)S(1)} collective-permute-done((bf16[128,128]{1,0:T(8,128)(2,1)S(1)}, bf16[128,128]{1,0:T(8,128)(2,1)S(1)}, u32[]{:S(2)}, u32[]{:S(2)}) %collective-permute-start.10) | collective-permute-done | bytes 32800 | tf_op jit(solution)/shard_map/ppermute | solution.py:427
  33.9 0.7 collective-permute-done.11.refs_8_
  34.6 1.3 %collective-permute-done.12.refs_9_ = bf16[128,128]{1,0:T(8,128)(2,1)S(1)} collective-permute-done((bf16[128,128]{1,0:T(8,128)(2,1)S(1)}, bf16[128,128]{1,0:T(8,128)(2,1)S(1)}, u32[]{:S(2)}, u32[]{:S(2)}) %collective-permute-start.12) | collective-permute-done | bytes 32800 | tf_op jit(solution)/shard_map/ppermute | solution.py:427
  36.3 1.1 step.8
  37.4 0.9 collective-permute-start.16
  38.3 3.0 %collective-permute-start.17 = (bf16[128,128]{1,0:T(8,128)(2,1)S(1)}, bf16[128,128]{1,0:T(8,128)(2,1)S(1)}, u32[]{:S(2)}, u32[]{:S(2)}) collective-permute-start(bf16[128,128]{1,0:T(8,128)(2,1)S(1)} %get-tuple-element.105), channel_id=1, source_target_pairs={{2,4},{4,2},{3,5},{5,3},{6,8},{8,6},{7,9},{9,7},{10,12},{12,10},{1... | collective-permute-start | bytes 98312 | tf_op jit(solution)/shard_map/ppermute | solution.py:427
  41.3 2.4 %collective-permute-start.18 = (bf16[128,128]{1,0:T(8,128)(2,1)S(1)}, bf16[128,128]{1,0:T(8,128)(2,1)S(1)}, u32[]{:S(2)}, u32[]{:S(2)}) collective-permute-start(bf16[128,128]{1,0:T(8,128)(2,1)S(1)} %get-tuple-element.106), channel_id=1, source_target_pairs={{1,2},{2,1},{3,4},{4,3},{5,6},{6,5},{7,8},{8,7},{9,10},{10,9},{11,... | collective-permute-start | bytes 98312 | tf_op jit(solution)/shard_map/ppermute | solution.py:427
  44.1 1.8 %collective-permute-done.17.refs_8_ = bf16[128,128]{1,0:T(8,128)(2,1)S(1)} collective-permute-done((bf16[128,128]{1,0:T(8,128)(2,1)S(1)}, bf16[128,128]{1,0:T(8,128)(2,1)S(1)}, u32[]{:S(2)}, u32[]{:S(2)}) %collective-permute-start.17) | collective-permute-done | bytes 32800 | tf_op jit(solution)/shard_map/ppermute | solution.py:427
  45.8 2.4 %collective-permute-done.18.refs_9_ = bf16[128,128]{1,0:T(8,128)(2,1)S(1)} collective-permute-done((bf16[128,128]{1,0:T(8,128)(2,1)S(1)}, bf16[128,128]{1,0:T(8,128)(2,1)S(1)}, u32[]{:S(2)}, u32[]{:S(2)}) %collective-permute-start.18) | collective-permute-done | bytes 32800 | tf_op jit(solution)/shard_map/ppermute | solution.py:427
  48.3 1.1 step.9
  49.5 3.5 %collective-permute-start.23 = (bf16[128,128]{1,0:T(8,128)(2,1)S(1)}, bf16[128,128]{1,0:T(8,128)(2,1)S(1)}, u32[]{:S(2)}, u32[]{:S(2)}) collective-permute-start(bf16[128,128]{1,0:T(8,128)(2,1)S(1)} %get-tuple-element.113), channel_id=1, source_target_pairs={{2,4},{4,2},{3,5},{5,3},{6,8},{8,6},{7,9},{9,7},{10,12},{12,10},{1... | collective-permute-start | bytes 98312 | tf_op jit(solution)/shard_map/ppermute | solution.py:427
  53.0 1.5 %collective-permute-start.24 = (bf16[128,128]{1,0:T(8,128)(2,1)S(1)}, bf16[128,128]{1,0:T(8,128)(2,1)S(1)}, u32[]{:S(2)}, u32[]{:S(2)}) collective-permute-start(bf16[128,128]{1,0:T(8,128)(2,1)S(1)} %get-tuple-element.114), channel_id=1, source_target_pairs={{1,2},{2,1},{3,4},{4,3},{5,6},{6,5},{7,8},{8,7},{9,10},{10,9},{11,... | collective-permute-start | bytes 98312 | tf_op jit(solution)/shard_map/ppermute | solution.py:427
  54.6 0.9 collective-permute-start.26
  55.5 1.0 collective-permute-done.22.refs_7_
  56.5 0.7 collective-permute-done.23.refs_8_
  57.2 2.9 %collective-permute-done.24.refs_9_ = bf16[128,128]{1,0:T(8,128)(2,1)S(1)} collective-permute-done((bf16[128,128]{1,0:T(8,128)(2,1)S(1)}, bf16[128,128]{1,0:T(8,128)(2,1)S(1)}, u32[]{:S(2)}, u32[]{:S(2)}) %collective-permute-start.24) | collective-permute-done | bytes 32800 | tf_op jit(solution)/shard_map/ppermute | solution.py:427
  60.1 1.2 step.10
  61.3 3.5 %collective-permute-start.29 = (bf16[128,128]{1,0:T(8,128)(2,1)S(1)}, bf16[128,128]{1,0:T(8,128)(2,1)S(1)}, u32[]{:S(2)}, u32[]{:S(2)}) collective-permute-start(bf16[128,128]{1,0:T(8,128)(2,1)S(1)} %get-tuple-element.121), channel_id=1, source_target_pairs={{2,4},{4,2},{3,5},{5,3},{6,8},{8,6},{7,9},{9,7},{10,12},{12,10},{1... | collective-permute-start | bytes 98312 | tf_op jit(solution)/shard_map/ppermute | solution.py:427
  64.8 1.4 %collective-permute-start.30 = (bf16[128,128]{1,0:T(8,128)(2,1)S(1)}, bf16[128,128]{1,0:T(8,128)(2,1)S(1)}, u32[]{:S(2)}, u32[]{:S(2)}) collective-permute-start(bf16[128,128]{1,0:T(8,128)(2,1)S(1)} %get-tuple-element.122), channel_id=1, source_target_pairs={{1,2},{2,1},{3,4},{4,3},{5,6},{6,5},{7,8},{8,7},{9,10},{10,9},{11,... | collective-permute-start | bytes 98312 | tf_op jit(solution)/shard_map/ppermute | solution.py:427
  66.5 1.8 %collective-permute-done.28.refs_7_ = bf16[128,128]{1,0:T(8,128)(2,1)S(1)} collective-permute-done((bf16[128,128]{1,0:T(8,128)(2,1)S(1)}, bf16[128,128]{1,0:T(8,128)(2,1)S(1)}, u32[]{:S(2)}, u32[]{:S(2)}) %collective-permute-start.28) | collective-permute-done | bytes 32800 | tf_op jit(solution)/shard_map/ppermute | solution.py:427
  68.9 2.9 %collective-permute-done.30.refs_9_ = bf16[128,128]{1,0:T(8,128)(2,1)S(1)} collective-permute-done((bf16[128,128]{1,0:T(8,128)(2,1)S(1)}, bf16[128,128]{1,0:T(8,128)(2,1)S(1)}, u32[]{:S(2)}, u32[]{:S(2)}) %collective-permute-start.30) | collective-permute-done | bytes 32800 | tf_op jit(solution)/shard_map/ppermute | solution.py:427
  71.8 1.2 step.11
  73.1 2.7 %collective-permute-start.35 = (bf16[128,128]{1,0:T(8,128)(2,1)S(1)}, bf16[128,128]{1,0:T(8,128)(2,1)S(1)}, u32[]{:S(2)}, u32[]{:S(2)}) collective-permute-start(bf16[128,128]{1,0:T(8,128)(2,1)S(1)} %get-tuple-element.129), channel_id=1, source_target_pairs={{2,4},{4,2},{3,5},{5,3},{6,8},{8,6},{7,9},{9,7},{10,12},{12,10},{1... | collective-permute-start | bytes 98312 | tf_op jit(solution)/shard_map/ppermute | solution.py:427
  75.7 2.2 %collective-permute-start.36 = (bf16[128,128]{1,0:T(8,128)(2,1)S(1)}, bf16[128,128]{1,0:T(8,128)(2,1)S(1)}, u32[]{:S(2)}, u32[]{:S(2)}) collective-permute-start(bf16[128,128]{1,0:T(8,128)(2,1)S(1)} %get-tuple-element.130), channel_id=1, source_target_pairs={{1,2},{2,1},{3,4},{4,3},{5,6},{6,5},{7,8},{8,7},{9,10},{10,9},{11,... | collective-permute-start | bytes 98312 | tf_op jit(solution)/shard_map/ppermute | solution.py:427
  78.1 1.9 %collective-permute-done.34.refs_7_ = bf16[128,128]{1,0:T(8,128)(2,1)S(1)} collective-permute-done((bf16[128,128]{1,0:T(8,128)(2,1)S(1)}, bf16[128,128]{1,0:T(8,128)(2,1)S(1)}, u32[]{:S(2)}, u32[]{:S(2)}) %collective-permute-start.34) | collective-permute-done | bytes 32800 | tf_op jit(solution)/shard_map/ppermute | solution.py:427
  80.0 0.7 collective-permute-done.35.refs_8_
  80.8 1.9 %collective-permute-done.36.refs_9_ = bf16[128,128]{1,0:T(8,128)(2,1)S(1)} collective-permute-done((bf16[128,128]{1,0:T(8,128)(2,1)S(1)}, bf16[128,128]{1,0:T(8,128)(2,1)S(1)}, u32[]{:S(2)}, u32[]{:S(2)}) %collective-permute-start.36) | collective-permute-done | bytes 32800 | tf_op jit(solution)/shard_map/ppermute | solution.py:427
  82.7 1.3 %step.12 = (bf16[2048,128]{1,0:T(8,128)(2,1)S(1)}, bf16[128,128]{1,0:T(8,128)(2,1)S(1)}, bf16[128,128]{1,0:T(8,128)(2,1)S(1)}, bf16[128,128]{1,0:T(8,128)(2,1)S(...) custom-call(s32[1]{0:T(128)} %bitcast.place_ref.refs_0_, ...), custom_call_target="tpu_custom_call" | custom-call | tf_op jit(solution)/shard_map/step/pallas_call | solution.py:282
  84.6 3.0 %collective-permute-start.41 = (bf16[128,128]{1,0:T(8,128)(2,1)S(1)}, bf16[128,128]{1,0:T(8,128)(2,1)S(1)}, u32[]{:S(2)}, u32[]{:S(2)}) collective-permute-start(bf16[128,128]{1,0:T(8,128)(2,1)S(1)} %get-tuple-element.137), channel_id=1, source_target_pairs={{2,4},{4,2},{3,5},{5,3},{6,8},{8,6},{7,9},{9,7},{10,12},{12,10},{1... | collective-permute-start | bytes 98312 | tf_op jit(solution)/shard_map/ppermute | solution.py:427
  87.6 2.4 %collective-permute-start.42 = (bf16[128,128]{1,0:T(8,128)(2,1)S(1)}, bf16[128,128]{1,0:T(8,128)(2,1)S(1)}, u32[]{:S(2)}, u32[]{:S(2)}) collective-permute-start(bf16[128,128]{1,0:T(8,128)(2,1)S(1)} %get-tuple-element.138), channel_id=1, source_target_pairs={{1,2},{2,1},{3,4},{4,3},{5,6},{6,5},{7,8},{8,7},{9,10},{10,9},{11,... | collective-permute-start | bytes 98312 | tf_op jit(solution)/shard_map/ppermute | solution.py:427
  90.0 0.8 collective-permute-done.40.refs_7_
  90.7 1.4 %collective-permute-done.41.refs_8_ = bf16[128,128]{1,0:T(8,128)(2,1)S(1)} collective-permute-done((bf16[128,128]{1,0:T(8,128)(2,1)S(1)}, bf16[128,128]{1,0:T(8,128)(2,1)S(1)}, u32[]{:S(2)}, u32[]{:S(2)}) %collective-permute-start.41) | collective-permute-done | bytes 32800 | tf_op jit(solution)/shard_map/ppermute | solution.py:427
  92.1 2.4 %collective-permute-done.42.refs_9_ = bf16[128,128]{1,0:T(8,128)(2,1)S(1)} collective-permute-done((bf16[128,128]{1,0:T(8,128)(2,1)S(1)}, bf16[128,128]{1,0:T(8,128)(2,1)S(1)}, u32[]{:S(2)}, u32[]{:S(2)}) %collective-permute-start.42) | collective-permute-done | bytes 32800 | tf_op jit(solution)/shard_map/ppermute | solution.py:427
  94.6 1.2 step.13
  95.8 3.5 %collective-permute-start.47 = (bf16[128,128]{1,0:T(8,128)(2,1)S(1)}, bf16[128,128]{1,0:T(8,128)(2,1)S(1)}, u32[]{:S(2)}, u32[]{:S(2)}) collective-permute-start(bf16[128,128]{1,0:T(8,128)(2,1)S(1)} %get-tuple-element.145), channel_id=1, source_target_pairs={{2,4},{4,2},{3,5},{5,3},{6,8},{8,6},{7,9},{9,7},{10,12},{12,10},{1... | collective-permute-start | bytes 98312 | tf_op jit(solution)/shard_map/ppermute | solution.py:427
  99.3 1.6 %collective-permute-start.48 = (bf16[128,128]{1,0:T(8,128)(2,1)S(1)}, bf16[128,128]{1,0:T(8,128)(2,1)S(1)}, u32[]{:S(2)}, u32[]{:S(2)}) collective-permute-start(bf16[128,128]{1,0:T(8,128)(2,1)S(1)} %get-tuple-element.146), channel_id=1, source_target_pairs={{1,2},{2,1},{3,4},{4,3},{5,6},{6,5},{7,8},{8,7},{9,10},{10,9},{11,... | collective-permute-start | bytes 98312 | tf_op jit(solution)/shard_map/ppermute | solution.py:427
  100.8 0.8 collective-permute-start.50
  101.7 1.1 collective-permute-done.46.refs_6_
  102.7 0.7 collective-permute-done.47.refs_7_
  103.4 2.8 %collective-permute-done.48.refs_8_ = bf16[128,128]{1,0:T(8,128)(2,1)S(1)} collective-permute-done((bf16[128,128]{1,0:T(8,128)(2,1)S(1)}, bf16[128,128]{1,0:T(8,128)(2,1)S(1)}, u32[]{:S(2)}, u32[]{:S(2)}) %collective-permute-start.48) | collective-permute-done | bytes 32800 | tf_op jit(solution)/shard_map/ppermute | solution.py:427
  106.2 1.8 %last.1 = (f32[2048,128]{1,0:T(8,128)S(1)}, f32[64,128]{1,0:T(8,128)S(1)}, f32[64,128]{1,0:T(8,128)S(1)}) custom-call(s32[1]{0:T(128)} %bitcast.place_ref.refs_0_, bf16[2048,384]{1,0:T(8,128)(2,1)S(1)} %get-tuple-element.80.refs_1_, bf16[2048,256]{1,0:T(8,128)(2,1)S(1)} %get-tuple-element.81.refs_2_, f32[256,128]{1,0:T(8,128)S(1)} %get-tuple-element.82.refs_3_, ...), custom_call_target="tpu_custom_call" | custom-call | tf_op jit(solution)/shard_map/last/pallas_call | solution.py:316
  108.1 1.2 collective-permute-done.52
  109.3 0.9 collective-permute-start.54
  110.2 2.5 %collective-permute-start.53 = (f32[64,128]{1,0:T(8,128)S(1)}, f32[64,128]{1,0:T(8,128)S(1)}, u32[]{:S(2)}, u32[]{:S(2)}) collective-permute-start(f32[64,128]{1,0:T(8,128)S(1)} %add.25), channel_id=1, source_target_pairs={{0,2},{1,3},{2,0},{3,1},{4,6},{5,7},{6,4},{7,5},{8,10},{9,11},{10,... | collective-permute-start | bytes 98312 | tf_op jit(solution)/shard_map/ppermute | solution.py:410
  112.8 1.5 %collective-permute-done.55 = f32[64,128]{1,0:T(8,128)S(1)} collective-permute-done((f32[64,128]{1,0:T(8,128)S(1)}, f32[64,128]{1,0:T(8,128)S(1)}, u32[]{:S(2)}, u32[]{:S(2)}) %collective-permute-start.55) | collective-permute-done | bytes 32800 | tf_op jit(solution)/shard_map/ppermute | solution.py:410
  114.7 2.1 %collective-permute-start.58 = (f32[64,128]{1,0:T(8,128)S(1)}, f32[64,128]{1,0:T(8,128)S(1)}, u32[]{:S(2)}, u32[]{:S(2)}) collective-permute-start(f32[64,128]{1,0:T(8,128)S(1)} %add_add_fusion.1), channel_id=1, source_target_pairs={{0,24},{1,25},{2,26},{3,27},{4,28},{5,29},{6,30},{7,31},{8,16},{9,... | collective-permute-start | bytes 98312 | tf_op jit(solution)/shard_map/ppermute | solution.py:410
  116.8 2.4 %collective-permute-start.56 = (f32[64,128]{1,0:T(8,128)S(1)}, f32[64,128]{1,0:T(8,128)S(1)}, u32[]{:S(2)}, u32[]{:S(2)}) collective-permute-start(f32[64,128]{1,0:T(8,128)S(1)} %add_add_fusion.1), channel_id=1, source_target_pairs={{0,8},{1,9},{2,10},{3,11},{4,12},{5,13},{6,14},{7,15},{8,0},{9,1},... | collective-permute-start | bytes 98312 | tf_op jit(solution)/shard_map/ppermute | solution.py:410
  119.1 1.5 %collective-permute-done.58 = f32[64,128]{1,0:T(8,128)S(1)} collective-permute-done((f32[64,128]{1,0:T(8,128)S(1)}, f32[64,128]{1,0:T(8,128)S(1)}, u32[]{:S(2)}, u32[]{:S(2)}) %collective-permute-start.58) | collective-permute-done | bytes 32800 | tf_op jit(solution)/shard_map/ppermute | solution.py:410
  120.6 0.9 collective-permute-done.57
  121.7 1.2 collective-permute-done.59.refs_2_
  122.9 7.1 %finish.1 = f32[2048,128]{1,0:T(8,128)} custom-call(s32[1]{0:T(128)} %bitcast.place_ref.refs_0_, f32[64,128]{1,0:T(8,128)S(1)} %add_add_fusion.refs_1_, f32[64,128]{1,0:T(8,128)S(1)} %collective-permute-done.59.refs_2_, f32[2048,128]{1,0:T(8,128)S(1)} %get-tuple-element.152.refs_3_), custom_call_target="tpu_custom_call" | custom-call | tf_op jit(solution)/shard_map/finish/pallas_call | solution.py:397
  (70 shorter events, 4.9 us)
Async XLA Ops:
  0.0 12.6 %collective-permute-start.3 = (s32[1,256]{1,0:T(1,128)}, s32[1,256]{1,0:T(1,128)S(1)}, u32[]{:S(2)}, u32[]{:S(2)}) collective-permute-start(s32[1,256]{1,0:T(1,128)} %bitcast.10), channel_id=1, source_target_pairs={{4,8},{8,4},{5,9},{9,5},{6,10},{10,6},{7,11},{11,7},{12,16},{16,12... | collective-permute-start | bytes 3080 | tf_op jit(solution)/shard_map/ppermute | solution.py:427
  6.0 6.6 %collective-permute-start.2 = (s32[1,256]{1,0:T(1,128)}, s32[1,256]{1,0:T(1,128)S(1)}, u32[]{:S(2)}, u32[]{:S(2)}) collective-permute-start(s32[1,256]{1,0:T(1,128)} %bitcast.11), channel_id=1, source_target_pairs={{0,4},{4,0},{1,5},{5,1},{2,6},{6,2},{3,7},{7,3},{8,12},{12,8},{9,1... | collective-permute-start | bytes 3080 | tf_op jit(solution)/shard_map/ppermute | solution.py:427
  6.0 7.4 %collective-permute-start.1 = (s32[1,256]{1,0:T(1,128)}, s32[1,256]{1,0:T(1,128)S(1)}, u32[]{:S(2)}, u32[]{:S(2)}) collective-permute-start(s32[1,256]{1,0:T(1,128)} %bitcast.12), channel_id=1, source_target_pairs={{2,4},{4,2},{3,5},{5,3},{6,8},{8,6},{7,9},{9,7},{10,12},{12,10},{1... | collective-permute-start | bytes 3080 | tf_op jit(solution)/shard_map/ppermute | solution.py:427
  8.8 4.5 %collective-permute-start = (s32[1,256]{1,0:T(1,128)}, s32[1,256]{1,0:T(1,128)S(1)}, u32[]{:S(2)}, u32[]{:S(2)}) collective-permute-start(s32[1,256]{1,0:T(1,128)} %bitcast.13), channel_id=1, source_target_pairs={{0,2},{2,0},{1,3},{3,1},{4,6},{6,4},{5,7},{7,5},{8,10},{10,8},{9,1... | collective-permute-start | bytes 3080 | tf_op jit(solution)/shard_map/ppermute | solution.py:427
  14.0 6.7 %collective-permute-start.4 = (bf16[128,128]{1,0:T(8,128)(2,1)S(1)}, bf16[128,128]{1,0:T(8,128)(2,1)S(1)}, u32[]{:S(2)}, u32[]{:S(2)}) collective-permute-start(bf16[128,128]{1,0:T(8,128)(2,1)S(1)} %get-tuple-element.89), channel_id=1, source_target_pairs={{4,8},{8,4},{5,9},{9,5},{6,10},{10,6},{7,11},{11,7},{12,16},{16,12... | collective-permute-start | bytes 98312 | tf_op jit(solution)/shard_map/ppermute | solution.py:427
  16.0 7.5 %collective-permute-start.5 = (bf16[128,128]{1,0:T(8,128)(2,1)S(1)}, bf16[128,128]{1,0:T(8,128)(2,1)S(1)}, u32[]{:S(2)}, u32[]{:S(2)}) collective-permute-start(bf16[128,128]{1,0:T(8,128)(2,1)S(1)} %get-tuple-element.90), channel_id=1, source_target_pairs={{2,4},{4,2},{3,5},{5,3},{6,8},{8,6},{7,9},{9,7},{10,12},{12,10},{1... | collective-permute-start | bytes 98312 | tf_op jit(solution)/shard_map/ppermute | solution.py:427
  18.8 6.9 %collective-permute-start.6 = (bf16[128,128]{1,0:T(8,128)(2,1)S(1)}, bf16[128,128]{1,0:T(8,128)(2,1)S(1)}, u32[]{:S(2)}, u32[]{:S(2)}) collective-permute-start(bf16[128,128]{1,0:T(8,128)(2,1)S(1)} %get-tuple-element.91), channel_id=1, source_target_pairs={{1,2},{2,1},{3,4},{4,3},{5,6},{6,5},{7,8},{8,7},{9,10},{10,9},{11,... | collective-permute-start | bytes 98312 | tf_op jit(solution)/shard_map/ppermute | solution.py:427
  19.7 6.1 %collective-permute-start.7 = (bf16[128,128]{1,0:T(8,128)(2,1)S(1)}, bf16[128,128]{1,0:T(8,128)(2,1)S(1)}, u32[]{:S(2)}, u32[]{:S(2)}) collective-permute-start(bf16[128,128]{1,0:T(8,128)(2,1)S(1)} %get-tuple-element.92), channel_id=1, source_target_pairs={{0,4},{4,0},{1,5},{5,1},{2,6},{6,2},{3,7},{7,3},{8,12},{12,8},{9,1... | collective-permute-start | bytes 98312 | tf_op jit(solution)/shard_map/ppermute | solution.py:427
  19.7 6.1 %collective-permute-start.8 = (bf16[128,128]{1,0:T(8,128)(2,1)S(1)}, bf16[128,128]{1,0:T(8,128)(2,1)S(1)}, u32[]{:S(2)}, u32[]{:S(2)}) collective-permute-start(bf16[128,128]{1,0:T(8,128)(2,1)S(1)} %get-tuple-element.93), channel_id=1, source_target_pairs={{0,2},{2,0},{1,3},{3,1},{4,6},{6,4},{5,7},{7,5},{8,10},{10,8},{9,1... | collective-permute-start | bytes 98312 | tf_op jit(solution)/shard_map/ppermute | solution.py:427
  20.7 5.1 %collective-permute-start.9 = (bf16[128,128]{1,0:T(8,128)(2,1)S(1)}, bf16[128,128]{1,0:T(8,128)(2,1)S(1)}, u32[]{:S(2)}, u32[]{:S(2)}) collective-permute-start(bf16[128,128]{1,0:T(8,128)(2,1)S(1)} %get-tuple-element.94), channel_id=1, source_target_pairs={{0,1},{1,0},{2,3},{3,2},{4,5},{5,4},{6,7},{7,6},{8,9},{9,8},{10,11... | collective-permute-start | bytes 98312 | tf_op jit(solution)/shard_map/ppermute | solution.py:427
  26.9 7.0 %collective-permute-start.10 = (bf16[128,128]{1,0:T(8,128)(2,1)S(1)}, bf16[128,128]{1,0:T(8,128)(2,1)S(1)}, u32[]{:S(2)}, u32[]{:S(2)}) collective-permute-start(bf16[128,128]{1,0:T(8,128)(2,1)S(1)} %get-tuple-element.96), channel_id=1, source_target_pairs={{4,8},{8,4},{5,9},{9,5},{6,10},{10,6},{7,11},{11,7},{12,16},{16,12... | collective-permute-start | bytes 98312 | tf_op jit(solution)/shard_map/ppermute | solution.py:427
  27.0 7.6 %collective-permute-start.11 = (bf16[128,128]{1,0:T(8,128)(2,1)S(1)}, bf16[128,128]{1,0:T(8,128)(2,1)S(1)}, u32[]{:S(2)}, u32[]{:S(2)}) collective-permute-start(bf16[128,128]{1,0:T(8,128)(2,1)S(1)} %get-tuple-element.97), channel_id=1, source_target_pairs={{2,4},{4,2},{3,5},{5,3},{6,8},{8,6},{7,9},{9,7},{10,12},{12,10},{1... | collective-permute-start | bytes 98312 | tf_op jit(solution)/shard_map/ppermute | solution.py:427
  29.0 7.0 %collective-permute-start.12 = (bf16[128,128]{1,0:T(8,128)(2,1)S(1)}, bf16[128,128]{1,0:T(8,128)(2,1)S(1)}, u32[]{:S(2)}, u32[]{:S(2)}) collective-permute-start(bf16[128,128]{1,0:T(8,128)(2,1)S(1)} %get-tuple-element.98), channel_id=1, source_target_pairs={{1,2},{2,1},{3,4},{4,3},{5,6},{6,5},{7,8},{8,7},{9,10},{10,9},{11,... | collective-permute-start | bytes 98312 | tf_op jit(solution)/shard_map/ppermute | solution.py:427
  32.0 4.2 %collective-permute-start.13 = (bf16[128,128]{1,0:T(8,128)(2,1)S(1)}, bf16[128,128]{1,0:T(8,128)(2,1)S(1)}, u32[]{:S(2)}, u32[]{:S(2)}) collective-permute-start(bf16[128,128]{1,0:T(8,128)(2,1)S(1)} %get-tuple-element.99), channel_id=1, source_target_pairs={{0,4},{4,0},{1,5},{5,1},{2,6},{6,2},{3,7},{7,3},{8,12},{12,8},{9,1... | collective-permute-start | bytes 98312 | tf_op jit(solution)/shard_map/ppermute | solution.py:427
  32.1 4.2 %collective-permute-start.14 = (bf16[128,128]{1,0:T(8,128)(2,1)S(1)}, bf16[128,128]{1,0:T(8,128)(2,1)S(1)}, u32[]{:S(2)}, u32[]{:S(2)}) collective-permute-start(bf16[128,128]{1,0:T(8,128)(2,1)S(1)} %get-tuple-element.100), channel_id=1, source_target_pairs={{0,2},{2,0},{1,3},{3,1},{4,6},{6,4},{5,7},{7,5},{8,10},{10,8},{9,1... | collective-permute-start | bytes 98312 | tf_op jit(solution)/shard_map/ppermute | solution.py:427
  33.9 2.3 %collective-permute-start.15 = (bf16[128,128]{1,0:T(8,128)(2,1)S(1)}, bf16[128,128]{1,0:T(8,128)(2,1)S(1)}, u32[]{:S(2)}, u32[]{:S(2)}) collective-permute-start(bf16[128,128]{1,0:T(8,128)(2,1)S(1)} %get-tuple-element.101), channel_id=1, source_target_pairs={{0,1},{1,0},{2,3},{3,2},{4,5},{5,4},{6,7},{7,6},{8,9},{9,8},{10,11... | collective-permute-start | bytes 98312 | tf_op jit(solution)/shard_map/ppermute | solution.py:427
  37.4 6.7 %collective-permute-start.16 = (bf16[128,128]{1,0:T(8,128)(2,1)S(1)}, bf16[128,128]{1,0:T(8,128)(2,1)S(1)}, u32[]{:S(2)}, u32[]{:S(2)}) collective-permute-start(bf16[128,128]{1,0:T(8,128)(2,1)S(1)} %get-tuple-element.104), channel_id=1, source_target_pairs={{4,8},{8,4},{5,9},{9,5},{6,10},{10,6},{7,11},{11,7},{12,16},{16,12... | collective-permute-start | bytes 98312 | tf_op jit(solution)/shard_map/ppermute | solution.py:427
  38.3 7.5 %collective-permute-start.17 = (bf16[128,128]{1,0:T(8,128)(2,1)S(1)}, bf16[128,128]{1,0:T(8,128)(2,1)S(1)}, u32[]{:S(2)}, u32[]{:S(2)}) collective-permute-start(bf16[128,128]{1,0:T(8,128)(2,1)S(1)} %get-tuple-element.105), channel_id=1, source_target_pairs={{2,4},{4,2},{3,5},{5,3},{6,8},{8,6},{7,9},{9,7},{10,12},{12,10},{1... | collective-permute-start | bytes 98312 | tf_op jit(solution)/shard_map/ppermute | solution.py:427
  41.3 6.9 %collective-permute-start.18 = (bf16[128,128]{1,0:T(8,128)(2,1)S(1)}, bf16[128,128]{1,0:T(8,128)(2,1)S(1)}, u32[]{:S(2)}, u32[]{:S(2)}) collective-permute-start(bf16[128,128]{1,0:T(8,128)(2,1)S(1)} %get-tuple-element.106), channel_id=1, source_target_pairs={{1,2},{2,1},{3,4},{4,3},{5,6},{6,5},{7,8},{8,7},{9,10},{10,9},{11,... | collective-permute-start | bytes 98312 | tf_op jit(solution)/shard_map/ppermute | solution.py:427
  43.7 4.6 %collective-permute-start.19 = (bf16[128,128]{1,0:T(8,128)(2,1)S(1)}, bf16[128,128]{1,0:T(8,128)(2,1)S(1)}, u32[]{:S(2)}, u32[]{:S(2)}) collective-permute-start(bf16[128,128]{1,0:T(8,128)(2,1)S(1)} %get-tuple-element.107), channel_id=1, source_target_pairs={{0,4},{4,0},{1,5},{5,1},{2,6},{6,2},{3,7},{7,3},{8,12},{12,8},{9,1... | collective-permute-start | bytes 98312 | tf_op jit(solution)/shard_map/ppermute | solution.py:427
  43.7 4.6 %collective-permute-start.20 = (bf16[128,128]{1,0:T(8,128)(2,1)S(1)}, bf16[128,128]{1,0:T(8,128)(2,1)S(1)}, u32[]{:S(2)}, u32[]{:S(2)}) collective-permute-start(bf16[128,128]{1,0:T(8,128)(2,1)S(1)} %get-tuple-element.108), channel_id=1, source_target_pairs={{0,2},{2,0},{1,3},{3,1},{4,6},{6,4},{5,7},{7,5},{8,10},{10,8},{9,1... | collective-permute-start | bytes 98312 | tf_op jit(solution)/shard_map/ppermute | solution.py:427
  44.1 4.2 %collective-permute-start.21 = (bf16[128,128]{1,0:T(8,128)(2,1)S(1)}, bf16[128,128]{1,0:T(8,128)(2,1)S(1)}, u32[]{:S(2)}, u32[]{:S(2)}) collective-permute-start(bf16[128,128]{1,0:T(8,128)(2,1)S(1)} %get-tuple-element.109), channel_id=1, source_target_pairs={{0,1},{1,0},{2,3},{3,2},{4,5},{5,4},{6,7},{7,6},{8,9},{9,8},{10,11... | collective-permute-start | bytes 98312 | tf_op jit(solution)/shard_map/ppermute | solution.py:427
  49.5 7.0 %collective-permute-start.22 = (bf16[128,128]{1,0:T(8,128)(2,1)S(1)}, bf16[128,128]{1,0:T(8,128)(2,1)S(1)}, u32[]{:S(2)}, u32[]{:S(2)}) collective-permute-start(bf16[128,128]{1,0:T(8,128)(2,1)S(1)} %get-tuple-element.112), channel_id=1, source_target_pairs={{4,8},{8,4},{5,9},{9,5},{6,10},{10,6},{7,11},{11,7},{12,16},{16,12... | collective-permute-start | bytes 98312 | tf_op jit(solution)/shard_map/ppermute | solution.py:427
  49.5 7.7 %collective-permute-start.23 = (bf16[128,128]{1,0:T(8,128)(2,1)S(1)}, bf16[128,128]{1,0:T(8,128)(2,1)S(1)}, u32[]{:S(2)}, u32[]{:S(2)}) collective-permute-start(bf16[128,128]{1,0:T(8,128)(2,1)S(1)} %get-tuple-element.113), channel_id=1, source_target_pairs={{2,4},{4,2},{3,5},{5,3},{6,8},{8,6},{7,9},{9,7},{10,12},{12,10},{1... | collective-permute-start | bytes 98312 | tf_op jit(solution)/shard_map/ppermute | solution.py:427
  53.0 7.0 %collective-permute-start.24 = (bf16[128,128]{1,0:T(8,128)(2,1)S(1)}, bf16[128,128]{1,0:T(8,128)(2,1)S(1)}, u32[]{:S(2)}, u32[]{:S(2)}) collective-permute-start(bf16[128,128]{1,0:T(8,128)(2,1)S(1)} %get-tuple-element.114), channel_id=1, source_target_pairs={{1,2},{2,1},{3,4},{4,3},{5,6},{6,5},{7,8},{8,7},{9,10},{10,9},{11,... | collective-permute-start | bytes 98312 | tf_op jit(solution)/shard_map/ppermute | solution.py:427
  54.6 5.5 %collective-permute-start.25 = (bf16[128,128]{1,0:T(8,128)(2,1)S(1)}, bf16[128,128]{1,0:T(8,128)(2,1)S(1)}, u32[]{:S(2)}, u32[]{:S(2)}) collective-permute-start(bf16[128,128]{1,0:T(8,128)(2,1)S(1)} %get-tuple-element.115), channel_id=1, source_target_pairs={{0,4},{4,0},{1,5},{5,1},{2,6},{6,2},{3,7},{7,3},{8,12},{12,8},{9,1... | collective-permute-start | bytes 98312 | tf_op jit(solution)/shard_map/ppermute | solution.py:427
  54.6 5.5 %collective-permute-start.26 = (bf16[128,128]{1,0:T(8,128)(2,1)S(1)}, bf16[128,128]{1,0:T(8,128)(2,1)S(1)}, u32[]{:S(2)}, u32[]{:S(2)}) collective-permute-start(bf16[128,128]{1,0:T(8,128)(2,1)S(1)} %get-tuple-element.116), channel_id=1, source_target_pairs={{0,2},{2,0},{1,3},{3,1},{4,6},{6,4},{5,7},{7,5},{8,10},{10,8},{9,1... | collective-permute-start | bytes 98312 | tf_op jit(solution)/shard_map/ppermute | solution.py:427
  56.5 3.6 %collective-permute-start.27 = (bf16[128,128]{1,0:T(8,128)(2,1)S(1)}, bf16[128,128]{1,0:T(8,128)(2,1)S(1)}, u32[]{:S(2)}, u32[]{:S(2)}) collective-permute-start(bf16[128,128]{1,0:T(8,128)(2,1)S(1)} %get-tuple-element.117), channel_id=1, source_target_pairs={{0,1},{1,0},{2,3},{3,2},{4,5},{5,4},{6,7},{7,6},{8,9},{9,8},{10,11... | collective-permute-start | bytes 98312 | tf_op jit(solution)/shard_map/ppermute | solution.py:427
  61.2 7.0 %collective-permute-start.28 = (bf16[128,128]{1,0:T(8,128)(2,1)S(1)}, bf16[128,128]{1,0:T(8,128)(2,1)S(1)}, u32[]{:S(2)}, u32[]{:S(2)}) collective-permute-start(bf16[128,128]{1,0:T(8,128)(2,1)S(1)} %get-tuple-element.120), channel_id=1, source_target_pairs={{4,8},{8,4},{5,9},{9,5},{6,10},{10,6},{7,11},{11,7},{12,16},{16,12... | collective-permute-start | bytes 98312 | tf_op jit(solution)/shard_map/ppermute | solution.py:427
  61.3 7.6 %collective-permute-start.29 = (bf16[128,128]{1,0:T(8,128)(2,1)S(1)}, bf16[128,128]{1,0:T(8,128)(2,1)S(1)}, u32[]{:S(2)}, u32[]{:S(2)}) collective-permute-start(bf16[128,128]{1,0:T(8,128)(2,1)S(1)} %get-tuple-element.121), channel_id=1, source_target_pairs={{2,4},{4,2},{3,5},{5,3},{6,8},{8,6},{7,9},{9,7},{10,12},{12,10},{1... | collective-permute-start | bytes 98312 | tf_op jit(solution)/shard_map/ppermute | solution.py:427
  64.8 7.0 %collective-permute-start.30 = (bf16[128,128]{1,0:T(8,128)(2,1)S(1)}, bf16[128,128]{1,0:T(8,128)(2,1)S(1)}, u32[]{:S(2)}, u32[]{:S(2)}) collective-permute-start(bf16[128,128]{1,0:T(8,128)(2,1)S(1)} %get-tuple-element.122), channel_id=1, source_target_pairs={{1,2},{2,1},{3,4},{4,3},{5,6},{6,5},{7,8},{8,7},{9,10},{10,9},{11,... | collective-permute-start | bytes 98312 | tf_op jit(solution)/shard_map/ppermute | solution.py:427
  66.2 5.6 %collective-permute-start.31 = (bf16[128,128]{1,0:T(8,128)(2,1)S(1)}, bf16[128,128]{1,0:T(8,128)(2,1)S(1)}, u32[]{:S(2)}, u32[]{:S(2)}) collective-permute-start(bf16[128,128]{1,0:T(8,128)(2,1)S(1)} %get-tuple-element.123), channel_id=1, source_target_pairs={{0,4},{4,0},{1,5},{5,1},{2,6},{6,2},{3,7},{7,3},{8,12},{12,8},{9,1... | collective-permute-start | bytes 98312 | tf_op jit(solution)/shard_map/ppermute | solution.py:427
  66.2 5.6 %collective-permute-start.32 = (bf16[128,128]{1,0:T(8,128)(2,1)S(1)}, bf16[128,128]{1,0:T(8,128)(2,1)S(1)}, u32[]{:S(2)}, u32[]{:S(2)}) collective-permute-start(bf16[128,128]{1,0:T(8,128)(2,1)S(1)} %get-tuple-element.124), channel_id=1, source_target_pairs={{0,2},{2,0},{1,3},{3,1},{4,6},{6,4},{5,7},{7,5},{8,10},{10,8},{9,1... | collective-permute-start | bytes 98312 | tf_op jit(solution)/shard_map/ppermute | solution.py:427
  68.3 3.6 %collective-permute-start.33 = (bf16[128,128]{1,0:T(8,128)(2,1)S(1)}, bf16[128,128]{1,0:T(8,128)(2,1)S(1)}, u32[]{:S(2)}, u32[]{:S(2)}) collective-permute-start(bf16[128,128]{1,0:T(8,128)(2,1)S(1)} %get-tuple-element.125), channel_id=1, source_target_pairs={{0,1},{1,0},{2,3},{3,2},{4,5},{5,4},{6,7},{7,6},{8,9},{9,8},{10,11... | collective-permute-start | bytes 98312 | tf_op jit(solution)/shard_map/ppermute | solution.py:427
  73.0 7.0 %collective-permute-start.34 = (bf16[128,128]{1,0:T(8,128)(2,1)S(1)}, bf16[128,128]{1,0:T(8,128)(2,1)S(1)}, u32[]{:S(2)}, u32[]{:S(2)}) collective-permute-start(bf16[128,128]{1,0:T(8,128)(2,1)S(1)} %get-tuple-element.128), channel_id=1, source_target_pairs={{4,8},{8,4},{5,9},{9,5},{6,10},{10,6},{7,11},{11,7},{12,16},{16,12... | collective-permute-start | bytes 98312 | tf_op jit(solution)/shard_map/ppermute | solution.py:427
  73.1 7.7 %collective-permute-start.35 = (bf16[128,128]{1,0:T(8,128)(2,1)S(1)}, bf16[128,128]{1,0:T(8,128)(2,1)S(1)}, u32[]{:S(2)}, u32[]{:S(2)}) collective-permute-start(bf16[128,128]{1,0:T(8,128)(2,1)S(1)} %get-tuple-element.129), channel_id=1, source_target_pairs={{2,4},{4,2},{3,5},{5,3},{6,8},{8,6},{7,9},{9,7},{10,12},{12,10},{1... | collective-permute-start | bytes 98312 | tf_op jit(solution)/shard_map/ppermute | solution.py:427
  75.7 6.9 %collective-permute-start.36 = (bf16[128,128]{1,0:T(8,128)(2,1)S(1)}, bf16[128,128]{1,0:T(8,128)(2,1)S(1)}, u32[]{:S(2)}, u32[]{:S(2)}) collective-permute-start(bf16[128,128]{1,0:T(8,128)(2,1)S(1)} %get-tuple-element.130), channel_id=1, source_target_pairs={{1,2},{2,1},{3,4},{4,3},{5,6},{6,5},{7,8},{8,7},{9,10},{10,9},{11,... | collective-permute-start | bytes 98312 | tf_op jit(solution)/shard_map/ppermute | solution.py:427
  78.0 4.7 %collective-permute-start.37 = (bf16[128,128]{1,0:T(8,128)(2,1)S(1)}, bf16[128,128]{1,0:T(8,128)(2,1)S(1)}, u32[]{:S(2)}, u32[]{:S(2)}) collective-permute-start(bf16[128,128]{1,0:T(8,128)(2,1)S(1)} %get-tuple-element.131), channel_id=1, source_target_pairs={{0,4},{4,0},{1,5},{5,1},{2,6},{6,2},{3,7},{7,3},{8,12},{12,8},{9,1... | collective-permute-start | bytes 98312 | tf_op jit(solution)/shard_map/ppermute | solution.py:427
  78.0 4.7 %collective-permute-start.38 = (bf16[128,128]{1,0:T(8,128)(2,1)S(1)}, bf16[128,128]{1,0:T(8,128)(2,1)S(1)}, u32[]{:S(2)}, u32[]{:S(2)}) collective-permute-start(bf16[128,128]{1,0:T(8,128)(2,1)S(1)} %get-tuple-element.132), channel_id=1, source_target_pairs={{0,2},{2,0},{1,3},{3,1},{4,6},{6,4},{5,7},{7,5},{8,10},{10,8},{9,1... | collective-permute-start | bytes 98312 | tf_op jit(solution)/shard_map/ppermute | solution.py:427
  80.0 2.6 %collective-permute-start.39 = (bf16[128,128]{1,0:T(8,128)(2,1)S(1)}, bf16[128,128]{1,0:T(8,128)(2,1)S(1)}, u32[]{:S(2)}, u32[]{:S(2)}) collective-permute-start(bf16[128,128]{1,0:T(8,128)(2,1)S(1)} %get-tuple-element.133), channel_id=1, source_target_pairs={{0,1},{1,0},{2,3},{3,2},{4,5},{5,4},{6,7},{7,6},{8,9},{9,8},{10,11... | collective-permute-start | bytes 98312 | tf_op jit(solution)/shard_map/ppermute | solution.py:427
  84.0 6.7 %collective-permute-start.40 = (bf16[128,128]{1,0:T(8,128)(2,1)S(1)}, bf16[128,128]{1,0:T(8,128)(2,1)S(1)}, u32[]{:S(2)}, u32[]{:S(2)}) collective-permute-start(bf16[128,128]{1,0:T(8,128)(2,1)S(1)} %get-tuple-element.136), channel_id=1, source_target_pairs={{4,8},{8,4},{5,9},{9,5},{6,10},{10,6},{7,11},{11,7},{12,16},{16,12... | collective-permute-start | bytes 98312 | tf_op jit(solution)/shard_map/ppermute | solution.py:427
  84.6 7.5 %collective-permute-start.41 = (bf16[128,128]{1,0:T(8,128)(2,1)S(1)}, bf16[128,128]{1,0:T(8,128)(2,1)S(1)}, u32[]{:S(2)}, u32[]{:S(2)}) collective-permute-start(bf16[128,128]{1,0:T(8,128)(2,1)S(1)} %get-tuple-element.137), channel_id=1, source_target_pairs={{2,4},{4,2},{3,5},{5,3},{6,8},{8,6},{7,9},{9,7},{10,12},{12,10},{1... | collective-permute-start | bytes 98312 | tf_op jit(solution)/shard_map/ppermute | solution.py:427
  87.6 6.9 %collective-permute-start.42 = (bf16[128,128]{1,0:T(8,128)(2,1)S(1)}, bf16[128,128]{1,0:T(8,128)(2,1)S(1)}, u32[]{:S(2)}, u32[]{:S(2)}) collective-permute-start(bf16[128,128]{1,0:T(8,128)(2,1)S(1)} %get-tuple-element.138), channel_id=1, source_target_pairs={{1,2},{2,1},{3,4},{4,3},{5,6},{6,5},{7,8},{8,7},{9,10},{10,9},{11,... | collective-permute-start | bytes 98312 | tf_op jit(solution)/shard_map/ppermute | solution.py:427
  90.0 4.6 %collective-permute-start.43 = (bf16[128,128]{1,0:T(8,128)(2,1)S(1)}, bf16[128,128]{1,0:T(8,128)(2,1)S(1)}, u32[]{:S(2)}, u32[]{:S(2)}) collective-permute-start(bf16[128,128]{1,0:T(8,128)(2,1)S(1)} %get-tuple-element.139), channel_id=1, source_target_pairs={{0,4},{4,0},{1,5},{5,1},{2,6},{6,2},{3,7},{7,3},{8,12},{12,8},{9,1... | collective-permute-start | bytes 98312 | tf_op jit(solution)/shard_map/ppermute | solution.py:427
  90.0 4.6 %collective-permute-start.44 = (bf16[128,128]{1,0:T(8,128)(2,1)S(1)}, bf16[128,128]{1,0:T(8,128)(2,1)S(1)}, u32[]{:S(2)}, u32[]{:S(2)}) collective-permute-start(bf16[128,128]{1,0:T(8,128)(2,1)S(1)} %get-tuple-element.140), channel_id=1, source_target_pairs={{0,2},{2,0},{1,3},{3,1},{4,6},{6,4},{5,7},{7,5},{8,10},{10,8},{9,1... | collective-permute-start | bytes 98312 | tf_op jit(solution)/shard_map/ppermute | solution.py:427
  90.7 3.8 %collective-permute-start.45 = (bf16[128,128]{1,0:T(8,128)(2,1)S(1)}, bf16[128,128]{1,0:T(8,128)(2,1)S(1)}, u32[]{:S(2)}, u32[]{:S(2)}) collective-permute-start(bf16[128,128]{1,0:T(8,128)(2,1)S(1)} %get-tuple-element.141), channel_id=1, source_target_pairs={{0,1},{1,0},{2,3},{3,2},{4,5},{5,4},{6,7},{7,6},{8,9},{9,8},{10,11... | collective-permute-start | bytes 98312 | tf_op jit(solution)/shard_map/ppermute | solution.py:427
  95.7 7.0 %collective-permute-start.46 = (bf16[128,128]{1,0:T(8,128)(2,1)S(1)}, bf16[128,128]{1,0:T(8,128)(2,1)S(1)}, u32[]{:S(2)}, u32[]{:S(2)}) collective-permute-start(bf16[128,128]{1,0:T(8,128)(2,1)S(1)} %get-tuple-element.144), channel_id=1, source_target_pairs={{4,8},{8,4},{5,9},{9,5},{6,10},{10,6},{7,11},{11,7},{12,16},{16,12... | collective-permute-start | bytes 98312 | tf_op jit(solution)/shard_map/ppermute | solution.py:427
  95.8 7.6 %collective-permute-start.47 = (bf16[128,128]{1,0:T(8,128)(2,1)S(1)}, bf16[128,128]{1,0:T(8,128)(2,1)S(1)}, u32[]{:S(2)}, u32[]{:S(2)}) collective-permute-start(bf16[128,128]{1,0:T(8,128)(2,1)S(1)} %get-tuple-element.145), channel_id=1, source_target_pairs={{2,4},{4,2},{3,5},{5,3},{6,8},{8,6},{7,9},{9,7},{10,12},{12,10},{1... | collective-permute-start | bytes 98312 | tf_op jit(solution)/shard_map/ppermute | solution.py:427
  99.3 7.0 %collective-permute-start.48 = (bf16[128,128]{1,0:T(8,128)(2,1)S(1)}, bf16[128,128]{1,0:T(8,128)(2,1)S(1)}, u32[]{:S(2)}, u32[]{:S(2)}) collective-permute-start(bf16[128,128]{1,0:T(8,128)(2,1)S(1)} %get-tuple-element.146), channel_id=1, source_target_pairs={{1,2},{2,1},{3,4},{4,3},{5,6},{6,5},{7,8},{8,7},{9,10},{10,9},{11,... | collective-permute-start | bytes 98312 | tf_op jit(solution)/shard_map/ppermute | solution.py:427
  100.8 5.4 %collective-permute-start.49 = (bf16[128,128]{1,0:T(8,128)(2,1)S(1)}, bf16[128,128]{1,0:T(8,128)(2,1)S(1)}, u32[]{:S(2)}, u32[]{:S(2)}) collective-permute-start(bf16[128,128]{1,0:T(8,128)(2,1)S(1)} %get-tuple-element.147), channel_id=1, source_target_pairs={{0,4},{4,0},{1,5},{5,1},{2,6},{6,2},{3,7},{7,3},{8,12},{12,8},{9,1... | collective-permute-start | bytes 98312 | tf_op jit(solution)/shard_map/ppermute | solution.py:427
  100.8 5.4 %collective-permute-start.50 = (bf16[128,128]{1,0:T(8,128)(2,1)S(1)}, bf16[128,128]{1,0:T(8,128)(2,1)S(1)}, u32[]{:S(2)}, u32[]{:S(2)}) collective-permute-start(bf16[128,128]{1,0:T(8,128)(2,1)S(1)} %get-tuple-element.148), channel_id=1, source_target_pairs={{0,2},{2,0},{1,3},{3,1},{4,6},{6,4},{5,7},{7,5},{8,10},{10,8},{9,1... | collective-permute-start | bytes 98312 | tf_op jit(solution)/shard_map/ppermute | solution.py:427
  102.7 3.5 %collective-permute-start.51 = (bf16[128,128]{1,0:T(8,128)(2,1)S(1)}, bf16[128,128]{1,0:T(8,128)(2,1)S(1)}, u32[]{:S(2)}, u32[]{:S(2)}) collective-permute-start(bf16[128,128]{1,0:T(8,128)(2,1)S(1)} %get-tuple-element.149), channel_id=1, source_target_pairs={{0,1},{1,0},{2,3},{3,2},{4,5},{5,4},{6,7},{7,6},{8,9},{9,8},{10,11... | collective-permute-start | bytes 98312 | tf_op jit(solution)/shard_map/ppermute | solution.py:427
  108.0 1.3 collective-permute-start.52
  109.3 4.9 %collective-permute-start.55 = (f32[64,128]{1,0:T(8,128)S(1)}, f32[64,128]{1,0:T(8,128)S(1)}, u32[]{:S(2)}, u32[]{:S(2)}) collective-permute-start(f32[64,128]{1,0:T(8,128)S(1)} %add.25), channel_id=1, source_target_pairs={{0,6},{1,7},{2,4},{3,5},{4,2},{5,3},{6,0},{7,1},{8,14},{9,15},{10,... | collective-permute-start | bytes 98312 | tf_op jit(solution)/shard_map/ppermute | solution.py:410
  109.3 4.9 %collective-permute-start.54 = (f32[64,128]{1,0:T(8,128)S(1)}, f32[64,128]{1,0:T(8,128)S(1)}, u32[]{:S(2)}, u32[]{:S(2)}) collective-permute-start(f32[64,128]{1,0:T(8,128)S(1)} %add.25), channel_id=1, source_target_pairs={{0,4},{1,5},{2,6},{3,7},{4,0},{5,1},{6,2},{7,3},{8,12},{9,13},{10,... | collective-permute-start | bytes 98312 | tf_op jit(solution)/shard_map/ppermute | solution.py:410
  110.2 4.4 %collective-permute-start.53 = (f32[64,128]{1,0:T(8,128)S(1)}, f32[64,128]{1,0:T(8,128)S(1)}, u32[]{:S(2)}, u32[]{:S(2)}) collective-permute-start(f32[64,128]{1,0:T(8,128)S(1)} %add.25), channel_id=1, source_target_pairs={{0,2},{1,3},{2,0},{3,1},{4,6},{5,7},{6,4},{7,5},{8,10},{9,11},{10,... | collective-permute-start | bytes 98312 | tf_op jit(solution)/shard_map/ppermute | solution.py:410
  114.7 6.0 %collective-permute-start.58 = (f32[64,128]{1,0:T(8,128)S(1)}, f32[64,128]{1,0:T(8,128)S(1)}, u32[]{:S(2)}, u32[]{:S(2)}) collective-permute-start(f32[64,128]{1,0:T(8,128)S(1)} %add_add_fusion.1), channel_id=1, source_target_pairs={{0,24},{1,25},{2,26},{3,27},{4,28},{5,29},{6,30},{7,31},{8,16},{9,... | collective-permute-start | bytes 98312 | tf_op jit(solution)/shard_map/ppermute | solution.py:410
  116.8 4.8 %collective-permute-start.57 = (f32[64,128]{1,0:T(8,128)S(1)}, f32[64,128]{1,0:T(8,128)S(1)}, u32[]{:S(2)}, u32[]{:S(2)}) collective-permute-start(f32[64,128]{1,0:T(8,128)S(1)} %add_add_fusion.1), channel_id=1, source_target_pairs={{0,16},{1,17},{2,18},{3,19},{4,20},{5,21},{6,22},{7,23},{8,24},{9,... | collective-permute-start | bytes 98312 | tf_op jit(solution)/shard_map/ppermute | solution.py:410
  116.8 4.8 %collective-permute-start.56 = (f32[64,128]{1,0:T(8,128)S(1)}, f32[64,128]{1,0:T(8,128)S(1)}, u32[]{:S(2)}, u32[]{:S(2)}) collective-permute-start(f32[64,128]{1,0:T(8,128)S(1)} %add_add_fusion.1), channel_id=1, source_target_pairs={{0,8},{1,9},{2,10},{3,11},{4,12},{5,13},{6,14},{7,15},{8,0},{9,1},... | collective-permute-start | bytes 98312 | tf_op jit(solution)/shard_map/ppermute | solution.py:410
  121.6 1.3 collective-permute-start.59

commit v5 on v4

--- a/solution.py
+++ b/solution.py
@@ -218,8 +218,40 @@
     )(place, field, *wanted)
 
 
-def advance(place_ref, band_ref, hot_ref, coef_ref, field_ref, prev_ref, got, scale, store):
+def inner_kernel(scale, *refs):
+    band_ref, field_ref, *prev_refs, part_ref = refs
     rows = field_ref.shape[0]
+    count = rows // BLK
+    for b in range(count):
+        block = pl.ds(b * BLK, BLK)
+        first, past = max(b - 1, 0), min(b + 2, count)
+        value = scale * dot(
+            band_ref[block, (first - b + 1) * BLK : (past - b + 1) * BLK],
+            field_ref[first * BLK : past * BLK, :],
+            ((1,), (0,)),
+        )
+        for prev_ref in prev_refs:
+            value = value - prev_ref[block, :].astype(F32)
+        part_ref[block, :] = value
+
+
+def inner(scale, band, field, *prev):
+    rows = field.shape[0]
+    return pl.pallas_call(
+        lambda *refs: inner_kernel(scale, *refs),
+        out_shape=jax.ShapeDtypeStruct((rows, VECS), F32),
+        in_specs=[VMEM] * (2 + len(prev)),
+        out_specs=VMEM,
+        compiler_params=PARAMS,
+        cost_estimate=pl.CostEstimate(
+            flops=2 * rows * 3 * BLK * VECS, bytes_accessed=4 * rows * 3 * BLK, transcendentals=0
+        ),
+        name="inner",
+    )(band, field, *prev)
+
+
+def advance(place_ref, band_ref, hot_ref, coef_ref, part_ref, got, scale, store):
+    rows = part_ref.shape[0]
     count = rows // BLK
     even = is_low(place_ref, 1)
     got = dict(zip(LINKS, got, strict=True))
@@ -236,72 +268,55 @@
         total = both[:, :VECS] + both[:, VECS:]
         if b == 0:
             total += dot(band_ref[block, :BLK], low, ((1,), (0,)))
-            total += dot(band_ref[block, BLK:], field_ref[: 2 * BLK, :], ((1,), (0,)))
-        elif b == count - 1:
-            total += dot(
-                band_ref[block, : 2 * BLK], field_ref[rows - 2 * BLK :, :], ((1,), (0,))
-            )
+        if b == count - 1:
             total += dot(band_ref[block, 2 * BLK :], high, ((1,), (0,)))
-        else:
-            total += dot(
-                band_ref[block, :], field_ref[pl.ds((b - 1) * BLK, 3 * BLK), :], ((1,), (0,))
-            )
-        value = total * scale
-        if prev_ref is not None:
-            value = value - prev_ref[block, :].astype(F32)
-        store(block, value)
+        store(block, part_ref[block, :] + total * scale)
     return even
 
 
-def step_kernel(scale, has_prev, has_next, *refs):
-    place_ref, band_ref, hot_ref, coef_ref, pick_mat_ref, field_ref = refs[:6]
-    refs = refs[6:]
-    prev_ref = None
-    if has_prev:
-        prev_ref, refs = refs[0], refs[1:]
-    got, refs = refs[:6], refs[6:]
+def step_kernel(scale, *refs):
+    place_ref, band_ref, hot_ref, coef_ref, pick_mat_ref, part_ref = refs[:6]
+    got, refs = refs[6:12], refs[12:]
     packed_ref, sent, next_refs = refs[0], refs[1:7], refs[7:]
 
     def store(block, value):
-        if has_next:
-            next_refs[0][block, :] = value
+        for next_ref in next_refs:
+            next_ref[block, :] = value
         packed_ref[block, :] = value.astype(BF16)
 
     even = advance(
-        place_ref, band_ref, hot_ref, coef_ref, field_ref, prev_ref, got, scale, store
-    )
-    rows = field_ref.shape[0]
+        place_ref, band_ref, hot_ref, coef_ref, part_ref, got, scale, store
+    )
+    rows = part_ref.shape[0]
     picked = dot(pick_mat_ref[...], packed_ref[...], ((1,), (0,)))
     send_out(even, packed_ref[:BLK, :], packed_ref[rows - BLK :, :], picked, sent)
 
 
-def step(scale, place, mats, field, prev, got, has_next=True):
-    rows = field.shape[0]
-    has_prev = prev is not None
-    before = (prev,) if has_prev else ()
-    return pl.pallas_call(
-        lambda *refs: step_kernel(scale, has_prev, has_next, *refs),
+def step(scale, place, mats, part, got, has_next=True):
+    rows = part.shape[0]
+    return pl.pallas_call(
+        lambda *refs: step_kernel(scale, *refs),
         out_shape=(
             jax.ShapeDtypeStruct((rows, VECS), BF16),
             *SENT,
             *(jax.ShapeDtypeStruct((rows, VECS), F32),) * has_next,
         ),
-        in_specs=[SMEM] + [VMEM] * (11 + len(before)),
+        in_specs=[SMEM] + [VMEM] * 11,
         out_specs=(VMEM,) * (7 + has_next),
         compiler_params=PARAMS,
         name="step",
-    )(place, *mats, field, *before, *got)
+    )(place, *mats, part, *got)
 
 
 def last_kernel(scale, *refs):
-    place_ref, band_ref, hot_ref, coef_ref, field_ref, prev_ref = refs[:6]
-    got, (next_ref, kept_ref, sent_ref) = refs[6:12], refs[12:]
+    place_ref, band_ref, hot_ref, coef_ref, part_ref = refs[:5]
+    got, (next_ref, kept_ref, sent_ref) = refs[5:11], refs[11:]
 
     def store(block, value):
         next_ref[block, :] = value
 
     advance(
-        place_ref, band_ref, hot_ref, coef_ref, field_ref, prev_ref, got, scale, store
+        place_ref, band_ref, hot_ref, coef_ref, part_ref, got, scale, store
     )
     value = next_ref[...]
     gram = dot(value, value, ((0,), (0,)), lax.Precision.HIGHEST)
@@ -311,19 +326,19 @@
     sent_ref[...] = jnp.where(low, gram[half:], gram[:half])
 
 
-def last(scale, place, mats, field, prev, got):
-    rows = field.shape[0]
+def last(scale, place, mats, part, got):
+    rows = part.shape[0]
     return pl.pallas_call(
         lambda *refs: last_kernel(scale, *refs),
         out_shape=(
             jax.ShapeDtypeStruct((rows, VECS), F32),
             *(jax.ShapeDtypeStruct((VECS // 2, VECS), F32),) * 2,
         ),
-        in_specs=[SMEM] + [VMEM] * 11,
+        in_specs=[SMEM] + [VMEM] * 10,
         out_specs=(VMEM,) * 3,
         compiler_params=PARAMS,
         name="last",
-    )(place, *mats, field, prev, *got)
+    )(place, *mats, part, *got)
 
 
 def total_of(terms):
@@ -451,19 +466,20 @@
     def exchange(sent):
         return [swap(v, *link) for v, link in zip(sent, LINKS, strict=True)]
 
-    previous, packed = field, field
     mats = (band, hot, coef, pick_mat)
-    got = exchange(sent)
-    packed, *sent, current = step(1.0 / HALF_WIDTH, here, mats, packed, None, got)
-    for _ in range(DEGREE - 3):
+    previous, packed = (), field
+    for k in range(DEGREE):
+        scale = (2.0 if k else 1.0) / HALF_WIDTH
         got = exchange(sent)
-        packed, *sent, following = step(2.0 / HALF_WIDTH, here, mats, packed, previous, got)
-        previous, current = current, following
-    got = exchange(sent)
-    packed, *sent = step(2.0 / HALF_WIDTH, here, mats, packed, previous, got, has_next=False)
-    previous = current
-    got = exchange(sent)
-    filtered, kept, sent = last(2.0 / HALF_WIDTH, here, mats[:3], packed, previous, got)
+        part = inner(scale, band, packed, *previous)
+        if k == DEGREE - 1:
+            filtered, kept, sent = last(scale, here, mats[:3], part, got)
+        else:
+            previous = (current,) if k else (field,)
+            has_next = k < DEGREE - 2
+            packed, *sent = step(scale, here, mats, part, got, has_next)
+            if has_next:
+                current = sent.pop()
     return finish(math.sqrt(total_rows), here, summed(kept, sent, count), filtered)
 
 

time: 130 us -> 127 us (0.977)
  waiting for transfers between devices: 45.6 us -> 41 us
  Pallas kernels: 20.8 us -> 22.2 us
    ppermute x52, waiting for transfers between devices: 38.9 us -> 34.2 us  [swap(): return lax.ppermute(value, AXES, swap_pairs(count, by, odd))]
    pallas_call x7 -> x15, Pallas kernels: 8.24 us -> 9.88 us  [the longest x7 5.27 us: step(): pl.pallas_call(lambda *refs: step_kernel(scale, *refs), out_shape=(jax.Sh...]
  transfers between devices with their start and end apart: 60 -> 60, of which waited for: 32 -> 31; matrix products, arithmetic and copies ran while one was open for 0% -> 0% of each run, Pallas kernels for 2% -> 6%
where the time goes in v5:
time: 127 us
  starting transfers between devices  63.3 us (50%)
  waiting for transfers between devices  41 us (32%)
  Pallas kernels  22.2 us (17%)
    ppermute x52, starting transfers between devices, swap(): return lax.ppermute(value, AXES, swap_pairs(count, by, odd))  55.3 us
    ppermute x52, waiting for transfers between devices, swap(): return lax.ppermute(value, AXES, swap_pairs(count, by, odd))  34.2 us
    ppermute x8, starting transfers between devices, swapped(): return lax.ppermute(value, AXES, [(i, i ^ mask) for i in range(count)])  8.08 us
    pallas_call x1, Pallas kernels, finish(): pl.pallas_call(lambda *refs: finish_kernel(scale, *refs), out_shape=jax.S...  7.14 us
    ppermute x8, waiting for transfers between devices, swapped(): return lax.ppermute(value, AXES, [(i, i ^ mask) for i in range(count)])  6.73 us
    pallas_call x7, Pallas kernels, step(): pl.pallas_call(lambda *refs: step_kernel(scale, *refs), out_shape=(jax.Sh...  5.27 us
    pallas_call x8, Pallas kernels, inner(): pl.pallas_call(lambda *refs: inner_kernel(scale, *refs), out_shape=jax.Sh...  4.6 us
    pallas_call x1, Pallas kernels, prepare(): pl.pallas_call(prepare_kernel, out_shape=(jax.ShapeDtypeStruct((rows, 3 *...  3.08 us
  transfers between devices with their start and end apart: 60, of which 31 were waited for; matrix products, arithmetic and copies ran while one was open for 0% of the time, Pallas kernels for 6%

profile of v5, /device:TPU:0, one launch (start us, length us, event | category | flops | bytes accessed | tf_op | source)
XLA Modules:
  0.0 126.8 jit_solution(13108041341312088395)
XLA Ops:
  0.0 6.0 %collective-permute-start.3 = (s32[1,256]{1,0:T(1,128)}, s32[1,256]{1,0:T(1,128)S(1)}, u32[]{:S(2)}, u32[]{:S(2)}) collective-permute-start(s32[1,256]{1,0:T(1,128)} %bitcast.10), channel_id=1, source_target_pairs={{4,8},{8,4},{5,9},{9,5},{6,10},{10,6},{7,11},{11,7},{12,16},{16,12... | collective-permute-start | bytes 3080 | tf_op jit(solution)/shard_map/ppermute | solution.py:442
  6.0 2.8 %collective-permute-start.1 = (s32[1,256]{1,0:T(1,128)}, s32[1,256]{1,0:T(1,128)S(1)}, u32[]{:S(2)}, u32[]{:S(2)}) collective-permute-start(s32[1,256]{1,0:T(1,128)} %bitcast.12), channel_id=1, source_target_pairs={{2,4},{4,2},{3,5},{5,3},{6,8},{8,6},{7,9},{9,7},{10,12},{12,10},{1... | collective-permute-start | bytes 3080 | tf_op jit(solution)/shard_map/ppermute | solution.py:442
  8.8 0.6 collective-permute-start
  9.5 3.1 %prepare.1 = (bf16[2048,384]{1,0:T(8,128)(2,1)S(1)}, bf16[2048,256]{1,0:T(8,128)(2,1)S(1)}, f32[256,128]{1,0:T(8,128)S(1)}, bf16[2048,128]{1,0:T(8,128)(2,1)S(1)}) custom-call(s32[1]{0:T(128)} %bitcast.place_ref.refs_0_, s32[1,256]{1,0:T(1,128)} %bitcast.8, f32[1,256]{1,0:T(1,128)} %bitcast.9, f32[3,8,2048]{2,1,0:T(8,128)} %bitcast.6, ...), custom_call_target="tpu_custom_call" | custom-call | tf_op jit(solution)/shard_map/prepare/pallas_call | solution.py:153
  12.6 0.8 collective-permute-done.1.w1
  13.4 0.6 first.1
  14.0 2.0 %collective-permute-start.4 = (bf16[128,128]{1,0:T(8,128)(2,1)S(1)}, bf16[128,128]{1,0:T(8,128)(2,1)S(1)}, u32[]{:S(2)}, u32[]{:S(2)}) collective-permute-start(bf16[128,128]{1,0:T(8,128)(2,1)S(1)} %get-tuple-element.89), channel_id=1, source_target_pairs={{4,8},{8,4},{5,9},{9,5},{6,10},{10,6},{7,11},{11,7},{12,16},{16,12... | collective-permute-start | bytes 98312 | tf_op jit(solution)/shard_map/ppermute | solution.py:442
  16.0 2.8 %collective-permute-start.5 = (bf16[128,128]{1,0:T(8,128)(2,1)S(1)}, bf16[128,128]{1,0:T(8,128)(2,1)S(1)}, u32[]{:S(2)}, u32[]{:S(2)}) collective-permute-start(bf16[128,128]{1,0:T(8,128)(2,1)S(1)} %get-tuple-element.90), channel_id=1, source_target_pairs={{2,4},{4,2},{3,5},{5,3},{6,8},{8,6},{7,9},{9,7},{10,12},{12,10},{1... | collective-permute-start | bytes 98312 | tf_op jit(solution)/shard_map/ppermute | solution.py:442
  18.8 0.8 collective-permute-start.6
  19.7 1.0 collective-permute-done.4.refs_6_
  21.7 1.9 %collective-permute-done.5.refs_7_ = bf16[128,128]{1,0:T(8,128)(2,1)S(1)} collective-permute-done((bf16[128,128]{1,0:T(8,128)(2,1)S(1)}, bf16[128,128]{1,0:T(8,128)(2,1)S(1)}, u32[]{:S(2)}, u32[]{:S(2)}) %collective-permute-start.5) | collective-permute-done | bytes 32800 | tf_op jit(solution)/shard_map/ppermute | solution.py:442
  23.5 2.2 %collective-permute-done.6.refs_8_ = bf16[128,128]{1,0:T(8,128)(2,1)S(1)} collective-permute-done((bf16[128,128]{1,0:T(8,128)(2,1)S(1)}, bf16[128,128]{1,0:T(8,128)(2,1)S(1)}, u32[]{:S(2)}, u32[]{:S(2)}) %collective-permute-start.6) | collective-permute-done | bytes 32800 | tf_op jit(solution)/shard_map/ppermute | solution.py:442
  25.8 0.7 step.7
  26.6 1.9 %collective-permute-start.11 = (bf16[128,128]{1,0:T(8,128)(2,1)S(1)}, bf16[128,128]{1,0:T(8,128)(2,1)S(1)}, u32[]{:S(2)}, u32[]{:S(2)}) collective-permute-start(bf16[128,128]{1,0:T(8,128)(2,1)S(1)} %get-tuple-element.97), channel_id=1, source_target_pairs={{2,4},{4,2},{3,5},{5,3},{6,8},{8,6},{7,9},{9,7},{10,12},{12,10},{1... | collective-permute-start | bytes 98312 | tf_op jit(solution)/shard_map/ppermute | solution.py:442
  28.6 3.1 %collective-permute-start.12 = (bf16[128,128]{1,0:T(8,128)(2,1)S(1)}, bf16[128,128]{1,0:T(8,128)(2,1)S(1)}, u32[]{:S(2)}, u32[]{:S(2)}) collective-permute-start(bf16[128,128]{1,0:T(8,128)(2,1)S(1)} %get-tuple-element.98), channel_id=1, source_target_pairs={{1,2},{2,1},{3,4},{4,3},{5,6},{6,5},{7,8},{8,7},{9,10},{10,9},{11,... | collective-permute-start | bytes 98312 | tf_op jit(solution)/shard_map/ppermute | solution.py:442
  31.7 1.9 %collective-permute-done.10.refs_6_ = bf16[128,128]{1,0:T(8,128)(2,1)S(1)} collective-permute-done((bf16[128,128]{1,0:T(8,128)(2,1)S(1)}, bf16[128,128]{1,0:T(8,128)(2,1)S(1)}, u32[]{:S(2)}, u32[]{:S(2)}) %collective-permute-start.10) | collective-permute-done | bytes 32800 | tf_op jit(solution)/shard_map/ppermute | solution.py:442
  34.2 1.3 %collective-permute-done.12.refs_8_ = bf16[128,128]{1,0:T(8,128)(2,1)S(1)} collective-permute-done((bf16[128,128]{1,0:T(8,128)(2,1)S(1)}, bf16[128,128]{1,0:T(8,128)(2,1)S(1)}, u32[]{:S(2)}, u32[]{:S(2)}) %collective-permute-start.12) | collective-permute-done | bytes 32800 | tf_op jit(solution)/shard_map/ppermute | solution.py:442
  35.8 0.7 step.8
  36.6 0.9 collective-permute-start.16
  37.5 3.0 %collective-permute-start.17 = (bf16[128,128]{1,0:T(8,128)(2,1)S(1)}, bf16[128,128]{1,0:T(8,128)(2,1)S(1)}, u32[]{:S(2)}, u32[]{:S(2)}) collective-permute-start(bf16[128,128]{1,0:T(8,128)(2,1)S(1)} %get-tuple-element.105), channel_id=1, source_target_pairs={{2,4},{4,2},{3,5},{5,3},{6,8},{8,6},{7,9},{9,7},{10,12},{12,10},{1... | collective-permute-start | bytes 98312 | tf_op jit(solution)/shard_map/ppermute | solution.py:442
  40.5 2.4 %collective-permute-start.18 = (bf16[128,128]{1,0:T(8,128)(2,1)S(1)}, bf16[128,128]{1,0:T(8,128)(2,1)S(1)}, u32[]{:S(2)}, u32[]{:S(2)}) collective-permute-start(bf16[128,128]{1,0:T(8,128)(2,1)S(1)} %get-tuple-element.106), channel_id=1, source_target_pairs={{1,2},{2,1},{3,4},{4,3},{5,6},{6,5},{7,8},{8,7},{9,10},{10,9},{11,... | collective-permute-start | bytes 98312 | tf_op jit(solution)/shard_map/ppermute | solution.py:442
  43.8 1.2 collective-permute-done.17.refs_7_
  45.0 2.4 %collective-permute-done.18.refs_8_ = bf16[128,128]{1,0:T(8,128)(2,1)S(1)} collective-permute-done((bf16[128,128]{1,0:T(8,128)(2,1)S(1)}, bf16[128,128]{1,0:T(8,128)(2,1)S(1)}, u32[]{:S(2)}, u32[]{:S(2)}) %collective-permute-start.18) | collective-permute-done | bytes 32800 | tf_op jit(solution)/shard_map/ppermute | solution.py:442
  47.5 0.8 step.9
  48.3 3.5 %collective-permute-start.23 = (bf16[128,128]{1,0:T(8,128)(2,1)S(1)}, bf16[128,128]{1,0:T(8,128)(2,1)S(1)}, u32[]{:S(2)}, u32[]{:S(2)}) collective-permute-start(bf16[128,128]{1,0:T(8,128)(2,1)S(1)} %get-tuple-element.113), channel_id=1, source_target_pairs={{2,4},{4,2},{3,5},{5,3},{6,8},{8,6},{7,9},{9,7},{10,12},{12,10},{1... | collective-permute-start | bytes 98312 | tf_op jit(solution)/shard_map/ppermute | solution.py:442
  51.8 1.6 %collective-permute-start.24 = (bf16[128,128]{1,0:T(8,128)(2,1)S(1)}, bf16[128,128]{1,0:T(8,128)(2,1)S(1)}, u32[]{:S(2)}, u32[]{:S(2)}) collective-permute-start(bf16[128,128]{1,0:T(8,128)(2,1)S(1)} %get-tuple-element.114), channel_id=1, source_target_pairs={{1,2},{2,1},{3,4},{4,3},{5,6},{6,5},{7,8},{8,7},{9,10},{10,9},{11,... | collective-permute-start | bytes 98312 | tf_op jit(solution)/shard_map/ppermute | solution.py:442
  53.4 0.9 collective-permute-start.26
  54.3 1.0 collective-permute-done.22.refs_6_
  56.0 2.9 %collective-permute-done.24.refs_8_ = bf16[128,128]{1,0:T(8,128)(2,1)S(1)} collective-permute-done((bf16[128,128]{1,0:T(8,128)(2,1)S(1)}, bf16[128,128]{1,0:T(8,128)(2,1)S(1)}, u32[]{:S(2)}, u32[]{:S(2)}) %collective-permute-start.24) | collective-permute-done | bytes 32800 | tf_op jit(solution)/shard_map/ppermute | solution.py:442
  58.9 0.8 step.10
  59.7 3.5 %collective-permute-start.29 = (bf16[128,128]{1,0:T(8,128)(2,1)S(1)}, bf16[128,128]{1,0:T(8,128)(2,1)S(1)}, u32[]{:S(2)}, u32[]{:S(2)}) collective-permute-start(bf16[128,128]{1,0:T(8,128)(2,1)S(1)} %get-tuple-element.121), channel_id=1, source_target_pairs={{2,4},{4,2},{3,5},{5,3},{6,8},{8,6},{7,9},{9,7},{10,12},{12,10},{1... | collective-permute-start | bytes 98312 | tf_op jit(solution)/shard_map/ppermute | solution.py:442
  63.2 1.5 %collective-permute-start.30 = (bf16[128,128]{1,0:T(8,128)(2,1)S(1)}, bf16[128,128]{1,0:T(8,128)(2,1)S(1)}, u32[]{:S(2)}, u32[]{:S(2)}) collective-permute-start(bf16[128,128]{1,0:T(8,128)(2,1)S(1)} %get-tuple-element.122), channel_id=1, source_target_pairs={{1,2},{2,1},{3,4},{4,3},{5,6},{6,5},{7,8},{8,7},{9,10},{10,9},{11,... | collective-permute-start | bytes 98312 | tf_op jit(solution)/shard_map/ppermute | solution.py:442
  64.9 1.8 %collective-permute-done.28.refs_6_ = bf16[128,128]{1,0:T(8,128)(2,1)S(1)} collective-permute-done((bf16[128,128]{1,0:T(8,128)(2,1)S(1)}, bf16[128,128]{1,0:T(8,128)(2,1)S(1)}, u32[]{:S(2)}, u32[]{:S(2)}) %collective-permute-start.28) | collective-permute-done | bytes 32800 | tf_op jit(solution)/shard_map/ppermute | solution.py:442
  66.7 0.6 inner.12.refs_5_
  67.3 2.9 %collective-permute-done.30.refs_8_ = bf16[128,128]{1,0:T(8,128)(2,1)S(1)} collective-permute-done((bf16[128,128]{1,0:T(8,128)(2,1)S(1)}, bf16[128,128]{1,0:T(8,128)(2,1)S(1)}, u32[]{:S(2)}, u32[]{:S(2)}) %collective-permute-start.30) | collective-permute-done | bytes 32800 | tf_op jit(solution)/shard_map/ppermute | solution.py:442
  70.3 0.8 step.11
  71.1 2.7 %collective-permute-start.35 = (bf16[128,128]{1,0:T(8,128)(2,1)S(1)}, bf16[128,128]{1,0:T(8,128)(2,1)S(1)}, u32[]{:S(2)}, u32[]{:S(2)}) collective-permute-start(bf16[128,128]{1,0:T(8,128)(2,1)S(1)} %get-tuple-element.129), channel_id=1, source_target_pairs={{2,4},{4,2},{3,5},{5,3},{6,8},{8,6},{7,9},{9,7},{10,12},{12,10},{1... | collective-permute-start | bytes 98312 | tf_op jit(solution)/shard_map/ppermute | solution.py:442
  73.8 2.2 %collective-permute-start.36 = (bf16[128,128]{1,0:T(8,128)(2,1)S(1)}, bf16[128,128]{1,0:T(8,128)(2,1)S(1)}, u32[]{:S(2)}, u32[]{:S(2)}) collective-permute-start(bf16[128,128]{1,0:T(8,128)(2,1)S(1)} %get-tuple-element.130), channel_id=1, source_target_pairs={{1,2},{2,1},{3,4},{4,3},{5,6},{6,5},{7,8},{8,7},{9,10},{10,9},{11,... | collective-permute-start | bytes 98312 | tf_op jit(solution)/shard_map/ppermute | solution.py:442
  76.2 1.9 %collective-permute-done.34.refs_6_ = bf16[128,128]{1,0:T(8,128)(2,1)S(1)} collective-permute-done((bf16[128,128]{1,0:T(8,128)(2,1)S(1)}, bf16[128,128]{1,0:T(8,128)(2,1)S(1)}, u32[]{:S(2)}, u32[]{:S(2)}) %collective-permute-start.34) | collective-permute-done | bytes 32800 | tf_op jit(solution)/shard_map/ppermute | solution.py:442
  78.1 0.8 inner.13.refs_5_
  78.9 1.9 %collective-permute-done.36.refs_8_ = bf16[128,128]{1,0:T(8,128)(2,1)S(1)} collective-permute-done((bf16[128,128]{1,0:T(8,128)(2,1)S(1)}, bf16[128,128]{1,0:T(8,128)(2,1)S(1)}, u32[]{:S(2)}, u32[]{:S(2)}) %collective-permute-start.36) | collective-permute-done | bytes 32800 | tf_op jit(solution)/shard_map/ppermute | solution.py:442
  80.7 0.8 step.12
  82.0 3.0 %collective-permute-start.41 = (bf16[128,128]{1,0:T(8,128)(2,1)S(1)}, bf16[128,128]{1,0:T(8,128)(2,1)S(1)}, u32[]{:S(2)}, u32[]{:S(2)}) collective-permute-start(bf16[128,128]{1,0:T(8,128)(2,1)S(1)} %get-tuple-element.137), channel_id=1, source_target_pairs={{2,4},{4,2},{3,5},{5,3},{6,8},{8,6},{7,9},{9,7},{10,12},{12,10},{1... | collective-permute-start | bytes 98312 | tf_op jit(solution)/shard_map/ppermute | solution.py:442
  85.1 2.3 %collective-permute-start.42 = (bf16[128,128]{1,0:T(8,128)(2,1)S(1)}, bf16[128,128]{1,0:T(8,128)(2,1)S(1)}, u32[]{:S(2)}, u32[]{:S(2)}) collective-permute-start(bf16[128,128]{1,0:T(8,128)(2,1)S(1)} %get-tuple-element.138), channel_id=1, source_target_pairs={{1,2},{2,1},{3,4},{4,3},{5,6},{6,5},{7,8},{8,7},{9,10},{10,9},{11,... | collective-permute-start | bytes 98312 | tf_op jit(solution)/shard_map/ppermute | solution.py:442
  87.4 0.8 collective-permute-done.40.refs_6_
  88.7 0.8 collective-permute-done.41.refs_7_
  89.6 2.4 %collective-permute-done.42.refs_8_ = bf16[128,128]{1,0:T(8,128)(2,1)S(1)} collective-permute-done((bf16[128,128]{1,0:T(8,128)(2,1)S(1)}, bf16[128,128]{1,0:T(8,128)(2,1)S(1)}, u32[]{:S(2)}, u32[]{:S(2)}) %collective-permute-start.42) | collective-permute-done | bytes 32800 | tf_op jit(solution)/shard_map/ppermute | solution.py:442
  92.0 0.7 step.13
  92.9 3.5 %collective-permute-start.47 = (bf16[128,128]{1,0:T(8,128)(2,1)S(1)}, bf16[128,128]{1,0:T(8,128)(2,1)S(1)}, u32[]{:S(2)}, u32[]{:S(2)}) collective-permute-start(bf16[128,128]{1,0:T(8,128)(2,1)S(1)} %get-tuple-element.145), channel_id=1, source_target_pairs={{2,4},{4,2},{3,5},{5,3},{6,8},{8,6},{7,9},{9,7},{10,12},{12,10},{1... | collective-permute-start | bytes 98312 | tf_op jit(solution)/shard_map/ppermute | solution.py:442
  96.3 1.6 %collective-permute-start.48 = (bf16[128,128]{1,0:T(8,128)(2,1)S(1)}, bf16[128,128]{1,0:T(8,128)(2,1)S(1)}, u32[]{:S(2)}, u32[]{:S(2)}) collective-permute-start(bf16[128,128]{1,0:T(8,128)(2,1)S(1)} %get-tuple-element.146), channel_id=1, source_target_pairs={{1,2},{2,1},{3,4},{4,3},{5,6},{6,5},{7,8},{8,7},{9,10},{10,9},{11,... | collective-permute-start | bytes 98312 | tf_op jit(solution)/shard_map/ppermute | solution.py:442
  97.9 0.8 collective-permute-start.50
  98.7 1.1 collective-permute-done.46.refs_5_
  100.5 2.8 %collective-permute-done.48.refs_7_ = bf16[128,128]{1,0:T(8,128)(2,1)S(1)} collective-permute-done((bf16[128,128]{1,0:T(8,128)(2,1)S(1)}, bf16[128,128]{1,0:T(8,128)(2,1)S(1)}, u32[]{:S(2)}, u32[]{:S(2)}) %collective-permute-start.48) | collective-permute-done | bytes 32800 | tf_op jit(solution)/shard_map/ppermute | solution.py:442
  103.3 1.5 %last.1 = (f32[2048,128]{1,0:T(8,128)S(1)}, f32[64,128]{1,0:T(8,128)S(1)}, f32[64,128]{1,0:T(8,128)S(1)}) custom-call(s32[1]{0:T(128)} %bitcast.place_ref.refs_0_, bf16[2048,384]{1,0:T(8,128)(2,1)S(1)} %get-tuple-element.80.refs_0_.refs_1_, bf16[2048,256]{1,0:T(8,128)(2,1)S(1)} %get-tuple-element.81.refs_2_, f32[256,128]{1,0:T(8,128)S(1)} %get-tuple-element.82.refs_3_, ...), custom_call_target="tpu_custom_call" | custom-call | tf_op jit(solution)/shard_map/last/pallas_call | solution.py:331
  104.9 1.2 collective-permute-done.52
  106.1 0.9 collective-permute-start.54
  107.0 2.5 %collective-permute-start.53 = (f32[64,128]{1,0:T(8,128)S(1)}, f32[64,128]{1,0:T(8,128)S(1)}, u32[]{:S(2)}, u32[]{:S(2)}) collective-permute-start(f32[64,128]{1,0:T(8,128)S(1)} %add.25), channel_id=1, source_target_pairs={{0,2},{1,3},{2,0},{3,1},{4,6},{5,7},{6,4},{7,5},{8,10},{9,11},{10,... | collective-permute-start | bytes 98312 | tf_op jit(solution)/shard_map/ppermute | solution.py:425
  109.5 1.5 %collective-permute-done.55 = f32[64,128]{1,0:T(8,128)S(1)} collective-permute-done((f32[64,128]{1,0:T(8,128)S(1)}, f32[64,128]{1,0:T(8,128)S(1)}, u32[]{:S(2)}, u32[]{:S(2)}) %collective-permute-start.55) | collective-permute-done | bytes 32800 | tf_op jit(solution)/shard_map/ppermute | solution.py:425
  111.4 2.1 %collective-permute-start.58 = (f32[64,128]{1,0:T(8,128)S(1)}, f32[64,128]{1,0:T(8,128)S(1)}, u32[]{:S(2)}, u32[]{:S(2)}) collective-permute-start(f32[64,128]{1,0:T(8,128)S(1)} %add_add_fusion.1), channel_id=1, source_target_pairs={{0,24},{1,25},{2,26},{3,27},{4,28},{5,29},{6,30},{7,31},{8,16},{9,... | collective-permute-start | bytes 98312 | tf_op jit(solution)/shard_map/ppermute | solution.py:425
  113.5 2.4 %collective-permute-start.56 = (f32[64,128]{1,0:T(8,128)S(1)}, f32[64,128]{1,0:T(8,128)S(1)}, u32[]{:S(2)}, u32[]{:S(2)}) collective-permute-start(f32[64,128]{1,0:T(8,128)S(1)} %add_add_fusion.1), channel_id=1, source_target_pairs={{0,8},{1,9},{2,10},{3,11},{4,12},{5,13},{6,14},{7,15},{8,0},{9,1},... | collective-permute-start | bytes 98312 | tf_op jit(solution)/shard_map/ppermute | solution.py:425
  115.9 1.5 %collective-permute-done.58 = f32[64,128]{1,0:T(8,128)S(1)} collective-permute-done((f32[64,128]{1,0:T(8,128)S(1)}, f32[64,128]{1,0:T(8,128)S(1)}, u32[]{:S(2)}, u32[]{:S(2)}) %collective-permute-start.58) | collective-permute-done | bytes 32800 | tf_op jit(solution)/shard_map/ppermute | solution.py:425
  117.4 0.9 collective-permute-done.57
  118.4 1.2 collective-permute-done.59.refs_2_
  119.6 7.1 %finish.1 = f32[2048,128]{1,0:T(8,128)} custom-call(s32[1]{0:T(128)} %bitcast.place_ref.refs_0_, f32[64,128]{1,0:T(8,128)S(1)} %add_add_fusion.refs_1_, f32[64,128]{1,0:T(8,128)S(1)} %collective-permute-done.59.refs_2_, f32[2048,128]{1,0:T(8,128)S(1)} %get-tuple-element.152.refs_3_), custom_call_target="tpu_custom_call" | custom-call | tf_op jit(solution)/shard_map/finish/pallas_call | solution.py:412
  (78 shorter events, 6.8 us)
Async XLA Ops:
  0.0 12.6 %collective-permute-start.3 = (s32[1,256]{1,0:T(1,128)}, s32[1,256]{1,0:T(1,128)S(1)}, u32[]{:S(2)}, u32[]{:S(2)}) collective-permute-start(s32[1,256]{1,0:T(1,128)} %bitcast.10), channel_id=1, source_target_pairs={{4,8},{8,4},{5,9},{9,5},{6,10},{10,6},{7,11},{11,7},{12,16},{16,12... | collective-permute-start | bytes 3080 | tf_op jit(solution)/shard_map/ppermute | solution.py:442
  6.0 6.6 %collective-permute-start.2 = (s32[1,256]{1,0:T(1,128)}, s32[1,256]{1,0:T(1,128)S(1)}, u32[]{:S(2)}, u32[]{:S(2)}) collective-permute-start(s32[1,256]{1,0:T(1,128)} %bitcast.11), channel_id=1, source_target_pairs={{0,4},{4,0},{1,5},{5,1},{2,6},{6,2},{3,7},{7,3},{8,12},{12,8},{9,1... | collective-permute-start | bytes 3080 | tf_op jit(solution)/shard_map/ppermute | solution.py:442
  6.0 7.4 %collective-permute-start.1 = (s32[1,256]{1,0:T(1,128)}, s32[1,256]{1,0:T(1,128)S(1)}, u32[]{:S(2)}, u32[]{:S(2)}) collective-permute-start(s32[1,256]{1,0:T(1,128)} %bitcast.12), channel_id=1, source_target_pairs={{2,4},{4,2},{3,5},{5,3},{6,8},{8,6},{7,9},{9,7},{10,12},{12,10},{1... | collective-permute-start | bytes 3080 | tf_op jit(solution)/shard_map/ppermute | solution.py:442
  8.8 4.5 %collective-permute-start = (s32[1,256]{1,0:T(1,128)}, s32[1,256]{1,0:T(1,128)S(1)}, u32[]{:S(2)}, u32[]{:S(2)}) collective-permute-start(s32[1,256]{1,0:T(1,128)} %bitcast.13), channel_id=1, source_target_pairs={{0,2},{2,0},{1,3},{3,1},{4,6},{6,4},{5,7},{7,5},{8,10},{10,8},{9,1... | collective-permute-start | bytes 3080 | tf_op jit(solution)/shard_map/ppermute | solution.py:442
  14.0 6.7 %collective-permute-start.4 = (bf16[128,128]{1,0:T(8,128)(2,1)S(1)}, bf16[128,128]{1,0:T(8,128)(2,1)S(1)}, u32[]{:S(2)}, u32[]{:S(2)}) collective-permute-start(bf16[128,128]{1,0:T(8,128)(2,1)S(1)} %get-tuple-element.89), channel_id=1, source_target_pairs={{4,8},{8,4},{5,9},{9,5},{6,10},{10,6},{7,11},{11,7},{12,16},{16,12... | collective-permute-start | bytes 98312 | tf_op jit(solution)/shard_map/ppermute | solution.py:442
  16.0 7.5 %collective-permute-start.5 = (bf16[128,128]{1,0:T(8,128)(2,1)S(1)}, bf16[128,128]{1,0:T(8,128)(2,1)S(1)}, u32[]{:S(2)}, u32[]{:S(2)}) collective-permute-start(bf16[128,128]{1,0:T(8,128)(2,1)S(1)} %get-tuple-element.90), channel_id=1, source_target_pairs={{2,4},{4,2},{3,5},{5,3},{6,8},{8,6},{7,9},{9,7},{10,12},{12,10},{1... | collective-permute-start | bytes 98312 | tf_op jit(solution)/shard_map/ppermute | solution.py:442
  18.8 6.9 %collective-permute-start.6 = (bf16[128,128]{1,0:T(8,128)(2,1)S(1)}, bf16[128,128]{1,0:T(8,128)(2,1)S(1)}, u32[]{:S(2)}, u32[]{:S(2)}) collective-permute-start(bf16[128,128]{1,0:T(8,128)(2,1)S(1)} %get-tuple-element.91), channel_id=1, source_target_pairs={{1,2},{2,1},{3,4},{4,3},{5,6},{6,5},{7,8},{8,7},{9,10},{10,9},{11,... | collective-permute-start | bytes 98312 | tf_op jit(solution)/shard_map/ppermute | solution.py:442
  19.7 6.1 %collective-permute-start.7 = (bf16[128,128]{1,0:T(8,128)(2,1)S(1)}, bf16[128,128]{1,0:T(8,128)(2,1)S(1)}, u32[]{:S(2)}, u32[]{:S(2)}) collective-permute-start(bf16[128,128]{1,0:T(8,128)(2,1)S(1)} %get-tuple-element.92), channel_id=1, source_target_pairs={{0,4},{4,0},{1,5},{5,1},{2,6},{6,2},{3,7},{7,3},{8,12},{12,8},{9,1... | collective-permute-start | bytes 98312 | tf_op jit(solution)/shard_map/ppermute | solution.py:442
  19.7 6.1 %collective-permute-start.8 = (bf16[128,128]{1,0:T(8,128)(2,1)S(1)}, bf16[128,128]{1,0:T(8,128)(2,1)S(1)}, u32[]{:S(2)}, u32[]{:S(2)}) collective-permute-start(bf16[128,128]{1,0:T(8,128)(2,1)S(1)} %get-tuple-element.93), channel_id=1, source_target_pairs={{0,2},{2,0},{1,3},{3,1},{4,6},{6,4},{5,7},{7,5},{8,10},{10,8},{9,1... | collective-permute-start | bytes 98312 | tf_op jit(solution)/shard_map/ppermute | solution.py:442
  20.7 5.1 %collective-permute-start.9 = (bf16[128,128]{1,0:T(8,128)(2,1)S(1)}, bf16[128,128]{1,0:T(8,128)(2,1)S(1)}, u32[]{:S(2)}, u32[]{:S(2)}) collective-permute-start(bf16[128,128]{1,0:T(8,128)(2,1)S(1)} %get-tuple-element.94), channel_id=1, source_target_pairs={{0,1},{1,0},{2,3},{3,2},{4,5},{5,4},{6,7},{7,6},{8,9},{9,8},{10,11... | collective-permute-start | bytes 98312 | tf_op jit(solution)/shard_map/ppermute | solution.py:442
  26.5 7.0 %collective-permute-start.10 = (bf16[128,128]{1,0:T(8,128)(2,1)S(1)}, bf16[128,128]{1,0:T(8,128)(2,1)S(1)}, u32[]{:S(2)}, u32[]{:S(2)}) collective-permute-start(bf16[128,128]{1,0:T(8,128)(2,1)S(1)} %get-tuple-element.96), channel_id=1, source_target_pairs={{4,8},{8,4},{5,9},{9,5},{6,10},{10,6},{7,11},{11,7},{12,16},{16,12... | collective-permute-start | bytes 98312 | tf_op jit(solution)/shard_map/ppermute | solution.py:442
  26.6 7.6 %collective-permute-start.11 = (bf16[128,128]{1,0:T(8,128)(2,1)S(1)}, bf16[128,128]{1,0:T(8,128)(2,1)S(1)}, u32[]{:S(2)}, u32[]{:S(2)}) collective-permute-start(bf16[128,128]{1,0:T(8,128)(2,1)S(1)} %get-tuple-element.97), channel_id=1, source_target_pairs={{2,4},{4,2},{3,5},{5,3},{6,8},{8,6},{7,9},{9,7},{10,12},{12,10},{1... | collective-permute-start | bytes 98312 | tf_op jit(solution)/shard_map/ppermute | solution.py:442
  28.6 7.0 %collective-permute-start.12 = (bf16[128,128]{1,0:T(8,128)(2,1)S(1)}, bf16[128,128]{1,0:T(8,128)(2,1)S(1)}, u32[]{:S(2)}, u32[]{:S(2)}) collective-permute-start(bf16[128,128]{1,0:T(8,128)(2,1)S(1)} %get-tuple-element.98), channel_id=1, source_target_pairs={{1,2},{2,1},{3,4},{4,3},{5,6},{6,5},{7,8},{8,7},{9,10},{10,9},{11,... | collective-permute-start | bytes 98312 | tf_op jit(solution)/shard_map/ppermute | solution.py:442
  31.6 4.2 %collective-permute-start.13 = (bf16[128,128]{1,0:T(8,128)(2,1)S(1)}, bf16[128,128]{1,0:T(8,128)(2,1)S(1)}, u32[]{:S(2)}, u32[]{:S(2)}) collective-permute-start(bf16[128,128]{1,0:T(8,128)(2,1)S(1)} %get-tuple-element.99), channel_id=1, source_target_pairs={{0,4},{4,0},{1,5},{5,1},{2,6},{6,2},{3,7},{7,3},{8,12},{12,8},{9,1... | collective-permute-start | bytes 98312 | tf_op jit(solution)/shard_map/ppermute | solution.py:442
  31.7 4.2 %collective-permute-start.14 = (bf16[128,128]{1,0:T(8,128)(2,1)S(1)}, bf16[128,128]{1,0:T(8,128)(2,1)S(1)}, u32[]{:S(2)}, u32[]{:S(2)}) collective-permute-start(bf16[128,128]{1,0:T(8,128)(2,1)S(1)} %get-tuple-element.100), channel_id=1, source_target_pairs={{0,2},{2,0},{1,3},{3,1},{4,6},{6,4},{5,7},{7,5},{8,10},{10,8},{9,1... | collective-permute-start | bytes 98312 | tf_op jit(solution)/shard_map/ppermute | solution.py:442
  33.5 2.3 %collective-permute-start.15 = (bf16[128,128]{1,0:T(8,128)(2,1)S(1)}, bf16[128,128]{1,0:T(8,128)(2,1)S(1)}, u32[]{:S(2)}, u32[]{:S(2)}) collective-permute-start(bf16[128,128]{1,0:T(8,128)(2,1)S(1)} %get-tuple-element.101), channel_id=1, source_target_pairs={{0,1},{1,0},{2,3},{3,2},{4,5},{5,4},{6,7},{7,6},{8,9},{9,8},{10,11... | collective-permute-start | bytes 98312 | tf_op jit(solution)/shard_map/ppermute | solution.py:442
  36.6 6.7 %collective-permute-start.16 = (bf16[128,128]{1,0:T(8,128)(2,1)S(1)}, bf16[128,128]{1,0:T(8,128)(2,1)S(1)}, u32[]{:S(2)}, u32[]{:S(2)}) collective-permute-start(bf16[128,128]{1,0:T(8,128)(2,1)S(1)} %get-tuple-element.104), channel_id=1, source_target_pairs={{4,8},{8,4},{5,9},{9,5},{6,10},{10,6},{7,11},{11,7},{12,16},{16,12... | collective-permute-start | bytes 98312 | tf_op jit(solution)/shard_map/ppermute | solution.py:442
  37.5 7.5 %collective-permute-start.17 = (bf16[128,128]{1,0:T(8,128)(2,1)S(1)}, bf16[128,128]{1,0:T(8,128)(2,1)S(1)}, u32[]{:S(2)}, u32[]{:S(2)}) collective-permute-start(bf16[128,128]{1,0:T(8,128)(2,1)S(1)} %get-tuple-element.105), channel_id=1, source_target_pairs={{2,4},{4,2},{3,5},{5,3},{6,8},{8,6},{7,9},{9,7},{10,12},{12,10},{1... | collective-permute-start | bytes 98312 | tf_op jit(solution)/shard_map/ppermute | solution.py:442
  40.5 6.9 %collective-permute-start.18 = (bf16[128,128]{1,0:T(8,128)(2,1)S(1)}, bf16[128,128]{1,0:T(8,128)(2,1)S(1)}, u32[]{:S(2)}, u32[]{:S(2)}) collective-permute-start(bf16[128,128]{1,0:T(8,128)(2,1)S(1)} %get-tuple-element.106), channel_id=1, source_target_pairs={{1,2},{2,1},{3,4},{4,3},{5,6},{6,5},{7,8},{8,7},{9,10},{10,9},{11,... | collective-permute-start | bytes 98312 | tf_op jit(solution)/shard_map/ppermute | solution.py:442
  42.9 4.6 %collective-permute-start.19 = (bf16[128,128]{1,0:T(8,128)(2,1)S(1)}, bf16[128,128]{1,0:T(8,128)(2,1)S(1)}, u32[]{:S(2)}, u32[]{:S(2)}) collective-permute-start(bf16[128,128]{1,0:T(8,128)(2,1)S(1)} %get-tuple-element.107), channel_id=1, source_target_pairs={{0,4},{4,0},{1,5},{5,1},{2,6},{6,2},{3,7},{7,3},{8,12},{12,8},{9,1... | collective-permute-start | bytes 98312 | tf_op jit(solution)/shard_map/ppermute | solution.py:442
  42.9 4.6 %collective-permute-start.20 = (bf16[128,128]{1,0:T(8,128)(2,1)S(1)}, bf16[128,128]{1,0:T(8,128)(2,1)S(1)}, u32[]{:S(2)}, u32[]{:S(2)}) collective-permute-start(bf16[128,128]{1,0:T(8,128)(2,1)S(1)} %get-tuple-element.108), channel_id=1, source_target_pairs={{0,2},{2,0},{1,3},{3,1},{4,6},{6,4},{5,7},{7,5},{8,10},{10,8},{9,1... | collective-permute-start | bytes 98312 | tf_op jit(solution)/shard_map/ppermute | solution.py:442
  43.3 4.2 %collective-permute-start.21 = (bf16[128,128]{1,0:T(8,128)(2,1)S(1)}, bf16[128,128]{1,0:T(8,128)(2,1)S(1)}, u32[]{:S(2)}, u32[]{:S(2)}) collective-permute-start(bf16[128,128]{1,0:T(8,128)(2,1)S(1)} %get-tuple-element.109), channel_id=1, source_target_pairs={{0,1},{1,0},{2,3},{3,2},{4,5},{5,4},{6,7},{7,6},{8,9},{9,8},{10,11... | collective-permute-start | bytes 98312 | tf_op jit(solution)/shard_map/ppermute | solution.py:442
  48.3 7.0 %collective-permute-start.22 = (bf16[128,128]{1,0:T(8,128)(2,1)S(1)}, bf16[128,128]{1,0:T(8,128)(2,1)S(1)}, u32[]{:S(2)}, u32[]{:S(2)}) collective-permute-start(bf16[128,128]{1,0:T(8,128)(2,1)S(1)} %get-tuple-element.112), channel_id=1, source_target_pairs={{4,8},{8,4},{5,9},{9,5},{6,10},{10,6},{7,11},{11,7},{12,16},{16,12... | collective-permute-start | bytes 98312 | tf_op jit(solution)/shard_map/ppermute | solution.py:442
  48.3 7.7 %collective-permute-start.23 = (bf16[128,128]{1,0:T(8,128)(2,1)S(1)}, bf16[128,128]{1,0:T(8,128)(2,1)S(1)}, u32[]{:S(2)}, u32[]{:S(2)}) collective-permute-start(bf16[128,128]{1,0:T(8,128)(2,1)S(1)} %get-tuple-element.113), channel_id=1, source_target_pairs={{2,4},{4,2},{3,5},{5,3},{6,8},{8,6},{7,9},{9,7},{10,12},{12,10},{1... | collective-permute-start | bytes 98312 | tf_op jit(solution)/shard_map/ppermute | solution.py:442
  51.8 7.0 %collective-permute-start.24 = (bf16[128,128]{1,0:T(8,128)(2,1)S(1)}, bf16[128,128]{1,0:T(8,128)(2,1)S(1)}, u32[]{:S(2)}, u32[]{:S(2)}) collective-permute-start(bf16[128,128]{1,0:T(8,128)(2,1)S(1)} %get-tuple-element.114), channel_id=1, source_target_pairs={{1,2},{2,1},{3,4},{4,3},{5,6},{6,5},{7,8},{8,7},{9,10},{10,9},{11,... | collective-permute-start | bytes 98312 | tf_op jit(solution)/shard_map/ppermute | solution.py:442
  53.4 5.5 %collective-permute-start.25 = (bf16[128,128]{1,0:T(8,128)(2,1)S(1)}, bf16[128,128]{1,0:T(8,128)(2,1)S(1)}, u32[]{:S(2)}, u32[]{:S(2)}) collective-permute-start(bf16[128,128]{1,0:T(8,128)(2,1)S(1)} %get-tuple-element.115), channel_id=1, source_target_pairs={{0,4},{4,0},{1,5},{5,1},{2,6},{6,2},{3,7},{7,3},{8,12},{12,8},{9,1... | collective-permute-start | bytes 98312 | tf_op jit(solution)/shard_map/ppermute | solution.py:442
  53.4 5.5 %collective-permute-start.26 = (bf16[128,128]{1,0:T(8,128)(2,1)S(1)}, bf16[128,128]{1,0:T(8,128)(2,1)S(1)}, u32[]{:S(2)}, u32[]{:S(2)}) collective-permute-start(bf16[128,128]{1,0:T(8,128)(2,1)S(1)} %get-tuple-element.116), channel_id=1, source_target_pairs={{0,2},{2,0},{1,3},{3,1},{4,6},{6,4},{5,7},{7,5},{8,10},{10,8},{9,1... | collective-permute-start | bytes 98312 | tf_op jit(solution)/shard_map/ppermute | solution.py:442
  55.3 3.6 %collective-permute-start.27 = (bf16[128,128]{1,0:T(8,128)(2,1)S(1)}, bf16[128,128]{1,0:T(8,128)(2,1)S(1)}, u32[]{:S(2)}, u32[]{:S(2)}) collective-permute-start(bf16[128,128]{1,0:T(8,128)(2,1)S(1)} %get-tuple-element.117), channel_id=1, source_target_pairs={{0,1},{1,0},{2,3},{3,2},{4,5},{5,4},{6,7},{7,6},{8,9},{9,8},{10,11... | collective-permute-start | bytes 98312 | tf_op jit(solution)/shard_map/ppermute | solution.py:442
  59.6 7.1 %collective-permute-start.28 = (bf16[128,128]{1,0:T(8,128)(2,1)S(1)}, bf16[128,128]{1,0:T(8,128)(2,1)S(1)}, u32[]{:S(2)}, u32[]{:S(2)}) collective-permute-start(bf16[128,128]{1,0:T(8,128)(2,1)S(1)} %get-tuple-element.120), channel_id=1, source_target_pairs={{4,8},{8,4},{5,9},{9,5},{6,10},{10,6},{7,11},{11,7},{12,16},{16,12... | collective-permute-start | bytes 98312 | tf_op jit(solution)/shard_map/ppermute | solution.py:442
  59.7 7.6 %collective-permute-start.29 = (bf16[128,128]{1,0:T(8,128)(2,1)S(1)}, bf16[128,128]{1,0:T(8,128)(2,1)S(1)}, u32[]{:S(2)}, u32[]{:S(2)}) collective-permute-start(bf16[128,128]{1,0:T(8,128)(2,1)S(1)} %get-tuple-element.121), channel_id=1, source_target_pairs={{2,4},{4,2},{3,5},{5,3},{6,8},{8,6},{7,9},{9,7},{10,12},{12,10},{1... | collective-permute-start | bytes 98312 | tf_op jit(solution)/shard_map/ppermute | solution.py:442
  63.2 7.0 %collective-permute-start.30 = (bf16[128,128]{1,0:T(8,128)(2,1)S(1)}, bf16[128,128]{1,0:T(8,128)(2,1)S(1)}, u32[]{:S(2)}, u32[]{:S(2)}) collective-permute-start(bf16[128,128]{1,0:T(8,128)(2,1)S(1)} %get-tuple-element.122), channel_id=1, source_target_pairs={{1,2},{2,1},{3,4},{4,3},{5,6},{6,5},{7,8},{8,7},{9,10},{10,9},{11,... | collective-permute-start | bytes 98312 | tf_op jit(solution)/shard_map/ppermute | solution.py:442
  64.6 5.6 %collective-permute-start.31 = (bf16[128,128]{1,0:T(8,128)(2,1)S(1)}, bf16[128,128]{1,0:T(8,128)(2,1)S(1)}, u32[]{:S(2)}, u32[]{:S(2)}) collective-permute-start(bf16[128,128]{1,0:T(8,128)(2,1)S(1)} %get-tuple-element.123), channel_id=1, source_target_pairs={{0,4},{4,0},{1,5},{5,1},{2,6},{6,2},{3,7},{7,3},{8,12},{12,8},{9,1... | collective-permute-start | bytes 98312 | tf_op jit(solution)/shard_map/ppermute | solution.py:442
  64.7 5.6 %collective-permute-start.32 = (bf16[128,128]{1,0:T(8,128)(2,1)S(1)}, bf16[128,128]{1,0:T(8,128)(2,1)S(1)}, u32[]{:S(2)}, u32[]{:S(2)}) collective-permute-start(bf16[128,128]{1,0:T(8,128)(2,1)S(1)} %get-tuple-element.124), channel_id=1, source_target_pairs={{0,2},{2,0},{1,3},{3,1},{4,6},{6,4},{5,7},{7,5},{8,10},{10,8},{9,1... | collective-permute-start | bytes 98312 | tf_op jit(solution)/shard_map/ppermute | solution.py:442
  66.7 3.6 %collective-permute-start.33 = (bf16[128,128]{1,0:T(8,128)(2,1)S(1)}, bf16[128,128]{1,0:T(8,128)(2,1)S(1)}, u32[]{:S(2)}, u32[]{:S(2)}) collective-permute-start(bf16[128,128]{1,0:T(8,128)(2,1)S(1)} %get-tuple-element.125), channel_id=1, source_target_pairs={{0,1},{1,0},{2,3},{3,2},{4,5},{5,4},{6,7},{7,6},{8,9},{9,8},{10,11... | collective-permute-start | bytes 98312 | tf_op jit(solution)/shard_map/ppermute | solution.py:442
  71.0 7.1 %collective-permute-start.34 = (bf16[128,128]{1,0:T(8,128)(2,1)S(1)}, bf16[128,128]{1,0:T(8,128)(2,1)S(1)}, u32[]{:S(2)}, u32[]{:S(2)}) collective-permute-start(bf16[128,128]{1,0:T(8,128)(2,1)S(1)} %get-tuple-element.128), channel_id=1, source_target_pairs={{4,8},{8,4},{5,9},{9,5},{6,10},{10,6},{7,11},{11,7},{12,16},{16,12... | collective-permute-start | bytes 98312 | tf_op jit(solution)/shard_map/ppermute | solution.py:442
  71.1 7.7 %collective-permute-start.35 = (bf16[128,128]{1,0:T(8,128)(2,1)S(1)}, bf16[128,128]{1,0:T(8,128)(2,1)S(1)}, u32[]{:S(2)}, u32[]{:S(2)}) collective-permute-start(bf16[128,128]{1,0:T(8,128)(2,1)S(1)} %get-tuple-element.129), channel_id=1, source_target_pairs={{2,4},{4,2},{3,5},{5,3},{6,8},{8,6},{7,9},{9,7},{10,12},{12,10},{1... | collective-permute-start | bytes 98312 | tf_op jit(solution)/shard_map/ppermute | solution.py:442
  73.8 6.9 %collective-permute-start.36 = (bf16[128,128]{1,0:T(8,128)(2,1)S(1)}, bf16[128,128]{1,0:T(8,128)(2,1)S(1)}, u32[]{:S(2)}, u32[]{:S(2)}) collective-permute-start(bf16[128,128]{1,0:T(8,128)(2,1)S(1)} %get-tuple-element.130), channel_id=1, source_target_pairs={{1,2},{2,1},{3,4},{4,3},{5,6},{6,5},{7,8},{8,7},{9,10},{10,9},{11,... | collective-permute-start | bytes 98312 | tf_op jit(solution)/shard_map/ppermute | solution.py:442
  76.0 4.7 %collective-permute-start.37 = (bf16[128,128]{1,0:T(8,128)(2,1)S(1)}, bf16[128,128]{1,0:T(8,128)(2,1)S(1)}, u32[]{:S(2)}, u32[]{:S(2)}) collective-permute-start(bf16[128,128]{1,0:T(8,128)(2,1)S(1)} %get-tuple-element.131), channel_id=1, source_target_pairs={{0,4},{4,0},{1,5},{5,1},{2,6},{6,2},{3,7},{7,3},{8,12},{12,8},{9,1... | collective-permute-start | bytes 98312 | tf_op jit(solution)/shard_map/ppermute | solution.py:442
  76.0 4.7 %collective-permute-start.38 = (bf16[128,128]{1,0:T(8,128)(2,1)S(1)}, bf16[128,128]{1,0:T(8,128)(2,1)S(1)}, u32[]{:S(2)}, u32[]{:S(2)}) collective-permute-start(bf16[128,128]{1,0:T(8,128)(2,1)S(1)} %get-tuple-element.132), channel_id=1, source_target_pairs={{0,2},{2,0},{1,3},{3,1},{4,6},{6,4},{5,7},{7,5},{8,10},{10,8},{9,1... | collective-permute-start | bytes 98312 | tf_op jit(solution)/shard_map/ppermute | solution.py:442
  78.1 2.7 %collective-permute-start.39 = (bf16[128,128]{1,0:T(8,128)(2,1)S(1)}, bf16[128,128]{1,0:T(8,128)(2,1)S(1)}, u32[]{:S(2)}, u32[]{:S(2)}) collective-permute-start(bf16[128,128]{1,0:T(8,128)(2,1)S(1)} %get-tuple-element.133), channel_id=1, source_target_pairs={{0,1},{1,0},{2,3},{3,2},{4,5},{5,4},{6,7},{7,6},{8,9},{9,8},{10,11... | collective-permute-start | bytes 98312 | tf_op jit(solution)/shard_map/ppermute | solution.py:442
  81.5 6.7 %collective-permute-start.40 = (bf16[128,128]{1,0:T(8,128)(2,1)S(1)}, bf16[128,128]{1,0:T(8,128)(2,1)S(1)}, u32[]{:S(2)}, u32[]{:S(2)}) collective-permute-start(bf16[128,128]{1,0:T(8,128)(2,1)S(1)} %get-tuple-element.136), channel_id=1, source_target_pairs={{4,8},{8,4},{5,9},{9,5},{6,10},{10,6},{7,11},{11,7},{12,16},{16,12... | collective-permute-start | bytes 98312 | tf_op jit(solution)/shard_map/ppermute | solution.py:442
  82.0 7.5 %collective-permute-start.41 = (bf16[128,128]{1,0:T(8,128)(2,1)S(1)}, bf16[128,128]{1,0:T(8,128)(2,1)S(1)}, u32[]{:S(2)}, u32[]{:S(2)}) collective-permute-start(bf16[128,128]{1,0:T(8,128)(2,1)S(1)} %get-tuple-element.137), channel_id=1, source_target_pairs={{2,4},{4,2},{3,5},{5,3},{6,8},{8,6},{7,9},{9,7},{10,12},{12,10},{1... | collective-permute-start | bytes 98312 | tf_op jit(solution)/shard_map/ppermute | solution.py:442
  85.1 6.9 %collective-permute-start.42 = (bf16[128,128]{1,0:T(8,128)(2,1)S(1)}, bf16[128,128]{1,0:T(8,128)(2,1)S(1)}, u32[]{:S(2)}, u32[]{:S(2)}) collective-permute-start(bf16[128,128]{1,0:T(8,128)(2,1)S(1)} %get-tuple-element.138), channel_id=1, source_target_pairs={{1,2},{2,1},{3,4},{4,3},{5,6},{6,5},{7,8},{8,7},{9,10},{10,9},{11,... | collective-permute-start | bytes 98312 | tf_op jit(solution)/shard_map/ppermute | solution.py:442
  87.4 4.6 %collective-permute-start.43 = (bf16[128,128]{1,0:T(8,128)(2,1)S(1)}, bf16[128,128]{1,0:T(8,128)(2,1)S(1)}, u32[]{:S(2)}, u32[]{:S(2)}) collective-permute-start(bf16[128,128]{1,0:T(8,128)(2,1)S(1)} %get-tuple-element.139), channel_id=1, source_target_pairs={{0,4},{4,0},{1,5},{5,1},{2,6},{6,2},{3,7},{7,3},{8,12},{12,8},{9,1... | collective-permute-start | bytes 98312 | tf_op jit(solution)/shard_map/ppermute | solution.py:442
  87.4 4.6 %collective-permute-start.44 = (bf16[128,128]{1,0:T(8,128)(2,1)S(1)}, bf16[128,128]{1,0:T(8,128)(2,1)S(1)}, u32[]{:S(2)}, u32[]{:S(2)}) collective-permute-start(bf16[128,128]{1,0:T(8,128)(2,1)S(1)} %get-tuple-element.140), channel_id=1, source_target_pairs={{0,2},{2,0},{1,3},{3,1},{4,6},{6,4},{5,7},{7,5},{8,10},{10,8},{9,1... | collective-permute-start | bytes 98312 | tf_op jit(solution)/shard_map/ppermute | solution.py:442
  88.2 3.8 %collective-permute-start.45 = (bf16[128,128]{1,0:T(8,128)(2,1)S(1)}, bf16[128,128]{1,0:T(8,128)(2,1)S(1)}, u32[]{:S(2)}, u32[]{:S(2)}) collective-permute-start(bf16[128,128]{1,0:T(8,128)(2,1)S(1)} %get-tuple-element.141), channel_id=1, source_target_pairs={{0,1},{1,0},{2,3},{3,2},{4,5},{5,4},{6,7},{7,6},{8,9},{9,8},{10,11... | collective-permute-start | bytes 98312 | tf_op jit(solution)/shard_map/ppermute | solution.py:442
  92.8 7.0 %collective-permute-start.46 = (bf16[128,128]{1,0:T(8,128)(2,1)S(1)}, bf16[128,128]{1,0:T(8,128)(2,1)S(1)}, u32[]{:S(2)}, u32[]{:S(2)}) collective-permute-start(bf16[128,128]{1,0:T(8,128)(2,1)S(1)} %get-tuple-element.144), channel_id=1, source_target_pairs={{4,8},{8,4},{5,9},{9,5},{6,10},{10,6},{7,11},{11,7},{12,16},{16,12... | collective-permute-start | bytes 98312 | tf_op jit(solution)/shard_map/ppermute | solution.py:442
  92.9 7.6 %collective-permute-start.47 = (bf16[128,128]{1,0:T(8,128)(2,1)S(1)}, bf16[128,128]{1,0:T(8,128)(2,1)S(1)}, u32[]{:S(2)}, u32[]{:S(2)}) collective-permute-start(bf16[128,128]{1,0:T(8,128)(2,1)S(1)} %get-tuple-element.145), channel_id=1, source_target_pairs={{2,4},{4,2},{3,5},{5,3},{6,8},{8,6},{7,9},{9,7},{10,12},{12,10},{1... | collective-permute-start | bytes 98312 | tf_op jit(solution)/shard_map/ppermute | solution.py:442
  96.3 7.0 %collective-permute-start.48 = (bf16[128,128]{1,0:T(8,128)(2,1)S(1)}, bf16[128,128]{1,0:T(8,128)(2,1)S(1)}, u32[]{:S(2)}, u32[]{:S(2)}) collective-permute-start(bf16[128,128]{1,0:T(8,128)(2,1)S(1)} %get-tuple-element.146), channel_id=1, source_target_pairs={{1,2},{2,1},{3,4},{4,3},{5,6},{6,5},{7,8},{8,7},{9,10},{10,9},{11,... | collective-permute-start | bytes 98312 | tf_op jit(solution)/shard_map/ppermute | solution.py:442
  97.9 5.4 %collective-permute-start.49 = (bf16[128,128]{1,0:T(8,128)(2,1)S(1)}, bf16[128,128]{1,0:T(8,128)(2,1)S(1)}, u32[]{:S(2)}, u32[]{:S(2)}) collective-permute-start(bf16[128,128]{1,0:T(8,128)(2,1)S(1)} %get-tuple-element.147), channel_id=1, source_target_pairs={{0,4},{4,0},{1,5},{5,1},{2,6},{6,2},{3,7},{7,3},{8,12},{12,8},{9,1... | collective-permute-start | bytes 98312 | tf_op jit(solution)/shard_map/ppermute | solution.py:442
  97.9 5.4 %collective-permute-start.50 = (bf16[128,128]{1,0:T(8,128)(2,1)S(1)}, bf16[128,128]{1,0:T(8,128)(2,1)S(1)}, u32[]{:S(2)}, u32[]{:S(2)}) collective-permute-start(bf16[128,128]{1,0:T(8,128)(2,1)S(1)} %get-tuple-element.148), channel_id=1, source_target_pairs={{0,2},{2,0},{1,3},{3,1},{4,6},{6,4},{5,7},{7,5},{8,10},{10,8},{9,1... | collective-permute-start | bytes 98312 | tf_op jit(solution)/shard_map/ppermute | solution.py:442
  99.8 3.5 %collective-permute-start.51 = (bf16[128,128]{1,0:T(8,128)(2,1)S(1)}, bf16[128,128]{1,0:T(8,128)(2,1)S(1)}, u32[]{:S(2)}, u32[]{:S(2)}) collective-permute-start(bf16[128,128]{1,0:T(8,128)(2,1)S(1)} %get-tuple-element.149), channel_id=1, source_target_pairs={{0,1},{1,0},{2,3},{3,2},{4,5},{5,4},{6,7},{7,6},{8,9},{9,8},{10,11... | collective-permute-start | bytes 98312 | tf_op jit(solution)/shard_map/ppermute | solution.py:442
  104.8 1.3 %collective-permute-start.52 = (f32[64,128]{1,0:T(8,128)S(1)}, f32[64,128]{1,0:T(8,128)S(1)}, u32[]{:S(2)}, u32[]{:S(2)}) collective-permute-start(f32[64,128]{1,0:T(8,128)S(1)} %get-tuple-element.151), channel_id=1, source_target_pairs={{0,1},{1,0},{2,3},{3,2},{4,5},{5,4},{6,7},{7,6},{8,9},{9,8},{10,11... | collective-permute-start | bytes 98312 | tf_op jit(solution)/shard_map/ppermute | solution.py:425
  106.1 5.0 %collective-permute-start.55 = (f32[64,128]{1,0:T(8,128)S(1)}, f32[64,128]{1,0:T(8,128)S(1)}, u32[]{:S(2)}, u32[]{:S(2)}) collective-permute-start(f32[64,128]{1,0:T(8,128)S(1)} %add.25), channel_id=1, source_target_pairs={{0,6},{1,7},{2,4},{3,5},{4,2},{5,3},{6,0},{7,1},{8,14},{9,15},{10,... | collective-permute-start | bytes 98312 | tf_op jit(solution)/shard_map/ppermute | solution.py:425
  106.1 4.9 %collective-permute-start.54 = (f32[64,128]{1,0:T(8,128)S(1)}, f32[64,128]{1,0:T(8,128)S(1)}, u32[]{:S(2)}, u32[]{:S(2)}) collective-permute-start(f32[64,128]{1,0:T(8,128)S(1)} %add.25), channel_id=1, source_target_pairs={{0,4},{1,5},{2,6},{3,7},{4,0},{5,1},{6,2},{7,3},{8,12},{9,13},{10,... | collective-permute-start | bytes 98312 | tf_op jit(solution)/shard_map/ppermute | solution.py:425
  107.0 4.4 %collective-permute-start.53 = (f32[64,128]{1,0:T(8,128)S(1)}, f32[64,128]{1,0:T(8,128)S(1)}, u32[]{:S(2)}, u32[]{:S(2)}) collective-permute-start(f32[64,128]{1,0:T(8,128)S(1)} %add.25), channel_id=1, source_target_pairs={{0,2},{1,3},{2,0},{3,1},{4,6},{5,7},{6,4},{7,5},{8,10},{9,11},{10,... | collective-permute-start | bytes 98312 | tf_op jit(solution)/shard_map/ppermute | solution.py:425
  111.4 6.0 %collective-permute-start.58 = (f32[64,128]{1,0:T(8,128)S(1)}, f32[64,128]{1,0:T(8,128)S(1)}, u32[]{:S(2)}, u32[]{:S(2)}) collective-permute-start(f32[64,128]{1,0:T(8,128)S(1)} %add_add_fusion.1), channel_id=1, source_target_pairs={{0,24},{1,25},{2,26},{3,27},{4,28},{5,29},{6,30},{7,31},{8,16},{9,... | collective-permute-start | bytes 98312 | tf_op jit(solution)/shard_map/ppermute | solution.py:425
  113.5 4.8 %collective-permute-start.57 = (f32[64,128]{1,0:T(8,128)S(1)}, f32[64,128]{1,0:T(8,128)S(1)}, u32[]{:S(2)}, u32[]{:S(2)}) collective-permute-start(f32[64,128]{1,0:T(8,128)S(1)} %add_add_fusion.1), channel_id=1, source_target_pairs={{0,16},{1,17},{2,18},{3,19},{4,20},{5,21},{6,22},{7,23},{8,24},{9,... | collective-permute-start | bytes 98312 | tf_op jit(solution)/shard_map/ppermute | solution.py:425
  113.5 4.8 %collective-permute-start.56 = (f32[64,128]{1,0:T(8,128)S(1)}, f32[64,128]{1,0:T(8,128)S(1)}, u32[]{:S(2)}, u32[]{:S(2)}) collective-permute-start(f32[64,128]{1,0:T(8,128)S(1)} %add_add_fusion.1), channel_id=1, source_target_pairs={{0,8},{1,9},{2,10},{3,11},{4,12},{5,13},{6,14},{7,15},{8,0},{9,1},... | collective-permute-start | bytes 98312 | tf_op jit(solution)/shard_map/ppermute | solution.py:425
  118.4 1.3 %collective-permute-start.59 = (f32[64,128]{1,0:T(8,128)S(1)}, f32[64,128]{1,0:T(8,128)S(1)}, u32[]{:S(2)}, u32[]{:S(2)}) collective-permute-start(f32[64,128]{1,0:T(8,128)S(1)} %add_add_fusion.refs_1_), channel_id=1, source_target_pairs={{0,1},{1,0},{2,3},{3,2},{4,5},{5,4},{6,7},{7,6},{8,9},{9,8},{10,11... | collective-permute-start | bytes 98312 | tf_op jit(solution)/shard_map/ppermute | solution.py:425

commit v6 on v5

--- a/solution.py
+++ b/solution.py
@@ -218,8 +218,23 @@
     )(place, field, *wanted)
 
 
-def inner_kernel(scale, *refs):
-    band_ref, field_ref, *prev_refs, part_ref = refs
+def with_parts(value):
+    high = value.astype(BF16)
+    low = (value - high.astype(F32)).astype(BF16)
+    return jnp.concatenate([high, low], axis=1)
+
+
+def parts_joined(both):
+    half = both.shape[1] // 2
+    return both[:, :half] + both[:, half:]
+
+
+def far_parts(coef_ref, got):
+    far = jnp.concatenate([got[link][:CAP, :] for link in FAR_LINKS], axis=0)
+    return with_parts(far.astype(F32) * coef_ref[...])
+
+
+def inner_walk(scale, band_ref, field_ref, prev_refs, part_ref):
     rows = field_ref.shape[0]
     count = rows // BLK
     for b in range(count):
@@ -235,77 +250,152 @@
         part_ref[block, :] = value
 
 
-def inner(scale, band, field, *prev):
-    rows = field.shape[0]
+def inside_of(ref):
+    return slice(BLK, ref.shape[0] - BLK)
+
+
+def picked_parts(pick_mat_ref, part_ref):
+    inside = inside_of(part_ref)
+    both = dot(pick_mat_ref[:, inside], with_parts(part_ref[inside, :]), ((1,), (0,)))
+    return parts_joined(both)
+
+
+def opening_kernel(scale, band_ref, hot_ref, pick_mat_ref, field_ref, part_ref, picked_ref, joint_ref):
+    inner_walk(scale, band_ref, field_ref, (), part_ref)
+    picked_ref[...] = picked_parts(pick_mat_ref, part_ref)
+    inside = inside_of(hot_ref)
+    joint = dot(pick_mat_ref[:, inside], hot_ref[inside, :], ((1,), (0,)))
+    joint_ref[...] = joint.astype(BF16)
+
+
+def opening(scale, band, hot, pick_mat, field):
+    rows, edges = hot.shape
     return pl.pallas_call(
-        lambda *refs: inner_kernel(scale, *refs),
-        out_shape=jax.ShapeDtypeStruct((rows, VECS), F32),
-        in_specs=[VMEM] * (2 + len(prev)),
-        out_specs=VMEM,
-        compiler_params=PARAMS,
-        cost_estimate=pl.CostEstimate(
-            flops=2 * rows * 3 * BLK * VECS, bytes_accessed=4 * rows * 3 * BLK, transcendentals=0
+        lambda *refs: opening_kernel(scale, *refs),
+        out_shape=(
+            jax.ShapeDtypeStruct((rows, VECS), F32),
+            jax.ShapeDtypeStruct((edges, VECS), F32),
+            jax.ShapeDtypeStruct((edges, edges), BF16),
         ),
+        in_specs=[VMEM] * 4,
+        out_specs=(VMEM,) * 3,
+        compiler_params=PARAMS,
+        cost_estimate=estimate(rows),
+        name="opening",
+    )(band, hot, pick_mat, field)
+
+
+def estimate(rows):
+    return pl.CostEstimate(
+        flops=2 * rows * 3 * BLK * VECS, bytes_accessed=4 * rows * 3 * BLK, transcendentals=0
+    )
+
+
+def inner_kernel(scale, before_scale, more, *refs):
+    band_ref, hot_ref, pick_mat_ref, known_ref, far_ref, edge_ref, prev_ref = refs[:7]
+    part_ref, more_refs, packed_ref = refs[7], refs[8:-1], refs[-1]
+    rows = known_ref.shape[0]
+    count = rows // BLK
+    for b in range(count):
+        block = pl.ds(b * BLK, BLK)
+        if b == 0:
+            value = edge_ref[:BLK, :]
+        elif b == count - 1:
+            value = edge_ref[BLK:, :]
+        else:
+            both = dot(hot_ref[block, :], far_ref[...], ((1,), (0,)))
+            value = known_ref[block, :] + parts_joined(both) * before_scale
+        if more:
+            more_refs[0][block, :] = value
+        packed_ref[block, :] = value.astype(BF16)
+    inner_walk(scale, band_ref, packed_ref, (prev_ref,), part_ref)
+    if more:
+        more_refs[1][...] = picked_parts(pick_mat_ref, part_ref)
+
+
+def inner(scale, before_scale, more, band, hot, pick_mat, known, far, edge, prev):
+    rows, edges = hot.shape
+    return pl.pallas_call(
+        lambda *refs: inner_kernel(scale, before_scale, more, *refs),
+        out_shape=(
+            jax.ShapeDtypeStruct((rows, VECS), F32),
+            *(
+                jax.ShapeDtypeStruct((rows, VECS), F32),
+                jax.ShapeDtypeStruct((edges, VECS), F32),
+            )[: 2 * more],
+        ),
+        in_specs=[VMEM] * 7,
+        out_specs=(VMEM,) * (1 + 2 * more),
+        scratch_shapes=[pltpu.VMEM((rows, VECS), BF16)],
+        compiler_params=PARAMS,
+        cost_estimate=estimate(rows),
         name="inner",
-    )(band, field, *prev)
-
-
-def advance(place_ref, band_ref, hot_ref, coef_ref, part_ref, got, scale, store):
+    )(band, hot, pick_mat, known, far, edge, prev)
+
+
+def advance(place_ref, band_ref, hot_ref, coef_ref, part_ref, got, scale, store, blocks):
     rows = part_ref.shape[0]
     count = rows // BLK
     even = is_low(place_ref, 1)
     got = dict(zip(LINKS, got, strict=True))
     low = jnp.where(even, got[1, 1][...], got[1, 0][...])
     high = jnp.where(even, got[1, 0][...], got[1, 1][...])
-    far = jnp.concatenate([got[link][:CAP, :] for link in FAR_LINKS], axis=0)
-    far = far.astype(F32) * coef_ref[...]
-    far_high = far.astype(BF16)
-    far_low = (far - far_high.astype(F32)).astype(BF16)
-    far = jnp.concatenate([far_high, far_low], axis=1)
-    for b in range(count):
+    far = far_parts(coef_ref, got)
+    for b in blocks:
         block = pl.ds(b * BLK, BLK)
-        both = dot(hot_ref[block, :], far, ((1,), (0,)))
-        total = both[:, :VECS] + both[:, VECS:]
+        total = parts_joined(dot(hot_ref[block, :], far, ((1,), (0,))))
         if b == 0:
             total += dot(band_ref[block, :BLK], low, ((1,), (0,)))
         if b == count - 1:
             total += dot(band_ref[block, 2 * BLK :], high, ((1,), (0,)))
         store(block, part_ref[block, :] + total * scale)
-    return even
+    return even, far
 
 
 def step_kernel(scale, *refs):
-    place_ref, band_ref, hot_ref, coef_ref, pick_mat_ref, part_ref = refs[:6]
-    got, refs = refs[6:12], refs[12:]
-    packed_ref, sent, next_refs = refs[0], refs[1:7], refs[7:]
+    place_ref, band_ref, hot_ref, coef_ref, joint_ref, pick_mat_ref, part_ref, picked_ref = refs[:8]
+    got, sent, (far_ref, edge_ref) = refs[8:14], refs[14:20], refs[20:]
+    rows = part_ref.shape[0]
+    ends = []
 
     def store(block, value):
-        for next_ref in next_refs:
-            next_ref[block, :] = value
-        packed_ref[block, :] = value.astype(BF16)
-
-    even = advance(
-        place_ref, band_ref, hot_ref, coef_ref, part_ref, got, scale, store
-    )
-    rows = part_ref.shape[0]
-    picked = dot(pick_mat_ref[...], packed_ref[...], ((1,), (0,)))
-    send_out(even, packed_ref[:BLK, :], packed_ref[rows - BLK :, :], picked, sent)
-
-
-def step(scale, place, mats, part, got, has_next=True):
-    rows = part.shape[0]
-    return pl.pallas_call(
+        edge_ref[pl.ds(len(ends) * BLK, BLK), :] = value
+        ends.append(value.astype(BF16))
+
+    even, far = advance(
+        place_ref,
+        band_ref,
+        hot_ref,
+        coef_ref,
+        part_ref,
+        got,
+        scale,
+        store,
+        (0, rows // BLK - 1),
+    )
+    far_ref[...] = far
+    first, last = ends
+    picked = picked_ref[...] + parts_joined(dot(joint_ref[...], far, ((1,), (0,)))) * scale
+    picked += dot(pick_mat_ref[:, :BLK], first, ((1,), (0,)))
+    picked += dot(pick_mat_ref[:, rows - BLK :], last, ((1,), (0,)))
+    send_out(even, first, last, picked, sent)
+
+
+def step(scale, place, mats, part, picked, got):
+    edges = picked.shape[0]
+    *sent, far, edge = pl.pallas_call(
         lambda *refs: step_kernel(scale, *refs),
         out_shape=(
-            jax.ShapeDtypeStruct((rows, VECS), BF16),
             *SENT,
-            *(jax.ShapeDtypeStruct((rows, VECS), F32),) * has_next,
+            jax.ShapeDtypeStruct((edges, 2 * VECS), BF16),
+            jax.ShapeDtypeStruct((2 * BLK, VECS), F32),
         ),
-        in_specs=[SMEM] + [VMEM] * 11,
-        out_specs=(VMEM,) * (7 + has_next),
+        in_specs=[SMEM] + [VMEM] * 13,
+        out_specs=(VMEM,) * 8,
         compiler_params=PARAMS,
         name="step",
-    )(place, *mats, part, *got)
+    )(place, *mats, part, picked, *got)
+    return sent, far, edge
 
 
 def last_kernel(scale, *refs):
@@ -316,7 +406,15 @@
         next_ref[block, :] = value
 
     advance(
-        place_ref, band_ref, hot_ref, coef_ref, part_ref, got, scale, store
+        place_ref,
+        band_ref,
+        hot_ref,
+        coef_ref,
+        part_ref,
+        got,
+        scale,
+        store,
+        range(part_ref.shape[0] // BLK),
     )
     value = next_ref[...]
     gram = dot(value, value, ((0,), (0,)), lax.Precision.HIGHEST)
@@ -466,20 +564,20 @@
     def exchange(sent):
         return [swap(v, *link) for v, link in zip(sent, LINKS, strict=True)]
 
-    mats = (band, hot, coef, pick_mat)
-    previous, packed = (), field
-    for k in range(DEGREE):
-        scale = (2.0 if k else 1.0) / HALF_WIDTH
+    got = exchange(sent)
+    before, scale = 1.0 / HALF_WIDTH, 2.0 / HALF_WIDTH
+    part, picked, joint = opening(before, band, hot, pick_mat, field)
+    previous = field
+    for k in range(1, DEGREE):
+        mats = (band, hot, coef, joint, pick_mat)
+        sent, far, edge = step(before, here, mats, part, picked, got)
         got = exchange(sent)
-        part = inner(scale, band, packed, *previous)
-        if k == DEGREE - 1:
-            filtered, kept, sent = last(scale, here, mats[:3], part, got)
-        else:
-            previous = (current,) if k else (field,)
-            has_next = k < DEGREE - 2
-            packed, *sent = step(scale, here, mats, part, got, has_next)
-            if has_next:
-                current = sent.pop()
+        more = k < DEGREE - 1
+        part, *rest = inner(scale, before, more, band, hot, pick_mat, part, far, edge, previous)
+        if more:
+            previous, picked = rest
+        before = scale
+    filtered, kept, sent = last(scale, here, (band, hot, coef), part, got)
     return finish(math.sqrt(total_rows), here, summed(kept, sent, count), filtered)
 
 

time: 127 us -> 124 us (0.976)
  waiting for transfers between devices: 41 us -> 36.8 us
  Pallas kernels: 22.2 us -> 23.7 us
    ppermute x52, waiting for transfers between devices: 34.2 us -> 30.1 us  [swap(): return lax.ppermute(value, AXES, swap_pairs(count, by, odd))]
    pallas_call x15, Pallas kernels: 9.88 us -> 11.4 us  [the longest x7 7.62 us: inner(): pl.pallas_call(lambda *refs: inner_kernel(scale, before_scale, more, *ref...]
  transfers between devices with their start and end apart: 60 -> 60, of which waited for: 31 -> 27; matrix products, arithmetic and copies ran while one was open for 0% -> 0% of each run, Pallas kernels for 6% -> 9%
where the time goes in v6:
time: 124 us
  starting transfers between devices  63.4 us (51%)
  waiting for transfers between devices  36.8 us (30%)
  Pallas kernels  23.7 us (19%)
    ppermute x52, starting transfers between devices, swap(): return lax.ppermute(value, AXES, swap_pairs(count, by, odd))  55.3 us
    ppermute x52, waiting for transfers between devices, swap(): return lax.ppermute(value, AXES, swap_pairs(count, by, odd))  30.1 us
    ppermute x8, starting transfers between devices, swapped(): return lax.ppermute(value, AXES, [(i, i ^ mask) for i in range(count)])  8.08 us
    pallas_call x7, Pallas kernels, inner(): pl.pallas_call(lambda *refs: inner_kernel(scale, before_scale, more, *ref...  7.62 us
    pallas_call x1, Pallas kernels, finish(): pl.pallas_call(lambda *refs: finish_kernel(scale, *refs), out_shape=jax.S...  7.14 us
    ppermute x8, waiting for transfers between devices, swapped(): return lax.ppermute(value, AXES, [(i, i ^ mask) for i in range(count)])  6.73 us
    pallas_call x1, Pallas kernels, prepare(): pl.pallas_call(prepare_kernel, out_shape=(jax.ShapeDtypeStruct((rows, 3 *...  3.08 us
    pallas_call x7, Pallas kernels, step(): pl.pallas_call(lambda *refs: step_kernel(scale, *refs), out_shape=(*SENT,...  2.79 us
  transfers between devices with their start and end apart: 60, of which 27 were waited for; matrix products, arithmetic and copies ran while one was open for 0% of the time, Pallas kernels for 9%

profile of v6, /device:TPU:0, one launch (start us, length us, event | category | flops | bytes accessed | tf_op | source)
XLA Modules:
  0.0 124.3 jit_solution(18249220268298353101)
XLA Ops:
  0.0 6.0 %collective-permute-start.3 = (s32[1,256]{1,0:T(1,128)}, s32[1,256]{1,0:T(1,128)S(1)}, u32[]{:S(2)}, u32[]{:S(2)}) collective-permute-start(s32[1,256]{1,0:T(1,128)} %bitcast.10), channel_id=1, source_target_pairs={{4,8},{8,4},{5,9},{9,5},{6,10},{10,6},{7,11},{11,7},{12,16},{16,12... | collective-permute-start | bytes 3080 | tf_op jit(solution)/shard_map/ppermute | solution.py:540
  6.0 2.8 %collective-permute-start.1 = (s32[1,256]{1,0:T(1,128)}, s32[1,256]{1,0:T(1,128)S(1)}, u32[]{:S(2)}, u32[]{:S(2)}) collective-permute-start(s32[1,256]{1,0:T(1,128)} %bitcast.12), channel_id=1, source_target_pairs={{2,4},{4,2},{3,5},{5,3},{6,8},{8,6},{7,9},{9,7},{10,12},{12,10},{1... | collective-permute-start | bytes 3080 | tf_op jit(solution)/shard_map/ppermute | solution.py:540
  8.8 0.6 collective-permute-start
  9.5 3.1 %prepare.1 = (bf16[2048,384]{1,0:T(8,128)(2,1)S(1)}, bf16[2048,256]{1,0:T(8,128)(2,1)S(1)}, f32[256,128]{1,0:T(8,128)S(1)}, bf16[2048,128]{1,0:T(8,128)(2,1)S(1)}) custom-call(s32[1]{0:T(128)} %bitcast.place_ref.refs_0_, s32[1,256]{1,0:T(1,128)} %bitcast.8, f32[1,256]{1,0:T(1,128)} %bitcast.9, f32[3,8,2048]{2,1,0:T(8,128)} %bitcast.6, ...), custom_call_target="tpu_custom_call" | custom-call | tf_op jit(solution)/shard_map/prepare/pallas_call | solution.py:153
  12.6 0.8 collective-permute-done.1.w1
  13.4 0.6 first.1
  14.0 2.0 %collective-permute-start.4 = (bf16[128,128]{1,0:T(8,128)(2,1)S(1)}, bf16[128,128]{1,0:T(8,128)(2,1)S(1)}, u32[]{:S(2)}, u32[]{:S(2)}) collective-permute-start(bf16[128,128]{1,0:T(8,128)(2,1)S(1)} %get-tuple-element.114), channel_id=1, source_target_pairs={{4,8},{8,4},{5,9},{9,5},{6,10},{10,6},{7,11},{11,7},{12,16},{16,12... | collective-permute-start | bytes 98312 | tf_op jit(solution)/shard_map/ppermute | solution.py:540
  16.0 2.8 %collective-permute-start.5 = (bf16[128,128]{1,0:T(8,128)(2,1)S(1)}, bf16[128,128]{1,0:T(8,128)(2,1)S(1)}, u32[]{:S(2)}, u32[]{:S(2)}) collective-permute-start(bf16[128,128]{1,0:T(8,128)(2,1)S(1)} %get-tuple-element.115), channel_id=1, source_target_pairs={{2,4},{4,2},{3,5},{5,3},{6,8},{8,6},{7,9},{9,7},{10,12},{12,10},{1... | collective-permute-start | bytes 98312 | tf_op jit(solution)/shard_map/ppermute | solution.py:540
  18.8 0.8 collective-permute-start.6
  19.7 1.0 collective-permute-done.4.refs_8_
  21.1 1.0 opening.1
  22.1 1.4 %collective-permute-done.5.refs_9_ = bf16[128,128]{1,0:T(8,128)(2,1)S(1)} collective-permute-done((bf16[128,128]{1,0:T(8,128)(2,1)S(1)}, bf16[128,128]{1,0:T(8,128)(2,1)S(1)}, u32[]{:S(2)}, u32[]{:S(2)}) %collective-permute-start.5) | collective-permute-done | bytes 32800 | tf_op jit(solution)/shard_map/ppermute | solution.py:540
  23.5 2.2 %collective-permute-done.6.refs_10_ = bf16[128,128]{1,0:T(8,128)(2,1)S(1)} collective-permute-done((bf16[128,128]{1,0:T(8,128)(2,1)S(1)}, bf16[128,128]{1,0:T(8,128)(2,1)S(1)}, u32[]{:S(2)}, u32[]{:S(2)}) %collective-permute-start.6) | collective-permute-done | bytes 32800 | tf_op jit(solution)/shard_map/ppermute | solution.py:540
  26.4 1.8 %collective-permute-start.11 = (bf16[128,128]{1,0:T(8,128)(2,1)S(1)}, bf16[128,128]{1,0:T(8,128)(2,1)S(1)}, u32[]{:S(2)}, u32[]{:S(2)}) collective-permute-start(bf16[128,128]{1,0:T(8,128)(2,1)S(1)} %get-tuple-element.125), channel_id=1, source_target_pairs={{2,4},{4,2},{3,5},{5,3},{6,8},{8,6},{7,9},{9,7},{10,12},{12,10},{1... | collective-permute-start | bytes 98312 | tf_op jit(solution)/shard_map/ppermute | solution.py:540
  28.2 3.1 %collective-permute-start.12 = (bf16[128,128]{1,0:T(8,128)(2,1)S(1)}, bf16[128,128]{1,0:T(8,128)(2,1)S(1)}, u32[]{:S(2)}, u32[]{:S(2)}) collective-permute-start(bf16[128,128]{1,0:T(8,128)(2,1)S(1)} %get-tuple-element.126), channel_id=1, source_target_pairs={{1,2},{2,1},{3,4},{4,3},{5,6},{6,5},{7,8},{8,7},{9,10},{10,9},{11,... | collective-permute-start | bytes 98312 | tf_op jit(solution)/shard_map/ppermute | solution.py:540
  31.3 1.9 %collective-permute-done.10.refs_8_ = bf16[128,128]{1,0:T(8,128)(2,1)S(1)} collective-permute-done((bf16[128,128]{1,0:T(8,128)(2,1)S(1)}, bf16[128,128]{1,0:T(8,128)(2,1)S(1)}, u32[]{:S(2)}, u32[]{:S(2)}) %collective-permute-start.10) | collective-permute-done | bytes 32800 | tf_op jit(solution)/shard_map/ppermute | solution.py:540
  33.2 1.1 inner.7
  34.3 0.9 collective-permute-done.12.refs_10_
  35.9 0.9 collective-permute-start.16
  36.8 3.0 %collective-permute-start.17 = (bf16[128,128]{1,0:T(8,128)(2,1)S(1)}, bf16[128,128]{1,0:T(8,128)(2,1)S(1)}, u32[]{:S(2)}, u32[]{:S(2)}) collective-permute-start(bf16[128,128]{1,0:T(8,128)(2,1)S(1)} %get-tuple-element.136), channel_id=1, source_target_pairs={{2,4},{4,2},{3,5},{5,3},{6,8},{8,6},{7,9},{9,7},{10,12},{12,10},{1... | collective-permute-start | bytes 98312 | tf_op jit(solution)/shard_map/ppermute | solution.py:540
  39.8 2.4 %collective-permute-start.18 = (bf16[128,128]{1,0:T(8,128)(2,1)S(1)}, bf16[128,128]{1,0:T(8,128)(2,1)S(1)}, u32[]{:S(2)}, u32[]{:S(2)}) collective-permute-start(bf16[128,128]{1,0:T(8,128)(2,1)S(1)} %get-tuple-element.137), channel_id=1, source_target_pairs={{1,2},{2,1},{3,4},{4,3},{5,6},{6,5},{7,8},{8,7},{9,10},{10,9},{11,... | collective-permute-start | bytes 98312 | tf_op jit(solution)/shard_map/ppermute | solution.py:540
  42.6 1.1 inner.8
  43.7 0.7 collective-permute-done.17.refs_9_
  44.4 2.4 %collective-permute-done.18.refs_10_ = bf16[128,128]{1,0:T(8,128)(2,1)S(1)} collective-permute-done((bf16[128,128]{1,0:T(8,128)(2,1)S(1)}, bf16[128,128]{1,0:T(8,128)(2,1)S(1)}, u32[]{:S(2)}, u32[]{:S(2)}) %collective-permute-start.18) | collective-permute-done | bytes 32800 | tf_op jit(solution)/shard_map/ppermute | solution.py:540
  47.5 3.3 %collective-permute-start.23 = (bf16[128,128]{1,0:T(8,128)(2,1)S(1)}, bf16[128,128]{1,0:T(8,128)(2,1)S(1)}, u32[]{:S(2)}, u32[]{:S(2)}) collective-permute-start(bf16[128,128]{1,0:T(8,128)(2,1)S(1)} %get-tuple-element.147), channel_id=1, source_target_pairs={{2,4},{4,2},{3,5},{5,3},{6,8},{8,6},{7,9},{9,7},{10,12},{12,10},{1... | collective-permute-start | bytes 98312 | tf_op jit(solution)/shard_map/ppermute | solution.py:540
  50.8 1.5 %collective-permute-start.24 = (bf16[128,128]{1,0:T(8,128)(2,1)S(1)}, bf16[128,128]{1,0:T(8,128)(2,1)S(1)}, u32[]{:S(2)}, u32[]{:S(2)}) collective-permute-start(bf16[128,128]{1,0:T(8,128)(2,1)S(1)} %get-tuple-element.148), channel_id=1, source_target_pairs={{1,2},{2,1},{3,4},{4,3},{5,6},{6,5},{7,8},{8,7},{9,10},{10,9},{11,... | collective-permute-start | bytes 98312 | tf_op jit(solution)/shard_map/ppermute | solution.py:540
  52.3 0.9 collective-permute-start.26
  53.2 1.0 collective-permute-done.22.refs_8_
  54.2 1.1 inner.9
  55.4 2.5 %collective-permute-done.24.refs_10_ = bf16[128,128]{1,0:T(8,128)(2,1)S(1)} collective-permute-done((bf16[128,128]{1,0:T(8,128)(2,1)S(1)}, bf16[128,128]{1,0:T(8,128)(2,1)S(1)}, u32[]{:S(2)}, u32[]{:S(2)}) %collective-permute-start.24) | collective-permute-done | bytes 32800 | tf_op jit(solution)/shard_map/ppermute | solution.py:540
  58.4 3.4 %collective-permute-start.29 = (bf16[128,128]{1,0:T(8,128)(2,1)S(1)}, bf16[128,128]{1,0:T(8,128)(2,1)S(1)}, u32[]{:S(2)}, u32[]{:S(2)}) collective-permute-start(bf16[128,128]{1,0:T(8,128)(2,1)S(1)} %get-tuple-element.158), channel_id=1, source_target_pairs={{2,4},{4,2},{3,5},{5,3},{6,8},{8,6},{7,9},{9,7},{10,12},{12,10},{1... | collective-permute-start | bytes 98312 | tf_op jit(solution)/shard_map/ppermute | solution.py:540
  61.8 1.4 %collective-permute-start.30 = (bf16[128,128]{1,0:T(8,128)(2,1)S(1)}, bf16[128,128]{1,0:T(8,128)(2,1)S(1)}, u32[]{:S(2)}, u32[]{:S(2)}) collective-permute-start(bf16[128,128]{1,0:T(8,128)(2,1)S(1)} %get-tuple-element.159), channel_id=1, source_target_pairs={{1,2},{2,1},{3,4},{4,3},{5,6},{6,5},{7,8},{8,7},{9,10},{10,9},{11,... | collective-permute-start | bytes 98312 | tf_op jit(solution)/shard_map/ppermute | solution.py:540
  63.5 1.8 %collective-permute-done.28.refs_8_ = bf16[128,128]{1,0:T(8,128)(2,1)S(1)} collective-permute-done((bf16[128,128]{1,0:T(8,128)(2,1)S(1)}, bf16[128,128]{1,0:T(8,128)(2,1)S(1)}, u32[]{:S(2)}, u32[]{:S(2)}) %collective-permute-start.28) | collective-permute-done | bytes 32800 | tf_op jit(solution)/shard_map/ppermute | solution.py:540
  65.3 1.1 inner.10
  66.4 2.4 %collective-permute-done.30.refs_10_ = bf16[128,128]{1,0:T(8,128)(2,1)S(1)} collective-permute-done((bf16[128,128]{1,0:T(8,128)(2,1)S(1)}, bf16[128,128]{1,0:T(8,128)(2,1)S(1)}, u32[]{:S(2)}, u32[]{:S(2)}) %collective-permute-start.30) | collective-permute-done | bytes 32800 | tf_op jit(solution)/shard_map/ppermute | solution.py:540
  69.4 2.6 %collective-permute-start.35 = (bf16[128,128]{1,0:T(8,128)(2,1)S(1)}, bf16[128,128]{1,0:T(8,128)(2,1)S(1)}, u32[]{:S(2)}, u32[]{:S(2)}) collective-permute-start(bf16[128,128]{1,0:T(8,128)(2,1)S(1)} %get-tuple-element.169), channel_id=1, source_target_pairs={{2,4},{4,2},{3,5},{5,3},{6,8},{8,6},{7,9},{9,7},{10,12},{12,10},{1... | collective-permute-start | bytes 98312 | tf_op jit(solution)/shard_map/ppermute | solution.py:540
  72.0 2.2 %collective-permute-start.36 = (bf16[128,128]{1,0:T(8,128)(2,1)S(1)}, bf16[128,128]{1,0:T(8,128)(2,1)S(1)}, u32[]{:S(2)}, u32[]{:S(2)}) collective-permute-start(bf16[128,128]{1,0:T(8,128)(2,1)S(1)} %get-tuple-element.170), channel_id=1, source_target_pairs={{1,2},{2,1},{3,4},{4,3},{5,6},{6,5},{7,8},{8,7},{9,10},{10,9},{11,... | collective-permute-start | bytes 98312 | tf_op jit(solution)/shard_map/ppermute | solution.py:540
  74.4 1.9 %collective-permute-done.34.refs_8_ = bf16[128,128]{1,0:T(8,128)(2,1)S(1)} collective-permute-done((bf16[128,128]{1,0:T(8,128)(2,1)S(1)}, bf16[128,128]{1,0:T(8,128)(2,1)S(1)}, u32[]{:S(2)}, u32[]{:S(2)}) %collective-permute-start.34) | collective-permute-done | bytes 32800 | tf_op jit(solution)/shard_map/ppermute | solution.py:540
  76.3 1.3 %inner.11 = (f32[2048,128]{1,0:T(8,128)S(1)}, f32[2048,128]{1,0:T(8,128)S(1)}, f32[256,128]{1,0:T(8,128)S(1)}) custom-call(bf16[2048,384]{1,0:T(8,128)(2,1)S(1)} %get-tuple-element.102.refs_0_.refs_1_, bf16[2048,256]{1,0:T(8,128)(2,1)S(1)} %get-tuple-element.103.refs_1_.refs_2_, bf16[256,2048]{1,0:T(8,128)(2,1)S(1)} %get-tuple-element.110.refs_2_.refs_5_, ...), custom_call_target="tpu_custom_call" | custom-call | flops 201326592 | bytes 3145728 | tf_op jit(solution)/shard_map/inner/pallas_call | solution.py:318
  77.6 1.3 %collective-permute-done.36.refs_10_ = bf16[128,128]{1,0:T(8,128)(2,1)S(1)} collective-permute-done((bf16[128,128]{1,0:T(8,128)(2,1)S(1)}, bf16[128,128]{1,0:T(8,128)(2,1)S(1)}, u32[]{:S(2)}, u32[]{:S(2)}) %collective-permute-start.36) | collective-permute-done | bytes 32800 | tf_op jit(solution)/shard_map/ppermute | solution.py:540
  79.4 0.5 collective-permute-start.40
  79.9 3.0 %collective-permute-start.41 = (bf16[128,128]{1,0:T(8,128)(2,1)S(1)}, bf16[128,128]{1,0:T(8,128)(2,1)S(1)}, u32[]{:S(2)}, u32[]{:S(2)}) collective-permute-start(bf16[128,128]{1,0:T(8,128)(2,1)S(1)} %get-tuple-element.180), channel_id=1, source_target_pairs={{2,4},{4,2},{3,5},{5,3},{6,8},{8,6},{7,9},{9,7},{10,12},{12,10},{1... | collective-permute-start | bytes 98312 | tf_op jit(solution)/shard_map/ppermute | solution.py:540
  82.9 2.4 %collective-permute-start.42 = (bf16[128,128]{1,0:T(8,128)(2,1)S(1)}, bf16[128,128]{1,0:T(8,128)(2,1)S(1)}, u32[]{:S(2)}, u32[]{:S(2)}) collective-permute-start(bf16[128,128]{1,0:T(8,128)(2,1)S(1)} %get-tuple-element.181), channel_id=1, source_target_pairs={{1,2},{2,1},{3,4},{4,3},{5,6},{6,5},{7,8},{8,7},{9,10},{10,9},{11,... | collective-permute-start | bytes 98312 | tf_op jit(solution)/shard_map/ppermute | solution.py:540
  85.3 0.8 collective-permute-done.40.refs_8_
  86.0 1.1 inner.12
  87.4 2.4 %collective-permute-done.42.refs_10_ = bf16[128,128]{1,0:T(8,128)(2,1)S(1)} collective-permute-done((bf16[128,128]{1,0:T(8,128)(2,1)S(1)}, bf16[128,128]{1,0:T(8,128)(2,1)S(1)}, u32[]{:S(2)}, u32[]{:S(2)}) %collective-permute-start.42) | collective-permute-done | bytes 32800 | tf_op jit(solution)/shard_map/ppermute | solution.py:540
  90.6 3.2 %collective-permute-start.47 = (bf16[128,128]{1,0:T(8,128)(2,1)S(1)}, bf16[128,128]{1,0:T(8,128)(2,1)S(1)}, u32[]{:S(2)}, u32[]{:S(2)}) collective-permute-start(bf16[128,128]{1,0:T(8,128)(2,1)S(1)} %get-tuple-element.189), channel_id=1, source_target_pairs={{2,4},{4,2},{3,5},{5,3},{6,8},{8,6},{7,9},{9,7},{10,12},{12,10},{1... | collective-permute-start | bytes 98312 | tf_op jit(solution)/shard_map/ppermute | solution.py:540
  93.8 1.6 %collective-permute-start.48 = (bf16[128,128]{1,0:T(8,128)(2,1)S(1)}, bf16[128,128]{1,0:T(8,128)(2,1)S(1)}, u32[]{:S(2)}, u32[]{:S(2)}) collective-permute-start(bf16[128,128]{1,0:T(8,128)(2,1)S(1)} %get-tuple-element.190), channel_id=1, source_target_pairs={{1,2},{2,1},{3,4},{4,3},{5,6},{6,5},{7,8},{8,7},{9,10},{10,9},{11,... | collective-permute-start | bytes 98312 | tf_op jit(solution)/shard_map/ppermute | solution.py:540
  95.4 0.8 collective-permute-start.50
  96.2 1.1 collective-permute-done.46.refs_5_
  97.3 0.8 inner.13.refs_4_
  98.2 2.6 %collective-permute-done.48.refs_7_ = bf16[128,128]{1,0:T(8,128)(2,1)S(1)} collective-permute-done((bf16[128,128]{1,0:T(8,128)(2,1)S(1)}, bf16[128,128]{1,0:T(8,128)(2,1)S(1)}, u32[]{:S(2)}, u32[]{:S(2)}) %collective-permute-start.48) | collective-permute-done | bytes 32800 | tf_op jit(solution)/shard_map/ppermute | solution.py:540
  100.8 1.5 %last.1 = (f32[2048,128]{1,0:T(8,128)S(1)}, f32[64,128]{1,0:T(8,128)S(1)}, f32[64,128]{1,0:T(8,128)S(1)}) custom-call(s32[1]{0:T(128)} %bitcast.place_ref.refs_0_, bf16[2048,384]{1,0:T(8,128)(2,1)S(1)} %get-tuple-element.102.refs_0_.refs_1_, bf16[2048,256]{1,0:T(8,128)(2,1)S(1)} %get-tuple-element.103.refs_1_.refs_2_, ...), custom_call_target="tpu_custom_call" | custom-call | tf_op jit(solution)/shard_map/last/pallas_call | solution.py:429
  102.4 1.2 collective-permute-done.52
  103.6 0.9 collective-permute-start.54
  104.5 2.5 %collective-permute-start.53 = (f32[64,128]{1,0:T(8,128)S(1)}, f32[64,128]{1,0:T(8,128)S(1)}, u32[]{:S(2)}, u32[]{:S(2)}) collective-permute-start(f32[64,128]{1,0:T(8,128)S(1)} %add.25), channel_id=1, source_target_pairs={{0,2},{1,3},{2,0},{3,1},{4,6},{5,7},{6,4},{7,5},{8,10},{9,11},{10,... | collective-permute-start | bytes 98312 | tf_op jit(solution)/shard_map/ppermute | solution.py:523
  107.0 1.5 %collective-permute-done.55 = f32[64,128]{1,0:T(8,128)S(1)} collective-permute-done((f32[64,128]{1,0:T(8,128)S(1)}, f32[64,128]{1,0:T(8,128)S(1)}, u32[]{:S(2)}, u32[]{:S(2)}) %collective-permute-start.55) | collective-permute-done | bytes 32800 | tf_op jit(solution)/shard_map/ppermute | solution.py:523
  108.5 0.4 collective-permute-done.53
  109.0 2.1 %collective-permute-start.58 = (f32[64,128]{1,0:T(8,128)S(1)}, f32[64,128]{1,0:T(8,128)S(1)}, u32[]{:S(2)}, u32[]{:S(2)}) collective-permute-start(f32[64,128]{1,0:T(8,128)S(1)} %add_add_fusion.1), channel_id=1, source_target_pairs={{0,24},{1,25},{2,26},{3,27},{4,28},{5,29},{6,30},{7,31},{8,16},{9,... | collective-permute-start | bytes 98312 | tf_op jit(solution)/shard_map/ppermute | solution.py:523
  111.0 2.4 %collective-permute-start.56 = (f32[64,128]{1,0:T(8,128)S(1)}, f32[64,128]{1,0:T(8,128)S(1)}, u32[]{:S(2)}, u32[]{:S(2)}) collective-permute-start(f32[64,128]{1,0:T(8,128)S(1)} %add_add_fusion.1), channel_id=1, source_target_pairs={{0,8},{1,9},{2,10},{3,11},{4,12},{5,13},{6,14},{7,15},{8,0},{9,1},... | collective-permute-start | bytes 98312 | tf_op jit(solution)/shard_map/ppermute | solution.py:523
  113.4 1.5 %collective-permute-done.58 = f32[64,128]{1,0:T(8,128)S(1)} collective-permute-done((f32[64,128]{1,0:T(8,128)S(1)}, f32[64,128]{1,0:T(8,128)S(1)}, u32[]{:S(2)}, u32[]{:S(2)}) %collective-permute-start.58) | collective-permute-done | bytes 32800 | tf_op jit(solution)/shard_map/ppermute | solution.py:523
  114.9 0.9 collective-permute-done.57
  115.9 1.2 collective-permute-done.59.refs_2_
  117.1 7.1 %finish.1 = f32[2048,128]{1,0:T(8,128)} custom-call(s32[1]{0:T(128)} %bitcast.place_ref.refs_0_, f32[64,128]{1,0:T(8,128)S(1)} %add_add_fusion.refs_1_, f32[64,128]{1,0:T(8,128)S(1)} %collective-permute-done.59.refs_2_, f32[2048,128]{1,0:T(8,128)S(1)} %get-tuple-element.196.refs_3_), custom_call_target="tpu_custom_call" | custom-call | tf_op jit(solution)/shard_map/finish/pallas_call | solution.py:510
  (78 shorter events, 6.1 us)
Async XLA Ops:
  0.0 12.6 %collective-permute-start.3 = (s32[1,256]{1,0:T(1,128)}, s32[1,256]{1,0:T(1,128)S(1)}, u32[]{:S(2)}, u32[]{:S(2)}) collective-permute-start(s32[1,256]{1,0:T(1,128)} %bitcast.10), channel_id=1, source_target_pairs={{4,8},{8,4},{5,9},{9,5},{6,10},{10,6},{7,11},{11,7},{12,16},{16,12... | collective-permute-start | bytes 3080 | tf_op jit(solution)/shard_map/ppermute | solution.py:540
  6.0 6.6 %collective-permute-start.2 = (s32[1,256]{1,0:T(1,128)}, s32[1,256]{1,0:T(1,128)S(1)}, u32[]{:S(2)}, u32[]{:S(2)}) collective-permute-start(s32[1,256]{1,0:T(1,128)} %bitcast.11), channel_id=1, source_target_pairs={{0,4},{4,0},{1,5},{5,1},{2,6},{6,2},{3,7},{7,3},{8,12},{12,8},{9,1... | collective-permute-start | bytes 3080 | tf_op jit(solution)/shard_map/ppermute | solution.py:540
  6.0 7.4 %collective-permute-start.1 = (s32[1,256]{1,0:T(1,128)}, s32[1,256]{1,0:T(1,128)S(1)}, u32[]{:S(2)}, u32[]{:S(2)}) collective-permute-start(s32[1,256]{1,0:T(1,128)} %bitcast.12), channel_id=1, source_target_pairs={{2,4},{4,2},{3,5},{5,3},{6,8},{8,6},{7,9},{9,7},{10,12},{12,10},{1... | collective-permute-start | bytes 3080 | tf_op jit(solution)/shard_map/ppermute | solution.py:540
  8.8 4.5 %collective-permute-start = (s32[1,256]{1,0:T(1,128)}, s32[1,256]{1,0:T(1,128)S(1)}, u32[]{:S(2)}, u32[]{:S(2)}) collective-permute-start(s32[1,256]{1,0:T(1,128)} %bitcast.13), channel_id=1, source_target_pairs={{0,2},{2,0},{1,3},{3,1},{4,6},{6,4},{5,7},{7,5},{8,10},{10,8},{9,1... | collective-permute-start | bytes 3080 | tf_op jit(solution)/shard_map/ppermute | solution.py:540
  14.0 6.7 %collective-permute-start.4 = (bf16[128,128]{1,0:T(8,128)(2,1)S(1)}, bf16[128,128]{1,0:T(8,128)(2,1)S(1)}, u32[]{:S(2)}, u32[]{:S(2)}) collective-permute-start(bf16[128,128]{1,0:T(8,128)(2,1)S(1)} %get-tuple-element.114), channel_id=1, source_target_pairs={{4,8},{8,4},{5,9},{9,5},{6,10},{10,6},{7,11},{11,7},{12,16},{16,12... | collective-permute-start | bytes 98312 | tf_op jit(solution)/shard_map/ppermute | solution.py:540
  16.0 7.5 %collective-permute-start.5 = (bf16[128,128]{1,0:T(8,128)(2,1)S(1)}, bf16[128,128]{1,0:T(8,128)(2,1)S(1)}, u32[]{:S(2)}, u32[]{:S(2)}) collective-permute-start(bf16[128,128]{1,0:T(8,128)(2,1)S(1)} %get-tuple-element.115), channel_id=1, source_target_pairs={{2,4},{4,2},{3,5},{5,3},{6,8},{8,6},{7,9},{9,7},{10,12},{12,10},{1... | collective-permute-start | bytes 98312 | tf_op jit(solution)/shard_map/ppermute | solution.py:540
  18.8 6.9 %collective-permute-start.6 = (bf16[128,128]{1,0:T(8,128)(2,1)S(1)}, bf16[128,128]{1,0:T(8,128)(2,1)S(1)}, u32[]{:S(2)}, u32[]{:S(2)}) collective-permute-start(bf16[128,128]{1,0:T(8,128)(2,1)S(1)} %get-tuple-element.116), channel_id=1, source_target_pairs={{1,2},{2,1},{3,4},{4,3},{5,6},{6,5},{7,8},{8,7},{9,10},{10,9},{11,... | collective-permute-start | bytes 98312 | tf_op jit(solution)/shard_map/ppermute | solution.py:540
  19.7 6.1 %collective-permute-start.7 = (bf16[128,128]{1,0:T(8,128)(2,1)S(1)}, bf16[128,128]{1,0:T(8,128)(2,1)S(1)}, u32[]{:S(2)}, u32[]{:S(2)}) collective-permute-start(bf16[128,128]{1,0:T(8,128)(2,1)S(1)} %get-tuple-element.117), channel_id=1, source_target_pairs={{0,4},{4,0},{1,5},{5,1},{2,6},{6,2},{3,7},{7,3},{8,12},{12,8},{9,1... | collective-permute-start | bytes 98312 | tf_op jit(solution)/shard_map/ppermute | solution.py:540
  19.7 6.1 %collective-permute-start.8 = (bf16[128,128]{1,0:T(8,128)(2,1)S(1)}, bf16[128,128]{1,0:T(8,128)(2,1)S(1)}, u32[]{:S(2)}, u32[]{:S(2)}) collective-permute-start(bf16[128,128]{1,0:T(8,128)(2,1)S(1)} %get-tuple-element.118), channel_id=1, source_target_pairs={{0,2},{2,0},{1,3},{3,1},{4,6},{6,4},{5,7},{7,5},{8,10},{10,8},{9,1... | collective-permute-start | bytes 98312 | tf_op jit(solution)/shard_map/ppermute | solution.py:540
  20.7 5.1 %collective-permute-start.9 = (bf16[128,128]{1,0:T(8,128)(2,1)S(1)}, bf16[128,128]{1,0:T(8,128)(2,1)S(1)}, u32[]{:S(2)}, u32[]{:S(2)}) collective-permute-start(bf16[128,128]{1,0:T(8,128)(2,1)S(1)} %get-tuple-element.119), channel_id=1, source_target_pairs={{0,1},{1,0},{2,3},{3,2},{4,5},{5,4},{6,7},{7,6},{8,9},{9,8},{10,11... | collective-permute-start | bytes 98312 | tf_op jit(solution)/shard_map/ppermute | solution.py:540
  26.2 7.0 %collective-permute-start.10 = (bf16[128,128]{1,0:T(8,128)(2,1)S(1)}, bf16[128,128]{1,0:T(8,128)(2,1)S(1)}, u32[]{:S(2)}, u32[]{:S(2)}) collective-permute-start(bf16[128,128]{1,0:T(8,128)(2,1)S(1)} %get-tuple-element.124), channel_id=1, source_target_pairs={{4,8},{8,4},{5,9},{9,5},{6,10},{10,6},{7,11},{11,7},{12,16},{16,12... | collective-permute-start | bytes 98312 | tf_op jit(solution)/shard_map/ppermute | solution.py:540
  26.4 7.9 %collective-permute-start.11 = (bf16[128,128]{1,0:T(8,128)(2,1)S(1)}, bf16[128,128]{1,0:T(8,128)(2,1)S(1)}, u32[]{:S(2)}, u32[]{:S(2)}) collective-permute-start(bf16[128,128]{1,0:T(8,128)(2,1)S(1)} %get-tuple-element.125), channel_id=1, source_target_pairs={{2,4},{4,2},{3,5},{5,3},{6,8},{8,6},{7,9},{9,7},{10,12},{12,10},{1... | collective-permute-start | bytes 98312 | tf_op jit(solution)/shard_map/ppermute | solution.py:540
  28.2 7.0 %collective-permute-start.12 = (bf16[128,128]{1,0:T(8,128)(2,1)S(1)}, bf16[128,128]{1,0:T(8,128)(2,1)S(1)}, u32[]{:S(2)}, u32[]{:S(2)}) collective-permute-start(bf16[128,128]{1,0:T(8,128)(2,1)S(1)} %get-tuple-element.126), channel_id=1, source_target_pairs={{1,2},{2,1},{3,4},{4,3},{5,6},{6,5},{7,8},{8,7},{9,10},{10,9},{11,... | collective-permute-start | bytes 98312 | tf_op jit(solution)/shard_map/ppermute | solution.py:540
  31.3 4.2 %collective-permute-start.13 = (bf16[128,128]{1,0:T(8,128)(2,1)S(1)}, bf16[128,128]{1,0:T(8,128)(2,1)S(1)}, u32[]{:S(2)}, u32[]{:S(2)}) collective-permute-start(bf16[128,128]{1,0:T(8,128)(2,1)S(1)} %get-tuple-element.127), channel_id=1, source_target_pairs={{0,4},{4,0},{1,5},{5,1},{2,6},{6,2},{3,7},{7,3},{8,12},{12,8},{9,1... | collective-permute-start | bytes 98312 | tf_op jit(solution)/shard_map/ppermute | solution.py:540
  31.3 4.2 %collective-permute-start.14 = (bf16[128,128]{1,0:T(8,128)(2,1)S(1)}, bf16[128,128]{1,0:T(8,128)(2,1)S(1)}, u32[]{:S(2)}, u32[]{:S(2)}) collective-permute-start(bf16[128,128]{1,0:T(8,128)(2,1)S(1)} %get-tuple-element.128), channel_id=1, source_target_pairs={{0,2},{2,0},{1,3},{3,1},{4,6},{6,4},{5,7},{7,5},{8,10},{10,8},{9,1... | collective-permute-start | bytes 98312 | tf_op jit(solution)/shard_map/ppermute | solution.py:540
  33.2 2.3 %collective-permute-start.15 = (bf16[128,128]{1,0:T(8,128)(2,1)S(1)}, bf16[128,128]{1,0:T(8,128)(2,1)S(1)}, u32[]{:S(2)}, u32[]{:S(2)}) collective-permute-start(bf16[128,128]{1,0:T(8,128)(2,1)S(1)} %get-tuple-element.129), channel_id=1, source_target_pairs={{0,1},{1,0},{2,3},{3,2},{4,5},{5,4},{6,7},{7,6},{8,9},{9,8},{10,11... | collective-permute-start | bytes 98312 | tf_op jit(solution)/shard_map/ppermute | solution.py:540
  35.9 6.7 %collective-permute-start.16 = (bf16[128,128]{1,0:T(8,128)(2,1)S(1)}, bf16[128,128]{1,0:T(8,128)(2,1)S(1)}, u32[]{:S(2)}, u32[]{:S(2)}) collective-permute-start(bf16[128,128]{1,0:T(8,128)(2,1)S(1)} %get-tuple-element.135), channel_id=1, source_target_pairs={{4,8},{8,4},{5,9},{9,5},{6,10},{10,6},{7,11},{11,7},{12,16},{16,12... | collective-permute-start | bytes 98312 | tf_op jit(solution)/shard_map/ppermute | solution.py:540
  36.8 7.5 %collective-permute-start.17 = (bf16[128,128]{1,0:T(8,128)(2,1)S(1)}, bf16[128,128]{1,0:T(8,128)(2,1)S(1)}, u32[]{:S(2)}, u32[]{:S(2)}) collective-permute-start(bf16[128,128]{1,0:T(8,128)(2,1)S(1)} %get-tuple-element.136), channel_id=1, source_target_pairs={{2,4},{4,2},{3,5},{5,3},{6,8},{8,6},{7,9},{9,7},{10,12},{12,10},{1... | collective-permute-start | bytes 98312 | tf_op jit(solution)/shard_map/ppermute | solution.py:540
  39.8 6.9 %collective-permute-start.18 = (bf16[128,128]{1,0:T(8,128)(2,1)S(1)}, bf16[128,128]{1,0:T(8,128)(2,1)S(1)}, u32[]{:S(2)}, u32[]{:S(2)}) collective-permute-start(bf16[128,128]{1,0:T(8,128)(2,1)S(1)} %get-tuple-element.137), channel_id=1, source_target_pairs={{1,2},{2,1},{3,4},{4,3},{5,6},{6,5},{7,8},{8,7},{9,10},{10,9},{11,... | collective-permute-start | bytes 98312 | tf_op jit(solution)/shard_map/ppermute | solution.py:540
  42.2 4.6 %collective-permute-start.19 = (bf16[128,128]{1,0:T(8,128)(2,1)S(1)}, bf16[128,128]{1,0:T(8,128)(2,1)S(1)}, u32[]{:S(2)}, u32[]{:S(2)}) collective-permute-start(bf16[128,128]{1,0:T(8,128)(2,1)S(1)} %get-tuple-element.138), channel_id=1, source_target_pairs={{0,4},{4,0},{1,5},{5,1},{2,6},{6,2},{3,7},{7,3},{8,12},{12,8},{9,1... | collective-permute-start | bytes 98312 | tf_op jit(solution)/shard_map/ppermute | solution.py:540
  42.2 4.6 %collective-permute-start.20 = (bf16[128,128]{1,0:T(8,128)(2,1)S(1)}, bf16[128,128]{1,0:T(8,128)(2,1)S(1)}, u32[]{:S(2)}, u32[]{:S(2)}) collective-permute-start(bf16[128,128]{1,0:T(8,128)(2,1)S(1)} %get-tuple-element.139), channel_id=1, source_target_pairs={{0,2},{2,0},{1,3},{3,1},{4,6},{6,4},{5,7},{7,5},{8,10},{10,8},{9,1... | collective-permute-start | bytes 98312 | tf_op jit(solution)/shard_map/ppermute | solution.py:540
  42.6 4.2 %collective-permute-start.21 = (bf16[128,128]{1,0:T(8,128)(2,1)S(1)}, bf16[128,128]{1,0:T(8,128)(2,1)S(1)}, u32[]{:S(2)}, u32[]{:S(2)}) collective-permute-start(bf16[128,128]{1,0:T(8,128)(2,1)S(1)} %get-tuple-element.140), channel_id=1, source_target_pairs={{0,1},{1,0},{2,3},{3,2},{4,5},{5,4},{6,7},{7,6},{8,9},{9,8},{10,11... | collective-permute-start | bytes 98312 | tf_op jit(solution)/shard_map/ppermute | solution.py:540
  47.2 7.0 %collective-permute-start.22 = (bf16[128,128]{1,0:T(8,128)(2,1)S(1)}, bf16[128,128]{1,0:T(8,128)(2,1)S(1)}, u32[]{:S(2)}, u32[]{:S(2)}) collective-permute-start(bf16[128,128]{1,0:T(8,128)(2,1)S(1)} %get-tuple-element.146), channel_id=1, source_target_pairs={{4,8},{8,4},{5,9},{9,5},{6,10},{10,6},{7,11},{11,7},{12,16},{16,12... | collective-permute-start | bytes 98312 | tf_op jit(solution)/shard_map/ppermute | solution.py:540
  47.5 7.8 %collective-permute-start.23 = (bf16[128,128]{1,0:T(8,128)(2,1)S(1)}, bf16[128,128]{1,0:T(8,128)(2,1)S(1)}, u32[]{:S(2)}, u32[]{:S(2)}) collective-permute-start(bf16[128,128]{1,0:T(8,128)(2,1)S(1)} %get-tuple-element.147), channel_id=1, source_target_pairs={{2,4},{4,2},{3,5},{5,3},{6,8},{8,6},{7,9},{9,7},{10,12},{12,10},{1... | collective-permute-start | bytes 98312 | tf_op jit(solution)/shard_map/ppermute | solution.py:540
  50.8 7.0 %collective-permute-start.24 = (bf16[128,128]{1,0:T(8,128)(2,1)S(1)}, bf16[128,128]{1,0:T(8,128)(2,1)S(1)}, u32[]{:S(2)}, u32[]{:S(2)}) collective-permute-start(bf16[128,128]{1,0:T(8,128)(2,1)S(1)} %get-tuple-element.148), channel_id=1, source_target_pairs={{1,2},{2,1},{3,4},{4,3},{5,6},{6,5},{7,8},{8,7},{9,10},{10,9},{11,... | collective-permute-start | bytes 98312 | tf_op jit(solution)/shard_map/ppermute | solution.py:540
  52.3 5.5 %collective-permute-start.25 = (bf16[128,128]{1,0:T(8,128)(2,1)S(1)}, bf16[128,128]{1,0:T(8,128)(2,1)S(1)}, u32[]{:S(2)}, u32[]{:S(2)}) collective-permute-start(bf16[128,128]{1,0:T(8,128)(2,1)S(1)} %get-tuple-element.149), channel_id=1, source_target_pairs={{0,4},{4,0},{1,5},{5,1},{2,6},{6,2},{3,7},{7,3},{8,12},{12,8},{9,1... | collective-permute-start | bytes 98312 | tf_op jit(solution)/shard_map/ppermute | solution.py:540
  52.3 5.5 %collective-permute-start.26 = (bf16[128,128]{1,0:T(8,128)(2,1)S(1)}, bf16[128,128]{1,0:T(8,128)(2,1)S(1)}, u32[]{:S(2)}, u32[]{:S(2)}) collective-permute-start(bf16[128,128]{1,0:T(8,128)(2,1)S(1)} %get-tuple-element.150), channel_id=1, source_target_pairs={{0,2},{2,0},{1,3},{3,1},{4,6},{6,4},{5,7},{7,5},{8,10},{10,8},{9,1... | collective-permute-start | bytes 98312 | tf_op jit(solution)/shard_map/ppermute | solution.py:540
  54.2 3.6 %collective-permute-start.27 = (bf16[128,128]{1,0:T(8,128)(2,1)S(1)}, bf16[128,128]{1,0:T(8,128)(2,1)S(1)}, u32[]{:S(2)}, u32[]{:S(2)}) collective-permute-start(bf16[128,128]{1,0:T(8,128)(2,1)S(1)} %get-tuple-element.151), channel_id=1, source_target_pairs={{0,1},{1,0},{2,3},{3,2},{4,5},{5,4},{6,7},{7,6},{8,9},{9,8},{10,11... | collective-permute-start | bytes 98312 | tf_op jit(solution)/shard_map/ppermute | solution.py:540
  58.2 7.1 %collective-permute-start.28 = (bf16[128,128]{1,0:T(8,128)(2,1)S(1)}, bf16[128,128]{1,0:T(8,128)(2,1)S(1)}, u32[]{:S(2)}, u32[]{:S(2)}) collective-permute-start(bf16[128,128]{1,0:T(8,128)(2,1)S(1)} %get-tuple-element.157), channel_id=1, source_target_pairs={{4,8},{8,4},{5,9},{9,5},{6,10},{10,6},{7,11},{11,7},{12,16},{16,12... | collective-permute-start | bytes 98312 | tf_op jit(solution)/shard_map/ppermute | solution.py:540
  58.4 8.0 %collective-permute-start.29 = (bf16[128,128]{1,0:T(8,128)(2,1)S(1)}, bf16[128,128]{1,0:T(8,128)(2,1)S(1)}, u32[]{:S(2)}, u32[]{:S(2)}) collective-permute-start(bf16[128,128]{1,0:T(8,128)(2,1)S(1)} %get-tuple-element.158), channel_id=1, source_target_pairs={{2,4},{4,2},{3,5},{5,3},{6,8},{8,6},{7,9},{9,7},{10,12},{12,10},{1... | collective-permute-start | bytes 98312 | tf_op jit(solution)/shard_map/ppermute | solution.py:540
  61.8 7.0 %collective-permute-start.30 = (bf16[128,128]{1,0:T(8,128)(2,1)S(1)}, bf16[128,128]{1,0:T(8,128)(2,1)S(1)}, u32[]{:S(2)}, u32[]{:S(2)}) collective-permute-start(bf16[128,128]{1,0:T(8,128)(2,1)S(1)} %get-tuple-element.159), channel_id=1, source_target_pairs={{1,2},{2,1},{3,4},{4,3},{5,6},{6,5},{7,8},{8,7},{9,10},{10,9},{11,... | collective-permute-start | bytes 98312 | tf_op jit(solution)/shard_map/ppermute | solution.py:540
  63.2 5.6 %collective-permute-start.31 = (bf16[128,128]{1,0:T(8,128)(2,1)S(1)}, bf16[128,128]{1,0:T(8,128)(2,1)S(1)}, u32[]{:S(2)}, u32[]{:S(2)}) collective-permute-start(bf16[128,128]{1,0:T(8,128)(2,1)S(1)} %get-tuple-element.160), channel_id=1, source_target_pairs={{0,4},{4,0},{1,5},{5,1},{2,6},{6,2},{3,7},{7,3},{8,12},{12,8},{9,1... | collective-permute-start | bytes 98312 | tf_op jit(solution)/shard_map/ppermute | solution.py:540
  63.2 5.6 %collective-permute-start.32 = (bf16[128,128]{1,0:T(8,128)(2,1)S(1)}, bf16[128,128]{1,0:T(8,128)(2,1)S(1)}, u32[]{:S(2)}, u32[]{:S(2)}) collective-permute-start(bf16[128,128]{1,0:T(8,128)(2,1)S(1)} %get-tuple-element.161), channel_id=1, source_target_pairs={{0,2},{2,0},{1,3},{3,1},{4,6},{6,4},{5,7},{7,5},{8,10},{10,8},{9,1... | collective-permute-start | bytes 98312 | tf_op jit(solution)/shard_map/ppermute | solution.py:540
  65.3 3.6 %collective-permute-start.33 = (bf16[128,128]{1,0:T(8,128)(2,1)S(1)}, bf16[128,128]{1,0:T(8,128)(2,1)S(1)}, u32[]{:S(2)}, u32[]{:S(2)}) collective-permute-start(bf16[128,128]{1,0:T(8,128)(2,1)S(1)} %get-tuple-element.162), channel_id=1, source_target_pairs={{0,1},{1,0},{2,3},{3,2},{4,5},{5,4},{6,7},{7,6},{8,9},{9,8},{10,11... | collective-permute-start | bytes 98312 | tf_op jit(solution)/shard_map/ppermute | solution.py:540
  69.2 7.0 %collective-permute-start.34 = (bf16[128,128]{1,0:T(8,128)(2,1)S(1)}, bf16[128,128]{1,0:T(8,128)(2,1)S(1)}, u32[]{:S(2)}, u32[]{:S(2)}) collective-permute-start(bf16[128,128]{1,0:T(8,128)(2,1)S(1)} %get-tuple-element.168), channel_id=1, source_target_pairs={{4,8},{8,4},{5,9},{9,5},{6,10},{10,6},{7,11},{11,7},{12,16},{16,12... | collective-permute-start | bytes 98312 | tf_op jit(solution)/shard_map/ppermute | solution.py:540
  69.4 8.2 %collective-permute-start.35 = (bf16[128,128]{1,0:T(8,128)(2,1)S(1)}, bf16[128,128]{1,0:T(8,128)(2,1)S(1)}, u32[]{:S(2)}, u32[]{:S(2)}) collective-permute-start(bf16[128,128]{1,0:T(8,128)(2,1)S(1)} %get-tuple-element.169), channel_id=1, source_target_pairs={{2,4},{4,2},{3,5},{5,3},{6,8},{8,6},{7,9},{9,7},{10,12},{12,10},{1... | collective-permute-start | bytes 98312 | tf_op jit(solution)/shard_map/ppermute | solution.py:540
  72.0 6.9 %collective-permute-start.36 = (bf16[128,128]{1,0:T(8,128)(2,1)S(1)}, bf16[128,128]{1,0:T(8,128)(2,1)S(1)}, u32[]{:S(2)}, u32[]{:S(2)}) collective-permute-start(bf16[128,128]{1,0:T(8,128)(2,1)S(1)} %get-tuple-element.170), channel_id=1, source_target_pairs={{1,2},{2,1},{3,4},{4,3},{5,6},{6,5},{7,8},{8,7},{9,10},{10,9},{11,... | collective-permute-start | bytes 98312 | tf_op jit(solution)/shard_map/ppermute | solution.py:540
  74.2 4.7 %collective-permute-start.37 = (bf16[128,128]{1,0:T(8,128)(2,1)S(1)}, bf16[128,128]{1,0:T(8,128)(2,1)S(1)}, u32[]{:S(2)}, u32[]{:S(2)}) collective-permute-start(bf16[128,128]{1,0:T(8,128)(2,1)S(1)} %get-tuple-element.171), channel_id=1, source_target_pairs={{0,4},{4,0},{1,5},{5,1},{2,6},{6,2},{3,7},{7,3},{8,12},{12,8},{9,1... | collective-permute-start | bytes 98312 | tf_op jit(solution)/shard_map/ppermute | solution.py:540
  74.2 4.7 %collective-permute-start.38 = (bf16[128,128]{1,0:T(8,128)(2,1)S(1)}, bf16[128,128]{1,0:T(8,128)(2,1)S(1)}, u32[]{:S(2)}, u32[]{:S(2)}) collective-permute-start(bf16[128,128]{1,0:T(8,128)(2,1)S(1)} %get-tuple-element.172), channel_id=1, source_target_pairs={{0,2},{2,0},{1,3},{3,1},{4,6},{6,4},{5,7},{7,5},{8,10},{10,8},{9,1... | collective-permute-start | bytes 98312 | tf_op jit(solution)/shard_map/ppermute | solution.py:540
  76.3 2.7 %collective-permute-start.39 = (bf16[128,128]{1,0:T(8,128)(2,1)S(1)}, bf16[128,128]{1,0:T(8,128)(2,1)S(1)}, u32[]{:S(2)}, u32[]{:S(2)}) collective-permute-start(bf16[128,128]{1,0:T(8,128)(2,1)S(1)} %get-tuple-element.173), channel_id=1, source_target_pairs={{0,1},{1,0},{2,3},{3,2},{4,5},{5,4},{6,7},{7,6},{8,9},{9,8},{10,11... | collective-permute-start | bytes 98312 | tf_op jit(solution)/shard_map/ppermute | solution.py:540
  79.4 6.7 %collective-permute-start.40 = (bf16[128,128]{1,0:T(8,128)(2,1)S(1)}, bf16[128,128]{1,0:T(8,128)(2,1)S(1)}, u32[]{:S(2)}, u32[]{:S(2)}) collective-permute-start(bf16[128,128]{1,0:T(8,128)(2,1)S(1)} %get-tuple-element.179), channel_id=1, source_target_pairs={{4,8},{8,4},{5,9},{9,5},{6,10},{10,6},{7,11},{11,7},{12,16},{16,12... | collective-permute-start | bytes 98312 | tf_op jit(solution)/shard_map/ppermute | solution.py:540
  79.9 7.5 %collective-permute-start.41 = (bf16[128,128]{1,0:T(8,128)(2,1)S(1)}, bf16[128,128]{1,0:T(8,128)(2,1)S(1)}, u32[]{:S(2)}, u32[]{:S(2)}) collective-permute-start(bf16[128,128]{1,0:T(8,128)(2,1)S(1)} %get-tuple-element.180), channel_id=1, source_target_pairs={{2,4},{4,2},{3,5},{5,3},{6,8},{8,6},{7,9},{9,7},{10,12},{12,10},{1... | collective-permute-start | bytes 98312 | tf_op jit(solution)/shard_map/ppermute | solution.py:540
  82.9 6.9 %collective-permute-start.42 = (bf16[128,128]{1,0:T(8,128)(2,1)S(1)}, bf16[128,128]{1,0:T(8,128)(2,1)S(1)}, u32[]{:S(2)}, u32[]{:S(2)}) collective-permute-start(bf16[128,128]{1,0:T(8,128)(2,1)S(1)} %get-tuple-element.181), channel_id=1, source_target_pairs={{1,2},{2,1},{3,4},{4,3},{5,6},{6,5},{7,8},{8,7},{9,10},{10,9},{11,... | collective-permute-start | bytes 98312 | tf_op jit(solution)/shard_map/ppermute | solution.py:540
  85.3 4.6 %collective-permute-start.43 = (bf16[128,128]{1,0:T(8,128)(2,1)S(1)}, bf16[128,128]{1,0:T(8,128)(2,1)S(1)}, u32[]{:S(2)}, u32[]{:S(2)}) collective-permute-start(bf16[128,128]{1,0:T(8,128)(2,1)S(1)} %get-tuple-element.182), channel_id=1, source_target_pairs={{0,4},{4,0},{1,5},{5,1},{2,6},{6,2},{3,7},{7,3},{8,12},{12,8},{9,1... | collective-permute-start | bytes 98312 | tf_op jit(solution)/shard_map/ppermute | solution.py:540
  85.3 4.6 %collective-permute-start.44 = (bf16[128,128]{1,0:T(8,128)(2,1)S(1)}, bf16[128,128]{1,0:T(8,128)(2,1)S(1)}, u32[]{:S(2)}, u32[]{:S(2)}) collective-permute-start(bf16[128,128]{1,0:T(8,128)(2,1)S(1)} %get-tuple-element.183), channel_id=1, source_target_pairs={{0,2},{2,0},{1,3},{3,1},{4,6},{6,4},{5,7},{7,5},{8,10},{10,8},{9,1... | collective-permute-start | bytes 98312 | tf_op jit(solution)/shard_map/ppermute | solution.py:540
  86.0 3.8 %collective-permute-start.45 = (bf16[128,128]{1,0:T(8,128)(2,1)S(1)}, bf16[128,128]{1,0:T(8,128)(2,1)S(1)}, u32[]{:S(2)}, u32[]{:S(2)}) collective-permute-start(bf16[128,128]{1,0:T(8,128)(2,1)S(1)} %get-tuple-element.184), channel_id=1, source_target_pairs={{0,1},{1,0},{2,3},{3,2},{4,5},{5,4},{6,7},{7,6},{8,9},{9,8},{10,11... | collective-permute-start | bytes 98312 | tf_op jit(solution)/shard_map/ppermute | solution.py:540
  90.3 7.0 %collective-permute-start.46 = (bf16[128,128]{1,0:T(8,128)(2,1)S(1)}, bf16[128,128]{1,0:T(8,128)(2,1)S(1)}, u32[]{:S(2)}, u32[]{:S(2)}) collective-permute-start(bf16[128,128]{1,0:T(8,128)(2,1)S(1)} %get-tuple-element.188), channel_id=1, source_target_pairs={{4,8},{8,4},{5,9},{9,5},{6,10},{10,6},{7,11},{11,7},{12,16},{16,12... | collective-permute-start | bytes 98312 | tf_op jit(solution)/shard_map/ppermute | solution.py:540
  90.6 7.6 %collective-permute-start.47 = (bf16[128,128]{1,0:T(8,128)(2,1)S(1)}, bf16[128,128]{1,0:T(8,128)(2,1)S(1)}, u32[]{:S(2)}, u32[]{:S(2)}) collective-permute-start(bf16[128,128]{1,0:T(8,128)(2,1)S(1)} %get-tuple-element.189), channel_id=1, source_target_pairs={{2,4},{4,2},{3,5},{5,3},{6,8},{8,6},{7,9},{9,7},{10,12},{12,10},{1... | collective-permute-start | bytes 98312 | tf_op jit(solution)/shard_map/ppermute | solution.py:540
  93.8 7.0 %collective-permute-start.48 = (bf16[128,128]{1,0:T(8,128)(2,1)S(1)}, bf16[128,128]{1,0:T(8,128)(2,1)S(1)}, u32[]{:S(2)}, u32[]{:S(2)}) collective-permute-start(bf16[128,128]{1,0:T(8,128)(2,1)S(1)} %get-tuple-element.190), channel_id=1, source_target_pairs={{1,2},{2,1},{3,4},{4,3},{5,6},{6,5},{7,8},{8,7},{9,10},{10,9},{11,... | collective-permute-start | bytes 98312 | tf_op jit(solution)/shard_map/ppermute | solution.py:540
  95.4 5.4 %collective-permute-start.49 = (bf16[128,128]{1,0:T(8,128)(2,1)S(1)}, bf16[128,128]{1,0:T(8,128)(2,1)S(1)}, u32[]{:S(2)}, u32[]{:S(2)}) collective-permute-start(bf16[128,128]{1,0:T(8,128)(2,1)S(1)} %get-tuple-element.191), channel_id=1, source_target_pairs={{0,4},{4,0},{1,5},{5,1},{2,6},{6,2},{3,7},{7,3},{8,12},{12,8},{9,1... | collective-permute-start | bytes 98312 | tf_op jit(solution)/shard_map/ppermute | solution.py:540
  95.4 5.4 %collective-permute-start.50 = (bf16[128,128]{1,0:T(8,128)(2,1)S(1)}, bf16[128,128]{1,0:T(8,128)(2,1)S(1)}, u32[]{:S(2)}, u32[]{:S(2)}) collective-permute-start(bf16[128,128]{1,0:T(8,128)(2,1)S(1)} %get-tuple-element.192), channel_id=1, source_target_pairs={{0,2},{2,0},{1,3},{3,1},{4,6},{6,4},{5,7},{7,5},{8,10},{10,8},{9,1... | collective-permute-start | bytes 98312 | tf_op jit(solution)/shard_map/ppermute | solution.py:540
  97.3 3.5 %collective-permute-start.51 = (bf16[128,128]{1,0:T(8,128)(2,1)S(1)}, bf16[128,128]{1,0:T(8,128)(2,1)S(1)}, u32[]{:S(2)}, u32[]{:S(2)}) collective-permute-start(bf16[128,128]{1,0:T(8,128)(2,1)S(1)} %get-tuple-element.193), channel_id=1, source_target_pairs={{0,1},{1,0},{2,3},{3,2},{4,5},{5,4},{6,7},{7,6},{8,9},{9,8},{10,11... | collective-permute-start | bytes 98312 | tf_op jit(solution)/shard_map/ppermute | solution.py:540
  102.3 1.3 %collective-permute-start.52 = (f32[64,128]{1,0:T(8,128)S(1)}, f32[64,128]{1,0:T(8,128)S(1)}, u32[]{:S(2)}, u32[]{:S(2)}) collective-permute-start(f32[64,128]{1,0:T(8,128)S(1)} %get-tuple-element.195), channel_id=1, source_target_pairs={{0,1},{1,0},{2,3},{3,2},{4,5},{5,4},{6,7},{7,6},{8,9},{9,8},{10,11... | collective-permute-start | bytes 98312 | tf_op jit(solution)/shard_map/ppermute | solution.py:523
  103.6 5.0 %collective-permute-start.55 = (f32[64,128]{1,0:T(8,128)S(1)}, f32[64,128]{1,0:T(8,128)S(1)}, u32[]{:S(2)}, u32[]{:S(2)}) collective-permute-start(f32[64,128]{1,0:T(8,128)S(1)} %add.25), channel_id=1, source_target_pairs={{0,6},{1,7},{2,4},{3,5},{4,2},{5,3},{6,0},{7,1},{8,14},{9,15},{10,... | collective-permute-start | bytes 98312 | tf_op jit(solution)/shard_map/ppermute | solution.py:523
  103.6 4.9 %collective-permute-start.54 = (f32[64,128]{1,0:T(8,128)S(1)}, f32[64,128]{1,0:T(8,128)S(1)}, u32[]{:S(2)}, u32[]{:S(2)}) collective-permute-start(f32[64,128]{1,0:T(8,128)S(1)} %add.25), channel_id=1, source_target_pairs={{0,4},{1,5},{2,6},{3,7},{4,0},{5,1},{6,2},{7,3},{8,12},{9,13},{10,... | collective-permute-start | bytes 98312 | tf_op jit(solution)/shard_map/ppermute | solution.py:523
  104.5 4.4 %collective-permute-start.53 = (f32[64,128]{1,0:T(8,128)S(1)}, f32[64,128]{1,0:T(8,128)S(1)}, u32[]{:S(2)}, u32[]{:S(2)}) collective-permute-start(f32[64,128]{1,0:T(8,128)S(1)} %add.25), channel_id=1, source_target_pairs={{0,2},{1,3},{2,0},{3,1},{4,6},{5,7},{6,4},{7,5},{8,10},{9,11},{10,... | collective-permute-start | bytes 98312 | tf_op jit(solution)/shard_map/ppermute | solution.py:523
  109.0 6.0 %collective-permute-start.58 = (f32[64,128]{1,0:T(8,128)S(1)}, f32[64,128]{1,0:T(8,128)S(1)}, u32[]{:S(2)}, u32[]{:S(2)}) collective-permute-start(f32[64,128]{1,0:T(8,128)S(1)} %add_add_fusion.1), channel_id=1, source_target_pairs={{0,24},{1,25},{2,26},{3,27},{4,28},{5,29},{6,30},{7,31},{8,16},{9,... | collective-permute-start | bytes 98312 | tf_op jit(solution)/shard_map/ppermute | solution.py:523
  111.0 4.8 %collective-permute-start.57 = (f32[64,128]{1,0:T(8,128)S(1)}, f32[64,128]{1,0:T(8,128)S(1)}, u32[]{:S(2)}, u32[]{:S(2)}) collective-permute-start(f32[64,128]{1,0:T(8,128)S(1)} %add_add_fusion.1), channel_id=1, source_target_pairs={{0,16},{1,17},{2,18},{3,19},{4,20},{5,21},{6,22},{7,23},{8,24},{9,... | collective-permute-start | bytes 98312 | tf_op jit(solution)/shard_map/ppermute | solution.py:523
  111.0 4.8 %collective-permute-start.56 = (f32[64,128]{1,0:T(8,128)S(1)}, f32[64,128]{1,0:T(8,128)S(1)}, u32[]{:S(2)}, u32[]{:S(2)}) collective-permute-start(f32[64,128]{1,0:T(8,128)S(1)} %add_add_fusion.1), channel_id=1, source_target_pairs={{0,8},{1,9},{2,10},{3,11},{4,12},{5,13},{6,14},{7,15},{8,0},{9,1},... | collective-permute-start | bytes 98312 | tf_op jit(solution)/shard_map/ppermute | solution.py:523
  115.9 1.3 %collective-permute-start.59 = (f32[64,128]{1,0:T(8,128)S(1)}, f32[64,128]{1,0:T(8,128)S(1)}, u32[]{:S(2)}, u32[]{:S(2)}) collective-permute-start(f32[64,128]{1,0:T(8,128)S(1)} %add_add_fusion.refs_1_), channel_id=1, source_target_pairs={{0,1},{1,0},{2,3},{3,2},{4,5},{5,4},{6,7},{7,6},{8,9},{9,8},{10,11... | collective-permute-start | bytes 98312 | tf_op jit(solution)/shard_map/ppermute | solution.py:523

commit v7 on v6

--- a/solution.py
+++ b/solution.py
@@ -403,7 +403,7 @@
     got, (next_ref, kept_ref, sent_ref) = refs[5:11], refs[11:]
 
     def store(block, value):
-        next_ref[block, :] = value
+        next_ref[block, :] = with_parts(value)
 
     advance(
         place_ref,
@@ -417,7 +417,8 @@
         range(part_ref.shape[0] // BLK),
     )
     value = next_ref[...]
-    gram = dot(value, value, ((0,), (0,)), lax.Precision.HIGHEST)
+    gram = parts_joined(dot(value, value, ((0,), (0,))))
+    gram = gram[:VECS] + gram[VECS:]
     half = VECS // 2
     low = is_low(place_ref, 1)
     kept_ref[...] = jnp.where(low, gram[:half], gram[half:])
@@ -429,7 +430,7 @@
     return pl.pallas_call(
         lambda *refs: last_kernel(scale, *refs),
         out_shape=(
-            jax.ShapeDtypeStruct((rows, VECS), F32),
+            jax.ShapeDtypeStruct((rows, 2 * VECS), BF16),
             *(jax.ShapeDtypeStruct((VECS // 2, VECS), F32),) * 2,
         ),
         in_specs=[SMEM] + [VMEM] * 10,
@@ -503,13 +504,23 @@
             columns = [spread(left[b][:, base + c : base + c + 1]) for c in range(width)]
             for side, rows in zip((left, right), factors):
                 side[b] = side[b] - total_of(c * r for c, r in zip(columns, rows))
-    out_ref[...] = dot(field_ref[...], inverse_ref[...], ((1,), (1,)), lax.Precision.HIGHEST)
+    factor = inverse_ref[...]
+    high = factor.astype(BF16)
+    rest = (factor - high.astype(F32)).astype(BF16)
+    factor = jnp.concatenate(
+        [
+            jnp.concatenate([high, high], axis=1),
+            jnp.concatenate([rest, jnp.zeros_like(rest)], axis=1),
+        ],
+        axis=0,
+    )
+    out_ref[...] = parts_joined(dot(field_ref[...], factor, ((1,), (1,))))
 
 
 def finish(scale, place, halves, field):
     return pl.pallas_call(
         lambda *refs: finish_kernel(scale, *refs),
-        out_shape=jax.ShapeDtypeStruct(field.shape, F32),
+        out_shape=jax.ShapeDtypeStruct((field.shape[0], VECS), F32),
         in_specs=[SMEM] + [VMEM] * 3,
         out_specs=VMEM,
         scratch_shapes=[pltpu.VMEM((VECS, VECS), F32)],

time: 124 us -> 123 us (level)
  transfers between devices with their start and end apart: 60 -> 60, of which waited for: 27 -> 27; matrix products, arithmetic and copies ran while one was open for 0% -> 0% of each run, Pallas kernels for 9% -> 10%
where the time goes in v7:
time: 123 us
  starting transfers between devices  63.4 us (52%)
  waiting for transfers between devices  36.8 us (30%)
  Pallas kernels  22.5 us (18%)
    ppermute x52, starting transfers between devices, swap(): return lax.ppermute(value, AXES, swap_pairs(count, by, odd))  55.3 us
    ppermute x52, waiting for transfers between devices, swap(): return lax.ppermute(value, AXES, swap_pairs(count, by, odd))  30.1 us
    ppermute x8, starting transfers between devices, swapped(): return lax.ppermute(value, AXES, [(i, i ^ mask) for i in range(count)])  8.08 us
    pallas_call x7, Pallas kernels, inner(): pl.pallas_call(lambda *refs: inner_kernel(scale, before_scale, more, *ref...  7.62 us
    ppermute x8, waiting for transfers between devices, swapped(): return lax.ppermute(value, AXES, [(i, i ^ mask) for i in range(count)])  6.73 us
    pallas_call x1, Pallas kernels, finish(): pl.pallas_call(lambda *refs: finish_kernel(scale, *refs), out_shape=jax.S...  6.6 us
    pallas_call x1, Pallas kernels, prepare(): pl.pallas_call(prepare_kernel, out_shape=(jax.ShapeDtypeStruct((rows, 3 *...  3.08 us
    pallas_call x7, Pallas kernels, step(): pl.pallas_call(lambda *refs: step_kernel(scale, *refs), out_shape=(*SENT,...  2.79 us
  transfers between devices with their start and end apart: 60, of which 27 were waited for; matrix products, arithmetic and copies ran while one was open for 0% of the time, Pallas kernels for 10%

profile of v7, /device:TPU:0, one launch (start us, length us, event | category | flops | bytes accessed | tf_op | source)
XLA Modules:
  0.0 123.1 jit_solution(11974270432579445632)
XLA Ops:
  0.0 6.0 %collective-permute-start.3 = (s32[1,256]{1,0:T(1,128)}, s32[1,256]{1,0:T(1,128)S(1)}, u32[]{:S(2)}, u32[]{:S(2)}) collective-permute-start(s32[1,256]{1,0:T(1,128)} %bitcast.10), channel_id=1, source_target_pairs={{4,8},{8,4},{5,9},{9,5},{6,10},{10,6},{7,11},{11,7},{12,16},{16,12... | collective-permute-start | bytes 3080 | tf_op jit(solution)/shard_map/ppermute | solution.py:551
  6.0 2.8 %collective-permute-start.1 = (s32[1,256]{1,0:T(1,128)}, s32[1,256]{1,0:T(1,128)S(1)}, u32[]{:S(2)}, u32[]{:S(2)}) collective-permute-start(s32[1,256]{1,0:T(1,128)} %bitcast.12), channel_id=1, source_target_pairs={{2,4},{4,2},{3,5},{5,3},{6,8},{8,6},{7,9},{9,7},{10,12},{12,10},{1... | collective-permute-start | bytes 3080 | tf_op jit(solution)/shard_map/ppermute | solution.py:551
  8.8 0.6 collective-permute-start
  9.5 3.1 %prepare.1 = (bf16[2048,384]{1,0:T(8,128)(2,1)S(1)}, bf16[2048,256]{1,0:T(8,128)(2,1)S(1)}, f32[256,128]{1,0:T(8,128)S(1)}, bf16[2048,128]{1,0:T(8,128)(2,1)S(1)}) custom-call(s32[1]{0:T(128)} %bitcast.place_ref.refs_0_, s32[1,256]{1,0:T(1,128)} %bitcast.8, f32[1,256]{1,0:T(1,128)} %bitcast.9, f32[3,8,2048]{2,1,0:T(8,128)} %bitcast.6, ...), custom_call_target="tpu_custom_call" | custom-call | tf_op jit(solution)/shard_map/prepare/pallas_call | solution.py:153
  12.6 0.8 collective-permute-done.1.w1
  13.4 0.6 first.1
  14.0 2.0 %collective-permute-start.4 = (bf16[128,128]{1,0:T(8,128)(2,1)S(1)}, bf16[128,128]{1,0:T(8,128)(2,1)S(1)}, u32[]{:S(2)}, u32[]{:S(2)}) collective-permute-start(bf16[128,128]{1,0:T(8,128)(2,1)S(1)} %get-tuple-element.114), channel_id=1, source_target_pairs={{4,8},{8,4},{5,9},{9,5},{6,10},{10,6},{7,11},{11,7},{12,16},{16,12... | collective-permute-start | bytes 98312 | tf_op jit(solution)/shard_map/ppermute | solution.py:551
  16.0 2.8 %collective-permute-start.5 = (bf16[128,128]{1,0:T(8,128)(2,1)S(1)}, bf16[128,128]{1,0:T(8,128)(2,1)S(1)}, u32[]{:S(2)}, u32[]{:S(2)}) collective-permute-start(bf16[128,128]{1,0:T(8,128)(2,1)S(1)} %get-tuple-element.115), channel_id=1, source_target_pairs={{2,4},{4,2},{3,5},{5,3},{6,8},{8,6},{7,9},{9,7},{10,12},{12,10},{1... | collective-permute-start | bytes 98312 | tf_op jit(solution)/shard_map/ppermute | solution.py:551
  18.8 0.8 collective-permute-start.6
  19.7 1.0 collective-permute-done.4.refs_8_
  21.1 1.0 opening.1
  22.1 1.4 %collective-permute-done.5.refs_9_ = bf16[128,128]{1,0:T(8,128)(2,1)S(1)} collective-permute-done((bf16[128,128]{1,0:T(8,128)(2,1)S(1)}, bf16[128,128]{1,0:T(8,128)(2,1)S(1)}, u32[]{:S(2)}, u32[]{:S(2)}) %collective-permute-start.5) | collective-permute-done | bytes 32800 | tf_op jit(solution)/shard_map/ppermute | solution.py:551
  23.5 2.2 %collective-permute-done.6.refs_10_ = bf16[128,128]{1,0:T(8,128)(2,1)S(1)} collective-permute-done((bf16[128,128]{1,0:T(8,128)(2,1)S(1)}, bf16[128,128]{1,0:T(8,128)(2,1)S(1)}, u32[]{:S(2)}, u32[]{:S(2)}) %collective-permute-start.6) | collective-permute-done | bytes 32800 | tf_op jit(solution)/shard_map/ppermute | solution.py:551
  26.4 1.8 %collective-permute-start.11 = (bf16[128,128]{1,0:T(8,128)(2,1)S(1)}, bf16[128,128]{1,0:T(8,128)(2,1)S(1)}, u32[]{:S(2)}, u32[]{:S(2)}) collective-permute-start(bf16[128,128]{1,0:T(8,128)(2,1)S(1)} %get-tuple-element.125), channel_id=1, source_target_pairs={{2,4},{4,2},{3,5},{5,3},{6,8},{8,6},{7,9},{9,7},{10,12},{12,10},{1... | collective-permute-start | bytes 98312 | tf_op jit(solution)/shard_map/ppermute | solution.py:551
  28.2 3.1 %collective-permute-start.12 = (bf16[128,128]{1,0:T(8,128)(2,1)S(1)}, bf16[128,128]{1,0:T(8,128)(2,1)S(1)}, u32[]{:S(2)}, u32[]{:S(2)}) collective-permute-start(bf16[128,128]{1,0:T(8,128)(2,1)S(1)} %get-tuple-element.126), channel_id=1, source_target_pairs={{1,2},{2,1},{3,4},{4,3},{5,6},{6,5},{7,8},{8,7},{9,10},{10,9},{11,... | collective-permute-start | bytes 98312 | tf_op jit(solution)/shard_map/ppermute | solution.py:551
  31.3 1.9 %collective-permute-done.10.refs_8_ = bf16[128,128]{1,0:T(8,128)(2,1)S(1)} collective-permute-done((bf16[128,128]{1,0:T(8,128)(2,1)S(1)}, bf16[128,128]{1,0:T(8,128)(2,1)S(1)}, u32[]{:S(2)}, u32[]{:S(2)}) %collective-permute-start.10) | collective-permute-done | bytes 32800 | tf_op jit(solution)/shard_map/ppermute | solution.py:551
  33.2 1.1 inner.7
  34.3 0.9 collective-permute-done.12.refs_10_
  35.9 0.9 collective-permute-start.16
  36.8 3.0 %collective-permute-start.17 = (bf16[128,128]{1,0:T(8,128)(2,1)S(1)}, bf16[128,128]{1,0:T(8,128)(2,1)S(1)}, u32[]{:S(2)}, u32[]{:S(2)}) collective-permute-start(bf16[128,128]{1,0:T(8,128)(2,1)S(1)} %get-tuple-element.136), channel_id=1, source_target_pairs={{2,4},{4,2},{3,5},{5,3},{6,8},{8,6},{7,9},{9,7},{10,12},{12,10},{1... | collective-permute-start | bytes 98312 | tf_op jit(solution)/shard_map/ppermute | solution.py:551
  39.8 2.4 %collective-permute-start.18 = (bf16[128,128]{1,0:T(8,128)(2,1)S(1)}, bf16[128,128]{1,0:T(8,128)(2,1)S(1)}, u32[]{:S(2)}, u32[]{:S(2)}) collective-permute-start(bf16[128,128]{1,0:T(8,128)(2,1)S(1)} %get-tuple-element.137), channel_id=1, source_target_pairs={{1,2},{2,1},{3,4},{4,3},{5,6},{6,5},{7,8},{8,7},{9,10},{10,9},{11,... | collective-permute-start | bytes 98312 | tf_op jit(solution)/shard_map/ppermute | solution.py:551
  42.6 1.1 inner.8
  43.7 0.7 collective-permute-done.17.refs_9_
  44.4 2.4 %collective-permute-done.18.refs_10_ = bf16[128,128]{1,0:T(8,128)(2,1)S(1)} collective-permute-done((bf16[128,128]{1,0:T(8,128)(2,1)S(1)}, bf16[128,128]{1,0:T(8,128)(2,1)S(1)}, u32[]{:S(2)}, u32[]{:S(2)}) %collective-permute-start.18) | collective-permute-done | bytes 32800 | tf_op jit(solution)/shard_map/ppermute | solution.py:551
  47.5 3.3 %collective-permute-start.23 = (bf16[128,128]{1,0:T(8,128)(2,1)S(1)}, bf16[128,128]{1,0:T(8,128)(2,1)S(1)}, u32[]{:S(2)}, u32[]{:S(2)}) collective-permute-start(bf16[128,128]{1,0:T(8,128)(2,1)S(1)} %get-tuple-element.147), channel_id=1, source_target_pairs={{2,4},{4,2},{3,5},{5,3},{6,8},{8,6},{7,9},{9,7},{10,12},{12,10},{1... | collective-permute-start | bytes 98312 | tf_op jit(solution)/shard_map/ppermute | solution.py:551
  50.8 1.5 %collective-permute-start.24 = (bf16[128,128]{1,0:T(8,128)(2,1)S(1)}, bf16[128,128]{1,0:T(8,128)(2,1)S(1)}, u32[]{:S(2)}, u32[]{:S(2)}) collective-permute-start(bf16[128,128]{1,0:T(8,128)(2,1)S(1)} %get-tuple-element.148), channel_id=1, source_target_pairs={{1,2},{2,1},{3,4},{4,3},{5,6},{6,5},{7,8},{8,7},{9,10},{10,9},{11,... | collective-permute-start | bytes 98312 | tf_op jit(solution)/shard_map/ppermute | solution.py:551
  52.3 0.9 collective-permute-start.26
  53.2 1.0 collective-permute-done.22.refs_8_
  54.2 1.1 inner.9
  55.4 2.5 %collective-permute-done.24.refs_10_ = bf16[128,128]{1,0:T(8,128)(2,1)S(1)} collective-permute-done((bf16[128,128]{1,0:T(8,128)(2,1)S(1)}, bf16[128,128]{1,0:T(8,128)(2,1)S(1)}, u32[]{:S(2)}, u32[]{:S(2)}) %collective-permute-start.24) | collective-permute-done | bytes 32800 | tf_op jit(solution)/shard_map/ppermute | solution.py:551
  58.4 3.4 %collective-permute-start.29 = (bf16[128,128]{1,0:T(8,128)(2,1)S(1)}, bf16[128,128]{1,0:T(8,128)(2,1)S(1)}, u32[]{:S(2)}, u32[]{:S(2)}) collective-permute-start(bf16[128,128]{1,0:T(8,128)(2,1)S(1)} %get-tuple-element.158), channel_id=1, source_target_pairs={{2,4},{4,2},{3,5},{5,3},{6,8},{8,6},{7,9},{9,7},{10,12},{12,10},{1... | collective-permute-start | bytes 98312 | tf_op jit(solution)/shard_map/ppermute | solution.py:551
  61.8 1.4 %collective-permute-start.30 = (bf16[128,128]{1,0:T(8,128)(2,1)S(1)}, bf16[128,128]{1,0:T(8,128)(2,1)S(1)}, u32[]{:S(2)}, u32[]{:S(2)}) collective-permute-start(bf16[128,128]{1,0:T(8,128)(2,1)S(1)} %get-tuple-element.159), channel_id=1, source_target_pairs={{1,2},{2,1},{3,4},{4,3},{5,6},{6,5},{7,8},{8,7},{9,10},{10,9},{11,... | collective-permute-start | bytes 98312 | tf_op jit(solution)/shard_map/ppermute | solution.py:551
  63.5 1.8 %collective-permute-done.28.refs_8_ = bf16[128,128]{1,0:T(8,128)(2,1)S(1)} collective-permute-done((bf16[128,128]{1,0:T(8,128)(2,1)S(1)}, bf16[128,128]{1,0:T(8,128)(2,1)S(1)}, u32[]{:S(2)}, u32[]{:S(2)}) %collective-permute-start.28) | collective-permute-done | bytes 32800 | tf_op jit(solution)/shard_map/ppermute | solution.py:551
  65.3 1.1 inner.10
  66.4 2.4 %collective-permute-done.30.refs_10_ = bf16[128,128]{1,0:T(8,128)(2,1)S(1)} collective-permute-done((bf16[128,128]{1,0:T(8,128)(2,1)S(1)}, bf16[128,128]{1,0:T(8,128)(2,1)S(1)}, u32[]{:S(2)}, u32[]{:S(2)}) %collective-permute-start.30) | collective-permute-done | bytes 32800 | tf_op jit(solution)/shard_map/ppermute | solution.py:551
  69.4 2.6 %collective-permute-start.35 = (bf16[128,128]{1,0:T(8,128)(2,1)S(1)}, bf16[128,128]{1,0:T(8,128)(2,1)S(1)}, u32[]{:S(2)}, u32[]{:S(2)}) collective-permute-start(bf16[128,128]{1,0:T(8,128)(2,1)S(1)} %get-tuple-element.169), channel_id=1, source_target_pairs={{2,4},{4,2},{3,5},{5,3},{6,8},{8,6},{7,9},{9,7},{10,12},{12,10},{1... | collective-permute-start | bytes 98312 | tf_op jit(solution)/shard_map/ppermute | solution.py:551
  72.0 2.2 %collective-permute-start.36 = (bf16[128,128]{1,0:T(8,128)(2,1)S(1)}, bf16[128,128]{1,0:T(8,128)(2,1)S(1)}, u32[]{:S(2)}, u32[]{:S(2)}) collective-permute-start(bf16[128,128]{1,0:T(8,128)(2,1)S(1)} %get-tuple-element.170), channel_id=1, source_target_pairs={{1,2},{2,1},{3,4},{4,3},{5,6},{6,5},{7,8},{8,7},{9,10},{10,9},{11,... | collective-permute-start | bytes 98312 | tf_op jit(solution)/shard_map/ppermute | solution.py:551
  74.4 1.9 %collective-permute-done.34.refs_8_ = bf16[128,128]{1,0:T(8,128)(2,1)S(1)} collective-permute-done((bf16[128,128]{1,0:T(8,128)(2,1)S(1)}, bf16[128,128]{1,0:T(8,128)(2,1)S(1)}, u32[]{:S(2)}, u32[]{:S(2)}) %collective-permute-start.34) | collective-permute-done | bytes 32800 | tf_op jit(solution)/shard_map/ppermute | solution.py:551
  76.3 1.3 %inner.11 = (f32[2048,128]{1,0:T(8,128)S(1)}, f32[2048,128]{1,0:T(8,128)S(1)}, f32[256,128]{1,0:T(8,128)S(1)}) custom-call(bf16[2048,384]{1,0:T(8,128)(2,1)S(1)} %get-tuple-element.102.refs_0_.refs_1_, bf16[2048,256]{1,0:T(8,128)(2,1)S(1)} %get-tuple-element.103.refs_1_.refs_2_, bf16[256,2048]{1,0:T(8,128)(2,1)S(1)} %get-tuple-element.110.refs_2_.refs_5_, ...), custom_call_target="tpu_custom_call" | custom-call | flops 201326592 | bytes 3145728 | tf_op jit(solution)/shard_map/inner/pallas_call | solution.py:318
  77.6 1.3 %collective-permute-done.36.refs_10_ = bf16[128,128]{1,0:T(8,128)(2,1)S(1)} collective-permute-done((bf16[128,128]{1,0:T(8,128)(2,1)S(1)}, bf16[128,128]{1,0:T(8,128)(2,1)S(1)}, u32[]{:S(2)}, u32[]{:S(2)}) %collective-permute-start.36) | collective-permute-done | bytes 32800 | tf_op jit(solution)/shard_map/ppermute | solution.py:551
  79.4 0.5 collective-permute-start.40
  79.9 3.0 %collective-permute-start.41 = (bf16[128,128]{1,0:T(8,128)(2,1)S(1)}, bf16[128,128]{1,0:T(8,128)(2,1)S(1)}, u32[]{:S(2)}, u32[]{:S(2)}) collective-permute-start(bf16[128,128]{1,0:T(8,128)(2,1)S(1)} %get-tuple-element.180), channel_id=1, source_target_pairs={{2,4},{4,2},{3,5},{5,3},{6,8},{8,6},{7,9},{9,7},{10,12},{12,10},{1... | collective-permute-start | bytes 98312 | tf_op jit(solution)/shard_map/ppermute | solution.py:551
  82.9 2.4 %collective-permute-start.42 = (bf16[128,128]{1,0:T(8,128)(2,1)S(1)}, bf16[128,128]{1,0:T(8,128)(2,1)S(1)}, u32[]{:S(2)}, u32[]{:S(2)}) collective-permute-start(bf16[128,128]{1,0:T(8,128)(2,1)S(1)} %get-tuple-element.181), channel_id=1, source_target_pairs={{1,2},{2,1},{3,4},{4,3},{5,6},{6,5},{7,8},{8,7},{9,10},{10,9},{11,... | collective-permute-start | bytes 98312 | tf_op jit(solution)/shard_map/ppermute | solution.py:551
  85.3 0.8 collective-permute-done.40.refs_8_
  86.0 1.1 inner.12
  87.4 2.4 %collective-permute-done.42.refs_10_ = bf16[128,128]{1,0:T(8,128)(2,1)S(1)} collective-permute-done((bf16[128,128]{1,0:T(8,128)(2,1)S(1)}, bf16[128,128]{1,0:T(8,128)(2,1)S(1)}, u32[]{:S(2)}, u32[]{:S(2)}) %collective-permute-start.42) | collective-permute-done | bytes 32800 | tf_op jit(solution)/shard_map/ppermute | solution.py:551
  90.6 3.2 %collective-permute-start.47 = (bf16[128,128]{1,0:T(8,128)(2,1)S(1)}, bf16[128,128]{1,0:T(8,128)(2,1)S(1)}, u32[]{:S(2)}, u32[]{:S(2)}) collective-permute-start(bf16[128,128]{1,0:T(8,128)(2,1)S(1)} %get-tuple-element.189), channel_id=1, source_target_pairs={{2,4},{4,2},{3,5},{5,3},{6,8},{8,6},{7,9},{9,7},{10,12},{12,10},{1... | collective-permute-start | bytes 98312 | tf_op jit(solution)/shard_map/ppermute | solution.py:551
  93.8 1.6 %collective-permute-start.48 = (bf16[128,128]{1,0:T(8,128)(2,1)S(1)}, bf16[128,128]{1,0:T(8,128)(2,1)S(1)}, u32[]{:S(2)}, u32[]{:S(2)}) collective-permute-start(bf16[128,128]{1,0:T(8,128)(2,1)S(1)} %get-tuple-element.190), channel_id=1, source_target_pairs={{1,2},{2,1},{3,4},{4,3},{5,6},{6,5},{7,8},{8,7},{9,10},{10,9},{11,... | collective-permute-start | bytes 98312 | tf_op jit(solution)/shard_map/ppermute | solution.py:551
  95.4 0.8 collective-permute-start.50
  96.2 1.1 collective-permute-done.46.refs_5_
  97.3 0.8 inner.13.refs_4_
  98.2 2.6 %collective-permute-done.48.refs_7_ = bf16[128,128]{1,0:T(8,128)(2,1)S(1)} collective-permute-done((bf16[128,128]{1,0:T(8,128)(2,1)S(1)}, bf16[128,128]{1,0:T(8,128)(2,1)S(1)}, u32[]{:S(2)}, u32[]{:S(2)}) %collective-permute-start.48) | collective-permute-done | bytes 32800 | tf_op jit(solution)/shard_map/ppermute | solution.py:551
  100.8 0.8 last.1
  101.7 1.2 collective-permute-done.52
  102.9 0.9 collective-permute-start.54
  103.8 2.5 %collective-permute-start.53 = (f32[64,128]{1,0:T(8,128)S(1)}, f32[64,128]{1,0:T(8,128)S(1)}, u32[]{:S(2)}, u32[]{:S(2)}) collective-permute-start(f32[64,128]{1,0:T(8,128)S(1)} %add.25), channel_id=1, source_target_pairs={{0,2},{1,3},{2,0},{3,1},{4,6},{5,7},{6,4},{7,5},{8,10},{9,11},{10,... | collective-permute-start | bytes 98312 | tf_op jit(solution)/shard_map/ppermute | solution.py:534
  106.4 1.5 %collective-permute-done.55 = f32[64,128]{1,0:T(8,128)S(1)} collective-permute-done((f32[64,128]{1,0:T(8,128)S(1)}, f32[64,128]{1,0:T(8,128)S(1)}, u32[]{:S(2)}, u32[]{:S(2)}) %collective-permute-start.55) | collective-permute-done | bytes 32800 | tf_op jit(solution)/shard_map/ppermute | solution.py:534
  107.8 0.4 collective-permute-done.53
  108.3 2.1 %collective-permute-start.58 = (f32[64,128]{1,0:T(8,128)S(1)}, f32[64,128]{1,0:T(8,128)S(1)}, u32[]{:S(2)}, u32[]{:S(2)}) collective-permute-start(f32[64,128]{1,0:T(8,128)S(1)} %add_add_fusion.1), channel_id=1, source_target_pairs={{0,24},{1,25},{2,26},{3,27},{4,28},{5,29},{6,30},{7,31},{8,16},{9,... | collective-permute-start | bytes 98312 | tf_op jit(solution)/shard_map/ppermute | solution.py:534
  110.4 2.4 %collective-permute-start.56 = (f32[64,128]{1,0:T(8,128)S(1)}, f32[64,128]{1,0:T(8,128)S(1)}, u32[]{:S(2)}, u32[]{:S(2)}) collective-permute-start(f32[64,128]{1,0:T(8,128)S(1)} %add_add_fusion.1), channel_id=1, source_target_pairs={{0,8},{1,9},{2,10},{3,11},{4,12},{5,13},{6,14},{7,15},{8,0},{9,1},... | collective-permute-start | bytes 98312 | tf_op jit(solution)/shard_map/ppermute | solution.py:534
  112.7 1.5 %collective-permute-done.58 = f32[64,128]{1,0:T(8,128)S(1)} collective-permute-done((f32[64,128]{1,0:T(8,128)S(1)}, f32[64,128]{1,0:T(8,128)S(1)}, u32[]{:S(2)}, u32[]{:S(2)}) %collective-permute-start.58) | collective-permute-done | bytes 32800 | tf_op jit(solution)/shard_map/ppermute | solution.py:534
  114.2 0.9 collective-permute-done.57
  115.3 1.2 collective-permute-done.59.refs_2_
  116.5 6.6 %finish.1 = f32[2048,128]{1,0:T(8,128)} custom-call(s32[1]{0:T(128)} %bitcast.place_ref.refs_0_, f32[64,128]{1,0:T(8,128)S(1)} %add_add_fusion.refs_1_, f32[64,128]{1,0:T(8,128)S(1)} %collective-permute-done.59.refs_2_, bf16[2048,256]{1,0:T(8,128)(2,1)S(1)} %get-tuple-element.196.refs_3_), custom_call_target="tpu_custom_call" | custom-call | tf_op jit(solution)/shard_map/finish/pallas_call | solution.py:521
  (78 shorter events, 6.1 us)
Async XLA Ops:
  0.0 12.6 %collective-permute-start.3 = (s32[1,256]{1,0:T(1,128)}, s32[1,256]{1,0:T(1,128)S(1)}, u32[]{:S(2)}, u32[]{:S(2)}) collective-permute-start(s32[1,256]{1,0:T(1,128)} %bitcast.10), channel_id=1, source_target_pairs={{4,8},{8,4},{5,9},{9,5},{6,10},{10,6},{7,11},{11,7},{12,16},{16,12... | collective-permute-start | bytes 3080 | tf_op jit(solution)/shard_map/ppermute | solution.py:551
  6.0 6.6 %collective-permute-start.2 = (s32[1,256]{1,0:T(1,128)}, s32[1,256]{1,0:T(1,128)S(1)}, u32[]{:S(2)}, u32[]{:S(2)}) collective-permute-start(s32[1,256]{1,0:T(1,128)} %bitcast.11), channel_id=1, source_target_pairs={{0,4},{4,0},{1,5},{5,1},{2,6},{6,2},{3,7},{7,3},{8,12},{12,8},{9,1... | collective-permute-start | bytes 3080 | tf_op jit(solution)/shard_map/ppermute | solution.py:551
  6.0 7.4 %collective-permute-start.1 = (s32[1,256]{1,0:T(1,128)}, s32[1,256]{1,0:T(1,128)S(1)}, u32[]{:S(2)}, u32[]{:S(2)}) collective-permute-start(s32[1,256]{1,0:T(1,128)} %bitcast.12), channel_id=1, source_target_pairs={{2,4},{4,2},{3,5},{5,3},{6,8},{8,6},{7,9},{9,7},{10,12},{12,10},{1... | collective-permute-start | bytes 3080 | tf_op jit(solution)/shard_map/ppermute | solution.py:551
  8.8 4.5 %collective-permute-start = (s32[1,256]{1,0:T(1,128)}, s32[1,256]{1,0:T(1,128)S(1)}, u32[]{:S(2)}, u32[]{:S(2)}) collective-permute-start(s32[1,256]{1,0:T(1,128)} %bitcast.13), channel_id=1, source_target_pairs={{0,2},{2,0},{1,3},{3,1},{4,6},{6,4},{5,7},{7,5},{8,10},{10,8},{9,1... | collective-permute-start | bytes 3080 | tf_op jit(solution)/shard_map/ppermute | solution.py:551
  14.0 6.7 %collective-permute-start.4 = (bf16[128,128]{1,0:T(8,128)(2,1)S(1)}, bf16[128,128]{1,0:T(8,128)(2,1)S(1)}, u32[]{:S(2)}, u32[]{:S(2)}) collective-permute-start(bf16[128,128]{1,0:T(8,128)(2,1)S(1)} %get-tuple-element.114), channel_id=1, source_target_pairs={{4,8},{8,4},{5,9},{9,5},{6,10},{10,6},{7,11},{11,7},{12,16},{16,12... | collective-permute-start | bytes 98312 | tf_op jit(solution)/shard_map/ppermute | solution.py:551
  16.0 7.5 %collective-permute-start.5 = (bf16[128,128]{1,0:T(8,128)(2,1)S(1)}, bf16[128,128]{1,0:T(8,128)(2,1)S(1)}, u32[]{:S(2)}, u32[]{:S(2)}) collective-permute-start(bf16[128,128]{1,0:T(8,128)(2,1)S(1)} %get-tuple-element.115), channel_id=1, source_target_pairs={{2,4},{4,2},{3,5},{5,3},{6,8},{8,6},{7,9},{9,7},{10,12},{12,10},{1... | collective-permute-start | bytes 98312 | tf_op jit(solution)/shard_map/ppermute | solution.py:551
  18.8 6.9 %collective-permute-start.6 = (bf16[128,128]{1,0:T(8,128)(2,1)S(1)}, bf16[128,128]{1,0:T(8,128)(2,1)S(1)}, u32[]{:S(2)}, u32[]{:S(2)}) collective-permute-start(bf16[128,128]{1,0:T(8,128)(2,1)S(1)} %get-tuple-element.116), channel_id=1, source_target_pairs={{1,2},{2,1},{3,4},{4,3},{5,6},{6,5},{7,8},{8,7},{9,10},{10,9},{11,... | collective-permute-start | bytes 98312 | tf_op jit(solution)/shard_map/ppermute | solution.py:551
  19.7 6.1 %collective-permute-start.7 = (bf16[128,128]{1,0:T(8,128)(2,1)S(1)}, bf16[128,128]{1,0:T(8,128)(2,1)S(1)}, u32[]{:S(2)}, u32[]{:S(2)}) collective-permute-start(bf16[128,128]{1,0:T(8,128)(2,1)S(1)} %get-tuple-element.117), channel_id=1, source_target_pairs={{0,4},{4,0},{1,5},{5,1},{2,6},{6,2},{3,7},{7,3},{8,12},{12,8},{9,1... | collective-permute-start | bytes 98312 | tf_op jit(solution)/shard_map/ppermute | solution.py:551
  19.7 6.1 %collective-permute-start.8 = (bf16[128,128]{1,0:T(8,128)(2,1)S(1)}, bf16[128,128]{1,0:T(8,128)(2,1)S(1)}, u32[]{:S(2)}, u32[]{:S(2)}) collective-permute-start(bf16[128,128]{1,0:T(8,128)(2,1)S(1)} %get-tuple-element.118), channel_id=1, source_target_pairs={{0,2},{2,0},{1,3},{3,1},{4,6},{6,4},{5,7},{7,5},{8,10},{10,8},{9,1... | collective-permute-start | bytes 98312 | tf_op jit(solution)/shard_map/ppermute | solution.py:551
  20.7 5.1 %collective-permute-start.9 = (bf16[128,128]{1,0:T(8,128)(2,1)S(1)}, bf16[128,128]{1,0:T(8,128)(2,1)S(1)}, u32[]{:S(2)}, u32[]{:S(2)}) collective-permute-start(bf16[128,128]{1,0:T(8,128)(2,1)S(1)} %get-tuple-element.119), channel_id=1, source_target_pairs={{0,1},{1,0},{2,3},{3,2},{4,5},{5,4},{6,7},{7,6},{8,9},{9,8},{10,11... | collective-permute-start | bytes 98312 | tf_op jit(solution)/shard_map/ppermute | solution.py:551
  26.2 7.0 %collective-permute-start.10 = (bf16[128,128]{1,0:T(8,128)(2,1)S(1)}, bf16[128,128]{1,0:T(8,128)(2,1)S(1)}, u32[]{:S(2)}, u32[]{:S(2)}) collective-permute-start(bf16[128,128]{1,0:T(8,128)(2,1)S(1)} %get-tuple-element.124), channel_id=1, source_target_pairs={{4,8},{8,4},{5,9},{9,5},{6,10},{10,6},{7,11},{11,7},{12,16},{16,12... | collective-permute-start | bytes 98312 | tf_op jit(solution)/shard_map/ppermute | solution.py:551
  26.4 7.9 %collective-permute-start.11 = (bf16[128,128]{1,0:T(8,128)(2,1)S(1)}, bf16[128,128]{1,0:T(8,128)(2,1)S(1)}, u32[]{:S(2)}, u32[]{:S(2)}) collective-permute-start(bf16[128,128]{1,0:T(8,128)(2,1)S(1)} %get-tuple-element.125), channel_id=1, source_target_pairs={{2,4},{4,2},{3,5},{5,3},{6,8},{8,6},{7,9},{9,7},{10,12},{12,10},{1... | collective-permute-start | bytes 98312 | tf_op jit(solution)/shard_map/ppermute | solution.py:551
  28.2 7.0 %collective-permute-start.12 = (bf16[128,128]{1,0:T(8,128)(2,1)S(1)}, bf16[128,128]{1,0:T(8,128)(2,1)S(1)}, u32[]{:S(2)}, u32[]{:S(2)}) collective-permute-start(bf16[128,128]{1,0:T(8,128)(2,1)S(1)} %get-tuple-element.126), channel_id=1, source_target_pairs={{1,2},{2,1},{3,4},{4,3},{5,6},{6,5},{7,8},{8,7},{9,10},{10,9},{11,... | collective-permute-start | bytes 98312 | tf_op jit(solution)/shard_map/ppermute | solution.py:551
  31.3 4.2 %collective-permute-start.13 = (bf16[128,128]{1,0:T(8,128)(2,1)S(1)}, bf16[128,128]{1,0:T(8,128)(2,1)S(1)}, u32[]{:S(2)}, u32[]{:S(2)}) collective-permute-start(bf16[128,128]{1,0:T(8,128)(2,1)S(1)} %get-tuple-element.127), channel_id=1, source_target_pairs={{0,4},{4,0},{1,5},{5,1},{2,6},{6,2},{3,7},{7,3},{8,12},{12,8},{9,1... | collective-permute-start | bytes 98312 | tf_op jit(solution)/shard_map/ppermute | solution.py:551
  31.3 4.2 %collective-permute-start.14 = (bf16[128,128]{1,0:T(8,128)(2,1)S(1)}, bf16[128,128]{1,0:T(8,128)(2,1)S(1)}, u32[]{:S(2)}, u32[]{:S(2)}) collective-permute-start(bf16[128,128]{1,0:T(8,128)(2,1)S(1)} %get-tuple-element.128), channel_id=1, source_target_pairs={{0,2},{2,0},{1,3},{3,1},{4,6},{6,4},{5,7},{7,5},{8,10},{10,8},{9,1... | collective-permute-start | bytes 98312 | tf_op jit(solution)/shard_map/ppermute | solution.py:551
  33.2 2.3 %collective-permute-start.15 = (bf16[128,128]{1,0:T(8,128)(2,1)S(1)}, bf16[128,128]{1,0:T(8,128)(2,1)S(1)}, u32[]{:S(2)}, u32[]{:S(2)}) collective-permute-start(bf16[128,128]{1,0:T(8,128)(2,1)S(1)} %get-tuple-element.129), channel_id=1, source_target_pairs={{0,1},{1,0},{2,3},{3,2},{4,5},{5,4},{6,7},{7,6},{8,9},{9,8},{10,11... | collective-permute-start | bytes 98312 | tf_op jit(solution)/shard_map/ppermute | solution.py:551
  35.9 6.7 %collective-permute-start.16 = (bf16[128,128]{1,0:T(8,128)(2,1)S(1)}, bf16[128,128]{1,0:T(8,128)(2,1)S(1)}, u32[]{:S(2)}, u32[]{:S(2)}) collective-permute-start(bf16[128,128]{1,0:T(8,128)(2,1)S(1)} %get-tuple-element.135), channel_id=1, source_target_pairs={{4,8},{8,4},{5,9},{9,5},{6,10},{10,6},{7,11},{11,7},{12,16},{16,12... | collective-permute-start | bytes 98312 | tf_op jit(solution)/shard_map/ppermute | solution.py:551
  36.8 7.5 %collective-permute-start.17 = (bf16[128,128]{1,0:T(8,128)(2,1)S(1)}, bf16[128,128]{1,0:T(8,128)(2,1)S(1)}, u32[]{:S(2)}, u32[]{:S(2)}) collective-permute-start(bf16[128,128]{1,0:T(8,128)(2,1)S(1)} %get-tuple-element.136), channel_id=1, source_target_pairs={{2,4},{4,2},{3,5},{5,3},{6,8},{8,6},{7,9},{9,7},{10,12},{12,10},{1... | collective-permute-start | bytes 98312 | tf_op jit(solution)/shard_map/ppermute | solution.py:551
  39.8 6.9 %collective-permute-start.18 = (bf16[128,128]{1,0:T(8,128)(2,1)S(1)}, bf16[128,128]{1,0:T(8,128)(2,1)S(1)}, u32[]{:S(2)}, u32[]{:S(2)}) collective-permute-start(bf16[128,128]{1,0:T(8,128)(2,1)S(1)} %get-tuple-element.137), channel_id=1, source_target_pairs={{1,2},{2,1},{3,4},{4,3},{5,6},{6,5},{7,8},{8,7},{9,10},{10,9},{11,... | collective-permute-start | bytes 98312 | tf_op jit(solution)/shard_map/ppermute | solution.py:551
  42.2 4.6 %collective-permute-start.19 = (bf16[128,128]{1,0:T(8,128)(2,1)S(1)}, bf16[128,128]{1,0:T(8,128)(2,1)S(1)}, u32[]{:S(2)}, u32[]{:S(2)}) collective-permute-start(bf16[128,128]{1,0:T(8,128)(2,1)S(1)} %get-tuple-element.138), channel_id=1, source_target_pairs={{0,4},{4,0},{1,5},{5,1},{2,6},{6,2},{3,7},{7,3},{8,12},{12,8},{9,1... | collective-permute-start | bytes 98312 | tf_op jit(solution)/shard_map/ppermute | solution.py:551
  42.2 4.6 %collective-permute-start.20 = (bf16[128,128]{1,0:T(8,128)(2,1)S(1)}, bf16[128,128]{1,0:T(8,128)(2,1)S(1)}, u32[]{:S(2)}, u32[]{:S(2)}) collective-permute-start(bf16[128,128]{1,0:T(8,128)(2,1)S(1)} %get-tuple-element.139), channel_id=1, source_target_pairs={{0,2},{2,0},{1,3},{3,1},{4,6},{6,4},{5,7},{7,5},{8,10},{10,8},{9,1... | collective-permute-start | bytes 98312 | tf_op jit(solution)/shard_map/ppermute | solution.py:551
  42.6 4.2 %collective-permute-start.21 = (bf16[128,128]{1,0:T(8,128)(2,1)S(1)}, bf16[128,128]{1,0:T(8,128)(2,1)S(1)}, u32[]{:S(2)}, u32[]{:S(2)}) collective-permute-start(bf16[128,128]{1,0:T(8,128)(2,1)S(1)} %get-tuple-element.140), channel_id=1, source_target_pairs={{0,1},{1,0},{2,3},{3,2},{4,5},{5,4},{6,7},{7,6},{8,9},{9,8},{10,11... | collective-permute-start | bytes 98312 | tf_op jit(solution)/shard_map/ppermute | solution.py:551
  47.2 7.0 %collective-permute-start.22 = (bf16[128,128]{1,0:T(8,128)(2,1)S(1)}, bf16[128,128]{1,0:T(8,128)(2,1)S(1)}, u32[]{:S(2)}, u32[]{:S(2)}) collective-permute-start(bf16[128,128]{1,0:T(8,128)(2,1)S(1)} %get-tuple-element.146), channel_id=1, source_target_pairs={{4,8},{8,4},{5,9},{9,5},{6,10},{10,6},{7,11},{11,7},{12,16},{16,12... | collective-permute-start | bytes 98312 | tf_op jit(solution)/shard_map/ppermute | solution.py:551
  47.5 7.8 %collective-permute-start.23 = (bf16[128,128]{1,0:T(8,128)(2,1)S(1)}, bf16[128,128]{1,0:T(8,128)(2,1)S(1)}, u32[]{:S(2)}, u32[]{:S(2)}) collective-permute-start(bf16[128,128]{1,0:T(8,128)(2,1)S(1)} %get-tuple-element.147), channel_id=1, source_target_pairs={{2,4},{4,2},{3,5},{5,3},{6,8},{8,6},{7,9},{9,7},{10,12},{12,10},{1... | collective-permute-start | bytes 98312 | tf_op jit(solution)/shard_map/ppermute | solution.py:551
  50.8 7.0 %collective-permute-start.24 = (bf16[128,128]{1,0:T(8,128)(2,1)S(1)}, bf16[128,128]{1,0:T(8,128)(2,1)S(1)}, u32[]{:S(2)}, u32[]{:S(2)}) collective-permute-start(bf16[128,128]{1,0:T(8,128)(2,1)S(1)} %get-tuple-element.148), channel_id=1, source_target_pairs={{1,2},{2,1},{3,4},{4,3},{5,6},{6,5},{7,8},{8,7},{9,10},{10,9},{11,... | collective-permute-start | bytes 98312 | tf_op jit(solution)/shard_map/ppermute | solution.py:551
  52.3 5.5 %collective-permute-start.25 = (bf16[128,128]{1,0:T(8,128)(2,1)S(1)}, bf16[128,128]{1,0:T(8,128)(2,1)S(1)}, u32[]{:S(2)}, u32[]{:S(2)}) collective-permute-start(bf16[128,128]{1,0:T(8,128)(2,1)S(1)} %get-tuple-element.149), channel_id=1, source_target_pairs={{0,4},{4,0},{1,5},{5,1},{2,6},{6,2},{3,7},{7,3},{8,12},{12,8},{9,1... | collective-permute-start | bytes 98312 | tf_op jit(solution)/shard_map/ppermute | solution.py:551
  52.3 5.5 %collective-permute-start.26 = (bf16[128,128]{1,0:T(8,128)(2,1)S(1)}, bf16[128,128]{1,0:T(8,128)(2,1)S(1)}, u32[]{:S(2)}, u32[]{:S(2)}) collective-permute-start(bf16[128,128]{1,0:T(8,128)(2,1)S(1)} %get-tuple-element.150), channel_id=1, source_target_pairs={{0,2},{2,0},{1,3},{3,1},{4,6},{6,4},{5,7},{7,5},{8,10},{10,8},{9,1... | collective-permute-start | bytes 98312 | tf_op jit(solution)/shard_map/ppermute | solution.py:551
  54.2 3.6 %collective-permute-start.27 = (bf16[128,128]{1,0:T(8,128)(2,1)S(1)}, bf16[128,128]{1,0:T(8,128)(2,1)S(1)}, u32[]{:S(2)}, u32[]{:S(2)}) collective-permute-start(bf16[128,128]{1,0:T(8,128)(2,1)S(1)} %get-tuple-element.151), channel_id=1, source_target_pairs={{0,1},{1,0},{2,3},{3,2},{4,5},{5,4},{6,7},{7,6},{8,9},{9,8},{10,11... | collective-permute-start | bytes 98312 | tf_op jit(solution)/shard_map/ppermute | solution.py:551
  58.2 7.1 %collective-permute-start.28 = (bf16[128,128]{1,0:T(8,128)(2,1)S(1)}, bf16[128,128]{1,0:T(8,128)(2,1)S(1)}, u32[]{:S(2)}, u32[]{:S(2)}) collective-permute-start(bf16[128,128]{1,0:T(8,128)(2,1)S(1)} %get-tuple-element.157), channel_id=1, source_target_pairs={{4,8},{8,4},{5,9},{9,5},{6,10},{10,6},{7,11},{11,7},{12,16},{16,12... | collective-permute-start | bytes 98312 | tf_op jit(solution)/shard_map/ppermute | solution.py:551
  58.4 8.0 %collective-permute-start.29 = (bf16[128,128]{1,0:T(8,128)(2,1)S(1)}, bf16[128,128]{1,0:T(8,128)(2,1)S(1)}, u32[]{:S(2)}, u32[]{:S(2)}) collective-permute-start(bf16[128,128]{1,0:T(8,128)(2,1)S(1)} %get-tuple-element.158), channel_id=1, source_target_pairs={{2,4},{4,2},{3,5},{5,3},{6,8},{8,6},{7,9},{9,7},{10,12},{12,10},{1... | collective-permute-start | bytes 98312 | tf_op jit(solution)/shard_map/ppermute | solution.py:551
  61.8 7.0 %collective-permute-start.30 = (bf16[128,128]{1,0:T(8,128)(2,1)S(1)}, bf16[128,128]{1,0:T(8,128)(2,1)S(1)}, u32[]{:S(2)}, u32[]{:S(2)}) collective-permute-start(bf16[128,128]{1,0:T(8,128)(2,1)S(1)} %get-tuple-element.159), channel_id=1, source_target_pairs={{1,2},{2,1},{3,4},{4,3},{5,6},{6,5},{7,8},{8,7},{9,10},{10,9},{11,... | collective-permute-start | bytes 98312 | tf_op jit(solution)/shard_map/ppermute | solution.py:551
  63.2 5.6 %collective-permute-start.31 = (bf16[128,128]{1,0:T(8,128)(2,1)S(1)}, bf16[128,128]{1,0:T(8,128)(2,1)S(1)}, u32[]{:S(2)}, u32[]{:S(2)}) collective-permute-start(bf16[128,128]{1,0:T(8,128)(2,1)S(1)} %get-tuple-element.160), channel_id=1, source_target_pairs={{0,4},{4,0},{1,5},{5,1},{2,6},{6,2},{3,7},{7,3},{8,12},{12,8},{9,1... | collective-permute-start | bytes 98312 | tf_op jit(solution)/shard_map/ppermute | solution.py:551
  63.2 5.6 %collective-permute-start.32 = (bf16[128,128]{1,0:T(8,128)(2,1)S(1)}, bf16[128,128]{1,0:T(8,128)(2,1)S(1)}, u32[]{:S(2)}, u32[]{:S(2)}) collective-permute-start(bf16[128,128]{1,0:T(8,128)(2,1)S(1)} %get-tuple-element.161), channel_id=1, source_target_pairs={{0,2},{2,0},{1,3},{3,1},{4,6},{6,4},{5,7},{7,5},{8,10},{10,8},{9,1... | collective-permute-start | bytes 98312 | tf_op jit(solution)/shard_map/ppermute | solution.py:551
  65.3 3.6 %collective-permute-start.33 = (bf16[128,128]{1,0:T(8,128)(2,1)S(1)}, bf16[128,128]{1,0:T(8,128)(2,1)S(1)}, u32[]{:S(2)}, u32[]{:S(2)}) collective-permute-start(bf16[128,128]{1,0:T(8,128)(2,1)S(1)} %get-tuple-element.162), channel_id=1, source_target_pairs={{0,1},{1,0},{2,3},{3,2},{4,5},{5,4},{6,7},{7,6},{8,9},{9,8},{10,11... | collective-permute-start | bytes 98312 | tf_op jit(solution)/shard_map/ppermute | solution.py:551
  69.2 7.0 %collective-permute-start.34 = (bf16[128,128]{1,0:T(8,128)(2,1)S(1)}, bf16[128,128]{1,0:T(8,128)(2,1)S(1)}, u32[]{:S(2)}, u32[]{:S(2)}) collective-permute-start(bf16[128,128]{1,0:T(8,128)(2,1)S(1)} %get-tuple-element.168), channel_id=1, source_target_pairs={{4,8},{8,4},{5,9},{9,5},{6,10},{10,6},{7,11},{11,7},{12,16},{16,12... | collective-permute-start | bytes 98312 | tf_op jit(solution)/shard_map/ppermute | solution.py:551
  69.4 8.2 %collective-permute-start.35 = (bf16[128,128]{1,0:T(8,128)(2,1)S(1)}, bf16[128,128]{1,0:T(8,128)(2,1)S(1)}, u32[]{:S(2)}, u32[]{:S(2)}) collective-permute-start(bf16[128,128]{1,0:T(8,128)(2,1)S(1)} %get-tuple-element.169), channel_id=1, source_target_pairs={{2,4},{4,2},{3,5},{5,3},{6,8},{8,6},{7,9},{9,7},{10,12},{12,10},{1... | collective-permute-start | bytes 98312 | tf_op jit(solution)/shard_map/ppermute | solution.py:551
  72.0 6.9 %collective-permute-start.36 = (bf16[128,128]{1,0:T(8,128)(2,1)S(1)}, bf16[128,128]{1,0:T(8,128)(2,1)S(1)}, u32[]{:S(2)}, u32[]{:S(2)}) collective-permute-start(bf16[128,128]{1,0:T(8,128)(2,1)S(1)} %get-tuple-element.170), channel_id=1, source_target_pairs={{1,2},{2,1},{3,4},{4,3},{5,6},{6,5},{7,8},{8,7},{9,10},{10,9},{11,... | collective-permute-start | bytes 98312 | tf_op jit(solution)/shard_map/ppermute | solution.py:551
  74.2 4.7 %collective-permute-start.37 = (bf16[128,128]{1,0:T(8,128)(2,1)S(1)}, bf16[128,128]{1,0:T(8,128)(2,1)S(1)}, u32[]{:S(2)}, u32[]{:S(2)}) collective-permute-start(bf16[128,128]{1,0:T(8,128)(2,1)S(1)} %get-tuple-element.171), channel_id=1, source_target_pairs={{0,4},{4,0},{1,5},{5,1},{2,6},{6,2},{3,7},{7,3},{8,12},{12,8},{9,1... | collective-permute-start | bytes 98312 | tf_op jit(solution)/shard_map/ppermute | solution.py:551
  74.2 4.7 %collective-permute-start.38 = (bf16[128,128]{1,0:T(8,128)(2,1)S(1)}, bf16[128,128]{1,0:T(8,128)(2,1)S(1)}, u32[]{:S(2)}, u32[]{:S(2)}) collective-permute-start(bf16[128,128]{1,0:T(8,128)(2,1)S(1)} %get-tuple-element.172), channel_id=1, source_target_pairs={{0,2},{2,0},{1,3},{3,1},{4,6},{6,4},{5,7},{7,5},{8,10},{10,8},{9,1... | collective-permute-start | bytes 98312 | tf_op jit(solution)/shard_map/ppermute | solution.py:551
  76.3 2.7 %collective-permute-start.39 = (bf16[128,128]{1,0:T(8,128)(2,1)S(1)}, bf16[128,128]{1,0:T(8,128)(2,1)S(1)}, u32[]{:S(2)}, u32[]{:S(2)}) collective-permute-start(bf16[128,128]{1,0:T(8,128)(2,1)S(1)} %get-tuple-element.173), channel_id=1, source_target_pairs={{0,1},{1,0},{2,3},{3,2},{4,5},{5,4},{6,7},{7,6},{8,9},{9,8},{10,11... | collective-permute-start | bytes 98312 | tf_op jit(solution)/shard_map/ppermute | solution.py:551
  79.4 6.7 %collective-permute-start.40 = (bf16[128,128]{1,0:T(8,128)(2,1)S(1)}, bf16[128,128]{1,0:T(8,128)(2,1)S(1)}, u32[]{:S(2)}, u32[]{:S(2)}) collective-permute-start(bf16[128,128]{1,0:T(8,128)(2,1)S(1)} %get-tuple-element.179), channel_id=1, source_target_pairs={{4,8},{8,4},{5,9},{9,5},{6,10},{10,6},{7,11},{11,7},{12,16},{16,12... | collective-permute-start | bytes 98312 | tf_op jit(solution)/shard_map/ppermute | solution.py:551
  79.9 7.5 %collective-permute-start.41 = (bf16[128,128]{1,0:T(8,128)(2,1)S(1)}, bf16[128,128]{1,0:T(8,128)(2,1)S(1)}, u32[]{:S(2)}, u32[]{:S(2)}) collective-permute-start(bf16[128,128]{1,0:T(8,128)(2,1)S(1)} %get-tuple-element.180), channel_id=1, source_target_pairs={{2,4},{4,2},{3,5},{5,3},{6,8},{8,6},{7,9},{9,7},{10,12},{12,10},{1... | collective-permute-start | bytes 98312 | tf_op jit(solution)/shard_map/ppermute | solution.py:551
  82.9 6.9 %collective-permute-start.42 = (bf16[128,128]{1,0:T(8,128)(2,1)S(1)}, bf16[128,128]{1,0:T(8,128)(2,1)S(1)}, u32[]{:S(2)}, u32[]{:S(2)}) collective-permute-start(bf16[128,128]{1,0:T(8,128)(2,1)S(1)} %get-tuple-element.181), channel_id=1, source_target_pairs={{1,2},{2,1},{3,4},{4,3},{5,6},{6,5},{7,8},{8,7},{9,10},{10,9},{11,... | collective-permute-start | bytes 98312 | tf_op jit(solution)/shard_map/ppermute | solution.py:551
  85.3 4.6 %collective-permute-start.43 = (bf16[128,128]{1,0:T(8,128)(2,1)S(1)}, bf16[128,128]{1,0:T(8,128)(2,1)S(1)}, u32[]{:S(2)}, u32[]{:S(2)}) collective-permute-start(bf16[128,128]{1,0:T(8,128)(2,1)S(1)} %get-tuple-element.182), channel_id=1, source_target_pairs={{0,4},{4,0},{1,5},{5,1},{2,6},{6,2},{3,7},{7,3},{8,12},{12,8},{9,1... | collective-permute-start | bytes 98312 | tf_op jit(solution)/shard_map/ppermute | solution.py:551
  85.3 4.6 %collective-permute-start.44 = (bf16[128,128]{1,0:T(8,128)(2,1)S(1)}, bf16[128,128]{1,0:T(8,128)(2,1)S(1)}, u32[]{:S(2)}, u32[]{:S(2)}) collective-permute-start(bf16[128,128]{1,0:T(8,128)(2,1)S(1)} %get-tuple-element.183), channel_id=1, source_target_pairs={{0,2},{2,0},{1,3},{3,1},{4,6},{6,4},{5,7},{7,5},{8,10},{10,8},{9,1... | collective-permute-start | bytes 98312 | tf_op jit(solution)/shard_map/ppermute | solution.py:551
  86.0 3.8 %collective-permute-start.45 = (bf16[128,128]{1,0:T(8,128)(2,1)S(1)}, bf16[128,128]{1,0:T(8,128)(2,1)S(1)}, u32[]{:S(2)}, u32[]{:S(2)}) collective-permute-start(bf16[128,128]{1,0:T(8,128)(2,1)S(1)} %get-tuple-element.184), channel_id=1, source_target_pairs={{0,1},{1,0},{2,3},{3,2},{4,5},{5,4},{6,7},{7,6},{8,9},{9,8},{10,11... | collective-permute-start | bytes 98312 | tf_op jit(solution)/shard_map/ppermute | solution.py:551
  90.3 7.0 %collective-permute-start.46 = (bf16[128,128]{1,0:T(8,128)(2,1)S(1)}, bf16[128,128]{1,0:T(8,128)(2,1)S(1)}, u32[]{:S(2)}, u32[]{:S(2)}) collective-permute-start(bf16[128,128]{1,0:T(8,128)(2,1)S(1)} %get-tuple-element.188), channel_id=1, source_target_pairs={{4,8},{8,4},{5,9},{9,5},{6,10},{10,6},{7,11},{11,7},{12,16},{16,12... | collective-permute-start | bytes 98312 | tf_op jit(solution)/shard_map/ppermute | solution.py:551
  90.6 7.6 %collective-permute-start.47 = (bf16[128,128]{1,0:T(8,128)(2,1)S(1)}, bf16[128,128]{1,0:T(8,128)(2,1)S(1)}, u32[]{:S(2)}, u32[]{:S(2)}) collective-permute-start(bf16[128,128]{1,0:T(8,128)(2,1)S(1)} %get-tuple-element.189), channel_id=1, source_target_pairs={{2,4},{4,2},{3,5},{5,3},{6,8},{8,6},{7,9},{9,7},{10,12},{12,10},{1... | collective-permute-start | bytes 98312 | tf_op jit(solution)/shard_map/ppermute | solution.py:551
  93.8 7.0 %collective-permute-start.48 = (bf16[128,128]{1,0:T(8,128)(2,1)S(1)}, bf16[128,128]{1,0:T(8,128)(2,1)S(1)}, u32[]{:S(2)}, u32[]{:S(2)}) collective-permute-start(bf16[128,128]{1,0:T(8,128)(2,1)S(1)} %get-tuple-element.190), channel_id=1, source_target_pairs={{1,2},{2,1},{3,4},{4,3},{5,6},{6,5},{7,8},{8,7},{9,10},{10,9},{11,... | collective-permute-start | bytes 98312 | tf_op jit(solution)/shard_map/ppermute | solution.py:551
  95.4 5.4 %collective-permute-start.49 = (bf16[128,128]{1,0:T(8,128)(2,1)S(1)}, bf16[128,128]{1,0:T(8,128)(2,1)S(1)}, u32[]{:S(2)}, u32[]{:S(2)}) collective-permute-start(bf16[128,128]{1,0:T(8,128)(2,1)S(1)} %get-tuple-element.191), channel_id=1, source_target_pairs={{0,4},{4,0},{1,5},{5,1},{2,6},{6,2},{3,7},{7,3},{8,12},{12,8},{9,1... | collective-permute-start | bytes 98312 | tf_op jit(solution)/shard_map/ppermute | solution.py:551
  95.4 5.4 %collective-permute-start.50 = (bf16[128,128]{1,0:T(8,128)(2,1)S(1)}, bf16[128,128]{1,0:T(8,128)(2,1)S(1)}, u32[]{:S(2)}, u32[]{:S(2)}) collective-permute-start(bf16[128,128]{1,0:T(8,128)(2,1)S(1)} %get-tuple-element.192), channel_id=1, source_target_pairs={{0,2},{2,0},{1,3},{3,1},{4,6},{6,4},{5,7},{7,5},{8,10},{10,8},{9,1... | collective-permute-start | bytes 98312 | tf_op jit(solution)/shard_map/ppermute | solution.py:551
  97.3 3.5 %collective-permute-start.51 = (bf16[128,128]{1,0:T(8,128)(2,1)S(1)}, bf16[128,128]{1,0:T(8,128)(2,1)S(1)}, u32[]{:S(2)}, u32[]{:S(2)}) collective-permute-start(bf16[128,128]{1,0:T(8,128)(2,1)S(1)} %get-tuple-element.193), channel_id=1, source_target_pairs={{0,1},{1,0},{2,3},{3,2},{4,5},{5,4},{6,7},{7,6},{8,9},{9,8},{10,11... | collective-permute-start | bytes 98312 | tf_op jit(solution)/shard_map/ppermute | solution.py:551
  101.6 1.3 %collective-permute-start.52 = (f32[64,128]{1,0:T(8,128)S(1)}, f32[64,128]{1,0:T(8,128)S(1)}, u32[]{:S(2)}, u32[]{:S(2)}) collective-permute-start(f32[64,128]{1,0:T(8,128)S(1)} %get-tuple-element.195), channel_id=1, source_target_pairs={{0,1},{1,0},{2,3},{3,2},{4,5},{5,4},{6,7},{7,6},{8,9},{9,8},{10,11... | collective-permute-start | bytes 98312 | tf_op jit(solution)/shard_map/ppermute | solution.py:534
  102.9 5.0 %collective-permute-start.55 = (f32[64,128]{1,0:T(8,128)S(1)}, f32[64,128]{1,0:T(8,128)S(1)}, u32[]{:S(2)}, u32[]{:S(2)}) collective-permute-start(f32[64,128]{1,0:T(8,128)S(1)} %add.25), channel_id=1, source_target_pairs={{0,6},{1,7},{2,4},{3,5},{4,2},{5,3},{6,0},{7,1},{8,14},{9,15},{10,... | collective-permute-start | bytes 98312 | tf_op jit(solution)/shard_map/ppermute | solution.py:534
  102.9 4.9 %collective-permute-start.54 = (f32[64,128]{1,0:T(8,128)S(1)}, f32[64,128]{1,0:T(8,128)S(1)}, u32[]{:S(2)}, u32[]{:S(2)}) collective-permute-start(f32[64,128]{1,0:T(8,128)S(1)} %add.25), channel_id=1, source_target_pairs={{0,4},{1,5},{2,6},{3,7},{4,0},{5,1},{6,2},{7,3},{8,12},{9,13},{10,... | collective-permute-start | bytes 98312 | tf_op jit(solution)/shard_map/ppermute | solution.py:534
  103.8 4.4 %collective-permute-start.53 = (f32[64,128]{1,0:T(8,128)S(1)}, f32[64,128]{1,0:T(8,128)S(1)}, u32[]{:S(2)}, u32[]{:S(2)}) collective-permute-start(f32[64,128]{1,0:T(8,128)S(1)} %add.25), channel_id=1, source_target_pairs={{0,2},{1,3},{2,0},{3,1},{4,6},{5,7},{6,4},{7,5},{8,10},{9,11},{10,... | collective-permute-start | bytes 98312 | tf_op jit(solution)/shard_map/ppermute | solution.py:534
  108.3 6.0 %collective-permute-start.58 = (f32[64,128]{1,0:T(8,128)S(1)}, f32[64,128]{1,0:T(8,128)S(1)}, u32[]{:S(2)}, u32[]{:S(2)}) collective-permute-start(f32[64,128]{1,0:T(8,128)S(1)} %add_add_fusion.1), channel_id=1, source_target_pairs={{0,24},{1,25},{2,26},{3,27},{4,28},{5,29},{6,30},{7,31},{8,16},{9,... | collective-permute-start | bytes 98312 | tf_op jit(solution)/shard_map/ppermute | solution.py:534
  110.4 4.8 %collective-permute-start.57 = (f32[64,128]{1,0:T(8,128)S(1)}, f32[64,128]{1,0:T(8,128)S(1)}, u32[]{:S(2)}, u32[]{:S(2)}) collective-permute-start(f32[64,128]{1,0:T(8,128)S(1)} %add_add_fusion.1), channel_id=1, source_target_pairs={{0,16},{1,17},{2,18},{3,19},{4,20},{5,21},{6,22},{7,23},{8,24},{9,... | collective-permute-start | bytes 98312 | tf_op jit(solution)/shard_map/ppermute | solution.py:534
  110.4 4.8 %collective-permute-start.56 = (f32[64,128]{1,0:T(8,128)S(1)}, f32[64,128]{1,0:T(8,128)S(1)}, u32[]{:S(2)}, u32[]{:S(2)}) collective-permute-start(f32[64,128]{1,0:T(8,128)S(1)} %add_add_fusion.1), channel_id=1, source_target_pairs={{0,8},{1,9},{2,10},{3,11},{4,12},{5,13},{6,14},{7,15},{8,0},{9,1},... | collective-permute-start | bytes 98312 | tf_op jit(solution)/shard_map/ppermute | solution.py:534
  115.2 1.3 %collective-permute-start.59 = (f32[64,128]{1,0:T(8,128)S(1)}, f32[64,128]{1,0:T(8,128)S(1)}, u32[]{:S(2)}, u32[]{:S(2)}) collective-permute-start(f32[64,128]{1,0:T(8,128)S(1)} %add_add_fusion.refs_1_), channel_id=1, source_target_pairs={{0,1},{1,0},{2,3},{3,2},{4,5},{5,4},{6,7},{7,6},{8,9},{9,8},{10,11... | collective-permute-start | bytes 98312 | tf_op jit(solution)/shard_map/ppermute | solution.py:534

commit v8 on v7

--- a/solution.py
+++ b/solution.py
@@ -448,7 +448,7 @@
     return terms[0]
 
 
-def finish_kernel(scale, place_ref, own_ref, other_ref, field_ref, out_ref, inverse_ref):
+def finish_kernel(scale, place_ref, own_ref, other_ref, field_ref, out_ref, inverse_ref, stage_ref, sems):
     width = 8
     shape = (width, VECS)
     panels = VECS // width
@@ -514,7 +514,16 @@
         ],
         axis=0,
     )
-    out_ref[...] = parts_joined(dot(field_ref[...], factor, ((1,), (1,))))
+    pieces = sems.shape[0]
+    rows = field_ref.shape[0] // pieces
+    copies = []
+    for i in range(pieces):
+        piece = pl.ds(i * rows, rows)
+        stage_ref[piece, :] = parts_joined(dot(field_ref[piece, :], factor, ((1,), (1,))))
+        copies.append(pltpu.make_async_copy(stage_ref.at[piece], out_ref.at[piece], sems.at[i]))
+        copies[i].start()
+    for copy in copies:
+        copy.wait()
 
 
 def finish(scale, place, halves, field):
@@ -522,8 +531,12 @@
         lambda *refs: finish_kernel(scale, *refs),
         out_shape=jax.ShapeDtypeStruct((field.shape[0], VECS), F32),
         in_specs=[SMEM] + [VMEM] * 3,
-        out_specs=VMEM,
-        scratch_shapes=[pltpu.VMEM((VECS, VECS), F32)],
+        out_specs=HBM,
+        scratch_shapes=[
+            pltpu.VMEM((VECS, VECS), F32),
+            pltpu.VMEM((field.shape[0], VECS), F32),
+            pltpu.SemaphoreType.DMA((4,)),
+        ],
         compiler_params=PARAMS,
         name="finish",
     )(place, *halves, field)
@@ -569,7 +582,9 @@
             )
         ),
     )
-    wanted, band = lax.optimization_barrier((wanted, band))
+    order = (3, 1, 2, 0)
+    *turned_round, band = lax.optimization_barrier((*(wanted[i] for i in order), band))
+    wanted = [turned_round[order.index(i)] for i in range(PEERS)]
     pick_mat, *sent = first(here, field, wanted)
 
     def exchange(sent):

time: 123 us -> 123 us (level)
  starting transfers between devices: 63.4 us -> 61.7 us
  waiting for transfers between devices: 36.8 us -> 38.3 us
    ppermute x52, starting transfers between devices: 55.3 us -> 53.7 us  [swap(): return lax.ppermute(value, AXES, swap_pairs(count, by, odd))]
    ppermute x52, waiting for transfers between devices: 30.1 us -> 31.6 us  [swap(): return lax.ppermute(value, AXES, swap_pairs(count, by, odd))]
  transfers between devices with their start and end apart: 60 -> 60, of which waited for: 27 -> 26; matrix products, arithmetic and copies ran while one was open for 0% -> 0% of each run, Pallas kernels for 10% -> 10%
where the time goes in v8:
time: 123 us
  starting transfers between devices  61.7 us (50%)
  waiting for transfers between devices  38.3 us (31%)
  Pallas kernels  22.5 us (18%)
    ppermute x52, starting transfers between devices, swap(): return lax.ppermute(value, AXES, swap_pairs(count, by, odd))  53.7 us
    ppermute x52, waiting for transfers between devices, swap(): return lax.ppermute(value, AXES, swap_pairs(count, by, odd))  31.6 us
    ppermute x8, starting transfers between devices, swapped(): return lax.ppermute(value, AXES, [(i, i ^ mask) for i in range(count)])  8.08 us
    pallas_call x7, Pallas kernels, inner(): pl.pallas_call(lambda *refs: inner_kernel(scale, before_scale, more, *ref...  7.64 us
    ppermute x8, waiting for transfers between devices, swapped(): return lax.ppermute(value, AXES, [(i, i ^ mask) for i in range(count)])  6.72 us
    pallas_call x1, Pallas kernels, finish(): pl.pallas_call(lambda *refs: finish_kernel(scale, *refs), out_shape=jax.S...  6.52 us
    pallas_call x1, Pallas kernels, prepare(): pl.pallas_call(prepare_kernel, out_shape=(jax.ShapeDtypeStruct((rows, 3 *...  3.08 us
    pallas_call x7, Pallas kernels, step(): pl.pallas_call(lambda *refs: step_kernel(scale, *refs), out_shape=(*SENT,...  2.8 us
  transfers between devices with their start and end apart: 60, of which 26 were waited for; matrix products, arithmetic and copies ran while one was open for 0% of the time, Pallas kernels for 10%

profile of v8, /device:TPU:0, one launch (start us, length us, event | category | flops | bytes accessed | tf_op | source)
XLA Modules:
  0.0 123.0 jit_solution(699895562560832614)
XLA Ops:
  0.0 2.9 %collective-permute-start.3 = (s32[1,256]{1,0:T(1,128)}, s32[1,256]{1,0:T(1,128)S(1)}, u32[]{:S(2)}, u32[]{:S(2)}) collective-permute-start(s32[1,256]{1,0:T(1,128)} %bitcast.10), channel_id=1, source_target_pairs={{0,2},{2,0},{1,3},{3,1},{4,6},{6,4},{5,7},{7,5},{8,10},{10,8},{9,1... | collective-permute-start | bytes 3080 | tf_op jit(solution)/shard_map/ppermute | solution.py:564
  2.9 1.5 %collective-permute-start.2 = (s32[1,256]{1,0:T(1,128)}, s32[1,256]{1,0:T(1,128)S(1)}, u32[]{:S(2)}, u32[]{:S(2)}) collective-permute-start(s32[1,256]{1,0:T(1,128)} %bitcast.11), channel_id=1, source_target_pairs={{0,4},{4,0},{1,5},{5,1},{2,6},{6,2},{3,7},{7,3},{8,12},{12,8},{9,1... | collective-permute-start | bytes 3080 | tf_op jit(solution)/shard_map/ppermute | solution.py:564
  4.5 3.5 %collective-permute-start.1 = (s32[1,256]{1,0:T(1,128)}, s32[1,256]{1,0:T(1,128)S(1)}, u32[]{:S(2)}, u32[]{:S(2)}) collective-permute-start(s32[1,256]{1,0:T(1,128)} %bitcast.12), channel_id=1, source_target_pairs={{2,4},{4,2},{3,5},{5,3},{6,8},{8,6},{7,9},{9,7},{10,12},{12,10},{1... | collective-permute-start | bytes 3080 | tf_op jit(solution)/shard_map/ppermute | solution.py:564
  8.0 1.5 %collective-permute-start = (s32[1,256]{1,0:T(1,128)}, s32[1,256]{1,0:T(1,128)S(1)}, u32[]{:S(2)}, u32[]{:S(2)}) collective-permute-start(s32[1,256]{1,0:T(1,128)} %bitcast.13), channel_id=1, source_target_pairs={{4,8},{8,4},{5,9},{9,5},{6,10},{10,6},{7,11},{11,7},{12,16},{16,12... | collective-permute-start | bytes 3080 | tf_op jit(solution)/shard_map/ppermute | solution.py:564
  9.5 3.1 %prepare.1 = (bf16[2048,384]{1,0:T(8,128)(2,1)S(1)}, bf16[2048,256]{1,0:T(8,128)(2,1)S(1)}, f32[256,128]{1,0:T(8,128)S(1)}, bf16[2048,128]{1,0:T(8,128)(2,1)S(1)}) custom-call(s32[1]{0:T(128)} %bitcast.place_ref.refs_0_, s32[1,256]{1,0:T(1,128)} %bitcast.8, f32[1,256]{1,0:T(1,128)} %bitcast.9, f32[3,8,2048]{2,1,0:T(8,128)} %bitcast.6, ...), custom_call_target="tpu_custom_call" | custom-call | tf_op jit(solution)/shard_map/prepare/pallas_call | solution.py:153
  12.6 1.8 %collective-permute-done.w3 = s32[1,256]{1,0:T(1,128)S(1)} collective-permute-done((s32[1,256]{1,0:T(1,128)}, s32[1,256]{1,0:T(1,128)S(1)}, u32[]{:S(2)}, u32[]{:S(2)}) %collective-permute-start) | collective-permute-done | bytes 1056 | tf_op jit(solution)/shard_map/ppermute | solution.py:564
  14.5 0.6 first.1
  15.1 1.6 %collective-permute-start.4 = (bf16[128,128]{1,0:T(8,128)(2,1)S(1)}, bf16[128,128]{1,0:T(8,128)(2,1)S(1)}, u32[]{:S(2)}, u32[]{:S(2)}) collective-permute-start(bf16[128,128]{1,0:T(8,128)(2,1)S(1)} %get-tuple-element.114), channel_id=1, source_target_pairs={{4,8},{8,4},{5,9},{9,5},{6,10},{10,6},{7,11},{11,7},{12,16},{16,12... | collective-permute-start | bytes 98312 | tf_op jit(solution)/shard_map/ppermute | solution.py:564
  16.6 2.0 %collective-permute-start.5 = (bf16[128,128]{1,0:T(8,128)(2,1)S(1)}, bf16[128,128]{1,0:T(8,128)(2,1)S(1)}, u32[]{:S(2)}, u32[]{:S(2)}) collective-permute-start(bf16[128,128]{1,0:T(8,128)(2,1)S(1)} %get-tuple-element.115), channel_id=1, source_target_pairs={{2,4},{4,2},{3,5},{5,3},{6,8},{8,6},{7,9},{9,7},{10,12},{12,10},{1... | collective-permute-start | bytes 98312 | tf_op jit(solution)/shard_map/ppermute | solution.py:564
  18.6 1.3 %collective-permute-start.6 = (bf16[128,128]{1,0:T(8,128)(2,1)S(1)}, bf16[128,128]{1,0:T(8,128)(2,1)S(1)}, u32[]{:S(2)}, u32[]{:S(2)}) collective-permute-start(bf16[128,128]{1,0:T(8,128)(2,1)S(1)} %get-tuple-element.116), channel_id=1, source_target_pairs={{1,2},{2,1},{3,4},{4,3},{5,6},{6,5},{7,8},{8,7},{9,10},{10,9},{11,... | collective-permute-start | bytes 98312 | tf_op jit(solution)/shard_map/ppermute | solution.py:564
  19.9 1.9 %collective-permute-done.4.refs_8_ = bf16[128,128]{1,0:T(8,128)(2,1)S(1)} collective-permute-done((bf16[128,128]{1,0:T(8,128)(2,1)S(1)}, bf16[128,128]{1,0:T(8,128)(2,1)S(1)}, u32[]{:S(2)}, u32[]{:S(2)}) %collective-permute-start.4) | collective-permute-done | bytes 32800 | tf_op jit(solution)/shard_map/ppermute | solution.py:564
  21.8 1.0 opening.1
  22.9 1.3 %collective-permute-done.5.refs_9_ = bf16[128,128]{1,0:T(8,128)(2,1)S(1)} collective-permute-done((bf16[128,128]{1,0:T(8,128)(2,1)S(1)}, bf16[128,128]{1,0:T(8,128)(2,1)S(1)}, u32[]{:S(2)}, u32[]{:S(2)}) %collective-permute-start.5) | collective-permute-done | bytes 32800 | tf_op jit(solution)/shard_map/ppermute | solution.py:564
  24.2 1.5 %collective-permute-done.6.refs_10_ = bf16[128,128]{1,0:T(8,128)(2,1)S(1)} collective-permute-done((bf16[128,128]{1,0:T(8,128)(2,1)S(1)}, bf16[128,128]{1,0:T(8,128)(2,1)S(1)}, u32[]{:S(2)}, u32[]{:S(2)}) %collective-permute-start.6) | collective-permute-done | bytes 32800 | tf_op jit(solution)/shard_map/ppermute | solution.py:564
  26.2 2.5 %collective-permute-start.11 = (bf16[128,128]{1,0:T(8,128)(2,1)S(1)}, bf16[128,128]{1,0:T(8,128)(2,1)S(1)}, u32[]{:S(2)}, u32[]{:S(2)}) collective-permute-start(bf16[128,128]{1,0:T(8,128)(2,1)S(1)} %get-tuple-element.125), channel_id=1, source_target_pairs={{2,4},{4,2},{3,5},{5,3},{6,8},{8,6},{7,9},{9,7},{10,12},{12,10},{1... | collective-permute-start | bytes 98312 | tf_op jit(solution)/shard_map/ppermute | solution.py:564
  28.8 2.3 %collective-permute-start.12 = (bf16[128,128]{1,0:T(8,128)(2,1)S(1)}, bf16[128,128]{1,0:T(8,128)(2,1)S(1)}, u32[]{:S(2)}, u32[]{:S(2)}) collective-permute-start(bf16[128,128]{1,0:T(8,128)(2,1)S(1)} %get-tuple-element.126), channel_id=1, source_target_pairs={{1,2},{2,1},{3,4},{4,3},{5,6},{6,5},{7,8},{8,7},{9,10},{10,9},{11,... | collective-permute-start | bytes 98312 | tf_op jit(solution)/shard_map/ppermute | solution.py:564
  31.1 2.0 %collective-permute-done.10.refs_8_ = bf16[128,128]{1,0:T(8,128)(2,1)S(1)} collective-permute-done((bf16[128,128]{1,0:T(8,128)(2,1)S(1)}, bf16[128,128]{1,0:T(8,128)(2,1)S(1)}, u32[]{:S(2)}, u32[]{:S(2)}) %collective-permute-start.10) | collective-permute-done | bytes 32800 | tf_op jit(solution)/shard_map/ppermute | solution.py:564
  33.1 1.1 inner.7
  34.2 1.5 %collective-permute-done.12.refs_10_ = bf16[128,128]{1,0:T(8,128)(2,1)S(1)} collective-permute-done((bf16[128,128]{1,0:T(8,128)(2,1)S(1)}, bf16[128,128]{1,0:T(8,128)(2,1)S(1)}, u32[]{:S(2)}, u32[]{:S(2)}) %collective-permute-start.12) | collective-permute-done | bytes 32800 | tf_op jit(solution)/shard_map/ppermute | solution.py:564
  36.1 0.6 collective-permute-start.16
  36.7 2.9 %collective-permute-start.17 = (bf16[128,128]{1,0:T(8,128)(2,1)S(1)}, bf16[128,128]{1,0:T(8,128)(2,1)S(1)}, u32[]{:S(2)}, u32[]{:S(2)}) collective-permute-start(bf16[128,128]{1,0:T(8,128)(2,1)S(1)} %get-tuple-element.136), channel_id=1, source_target_pairs={{2,4},{4,2},{3,5},{5,3},{6,8},{8,6},{7,9},{9,7},{10,12},{12,10},{1... | collective-permute-start | bytes 98312 | tf_op jit(solution)/shard_map/ppermute | solution.py:564
  39.6 2.4 %collective-permute-start.18 = (bf16[128,128]{1,0:T(8,128)(2,1)S(1)}, bf16[128,128]{1,0:T(8,128)(2,1)S(1)}, u32[]{:S(2)}, u32[]{:S(2)}) collective-permute-start(bf16[128,128]{1,0:T(8,128)(2,1)S(1)} %get-tuple-element.137), channel_id=1, source_target_pairs={{1,2},{2,1},{3,4},{4,3},{5,6},{6,5},{7,8},{8,7},{9,10},{10,9},{11,... | collective-permute-start | bytes 98312 | tf_op jit(solution)/shard_map/ppermute | solution.py:564
  42.1 0.7 collective-permute-done.16.refs_8_
  42.8 1.1 inner.8
  44.2 2.4 %collective-permute-done.18.refs_10_ = bf16[128,128]{1,0:T(8,128)(2,1)S(1)} collective-permute-done((bf16[128,128]{1,0:T(8,128)(2,1)S(1)}, bf16[128,128]{1,0:T(8,128)(2,1)S(1)}, u32[]{:S(2)}, u32[]{:S(2)}) %collective-permute-start.18) | collective-permute-done | bytes 32800 | tf_op jit(solution)/shard_map/ppermute | solution.py:564
  47.3 3.3 %collective-permute-start.23 = (bf16[128,128]{1,0:T(8,128)(2,1)S(1)}, bf16[128,128]{1,0:T(8,128)(2,1)S(1)}, u32[]{:S(2)}, u32[]{:S(2)}) collective-permute-start(bf16[128,128]{1,0:T(8,128)(2,1)S(1)} %get-tuple-element.147), channel_id=1, source_target_pairs={{2,4},{4,2},{3,5},{5,3},{6,8},{8,6},{7,9},{9,7},{10,12},{12,10},{1... | collective-permute-start | bytes 98312 | tf_op jit(solution)/shard_map/ppermute | solution.py:564
  50.6 1.5 %collective-permute-start.24 = (bf16[128,128]{1,0:T(8,128)(2,1)S(1)}, bf16[128,128]{1,0:T(8,128)(2,1)S(1)}, u32[]{:S(2)}, u32[]{:S(2)}) collective-permute-start(bf16[128,128]{1,0:T(8,128)(2,1)S(1)} %get-tuple-element.148), channel_id=1, source_target_pairs={{1,2},{2,1},{3,4},{4,3},{5,6},{6,5},{7,8},{8,7},{9,10},{10,9},{11,... | collective-permute-start | bytes 98312 | tf_op jit(solution)/shard_map/ppermute | solution.py:564
  52.1 1.0 collective-permute-start.26
  53.1 0.9 collective-permute-done.22.refs_8_
  54.0 1.1 inner.9
  55.1 2.6 %collective-permute-done.24.refs_10_ = bf16[128,128]{1,0:T(8,128)(2,1)S(1)} collective-permute-done((bf16[128,128]{1,0:T(8,128)(2,1)S(1)}, bf16[128,128]{1,0:T(8,128)(2,1)S(1)}, u32[]{:S(2)}, u32[]{:S(2)}) %collective-permute-start.24) | collective-permute-done | bytes 32800 | tf_op jit(solution)/shard_map/ppermute | solution.py:564
  58.3 3.3 %collective-permute-start.29 = (bf16[128,128]{1,0:T(8,128)(2,1)S(1)}, bf16[128,128]{1,0:T(8,128)(2,1)S(1)}, u32[]{:S(2)}, u32[]{:S(2)}) collective-permute-start(bf16[128,128]{1,0:T(8,128)(2,1)S(1)} %get-tuple-element.158), channel_id=1, source_target_pairs={{2,4},{4,2},{3,5},{5,3},{6,8},{8,6},{7,9},{9,7},{10,12},{12,10},{1... | collective-permute-start | bytes 98312 | tf_op jit(solution)/shard_map/ppermute | solution.py:564
  61.6 1.4 %collective-permute-start.30 = (bf16[128,128]{1,0:T(8,128)(2,1)S(1)}, bf16[128,128]{1,0:T(8,128)(2,1)S(1)}, u32[]{:S(2)}, u32[]{:S(2)}) collective-permute-start(bf16[128,128]{1,0:T(8,128)(2,1)S(1)} %get-tuple-element.159), channel_id=1, source_target_pairs={{1,2},{2,1},{3,4},{4,3},{5,6},{6,5},{7,8},{8,7},{9,10},{10,9},{11,... | collective-permute-start | bytes 98312 | tf_op jit(solution)/shard_map/ppermute | solution.py:564
  63.3 1.9 %collective-permute-done.28.refs_8_ = bf16[128,128]{1,0:T(8,128)(2,1)S(1)} collective-permute-done((bf16[128,128]{1,0:T(8,128)(2,1)S(1)}, bf16[128,128]{1,0:T(8,128)(2,1)S(1)}, u32[]{:S(2)}, u32[]{:S(2)}) %collective-permute-start.28) | collective-permute-done | bytes 32800 | tf_op jit(solution)/shard_map/ppermute | solution.py:564
  65.1 1.1 inner.10
  66.2 2.4 %collective-permute-done.30.refs_10_ = bf16[128,128]{1,0:T(8,128)(2,1)S(1)} collective-permute-done((bf16[128,128]{1,0:T(8,128)(2,1)S(1)}, bf16[128,128]{1,0:T(8,128)(2,1)S(1)}, u32[]{:S(2)}, u32[]{:S(2)}) %collective-permute-start.30) | collective-permute-done | bytes 32800 | tf_op jit(solution)/shard_map/ppermute | solution.py:564
  69.3 2.5 %collective-permute-start.35 = (bf16[128,128]{1,0:T(8,128)(2,1)S(1)}, bf16[128,128]{1,0:T(8,128)(2,1)S(1)}, u32[]{:S(2)}, u32[]{:S(2)}) collective-permute-start(bf16[128,128]{1,0:T(8,128)(2,1)S(1)} %get-tuple-element.169), channel_id=1, source_target_pairs={{2,4},{4,2},{3,5},{5,3},{6,8},{8,6},{7,9},{9,7},{10,12},{12,10},{1... | collective-permute-start | bytes 98312 | tf_op jit(solution)/shard_map/ppermute | solution.py:564
  71.8 2.3 %collective-permute-start.36 = (bf16[128,128]{1,0:T(8,128)(2,1)S(1)}, bf16[128,128]{1,0:T(8,128)(2,1)S(1)}, u32[]{:S(2)}, u32[]{:S(2)}) collective-permute-start(bf16[128,128]{1,0:T(8,128)(2,1)S(1)} %get-tuple-element.170), channel_id=1, source_target_pairs={{1,2},{2,1},{3,4},{4,3},{5,6},{6,5},{7,8},{8,7},{9,10},{10,9},{11,... | collective-permute-start | bytes 98312 | tf_op jit(solution)/shard_map/ppermute | solution.py:564
  74.2 1.9 %collective-permute-done.34.refs_8_ = bf16[128,128]{1,0:T(8,128)(2,1)S(1)} collective-permute-done((bf16[128,128]{1,0:T(8,128)(2,1)S(1)}, bf16[128,128]{1,0:T(8,128)(2,1)S(1)}, u32[]{:S(2)}, u32[]{:S(2)}) %collective-permute-start.34) | collective-permute-done | bytes 32800 | tf_op jit(solution)/shard_map/ppermute | solution.py:564
  76.1 1.3 %inner.11 = (f32[2048,128]{1,0:T(8,128)S(1)}, f32[2048,128]{1,0:T(8,128)S(1)}, f32[256,128]{1,0:T(8,128)S(1)}) custom-call(bf16[2048,384]{1,0:T(8,128)(2,1)S(1)} %get-tuple-element.102.refs_0_.refs_1_, bf16[2048,256]{1,0:T(8,128)(2,1)S(1)} %get-tuple-element.103.refs_1_.refs_2_, bf16[256,2048]{1,0:T(8,128)(2,1)S(1)} %get-tuple-element.110.refs_2_.refs_5_, ...), custom_call_target="tpu_custom_call" | custom-call | flops 201326592 | bytes 3145728 | tf_op jit(solution)/shard_map/inner/pallas_call | solution.py:318
  77.5 1.3 %collective-permute-done.36.refs_10_ = bf16[128,128]{1,0:T(8,128)(2,1)S(1)} collective-permute-done((bf16[128,128]{1,0:T(8,128)(2,1)S(1)}, bf16[128,128]{1,0:T(8,128)(2,1)S(1)}, u32[]{:S(2)}, u32[]{:S(2)}) %collective-permute-start.36) | collective-permute-done | bytes 32800 | tf_op jit(solution)/shard_map/ppermute | solution.py:564
  79.2 0.5 collective-permute-start.40
  79.7 3.0 %collective-permute-start.41 = (bf16[128,128]{1,0:T(8,128)(2,1)S(1)}, bf16[128,128]{1,0:T(8,128)(2,1)S(1)}, u32[]{:S(2)}, u32[]{:S(2)}) collective-permute-start(bf16[128,128]{1,0:T(8,128)(2,1)S(1)} %get-tuple-element.180), channel_id=1, source_target_pairs={{2,4},{4,2},{3,5},{5,3},{6,8},{8,6},{7,9},{9,7},{10,12},{12,10},{1... | collective-permute-start | bytes 98312 | tf_op jit(solution)/shard_map/ppermute | solution.py:564
  82.8 2.3 %collective-permute-start.42 = (bf16[128,128]{1,0:T(8,128)(2,1)S(1)}, bf16[128,128]{1,0:T(8,128)(2,1)S(1)}, u32[]{:S(2)}, u32[]{:S(2)}) collective-permute-start(bf16[128,128]{1,0:T(8,128)(2,1)S(1)} %get-tuple-element.181), channel_id=1, source_target_pairs={{1,2},{2,1},{3,4},{4,3},{5,6},{6,5},{7,8},{8,7},{9,10},{10,9},{11,... | collective-permute-start | bytes 98312 | tf_op jit(solution)/shard_map/ppermute | solution.py:564
  85.1 0.7 collective-permute-done.40.refs_8_
  85.9 1.1 inner.12
  87.2 2.5 %collective-permute-done.42.refs_10_ = bf16[128,128]{1,0:T(8,128)(2,1)S(1)} collective-permute-done((bf16[128,128]{1,0:T(8,128)(2,1)S(1)}, bf16[128,128]{1,0:T(8,128)(2,1)S(1)}, u32[]{:S(2)}, u32[]{:S(2)}) %collective-permute-start.42) | collective-permute-done | bytes 32800 | tf_op jit(solution)/shard_map/ppermute | solution.py:564
  90.4 3.2 %collective-permute-start.47 = (bf16[128,128]{1,0:T(8,128)(2,1)S(1)}, bf16[128,128]{1,0:T(8,128)(2,1)S(1)}, u32[]{:S(2)}, u32[]{:S(2)}) collective-permute-start(bf16[128,128]{1,0:T(8,128)(2,1)S(1)} %get-tuple-element.189), channel_id=1, source_target_pairs={{2,4},{4,2},{3,5},{5,3},{6,8},{8,6},{7,9},{9,7},{10,12},{12,10},{1... | collective-permute-start | bytes 98312 | tf_op jit(solution)/shard_map/ppermute | solution.py:564
  93.7 1.6 %collective-permute-start.48 = (bf16[128,128]{1,0:T(8,128)(2,1)S(1)}, bf16[128,128]{1,0:T(8,128)(2,1)S(1)}, u32[]{:S(2)}, u32[]{:S(2)}) collective-permute-start(bf16[128,128]{1,0:T(8,128)(2,1)S(1)} %get-tuple-element.190), channel_id=1, source_target_pairs={{1,2},{2,1},{3,4},{4,3},{5,6},{6,5},{7,8},{8,7},{9,10},{10,9},{11,... | collective-permute-start | bytes 98312 | tf_op jit(solution)/shard_map/ppermute | solution.py:564
  95.2 0.8 collective-permute-start.50
  96.1 1.1 collective-permute-done.46.refs_5_
  97.1 0.8 inner.13.refs_4_
  98.0 2.6 %collective-permute-done.48.refs_7_ = bf16[128,128]{1,0:T(8,128)(2,1)S(1)} collective-permute-done((bf16[128,128]{1,0:T(8,128)(2,1)S(1)}, bf16[128,128]{1,0:T(8,128)(2,1)S(1)}, u32[]{:S(2)}, u32[]{:S(2)}) %collective-permute-start.48) | collective-permute-done | bytes 32800 | tf_op jit(solution)/shard_map/ppermute | solution.py:564
  100.6 0.8 last.1
  101.5 1.2 collective-permute-done.52
  102.7 0.9 collective-permute-start.54
  103.7 2.5 %collective-permute-start.53 = (f32[64,128]{1,0:T(8,128)S(1)}, f32[64,128]{1,0:T(8,128)S(1)}, u32[]{:S(2)}, u32[]{:S(2)}) collective-permute-start(f32[64,128]{1,0:T(8,128)S(1)} %add.25), channel_id=1, source_target_pairs={{0,2},{1,3},{2,0},{3,1},{4,6},{5,7},{6,4},{7,5},{8,10},{9,11},{10,... | collective-permute-start | bytes 98312 | tf_op jit(solution)/shard_map/ppermute | solution.py:547
  106.2 1.5 %collective-permute-done.55 = f32[64,128]{1,0:T(8,128)S(1)} collective-permute-done((f32[64,128]{1,0:T(8,128)S(1)}, f32[64,128]{1,0:T(8,128)S(1)}, u32[]{:S(2)}, u32[]{:S(2)}) %collective-permute-start.55) | collective-permute-done | bytes 32800 | tf_op jit(solution)/shard_map/ppermute | solution.py:547
  108.1 2.1 %collective-permute-start.58 = (f32[64,128]{1,0:T(8,128)S(1)}, f32[64,128]{1,0:T(8,128)S(1)}, u32[]{:S(2)}, u32[]{:S(2)}) collective-permute-start(f32[64,128]{1,0:T(8,128)S(1)} %add_add_fusion.1), channel_id=1, source_target_pairs={{0,24},{1,25},{2,26},{3,27},{4,28},{5,29},{6,30},{7,31},{8,16},{9,... | collective-permute-start | bytes 98312 | tf_op jit(solution)/shard_map/ppermute | solution.py:547
  110.2 2.4 %collective-permute-start.56 = (f32[64,128]{1,0:T(8,128)S(1)}, f32[64,128]{1,0:T(8,128)S(1)}, u32[]{:S(2)}, u32[]{:S(2)}) collective-permute-start(f32[64,128]{1,0:T(8,128)S(1)} %add_add_fusion.1), channel_id=1, source_target_pairs={{0,8},{1,9},{2,10},{3,11},{4,12},{5,13},{6,14},{7,15},{8,0},{9,1},... | collective-permute-start | bytes 98312 | tf_op jit(solution)/shard_map/ppermute | solution.py:547
  112.6 1.5 %collective-permute-done.58 = f32[64,128]{1,0:T(8,128)S(1)} collective-permute-done((f32[64,128]{1,0:T(8,128)S(1)}, f32[64,128]{1,0:T(8,128)S(1)}, u32[]{:S(2)}, u32[]{:S(2)}) %collective-permute-start.58) | collective-permute-done | bytes 32800 | tf_op jit(solution)/shard_map/ppermute | solution.py:547
  114.1 0.9 collective-permute-done.57
  115.1 1.2 collective-permute-done.59.refs_2_
  116.3 6.5 %finish.1 = f32[2048,128]{1,0:T(8,128)} custom-call(s32[1]{0:T(128)} %bitcast.place_ref.refs_0_, f32[64,128]{1,0:T(8,128)S(1)} %add_add_fusion.refs_1_, f32[64,128]{1,0:T(8,128)S(1)} %collective-permute-done.59.refs_2_, bf16[2048,256]{1,0:T(8,128)(2,1)S(1)} %get-tuple-element.196.refs_3_), custom_call_target="tpu_custom_call" | custom-call | tf_op jit(solution)/shard_map/finish/pallas_call | solution.py:530
  (78 shorter events, 5.6 us)
Async XLA Ops:
  0.0 12.6 %collective-permute-start.3 = (s32[1,256]{1,0:T(1,128)}, s32[1,256]{1,0:T(1,128)S(1)}, u32[]{:S(2)}, u32[]{:S(2)}) collective-permute-start(s32[1,256]{1,0:T(1,128)} %bitcast.10), channel_id=1, source_target_pairs={{0,2},{2,0},{1,3},{3,1},{4,6},{6,4},{5,7},{7,5},{8,10},{10,8},{9,1... | collective-permute-start | bytes 3080 | tf_op jit(solution)/shard_map/ppermute | solution.py:564
  2.9 9.7 %collective-permute-start.2 = (s32[1,256]{1,0:T(1,128)}, s32[1,256]{1,0:T(1,128)S(1)}, u32[]{:S(2)}, u32[]{:S(2)}) collective-permute-start(s32[1,256]{1,0:T(1,128)} %bitcast.11), channel_id=1, source_target_pairs={{0,4},{4,0},{1,5},{5,1},{2,6},{6,2},{3,7},{7,3},{8,12},{12,8},{9,1... | collective-permute-start | bytes 3080 | tf_op jit(solution)/shard_map/ppermute | solution.py:564
  4.5 8.2 %collective-permute-start.1 = (s32[1,256]{1,0:T(1,128)}, s32[1,256]{1,0:T(1,128)S(1)}, u32[]{:S(2)}, u32[]{:S(2)}) collective-permute-start(s32[1,256]{1,0:T(1,128)} %bitcast.12), channel_id=1, source_target_pairs={{2,4},{4,2},{3,5},{5,3},{6,8},{8,6},{7,9},{9,7},{10,12},{12,10},{1... | collective-permute-start | bytes 3080 | tf_op jit(solution)/shard_map/ppermute | solution.py:564
  8.0 6.5 %collective-permute-start = (s32[1,256]{1,0:T(1,128)}, s32[1,256]{1,0:T(1,128)S(1)}, u32[]{:S(2)}, u32[]{:S(2)}) collective-permute-start(s32[1,256]{1,0:T(1,128)} %bitcast.13), channel_id=1, source_target_pairs={{4,8},{8,4},{5,9},{9,5},{6,10},{10,6},{7,11},{11,7},{12,16},{16,12... | collective-permute-start | bytes 3080 | tf_op jit(solution)/shard_map/ppermute | solution.py:564
  15.1 6.8 %collective-permute-start.4 = (bf16[128,128]{1,0:T(8,128)(2,1)S(1)}, bf16[128,128]{1,0:T(8,128)(2,1)S(1)}, u32[]{:S(2)}, u32[]{:S(2)}) collective-permute-start(bf16[128,128]{1,0:T(8,128)(2,1)S(1)} %get-tuple-element.114), channel_id=1, source_target_pairs={{4,8},{8,4},{5,9},{9,5},{6,10},{10,6},{7,11},{11,7},{12,16},{16,12... | collective-permute-start | bytes 98312 | tf_op jit(solution)/shard_map/ppermute | solution.py:564
  16.6 7.5 %collective-permute-start.5 = (bf16[128,128]{1,0:T(8,128)(2,1)S(1)}, bf16[128,128]{1,0:T(8,128)(2,1)S(1)}, u32[]{:S(2)}, u32[]{:S(2)}) collective-permute-start(bf16[128,128]{1,0:T(8,128)(2,1)S(1)} %get-tuple-element.115), channel_id=1, source_target_pairs={{2,4},{4,2},{3,5},{5,3},{6,8},{8,6},{7,9},{9,7},{10,12},{12,10},{1... | collective-permute-start | bytes 98312 | tf_op jit(solution)/shard_map/ppermute | solution.py:564
  18.6 7.0 %collective-permute-start.6 = (bf16[128,128]{1,0:T(8,128)(2,1)S(1)}, bf16[128,128]{1,0:T(8,128)(2,1)S(1)}, u32[]{:S(2)}, u32[]{:S(2)}) collective-permute-start(bf16[128,128]{1,0:T(8,128)(2,1)S(1)} %get-tuple-element.116), channel_id=1, source_target_pairs={{1,2},{2,1},{3,4},{4,3},{5,6},{6,5},{7,8},{8,7},{9,10},{10,9},{11,... | collective-permute-start | bytes 98312 | tf_op jit(solution)/shard_map/ppermute | solution.py:564
  19.9 5.7 %collective-permute-start.7 = (bf16[128,128]{1,0:T(8,128)(2,1)S(1)}, bf16[128,128]{1,0:T(8,128)(2,1)S(1)}, u32[]{:S(2)}, u32[]{:S(2)}) collective-permute-start(bf16[128,128]{1,0:T(8,128)(2,1)S(1)} %get-tuple-element.117), channel_id=1, source_target_pairs={{0,4},{4,0},{1,5},{5,1},{2,6},{6,2},{3,7},{7,3},{8,12},{12,8},{9,1... | collective-permute-start | bytes 98312 | tf_op jit(solution)/shard_map/ppermute | solution.py:564
  19.9 5.7 %collective-permute-start.8 = (bf16[128,128]{1,0:T(8,128)(2,1)S(1)}, bf16[128,128]{1,0:T(8,128)(2,1)S(1)}, u32[]{:S(2)}, u32[]{:S(2)}) collective-permute-start(bf16[128,128]{1,0:T(8,128)(2,1)S(1)} %get-tuple-element.118), channel_id=1, source_target_pairs={{0,2},{2,0},{1,3},{3,1},{4,6},{6,4},{5,7},{7,5},{8,10},{10,8},{9,1... | collective-permute-start | bytes 98312 | tf_op jit(solution)/shard_map/ppermute | solution.py:564
  21.8 3.8 %collective-permute-start.9 = (bf16[128,128]{1,0:T(8,128)(2,1)S(1)}, bf16[128,128]{1,0:T(8,128)(2,1)S(1)}, u32[]{:S(2)}, u32[]{:S(2)}) collective-permute-start(bf16[128,128]{1,0:T(8,128)(2,1)S(1)} %get-tuple-element.119), channel_id=1, source_target_pairs={{0,1},{1,0},{2,3},{3,2},{4,5},{5,4},{6,7},{7,6},{8,9},{9,8},{10,11... | collective-permute-start | bytes 98312 | tf_op jit(solution)/shard_map/ppermute | solution.py:564
  26.0 7.0 %collective-permute-start.10 = (bf16[128,128]{1,0:T(8,128)(2,1)S(1)}, bf16[128,128]{1,0:T(8,128)(2,1)S(1)}, u32[]{:S(2)}, u32[]{:S(2)}) collective-permute-start(bf16[128,128]{1,0:T(8,128)(2,1)S(1)} %get-tuple-element.124), channel_id=1, source_target_pairs={{4,8},{8,4},{5,9},{9,5},{6,10},{10,6},{7,11},{11,7},{12,16},{16,12... | collective-permute-start | bytes 98312 | tf_op jit(solution)/shard_map/ppermute | solution.py:564
  26.2 8.0 %collective-permute-start.11 = (bf16[128,128]{1,0:T(8,128)(2,1)S(1)}, bf16[128,128]{1,0:T(8,128)(2,1)S(1)}, u32[]{:S(2)}, u32[]{:S(2)}) collective-permute-start(bf16[128,128]{1,0:T(8,128)(2,1)S(1)} %get-tuple-element.125), channel_id=1, source_target_pairs={{2,4},{4,2},{3,5},{5,3},{6,8},{8,6},{7,9},{9,7},{10,12},{12,10},{1... | collective-permute-start | bytes 98312 | tf_op jit(solution)/shard_map/ppermute | solution.py:564
  28.8 6.9 %collective-permute-start.12 = (bf16[128,128]{1,0:T(8,128)(2,1)S(1)}, bf16[128,128]{1,0:T(8,128)(2,1)S(1)}, u32[]{:S(2)}, u32[]{:S(2)}) collective-permute-start(bf16[128,128]{1,0:T(8,128)(2,1)S(1)} %get-tuple-element.126), channel_id=1, source_target_pairs={{1,2},{2,1},{3,4},{4,3},{5,6},{6,5},{7,8},{8,7},{9,10},{10,9},{11,... | collective-permute-start | bytes 98312 | tf_op jit(solution)/shard_map/ppermute | solution.py:564
  31.1 4.6 %collective-permute-start.13 = (bf16[128,128]{1,0:T(8,128)(2,1)S(1)}, bf16[128,128]{1,0:T(8,128)(2,1)S(1)}, u32[]{:S(2)}, u32[]{:S(2)}) collective-permute-start(bf16[128,128]{1,0:T(8,128)(2,1)S(1)} %get-tuple-element.127), channel_id=1, source_target_pairs={{0,4},{4,0},{1,5},{5,1},{2,6},{6,2},{3,7},{7,3},{8,12},{12,8},{9,1... | collective-permute-start | bytes 98312 | tf_op jit(solution)/shard_map/ppermute | solution.py:564
  31.1 4.6 %collective-permute-start.14 = (bf16[128,128]{1,0:T(8,128)(2,1)S(1)}, bf16[128,128]{1,0:T(8,128)(2,1)S(1)}, u32[]{:S(2)}, u32[]{:S(2)}) collective-permute-start(bf16[128,128]{1,0:T(8,128)(2,1)S(1)} %get-tuple-element.128), channel_id=1, source_target_pairs={{0,2},{2,0},{1,3},{3,1},{4,6},{6,4},{5,7},{7,5},{8,10},{10,8},{9,1... | collective-permute-start | bytes 98312 | tf_op jit(solution)/shard_map/ppermute | solution.py:564
  33.1 2.6 %collective-permute-start.15 = (bf16[128,128]{1,0:T(8,128)(2,1)S(1)}, bf16[128,128]{1,0:T(8,128)(2,1)S(1)}, u32[]{:S(2)}, u32[]{:S(2)}) collective-permute-start(bf16[128,128]{1,0:T(8,128)(2,1)S(1)} %get-tuple-element.129), channel_id=1, source_target_pairs={{0,1},{1,0},{2,3},{3,2},{4,5},{5,4},{6,7},{7,6},{8,9},{9,8},{10,11... | collective-permute-start | bytes 98312 | tf_op jit(solution)/shard_map/ppermute | solution.py:564
  36.1 6.7 %collective-permute-start.16 = (bf16[128,128]{1,0:T(8,128)(2,1)S(1)}, bf16[128,128]{1,0:T(8,128)(2,1)S(1)}, u32[]{:S(2)}, u32[]{:S(2)}) collective-permute-start(bf16[128,128]{1,0:T(8,128)(2,1)S(1)} %get-tuple-element.135), channel_id=1, source_target_pairs={{4,8},{8,4},{5,9},{9,5},{6,10},{10,6},{7,11},{11,7},{12,16},{16,12... | collective-permute-start | bytes 98312 | tf_op jit(solution)/shard_map/ppermute | solution.py:564
  36.7 7.5 %collective-permute-start.17 = (bf16[128,128]{1,0:T(8,128)(2,1)S(1)}, bf16[128,128]{1,0:T(8,128)(2,1)S(1)}, u32[]{:S(2)}, u32[]{:S(2)}) collective-permute-start(bf16[128,128]{1,0:T(8,128)(2,1)S(1)} %get-tuple-element.136), channel_id=1, source_target_pairs={{2,4},{4,2},{3,5},{5,3},{6,8},{8,6},{7,9},{9,7},{10,12},{12,10},{1... | collective-permute-start | bytes 98312 | tf_op jit(solution)/shard_map/ppermute | solution.py:564
  39.6 6.9 %collective-permute-start.18 = (bf16[128,128]{1,0:T(8,128)(2,1)S(1)}, bf16[128,128]{1,0:T(8,128)(2,1)S(1)}, u32[]{:S(2)}, u32[]{:S(2)}) collective-permute-start(bf16[128,128]{1,0:T(8,128)(2,1)S(1)} %get-tuple-element.137), channel_id=1, source_target_pairs={{1,2},{2,1},{3,4},{4,3},{5,6},{6,5},{7,8},{8,7},{9,10},{10,9},{11,... | collective-permute-start | bytes 98312 | tf_op jit(solution)/shard_map/ppermute | solution.py:564
  42.1 4.5 %collective-permute-start.19 = (bf16[128,128]{1,0:T(8,128)(2,1)S(1)}, bf16[128,128]{1,0:T(8,128)(2,1)S(1)}, u32[]{:S(2)}, u32[]{:S(2)}) collective-permute-start(bf16[128,128]{1,0:T(8,128)(2,1)S(1)} %get-tuple-element.138), channel_id=1, source_target_pairs={{0,4},{4,0},{1,5},{5,1},{2,6},{6,2},{3,7},{7,3},{8,12},{12,8},{9,1... | collective-permute-start | bytes 98312 | tf_op jit(solution)/shard_map/ppermute | solution.py:564
  42.1 4.5 %collective-permute-start.20 = (bf16[128,128]{1,0:T(8,128)(2,1)S(1)}, bf16[128,128]{1,0:T(8,128)(2,1)S(1)}, u32[]{:S(2)}, u32[]{:S(2)}) collective-permute-start(bf16[128,128]{1,0:T(8,128)(2,1)S(1)} %get-tuple-element.139), channel_id=1, source_target_pairs={{0,2},{2,0},{1,3},{3,1},{4,6},{6,4},{5,7},{7,5},{8,10},{10,8},{9,1... | collective-permute-start | bytes 98312 | tf_op jit(solution)/shard_map/ppermute | solution.py:564
  42.8 3.8 %collective-permute-start.21 = (bf16[128,128]{1,0:T(8,128)(2,1)S(1)}, bf16[128,128]{1,0:T(8,128)(2,1)S(1)}, u32[]{:S(2)}, u32[]{:S(2)}) collective-permute-start(bf16[128,128]{1,0:T(8,128)(2,1)S(1)} %get-tuple-element.140), channel_id=1, source_target_pairs={{0,1},{1,0},{2,3},{3,2},{4,5},{5,4},{6,7},{7,6},{8,9},{9,8},{10,11... | collective-permute-start | bytes 98312 | tf_op jit(solution)/shard_map/ppermute | solution.py:564
  47.0 7.0 %collective-permute-start.22 = (bf16[128,128]{1,0:T(8,128)(2,1)S(1)}, bf16[128,128]{1,0:T(8,128)(2,1)S(1)}, u32[]{:S(2)}, u32[]{:S(2)}) collective-permute-start(bf16[128,128]{1,0:T(8,128)(2,1)S(1)} %get-tuple-element.146), channel_id=1, source_target_pairs={{4,8},{8,4},{5,9},{9,5},{6,10},{10,6},{7,11},{11,7},{12,16},{16,12... | collective-permute-start | bytes 98312 | tf_op jit(solution)/shard_map/ppermute | solution.py:564
  47.3 7.8 %collective-permute-start.23 = (bf16[128,128]{1,0:T(8,128)(2,1)S(1)}, bf16[128,128]{1,0:T(8,128)(2,1)S(1)}, u32[]{:S(2)}, u32[]{:S(2)}) collective-permute-start(bf16[128,128]{1,0:T(8,128)(2,1)S(1)} %get-tuple-element.147), channel_id=1, source_target_pairs={{2,4},{4,2},{3,5},{5,3},{6,8},{8,6},{7,9},{9,7},{10,12},{12,10},{1... | collective-permute-start | bytes 98312 | tf_op jit(solution)/shard_map/ppermute | solution.py:564
  50.6 7.0 %collective-permute-start.24 = (bf16[128,128]{1,0:T(8,128)(2,1)S(1)}, bf16[128,128]{1,0:T(8,128)(2,1)S(1)}, u32[]{:S(2)}, u32[]{:S(2)}) collective-permute-start(bf16[128,128]{1,0:T(8,128)(2,1)S(1)} %get-tuple-element.148), channel_id=1, source_target_pairs={{1,2},{2,1},{3,4},{4,3},{5,6},{6,5},{7,8},{8,7},{9,10},{10,9},{11,... | collective-permute-start | bytes 98312 | tf_op jit(solution)/shard_map/ppermute | solution.py:564
  52.1 5.5 %collective-permute-start.25 = (bf16[128,128]{1,0:T(8,128)(2,1)S(1)}, bf16[128,128]{1,0:T(8,128)(2,1)S(1)}, u32[]{:S(2)}, u32[]{:S(2)}) collective-permute-start(bf16[128,128]{1,0:T(8,128)(2,1)S(1)} %get-tuple-element.149), channel_id=1, source_target_pairs={{0,4},{4,0},{1,5},{5,1},{2,6},{6,2},{3,7},{7,3},{8,12},{12,8},{9,1... | collective-permute-start | bytes 98312 | tf_op jit(solution)/shard_map/ppermute | solution.py:564
  52.1 5.5 %collective-permute-start.26 = (bf16[128,128]{1,0:T(8,128)(2,1)S(1)}, bf16[128,128]{1,0:T(8,128)(2,1)S(1)}, u32[]{:S(2)}, u32[]{:S(2)}) collective-permute-start(bf16[128,128]{1,0:T(8,128)(2,1)S(1)} %get-tuple-element.150), channel_id=1, source_target_pairs={{0,2},{2,0},{1,3},{3,1},{4,6},{6,4},{5,7},{7,5},{8,10},{10,8},{9,1... | collective-permute-start | bytes 98312 | tf_op jit(solution)/shard_map/ppermute | solution.py:564
  53.9 3.7 %collective-permute-start.27 = (bf16[128,128]{1,0:T(8,128)(2,1)S(1)}, bf16[128,128]{1,0:T(8,128)(2,1)S(1)}, u32[]{:S(2)}, u32[]{:S(2)}) collective-permute-start(bf16[128,128]{1,0:T(8,128)(2,1)S(1)} %get-tuple-element.151), channel_id=1, source_target_pairs={{0,1},{1,0},{2,3},{3,2},{4,5},{5,4},{6,7},{7,6},{8,9},{9,8},{10,11... | collective-permute-start | bytes 98312 | tf_op jit(solution)/shard_map/ppermute | solution.py:564
  58.1 7.1 %collective-permute-start.28 = (bf16[128,128]{1,0:T(8,128)(2,1)S(1)}, bf16[128,128]{1,0:T(8,128)(2,1)S(1)}, u32[]{:S(2)}, u32[]{:S(2)}) collective-permute-start(bf16[128,128]{1,0:T(8,128)(2,1)S(1)} %get-tuple-element.157), channel_id=1, source_target_pairs={{4,8},{8,4},{5,9},{9,5},{6,10},{10,6},{7,11},{11,7},{12,16},{16,12... | collective-permute-start | bytes 98312 | tf_op jit(solution)/shard_map/ppermute | solution.py:564
  58.3 8.0 %collective-permute-start.29 = (bf16[128,128]{1,0:T(8,128)(2,1)S(1)}, bf16[128,128]{1,0:T(8,128)(2,1)S(1)}, u32[]{:S(2)}, u32[]{:S(2)}) collective-permute-start(bf16[128,128]{1,0:T(8,128)(2,1)S(1)} %get-tuple-element.158), channel_id=1, source_target_pairs={{2,4},{4,2},{3,5},{5,3},{6,8},{8,6},{7,9},{9,7},{10,12},{12,10},{1... | collective-permute-start | bytes 98312 | tf_op jit(solution)/shard_map/ppermute | solution.py:564
  61.6 7.0 %collective-permute-start.30 = (bf16[128,128]{1,0:T(8,128)(2,1)S(1)}, bf16[128,128]{1,0:T(8,128)(2,1)S(1)}, u32[]{:S(2)}, u32[]{:S(2)}) collective-permute-start(bf16[128,128]{1,0:T(8,128)(2,1)S(1)} %get-tuple-element.159), channel_id=1, source_target_pairs={{1,2},{2,1},{3,4},{4,3},{5,6},{6,5},{7,8},{8,7},{9,10},{10,9},{11,... | collective-permute-start | bytes 98312 | tf_op jit(solution)/shard_map/ppermute | solution.py:564
  63.1 5.6 %collective-permute-start.31 = (bf16[128,128]{1,0:T(8,128)(2,1)S(1)}, bf16[128,128]{1,0:T(8,128)(2,1)S(1)}, u32[]{:S(2)}, u32[]{:S(2)}) collective-permute-start(bf16[128,128]{1,0:T(8,128)(2,1)S(1)} %get-tuple-element.160), channel_id=1, source_target_pairs={{0,4},{4,0},{1,5},{5,1},{2,6},{6,2},{3,7},{7,3},{8,12},{12,8},{9,1... | collective-permute-start | bytes 98312 | tf_op jit(solution)/shard_map/ppermute | solution.py:564
  63.1 5.6 %collective-permute-start.32 = (bf16[128,128]{1,0:T(8,128)(2,1)S(1)}, bf16[128,128]{1,0:T(8,128)(2,1)S(1)}, u32[]{:S(2)}, u32[]{:S(2)}) collective-permute-start(bf16[128,128]{1,0:T(8,128)(2,1)S(1)} %get-tuple-element.161), channel_id=1, source_target_pairs={{0,2},{2,0},{1,3},{3,1},{4,6},{6,4},{5,7},{7,5},{8,10},{10,8},{9,1... | collective-permute-start | bytes 98312 | tf_op jit(solution)/shard_map/ppermute | solution.py:564
  65.1 3.5 %collective-permute-start.33 = (bf16[128,128]{1,0:T(8,128)(2,1)S(1)}, bf16[128,128]{1,0:T(8,128)(2,1)S(1)}, u32[]{:S(2)}, u32[]{:S(2)}) collective-permute-start(bf16[128,128]{1,0:T(8,128)(2,1)S(1)} %get-tuple-element.162), channel_id=1, source_target_pairs={{0,1},{1,0},{2,3},{3,2},{4,5},{5,4},{6,7},{7,6},{8,9},{9,8},{10,11... | collective-permute-start | bytes 98312 | tf_op jit(solution)/shard_map/ppermute | solution.py:564
  69.1 7.1 %collective-permute-start.34 = (bf16[128,128]{1,0:T(8,128)(2,1)S(1)}, bf16[128,128]{1,0:T(8,128)(2,1)S(1)}, u32[]{:S(2)}, u32[]{:S(2)}) collective-permute-start(bf16[128,128]{1,0:T(8,128)(2,1)S(1)} %get-tuple-element.168), channel_id=1, source_target_pairs={{4,8},{8,4},{5,9},{9,5},{6,10},{10,6},{7,11},{11,7},{12,16},{16,12... | collective-permute-start | bytes 98312 | tf_op jit(solution)/shard_map/ppermute | solution.py:564
  69.3 8.2 %collective-permute-start.35 = (bf16[128,128]{1,0:T(8,128)(2,1)S(1)}, bf16[128,128]{1,0:T(8,128)(2,1)S(1)}, u32[]{:S(2)}, u32[]{:S(2)}) collective-permute-start(bf16[128,128]{1,0:T(8,128)(2,1)S(1)} %get-tuple-element.169), channel_id=1, source_target_pairs={{2,4},{4,2},{3,5},{5,3},{6,8},{8,6},{7,9},{9,7},{10,12},{12,10},{1... | collective-permute-start | bytes 98312 | tf_op jit(solution)/shard_map/ppermute | solution.py:564
  71.8 6.9 %collective-permute-start.36 = (bf16[128,128]{1,0:T(8,128)(2,1)S(1)}, bf16[128,128]{1,0:T(8,128)(2,1)S(1)}, u32[]{:S(2)}, u32[]{:S(2)}) collective-permute-start(bf16[128,128]{1,0:T(8,128)(2,1)S(1)} %get-tuple-element.170), channel_id=1, source_target_pairs={{1,2},{2,1},{3,4},{4,3},{5,6},{6,5},{7,8},{8,7},{9,10},{10,9},{11,... | collective-permute-start | bytes 98312 | tf_op jit(solution)/shard_map/ppermute | solution.py:564
  74.1 4.7 %collective-permute-start.37 = (bf16[128,128]{1,0:T(8,128)(2,1)S(1)}, bf16[128,128]{1,0:T(8,128)(2,1)S(1)}, u32[]{:S(2)}, u32[]{:S(2)}) collective-permute-start(bf16[128,128]{1,0:T(8,128)(2,1)S(1)} %get-tuple-element.171), channel_id=1, source_target_pairs={{0,4},{4,0},{1,5},{5,1},{2,6},{6,2},{3,7},{7,3},{8,12},{12,8},{9,1... | collective-permute-start | bytes 98312 | tf_op jit(solution)/shard_map/ppermute | solution.py:564
  74.1 4.7 %collective-permute-start.38 = (bf16[128,128]{1,0:T(8,128)(2,1)S(1)}, bf16[128,128]{1,0:T(8,128)(2,1)S(1)}, u32[]{:S(2)}, u32[]{:S(2)}) collective-permute-start(bf16[128,128]{1,0:T(8,128)(2,1)S(1)} %get-tuple-element.172), channel_id=1, source_target_pairs={{0,2},{2,0},{1,3},{3,1},{4,6},{6,4},{5,7},{7,5},{8,10},{10,8},{9,1... | collective-permute-start | bytes 98312 | tf_op jit(solution)/shard_map/ppermute | solution.py:564
  76.1 2.6 %collective-permute-start.39 = (bf16[128,128]{1,0:T(8,128)(2,1)S(1)}, bf16[128,128]{1,0:T(8,128)(2,1)S(1)}, u32[]{:S(2)}, u32[]{:S(2)}) collective-permute-start(bf16[128,128]{1,0:T(8,128)(2,1)S(1)} %get-tuple-element.173), channel_id=1, source_target_pairs={{0,1},{1,0},{2,3},{3,2},{4,5},{5,4},{6,7},{7,6},{8,9},{9,8},{10,11... | collective-permute-start | bytes 98312 | tf_op jit(solution)/shard_map/ppermute | solution.py:564
  79.2 6.7 %collective-permute-start.40 = (bf16[128,128]{1,0:T(8,128)(2,1)S(1)}, bf16[128,128]{1,0:T(8,128)(2,1)S(1)}, u32[]{:S(2)}, u32[]{:S(2)}) collective-permute-start(bf16[128,128]{1,0:T(8,128)(2,1)S(1)} %get-tuple-element.179), channel_id=1, source_target_pairs={{4,8},{8,4},{5,9},{9,5},{6,10},{10,6},{7,11},{11,7},{12,16},{16,12... | collective-permute-start | bytes 98312 | tf_op jit(solution)/shard_map/ppermute | solution.py:564
  79.7 7.5 %collective-permute-start.41 = (bf16[128,128]{1,0:T(8,128)(2,1)S(1)}, bf16[128,128]{1,0:T(8,128)(2,1)S(1)}, u32[]{:S(2)}, u32[]{:S(2)}) collective-permute-start(bf16[128,128]{1,0:T(8,128)(2,1)S(1)} %get-tuple-element.180), channel_id=1, source_target_pairs={{2,4},{4,2},{3,5},{5,3},{6,8},{8,6},{7,9},{9,7},{10,12},{12,10},{1... | collective-permute-start | bytes 98312 | tf_op jit(solution)/shard_map/ppermute | solution.py:564
  82.8 6.9 %collective-permute-start.42 = (bf16[128,128]{1,0:T(8,128)(2,1)S(1)}, bf16[128,128]{1,0:T(8,128)(2,1)S(1)}, u32[]{:S(2)}, u32[]{:S(2)}) collective-permute-start(bf16[128,128]{1,0:T(8,128)(2,1)S(1)} %get-tuple-element.181), channel_id=1, source_target_pairs={{1,2},{2,1},{3,4},{4,3},{5,6},{6,5},{7,8},{8,7},{9,10},{10,9},{11,... | collective-permute-start | bytes 98312 | tf_op jit(solution)/shard_map/ppermute | solution.py:564
  85.1 4.6 %collective-permute-start.43 = (bf16[128,128]{1,0:T(8,128)(2,1)S(1)}, bf16[128,128]{1,0:T(8,128)(2,1)S(1)}, u32[]{:S(2)}, u32[]{:S(2)}) collective-permute-start(bf16[128,128]{1,0:T(8,128)(2,1)S(1)} %get-tuple-element.182), channel_id=1, source_target_pairs={{0,4},{4,0},{1,5},{5,1},{2,6},{6,2},{3,7},{7,3},{8,12},{12,8},{9,1... | collective-permute-start | bytes 98312 | tf_op jit(solution)/shard_map/ppermute | solution.py:564
  85.1 4.6 %collective-permute-start.44 = (bf16[128,128]{1,0:T(8,128)(2,1)S(1)}, bf16[128,128]{1,0:T(8,128)(2,1)S(1)}, u32[]{:S(2)}, u32[]{:S(2)}) collective-permute-start(bf16[128,128]{1,0:T(8,128)(2,1)S(1)} %get-tuple-element.183), channel_id=1, source_target_pairs={{0,2},{2,0},{1,3},{3,1},{4,6},{6,4},{5,7},{7,5},{8,10},{10,8},{9,1... | collective-permute-start | bytes 98312 | tf_op jit(solution)/shard_map/ppermute | solution.py:564
  85.8 3.9 %collective-permute-start.45 = (bf16[128,128]{1,0:T(8,128)(2,1)S(1)}, bf16[128,128]{1,0:T(8,128)(2,1)S(1)}, u32[]{:S(2)}, u32[]{:S(2)}) collective-permute-start(bf16[128,128]{1,0:T(8,128)(2,1)S(1)} %get-tuple-element.184), channel_id=1, source_target_pairs={{0,1},{1,0},{2,3},{3,2},{4,5},{5,4},{6,7},{7,6},{8,9},{9,8},{10,11... | collective-permute-start | bytes 98312 | tf_op jit(solution)/shard_map/ppermute | solution.py:564
  90.1 7.0 %collective-permute-start.46 = (bf16[128,128]{1,0:T(8,128)(2,1)S(1)}, bf16[128,128]{1,0:T(8,128)(2,1)S(1)}, u32[]{:S(2)}, u32[]{:S(2)}) collective-permute-start(bf16[128,128]{1,0:T(8,128)(2,1)S(1)} %get-tuple-element.188), channel_id=1, source_target_pairs={{4,8},{8,4},{5,9},{9,5},{6,10},{10,6},{7,11},{11,7},{12,16},{16,12... | collective-permute-start | bytes 98312 | tf_op jit(solution)/shard_map/ppermute | solution.py:564
  90.4 7.6 %collective-permute-start.47 = (bf16[128,128]{1,0:T(8,128)(2,1)S(1)}, bf16[128,128]{1,0:T(8,128)(2,1)S(1)}, u32[]{:S(2)}, u32[]{:S(2)}) collective-permute-start(bf16[128,128]{1,0:T(8,128)(2,1)S(1)} %get-tuple-element.189), channel_id=1, source_target_pairs={{2,4},{4,2},{3,5},{5,3},{6,8},{8,6},{7,9},{9,7},{10,12},{12,10},{1... | collective-permute-start | bytes 98312 | tf_op jit(solution)/shard_map/ppermute | solution.py:564
  93.7 7.0 %collective-permute-start.48 = (bf16[128,128]{1,0:T(8,128)(2,1)S(1)}, bf16[128,128]{1,0:T(8,128)(2,1)S(1)}, u32[]{:S(2)}, u32[]{:S(2)}) collective-permute-start(bf16[128,128]{1,0:T(8,128)(2,1)S(1)} %get-tuple-element.190), channel_id=1, source_target_pairs={{1,2},{2,1},{3,4},{4,3},{5,6},{6,5},{7,8},{8,7},{9,10},{10,9},{11,... | collective-permute-start | bytes 98312 | tf_op jit(solution)/shard_map/ppermute | solution.py:564
  95.2 5.4 %collective-permute-start.49 = (bf16[128,128]{1,0:T(8,128)(2,1)S(1)}, bf16[128,128]{1,0:T(8,128)(2,1)S(1)}, u32[]{:S(2)}, u32[]{:S(2)}) collective-permute-start(bf16[128,128]{1,0:T(8,128)(2,1)S(1)} %get-tuple-element.191), channel_id=1, source_target_pairs={{0,4},{4,0},{1,5},{5,1},{2,6},{6,2},{3,7},{7,3},{8,12},{12,8},{9,1... | collective-permute-start | bytes 98312 | tf_op jit(solution)/shard_map/ppermute | solution.py:564
  95.2 5.4 %collective-permute-start.50 = (bf16[128,128]{1,0:T(8,128)(2,1)S(1)}, bf16[128,128]{1,0:T(8,128)(2,1)S(1)}, u32[]{:S(2)}, u32[]{:S(2)}) collective-permute-start(bf16[128,128]{1,0:T(8,128)(2,1)S(1)} %get-tuple-element.192), channel_id=1, source_target_pairs={{0,2},{2,0},{1,3},{3,1},{4,6},{6,4},{5,7},{7,5},{8,10},{10,8},{9,1... | collective-permute-start | bytes 98312 | tf_op jit(solution)/shard_map/ppermute | solution.py:564
  97.1 3.5 %collective-permute-start.51 = (bf16[128,128]{1,0:T(8,128)(2,1)S(1)}, bf16[128,128]{1,0:T(8,128)(2,1)S(1)}, u32[]{:S(2)}, u32[]{:S(2)}) collective-permute-start(bf16[128,128]{1,0:T(8,128)(2,1)S(1)} %get-tuple-element.193), channel_id=1, source_target_pairs={{0,1},{1,0},{2,3},{3,2},{4,5},{5,4},{6,7},{7,6},{8,9},{9,8},{10,11... | collective-permute-start | bytes 98312 | tf_op jit(solution)/shard_map/ppermute | solution.py:564
  101.4 1.3 %collective-permute-start.52 = (f32[64,128]{1,0:T(8,128)S(1)}, f32[64,128]{1,0:T(8,128)S(1)}, u32[]{:S(2)}, u32[]{:S(2)}) collective-permute-start(f32[64,128]{1,0:T(8,128)S(1)} %get-tuple-element.195), channel_id=1, source_target_pairs={{0,1},{1,0},{2,3},{3,2},{4,5},{5,4},{6,7},{7,6},{8,9},{9,8},{10,11... | collective-permute-start | bytes 98312 | tf_op jit(solution)/shard_map/ppermute | solution.py:547
  102.7 4.9 %collective-permute-start.55 = (f32[64,128]{1,0:T(8,128)S(1)}, f32[64,128]{1,0:T(8,128)S(1)}, u32[]{:S(2)}, u32[]{:S(2)}) collective-permute-start(f32[64,128]{1,0:T(8,128)S(1)} %add.25), channel_id=1, source_target_pairs={{0,6},{1,7},{2,4},{3,5},{4,2},{5,3},{6,0},{7,1},{8,14},{9,15},{10,... | collective-permute-start | bytes 98312 | tf_op jit(solution)/shard_map/ppermute | solution.py:547
  102.7 4.9 %collective-permute-start.54 = (f32[64,128]{1,0:T(8,128)S(1)}, f32[64,128]{1,0:T(8,128)S(1)}, u32[]{:S(2)}, u32[]{:S(2)}) collective-permute-start(f32[64,128]{1,0:T(8,128)S(1)} %add.25), channel_id=1, source_target_pairs={{0,4},{1,5},{2,6},{3,7},{4,0},{5,1},{6,2},{7,3},{8,12},{9,13},{10,... | collective-permute-start | bytes 98312 | tf_op jit(solution)/shard_map/ppermute | solution.py:547
  103.7 4.4 %collective-permute-start.53 = (f32[64,128]{1,0:T(8,128)S(1)}, f32[64,128]{1,0:T(8,128)S(1)}, u32[]{:S(2)}, u32[]{:S(2)}) collective-permute-start(f32[64,128]{1,0:T(8,128)S(1)} %add.25), channel_id=1, source_target_pairs={{0,2},{1,3},{2,0},{3,1},{4,6},{5,7},{6,4},{7,5},{8,10},{9,11},{10,... | collective-permute-start | bytes 98312 | tf_op jit(solution)/shard_map/ppermute | solution.py:547
  108.1 6.0 %collective-permute-start.58 = (f32[64,128]{1,0:T(8,128)S(1)}, f32[64,128]{1,0:T(8,128)S(1)}, u32[]{:S(2)}, u32[]{:S(2)}) collective-permute-start(f32[64,128]{1,0:T(8,128)S(1)} %add_add_fusion.1), channel_id=1, source_target_pairs={{0,24},{1,25},{2,26},{3,27},{4,28},{5,29},{6,30},{7,31},{8,16},{9,... | collective-permute-start | bytes 98312 | tf_op jit(solution)/shard_map/ppermute | solution.py:547
  110.2 4.8 %collective-permute-start.57 = (f32[64,128]{1,0:T(8,128)S(1)}, f32[64,128]{1,0:T(8,128)S(1)}, u32[]{:S(2)}, u32[]{:S(2)}) collective-permute-start(f32[64,128]{1,0:T(8,128)S(1)} %add_add_fusion.1), channel_id=1, source_target_pairs={{0,16},{1,17},{2,18},{3,19},{4,20},{5,21},{6,22},{7,23},{8,24},{9,... | collective-permute-start | bytes 98312 | tf_op jit(solution)/shard_map/ppermute | solution.py:547
  110.2 4.8 %collective-permute-start.56 = (f32[64,128]{1,0:T(8,128)S(1)}, f32[64,128]{1,0:T(8,128)S(1)}, u32[]{:S(2)}, u32[]{:S(2)}) collective-permute-start(f32[64,128]{1,0:T(8,128)S(1)} %add_add_fusion.1), channel_id=1, source_target_pairs={{0,8},{1,9},{2,10},{3,11},{4,12},{5,13},{6,14},{7,15},{8,0},{9,1},... | collective-permute-start | bytes 98312 | tf_op jit(solution)/shard_map/ppermute | solution.py:547
  115.0 1.3 %collective-permute-start.59 = (f32[64,128]{1,0:T(8,128)S(1)}, f32[64,128]{1,0:T(8,128)S(1)}, u32[]{:S(2)}, u32[]{:S(2)}) collective-permute-start(f32[64,128]{1,0:T(8,128)S(1)} %add_add_fusion.refs_1_), channel_id=1, source_target_pairs={{0,1},{1,0},{2,3},{3,2},{4,5},{5,4},{6,7},{7,6},{8,9},{9,8},{10,11... | collective-permute-start | bytes 98312 | tf_op jit(solution)/shard_map/ppermute | solution.py:547

commit v9 on v8

--- a/solution.py
+++ b/solution.py
@@ -535,7 +535,7 @@
         scratch_shapes=[
             pltpu.VMEM((VECS, VECS), F32),
             pltpu.VMEM((field.shape[0], VECS), F32),
-            pltpu.SemaphoreType.DMA((4,)),
+            pltpu.SemaphoreType.DMA((8,)),
         ],
         compiler_params=PARAMS,
         name="finish",

time: 123 us -> 123 us (level)
  no operation moved by 1% of the time
where the time goes in v9:
time: 123 us
  starting transfers between devices  61.7 us (50%)
  waiting for transfers between devices  38.3 us (31%)
  Pallas kernels  22.4 us (18%)
    ppermute x52, starting transfers between devices, swap(): return lax.ppermute(value, AXES, swap_pairs(count, by, odd))  53.7 us
    ppermute x52, waiting for transfers between devices, swap(): return lax.ppermute(value, AXES, swap_pairs(count, by, odd))  31.6 us
    ppermute x8, starting transfers between devices, swapped(): return lax.ppermute(value, AXES, [(i, i ^ mask) for i in range(count)])  8.08 us
    pallas_call x7, Pallas kernels, inner(): pl.pallas_call(lambda *refs: inner_kernel(scale, before_scale, more, *ref...  7.64 us
    ppermute x8, waiting for transfers between devices, swapped(): return lax.ppermute(value, AXES, [(i, i ^ mask) for i in range(count)])  6.72 us
    pallas_call x1, Pallas kernels, finish(): pl.pallas_call(lambda *refs: finish_kernel(scale, *refs), out_shape=jax.S...  6.48 us
    pallas_call x1, Pallas kernels, prepare(): pl.pallas_call(prepare_kernel, out_shape=(jax.ShapeDtypeStruct((rows, 3 *...  3.08 us
    pallas_call x7, Pallas kernels, step(): pl.pallas_call(lambda *refs: step_kernel(scale, *refs), out_shape=(*SENT,...  2.8 us
  transfers between devices with their start and end apart: 60, of which 26 were waited for; matrix products, arithmetic and copies ran while one was open for 0% of the time, Pallas kernels for 10%

profile of v9, /device:TPU:0, one launch (start us, length us, event | category | flops | bytes accessed | tf_op | source)
XLA Modules:
  0.0 122.9 jit_solution(17255827796089351460)
XLA Ops:
  0.0 2.9 %collective-permute-start.3 = (s32[1,256]{1,0:T(1,128)}, s32[1,256]{1,0:T(1,128)S(1)}, u32[]{:S(2)}, u32[]{:S(2)}) collective-permute-start(s32[1,256]{1,0:T(1,128)} %bitcast.10), channel_id=1, source_target_pairs={{0,2},{2,0},{1,3},{3,1},{4,6},{6,4},{5,7},{7,5},{8,10},{10,8},{9,1... | collective-permute-start | bytes 3080 | tf_op jit(solution)/shard_map/ppermute | solution.py:564
  2.9 1.5 %collective-permute-start.2 = (s32[1,256]{1,0:T(1,128)}, s32[1,256]{1,0:T(1,128)S(1)}, u32[]{:S(2)}, u32[]{:S(2)}) collective-permute-start(s32[1,256]{1,0:T(1,128)} %bitcast.11), channel_id=1, source_target_pairs={{0,4},{4,0},{1,5},{5,1},{2,6},{6,2},{3,7},{7,3},{8,12},{12,8},{9,1... | collective-permute-start | bytes 3080 | tf_op jit(solution)/shard_map/ppermute | solution.py:564
  4.5 3.5 %collective-permute-start.1 = (s32[1,256]{1,0:T(1,128)}, s32[1,256]{1,0:T(1,128)S(1)}, u32[]{:S(2)}, u32[]{:S(2)}) collective-permute-start(s32[1,256]{1,0:T(1,128)} %bitcast.12), channel_id=1, source_target_pairs={{2,4},{4,2},{3,5},{5,3},{6,8},{8,6},{7,9},{9,7},{10,12},{12,10},{1... | collective-permute-start | bytes 3080 | tf_op jit(solution)/shard_map/ppermute | solution.py:564
  8.0 1.5 %collective-permute-start = (s32[1,256]{1,0:T(1,128)}, s32[1,256]{1,0:T(1,128)S(1)}, u32[]{:S(2)}, u32[]{:S(2)}) collective-permute-start(s32[1,256]{1,0:T(1,128)} %bitcast.13), channel_id=1, source_target_pairs={{4,8},{8,4},{5,9},{9,5},{6,10},{10,6},{7,11},{11,7},{12,16},{16,12... | collective-permute-start | bytes 3080 | tf_op jit(solution)/shard_map/ppermute | solution.py:564
  9.5 3.1 %prepare.1 = (bf16[2048,384]{1,0:T(8,128)(2,1)S(1)}, bf16[2048,256]{1,0:T(8,128)(2,1)S(1)}, f32[256,128]{1,0:T(8,128)S(1)}, bf16[2048,128]{1,0:T(8,128)(2,1)S(1)}) custom-call(s32[1]{0:T(128)} %bitcast.place_ref.refs_0_, s32[1,256]{1,0:T(1,128)} %bitcast.8, f32[1,256]{1,0:T(1,128)} %bitcast.9, f32[3,8,2048]{2,1,0:T(8,128)} %bitcast.6, ...), custom_call_target="tpu_custom_call" | custom-call | tf_op jit(solution)/shard_map/prepare/pallas_call | solution.py:153
  12.6 1.8 %collective-permute-done.w3 = s32[1,256]{1,0:T(1,128)S(1)} collective-permute-done((s32[1,256]{1,0:T(1,128)}, s32[1,256]{1,0:T(1,128)S(1)}, u32[]{:S(2)}, u32[]{:S(2)}) %collective-permute-start) | collective-permute-done | bytes 1056 | tf_op jit(solution)/shard_map/ppermute | solution.py:564
  14.5 0.6 first.1
  15.1 1.6 %collective-permute-start.4 = (bf16[128,128]{1,0:T(8,128)(2,1)S(1)}, bf16[128,128]{1,0:T(8,128)(2,1)S(1)}, u32[]{:S(2)}, u32[]{:S(2)}) collective-permute-start(bf16[128,128]{1,0:T(8,128)(2,1)S(1)} %get-tuple-element.114), channel_id=1, source_target_pairs={{4,8},{8,4},{5,9},{9,5},{6,10},{10,6},{7,11},{11,7},{12,16},{16,12... | collective-permute-start | bytes 98312 | tf_op jit(solution)/shard_map/ppermute | solution.py:564
  16.6 2.0 %collective-permute-start.5 = (bf16[128,128]{1,0:T(8,128)(2,1)S(1)}, bf16[128,128]{1,0:T(8,128)(2,1)S(1)}, u32[]{:S(2)}, u32[]{:S(2)}) collective-permute-start(bf16[128,128]{1,0:T(8,128)(2,1)S(1)} %get-tuple-element.115), channel_id=1, source_target_pairs={{2,4},{4,2},{3,5},{5,3},{6,8},{8,6},{7,9},{9,7},{10,12},{12,10},{1... | collective-permute-start | bytes 98312 | tf_op jit(solution)/shard_map/ppermute | solution.py:564
  18.6 1.3 %collective-permute-start.6 = (bf16[128,128]{1,0:T(8,128)(2,1)S(1)}, bf16[128,128]{1,0:T(8,128)(2,1)S(1)}, u32[]{:S(2)}, u32[]{:S(2)}) collective-permute-start(bf16[128,128]{1,0:T(8,128)(2,1)S(1)} %get-tuple-element.116), channel_id=1, source_target_pairs={{1,2},{2,1},{3,4},{4,3},{5,6},{6,5},{7,8},{8,7},{9,10},{10,9},{11,... | collective-permute-start | bytes 98312 | tf_op jit(solution)/shard_map/ppermute | solution.py:564
  19.9 1.9 %collective-permute-done.4.refs_8_ = bf16[128,128]{1,0:T(8,128)(2,1)S(1)} collective-permute-done((bf16[128,128]{1,0:T(8,128)(2,1)S(1)}, bf16[128,128]{1,0:T(8,128)(2,1)S(1)}, u32[]{:S(2)}, u32[]{:S(2)}) %collective-permute-start.4) | collective-permute-done | bytes 32800 | tf_op jit(solution)/shard_map/ppermute | solution.py:564
  21.8 1.0 opening.1
  22.9 1.3 %collective-permute-done.5.refs_9_ = bf16[128,128]{1,0:T(8,128)(2,1)S(1)} collective-permute-done((bf16[128,128]{1,0:T(8,128)(2,1)S(1)}, bf16[128,128]{1,0:T(8,128)(2,1)S(1)}, u32[]{:S(2)}, u32[]{:S(2)}) %collective-permute-start.5) | collective-permute-done | bytes 32800 | tf_op jit(solution)/shard_map/ppermute | solution.py:564
  24.2 1.5 %collective-permute-done.6.refs_10_ = bf16[128,128]{1,0:T(8,128)(2,1)S(1)} collective-permute-done((bf16[128,128]{1,0:T(8,128)(2,1)S(1)}, bf16[128,128]{1,0:T(8,128)(2,1)S(1)}, u32[]{:S(2)}, u32[]{:S(2)}) %collective-permute-start.6) | collective-permute-done | bytes 32800 | tf_op jit(solution)/shard_map/ppermute | solution.py:564
  26.2 2.5 %collective-permute-start.11 = (bf16[128,128]{1,0:T(8,128)(2,1)S(1)}, bf16[128,128]{1,0:T(8,128)(2,1)S(1)}, u32[]{:S(2)}, u32[]{:S(2)}) collective-permute-start(bf16[128,128]{1,0:T(8,128)(2,1)S(1)} %get-tuple-element.125), channel_id=1, source_target_pairs={{2,4},{4,2},{3,5},{5,3},{6,8},{8,6},{7,9},{9,7},{10,12},{12,10},{1... | collective-permute-start | bytes 98312 | tf_op jit(solution)/shard_map/ppermute | solution.py:564
  28.8 2.3 %collective-permute-start.12 = (bf16[128,128]{1,0:T(8,128)(2,1)S(1)}, bf16[128,128]{1,0:T(8,128)(2,1)S(1)}, u32[]{:S(2)}, u32[]{:S(2)}) collective-permute-start(bf16[128,128]{1,0:T(8,128)(2,1)S(1)} %get-tuple-element.126), channel_id=1, source_target_pairs={{1,2},{2,1},{3,4},{4,3},{5,6},{6,5},{7,8},{8,7},{9,10},{10,9},{11,... | collective-permute-start | bytes 98312 | tf_op jit(solution)/shard_map/ppermute | solution.py:564
  31.1 2.0 %collective-permute-done.10.refs_8_ = bf16[128,128]{1,0:T(8,128)(2,1)S(1)} collective-permute-done((bf16[128,128]{1,0:T(8,128)(2,1)S(1)}, bf16[128,128]{1,0:T(8,128)(2,1)S(1)}, u32[]{:S(2)}, u32[]{:S(2)}) %collective-permute-start.10) | collective-permute-done | bytes 32800 | tf_op jit(solution)/shard_map/ppermute | solution.py:564
  33.1 1.1 inner.7
  34.2 1.5 %collective-permute-done.12.refs_10_ = bf16[128,128]{1,0:T(8,128)(2,1)S(1)} collective-permute-done((bf16[128,128]{1,0:T(8,128)(2,1)S(1)}, bf16[128,128]{1,0:T(8,128)(2,1)S(1)}, u32[]{:S(2)}, u32[]{:S(2)}) %collective-permute-start.12) | collective-permute-done | bytes 32800 | tf_op jit(solution)/shard_map/ppermute | solution.py:564
  36.1 0.6 collective-permute-start.16
  36.7 2.9 %collective-permute-start.17 = (bf16[128,128]{1,0:T(8,128)(2,1)S(1)}, bf16[128,128]{1,0:T(8,128)(2,1)S(1)}, u32[]{:S(2)}, u32[]{:S(2)}) collective-permute-start(bf16[128,128]{1,0:T(8,128)(2,1)S(1)} %get-tuple-element.136), channel_id=1, source_target_pairs={{2,4},{4,2},{3,5},{5,3},{6,8},{8,6},{7,9},{9,7},{10,12},{12,10},{1... | collective-permute-start | bytes 98312 | tf_op jit(solution)/shard_map/ppermute | solution.py:564
  39.6 2.4 %collective-permute-start.18 = (bf16[128,128]{1,0:T(8,128)(2,1)S(1)}, bf16[128,128]{1,0:T(8,128)(2,1)S(1)}, u32[]{:S(2)}, u32[]{:S(2)}) collective-permute-start(bf16[128,128]{1,0:T(8,128)(2,1)S(1)} %get-tuple-element.137), channel_id=1, source_target_pairs={{1,2},{2,1},{3,4},{4,3},{5,6},{6,5},{7,8},{8,7},{9,10},{10,9},{11,... | collective-permute-start | bytes 98312 | tf_op jit(solution)/shard_map/ppermute | solution.py:564
  42.1 0.7 collective-permute-done.16.refs_8_
  42.8 1.1 inner.8
  44.2 2.4 %collective-permute-done.18.refs_10_ = bf16[128,128]{1,0:T(8,128)(2,1)S(1)} collective-permute-done((bf16[128,128]{1,0:T(8,128)(2,1)S(1)}, bf16[128,128]{1,0:T(8,128)(2,1)S(1)}, u32[]{:S(2)}, u32[]{:S(2)}) %collective-permute-start.18) | collective-permute-done | bytes 32800 | tf_op jit(solution)/shard_map/ppermute | solution.py:564
  47.3 3.3 %collective-permute-start.23 = (bf16[128,128]{1,0:T(8,128)(2,1)S(1)}, bf16[128,128]{1,0:T(8,128)(2,1)S(1)}, u32[]{:S(2)}, u32[]{:S(2)}) collective-permute-start(bf16[128,128]{1,0:T(8,128)(2,1)S(1)} %get-tuple-element.147), channel_id=1, source_target_pairs={{2,4},{4,2},{3,5},{5,3},{6,8},{8,6},{7,9},{9,7},{10,12},{12,10},{1... | collective-permute-start | bytes 98312 | tf_op jit(solution)/shard_map/ppermute | solution.py:564
  50.6 1.5 %collective-permute-start.24 = (bf16[128,128]{1,0:T(8,128)(2,1)S(1)}, bf16[128,128]{1,0:T(8,128)(2,1)S(1)}, u32[]{:S(2)}, u32[]{:S(2)}) collective-permute-start(bf16[128,128]{1,0:T(8,128)(2,1)S(1)} %get-tuple-element.148), channel_id=1, source_target_pairs={{1,2},{2,1},{3,4},{4,3},{5,6},{6,5},{7,8},{8,7},{9,10},{10,9},{11,... | collective-permute-start | bytes 98312 | tf_op jit(solution)/shard_map/ppermute | solution.py:564
  52.1 1.0 collective-permute-start.26
  53.1 0.9 collective-permute-done.22.refs_8_
  54.0 1.1 inner.9
  55.1 2.6 %collective-permute-done.24.refs_10_ = bf16[128,128]{1,0:T(8,128)(2,1)S(1)} collective-permute-done((bf16[128,128]{1,0:T(8,128)(2,1)S(1)}, bf16[128,128]{1,0:T(8,128)(2,1)S(1)}, u32[]{:S(2)}, u32[]{:S(2)}) %collective-permute-start.24) | collective-permute-done | bytes 32800 | tf_op jit(solution)/shard_map/ppermute | solution.py:564
  58.3 3.3 %collective-permute-start.29 = (bf16[128,128]{1,0:T(8,128)(2,1)S(1)}, bf16[128,128]{1,0:T(8,128)(2,1)S(1)}, u32[]{:S(2)}, u32[]{:S(2)}) collective-permute-start(bf16[128,128]{1,0:T(8,128)(2,1)S(1)} %get-tuple-element.158), channel_id=1, source_target_pairs={{2,4},{4,2},{3,5},{5,3},{6,8},{8,6},{7,9},{9,7},{10,12},{12,10},{1... | collective-permute-start | bytes 98312 | tf_op jit(solution)/shard_map/ppermute | solution.py:564
  61.6 1.4 %collective-permute-start.30 = (bf16[128,128]{1,0:T(8,128)(2,1)S(1)}, bf16[128,128]{1,0:T(8,128)(2,1)S(1)}, u32[]{:S(2)}, u32[]{:S(2)}) collective-permute-start(bf16[128,128]{1,0:T(8,128)(2,1)S(1)} %get-tuple-element.159), channel_id=1, source_target_pairs={{1,2},{2,1},{3,4},{4,3},{5,6},{6,5},{7,8},{8,7},{9,10},{10,9},{11,... | collective-permute-start | bytes 98312 | tf_op jit(solution)/shard_map/ppermute | solution.py:564
  63.3 1.9 %collective-permute-done.28.refs_8_ = bf16[128,128]{1,0:T(8,128)(2,1)S(1)} collective-permute-done((bf16[128,128]{1,0:T(8,128)(2,1)S(1)}, bf16[128,128]{1,0:T(8,128)(2,1)S(1)}, u32[]{:S(2)}, u32[]{:S(2)}) %collective-permute-start.28) | collective-permute-done | bytes 32800 | tf_op jit(solution)/shard_map/ppermute | solution.py:564
  65.1 1.1 inner.10
  66.2 2.4 %collective-permute-done.30.refs_10_ = bf16[128,128]{1,0:T(8,128)(2,1)S(1)} collective-permute-done((bf16[128,128]{1,0:T(8,128)(2,1)S(1)}, bf16[128,128]{1,0:T(8,128)(2,1)S(1)}, u32[]{:S(2)}, u32[]{:S(2)}) %collective-permute-start.30) | collective-permute-done | bytes 32800 | tf_op jit(solution)/shard_map/ppermute | solution.py:564
  69.3 2.5 %collective-permute-start.35 = (bf16[128,128]{1,0:T(8,128)(2,1)S(1)}, bf16[128,128]{1,0:T(8,128)(2,1)S(1)}, u32[]{:S(2)}, u32[]{:S(2)}) collective-permute-start(bf16[128,128]{1,0:T(8,128)(2,1)S(1)} %get-tuple-element.169), channel_id=1, source_target_pairs={{2,4},{4,2},{3,5},{5,3},{6,8},{8,6},{7,9},{9,7},{10,12},{12,10},{1... | collective-permute-start | bytes 98312 | tf_op jit(solution)/shard_map/ppermute | solution.py:564
  71.8 2.3 %collective-permute-start.36 = (bf16[128,128]{1,0:T(8,128)(2,1)S(1)}, bf16[128,128]{1,0:T(8,128)(2,1)S(1)}, u32[]{:S(2)}, u32[]{:S(2)}) collective-permute-start(bf16[128,128]{1,0:T(8,128)(2,1)S(1)} %get-tuple-element.170), channel_id=1, source_target_pairs={{1,2},{2,1},{3,4},{4,3},{5,6},{6,5},{7,8},{8,7},{9,10},{10,9},{11,... | collective-permute-start | bytes 98312 | tf_op jit(solution)/shard_map/ppermute | solution.py:564
  74.2 1.9 %collective-permute-done.34.refs_8_ = bf16[128,128]{1,0:T(8,128)(2,1)S(1)} collective-permute-done((bf16[128,128]{1,0:T(8,128)(2,1)S(1)}, bf16[128,128]{1,0:T(8,128)(2,1)S(1)}, u32[]{:S(2)}, u32[]{:S(2)}) %collective-permute-start.34) | collective-permute-done | bytes 32800 | tf_op jit(solution)/shard_map/ppermute | solution.py:564
  76.1 1.3 %inner.11 = (f32[2048,128]{1,0:T(8,128)S(1)}, f32[2048,128]{1,0:T(8,128)S(1)}, f32[256,128]{1,0:T(8,128)S(1)}) custom-call(bf16[2048,384]{1,0:T(8,128)(2,1)S(1)} %get-tuple-element.102.refs_0_.refs_1_, bf16[2048,256]{1,0:T(8,128)(2,1)S(1)} %get-tuple-element.103.refs_1_.refs_2_, bf16[256,2048]{1,0:T(8,128)(2,1)S(1)} %get-tuple-element.110.refs_2_.refs_5_, ...), custom_call_target="tpu_custom_call" | custom-call | flops 201326592 | bytes 3145728 | tf_op jit(solution)/shard_map/inner/pallas_call | solution.py:318
  77.5 1.3 %collective-permute-done.36.refs_10_ = bf16[128,128]{1,0:T(8,128)(2,1)S(1)} collective-permute-done((bf16[128,128]{1,0:T(8,128)(2,1)S(1)}, bf16[128,128]{1,0:T(8,128)(2,1)S(1)}, u32[]{:S(2)}, u32[]{:S(2)}) %collective-permute-start.36) | collective-permute-done | bytes 32800 | tf_op jit(solution)/shard_map/ppermute | solution.py:564
  79.2 0.5 collective-permute-start.40
  79.7 3.0 %collective-permute-start.41 = (bf16[128,128]{1,0:T(8,128)(2,1)S(1)}, bf16[128,128]{1,0:T(8,128)(2,1)S(1)}, u32[]{:S(2)}, u32[]{:S(2)}) collective-permute-start(bf16[128,128]{1,0:T(8,128)(2,1)S(1)} %get-tuple-element.180), channel_id=1, source_target_pairs={{2,4},{4,2},{3,5},{5,3},{6,8},{8,6},{7,9},{9,7},{10,12},{12,10},{1... | collective-permute-start | bytes 98312 | tf_op jit(solution)/shard_map/ppermute | solution.py:564
  82.8 2.3 %collective-permute-start.42 = (bf16[128,128]{1,0:T(8,128)(2,1)S(1)}, bf16[128,128]{1,0:T(8,128)(2,1)S(1)}, u32[]{:S(2)}, u32[]{:S(2)}) collective-permute-start(bf16[128,128]{1,0:T(8,128)(2,1)S(1)} %get-tuple-element.181), channel_id=1, source_target_pairs={{1,2},{2,1},{3,4},{4,3},{5,6},{6,5},{7,8},{8,7},{9,10},{10,9},{11,... | collective-permute-start | bytes 98312 | tf_op jit(solution)/shard_map/ppermute | solution.py:564
  85.1 0.7 collective-permute-done.40.refs_8_
  85.9 1.1 inner.12
  87.2 2.5 %collective-permute-done.42.refs_10_ = bf16[128,128]{1,0:T(8,128)(2,1)S(1)} collective-permute-done((bf16[128,128]{1,0:T(8,128)(2,1)S(1)}, bf16[128,128]{1,0:T(8,128)(2,1)S(1)}, u32[]{:S(2)}, u32[]{:S(2)}) %collective-permute-start.42) | collective-permute-done | bytes 32800 | tf_op jit(solution)/shard_map/ppermute | solution.py:564
  90.4 3.2 %collective-permute-start.47 = (bf16[128,128]{1,0:T(8,128)(2,1)S(1)}, bf16[128,128]{1,0:T(8,128)(2,1)S(1)}, u32[]{:S(2)}, u32[]{:S(2)}) collective-permute-start(bf16[128,128]{1,0:T(8,128)(2,1)S(1)} %get-tuple-element.189), channel_id=1, source_target_pairs={{2,4},{4,2},{3,5},{5,3},{6,8},{8,6},{7,9},{9,7},{10,12},{12,10},{1... | collective-permute-start | bytes 98312 | tf_op jit(solution)/shard_map/ppermute | solution.py:564
  93.7 1.6 %collective-permute-start.48 = (bf16[128,128]{1,0:T(8,128)(2,1)S(1)}, bf16[128,128]{1,0:T(8,128)(2,1)S(1)}, u32[]{:S(2)}, u32[]{:S(2)}) collective-permute-start(bf16[128,128]{1,0:T(8,128)(2,1)S(1)} %get-tuple-element.190), channel_id=1, source_target_pairs={{1,2},{2,1},{3,4},{4,3},{5,6},{6,5},{7,8},{8,7},{9,10},{10,9},{11,... | collective-permute-start | bytes 98312 | tf_op jit(solution)/shard_map/ppermute | solution.py:564
  95.2 0.8 collective-permute-start.50
  96.1 1.1 collective-permute-done.46.refs_5_
  97.1 0.8 inner.13.refs_4_
  98.0 2.6 %collective-permute-done.48.refs_7_ = bf16[128,128]{1,0:T(8,128)(2,1)S(1)} collective-permute-done((bf16[128,128]{1,0:T(8,128)(2,1)S(1)}, bf16[128,128]{1,0:T(8,128)(2,1)S(1)}, u32[]{:S(2)}, u32[]{:S(2)}) %collective-permute-start.48) | collective-permute-done | bytes 32800 | tf_op jit(solution)/shard_map/ppermute | solution.py:564
  100.6 0.8 last.1
  101.5 1.2 collective-permute-done.52
  102.7 0.9 collective-permute-start.54
  103.7 2.5 %collective-permute-start.53 = (f32[64,128]{1,0:T(8,128)S(1)}, f32[64,128]{1,0:T(8,128)S(1)}, u32[]{:S(2)}, u32[]{:S(2)}) collective-permute-start(f32[64,128]{1,0:T(8,128)S(1)} %add.25), channel_id=1, source_target_pairs={{0,2},{1,3},{2,0},{3,1},{4,6},{5,7},{6,4},{7,5},{8,10},{9,11},{10,... | collective-permute-start | bytes 98312 | tf_op jit(solution)/shard_map/ppermute | solution.py:547
  106.2 1.5 %collective-permute-done.55 = f32[64,128]{1,0:T(8,128)S(1)} collective-permute-done((f32[64,128]{1,0:T(8,128)S(1)}, f32[64,128]{1,0:T(8,128)S(1)}, u32[]{:S(2)}, u32[]{:S(2)}) %collective-permute-start.55) | collective-permute-done | bytes 32800 | tf_op jit(solution)/shard_map/ppermute | solution.py:547
  108.1 2.1 %collective-permute-start.58 = (f32[64,128]{1,0:T(8,128)S(1)}, f32[64,128]{1,0:T(8,128)S(1)}, u32[]{:S(2)}, u32[]{:S(2)}) collective-permute-start(f32[64,128]{1,0:T(8,128)S(1)} %add_add_fusion.1), channel_id=1, source_target_pairs={{0,24},{1,25},{2,26},{3,27},{4,28},{5,29},{6,30},{7,31},{8,16},{9,... | collective-permute-start | bytes 98312 | tf_op jit(solution)/shard_map/ppermute | solution.py:547
  110.2 2.4 %collective-permute-start.56 = (f32[64,128]{1,0:T(8,128)S(1)}, f32[64,128]{1,0:T(8,128)S(1)}, u32[]{:S(2)}, u32[]{:S(2)}) collective-permute-start(f32[64,128]{1,0:T(8,128)S(1)} %add_add_fusion.1), channel_id=1, source_target_pairs={{0,8},{1,9},{2,10},{3,11},{4,12},{5,13},{6,14},{7,15},{8,0},{9,1},... | collective-permute-start | bytes 98312 | tf_op jit(solution)/shard_map/ppermute | solution.py:547
  112.6 1.5 %collective-permute-done.58 = f32[64,128]{1,0:T(8,128)S(1)} collective-permute-done((f32[64,128]{1,0:T(8,128)S(1)}, f32[64,128]{1,0:T(8,128)S(1)}, u32[]{:S(2)}, u32[]{:S(2)}) %collective-permute-start.58) | collective-permute-done | bytes 32800 | tf_op jit(solution)/shard_map/ppermute | solution.py:547
  114.1 0.9 collective-permute-done.57
  115.1 1.2 collective-permute-done.59.refs_2_
  116.3 6.5 %finish.1 = f32[2048,128]{1,0:T(8,128)} custom-call(s32[1]{0:T(128)} %bitcast.place_ref.refs_0_, f32[64,128]{1,0:T(8,128)S(1)} %add_add_fusion.refs_1_, f32[64,128]{1,0:T(8,128)S(1)} %collective-permute-done.59.refs_2_, bf16[2048,256]{1,0:T(8,128)(2,1)S(1)} %get-tuple-element.196.refs_3_), custom_call_target="tpu_custom_call" | custom-call | tf_op jit(solution)/shard_map/finish/pallas_call | solution.py:530
  (78 shorter events, 5.6 us)
Async XLA Ops:
  0.0 12.6 %collective-permute-start.3 = (s32[1,256]{1,0:T(1,128)}, s32[1,256]{1,0:T(1,128)S(1)}, u32[]{:S(2)}, u32[]{:S(2)}) collective-permute-start(s32[1,256]{1,0:T(1,128)} %bitcast.10), channel_id=1, source_target_pairs={{0,2},{2,0},{1,3},{3,1},{4,6},{6,4},{5,7},{7,5},{8,10},{10,8},{9,1... | collective-permute-start | bytes 3080 | tf_op jit(solution)/shard_map/ppermute | solution.py:564
  2.9 9.7 %collective-permute-start.2 = (s32[1,256]{1,0:T(1,128)}, s32[1,256]{1,0:T(1,128)S(1)}, u32[]{:S(2)}, u32[]{:S(2)}) collective-permute-start(s32[1,256]{1,0:T(1,128)} %bitcast.11), channel_id=1, source_target_pairs={{0,4},{4,0},{1,5},{5,1},{2,6},{6,2},{3,7},{7,3},{8,12},{12,8},{9,1... | collective-permute-start | bytes 3080 | tf_op jit(solution)/shard_map/ppermute | solution.py:564
  4.5 8.2 %collective-permute-start.1 = (s32[1,256]{1,0:T(1,128)}, s32[1,256]{1,0:T(1,128)S(1)}, u32[]{:S(2)}, u32[]{:S(2)}) collective-permute-start(s32[1,256]{1,0:T(1,128)} %bitcast.12), channel_id=1, source_target_pairs={{2,4},{4,2},{3,5},{5,3},{6,8},{8,6},{7,9},{9,7},{10,12},{12,10},{1... | collective-permute-start | bytes 3080 | tf_op jit(solution)/shard_map/ppermute | solution.py:564
  8.0 6.5 %collective-permute-start = (s32[1,256]{1,0:T(1,128)}, s32[1,256]{1,0:T(1,128)S(1)}, u32[]{:S(2)}, u32[]{:S(2)}) collective-permute-start(s32[1,256]{1,0:T(1,128)} %bitcast.13), channel_id=1, source_target_pairs={{4,8},{8,4},{5,9},{9,5},{6,10},{10,6},{7,11},{11,7},{12,16},{16,12... | collective-permute-start | bytes 3080 | tf_op jit(solution)/shard_map/ppermute | solution.py:564
  15.1 6.8 %collective-permute-start.4 = (bf16[128,128]{1,0:T(8,128)(2,1)S(1)}, bf16[128,128]{1,0:T(8,128)(2,1)S(1)}, u32[]{:S(2)}, u32[]{:S(2)}) collective-permute-start(bf16[128,128]{1,0:T(8,128)(2,1)S(1)} %get-tuple-element.114), channel_id=1, source_target_pairs={{4,8},{8,4},{5,9},{9,5},{6,10},{10,6},{7,11},{11,7},{12,16},{16,12... | collective-permute-start | bytes 98312 | tf_op jit(solution)/shard_map/ppermute | solution.py:564
  16.6 7.5 %collective-permute-start.5 = (bf16[128,128]{1,0:T(8,128)(2,1)S(1)}, bf16[128,128]{1,0:T(8,128)(2,1)S(1)}, u32[]{:S(2)}, u32[]{:S(2)}) collective-permute-start(bf16[128,128]{1,0:T(8,128)(2,1)S(1)} %get-tuple-element.115), channel_id=1, source_target_pairs={{2,4},{4,2},{3,5},{5,3},{6,8},{8,6},{7,9},{9,7},{10,12},{12,10},{1... | collective-permute-start | bytes 98312 | tf_op jit(solution)/shard_map/ppermute | solution.py:564
  18.6 7.0 %collective-permute-start.6 = (bf16[128,128]{1,0:T(8,128)(2,1)S(1)}, bf16[128,128]{1,0:T(8,128)(2,1)S(1)}, u32[]{:S(2)}, u32[]{:S(2)}) collective-permute-start(bf16[128,128]{1,0:T(8,128)(2,1)S(1)} %get-tuple-element.116), channel_id=1, source_target_pairs={{1,2},{2,1},{3,4},{4,3},{5,6},{6,5},{7,8},{8,7},{9,10},{10,9},{11,... | collective-permute-start | bytes 98312 | tf_op jit(solution)/shard_map/ppermute | solution.py:564
  19.9 5.7 %collective-permute-start.7 = (bf16[128,128]{1,0:T(8,128)(2,1)S(1)}, bf16[128,128]{1,0:T(8,128)(2,1)S(1)}, u32[]{:S(2)}, u32[]{:S(2)}) collective-permute-start(bf16[128,128]{1,0:T(8,128)(2,1)S(1)} %get-tuple-element.117), channel_id=1, source_target_pairs={{0,4},{4,0},{1,5},{5,1},{2,6},{6,2},{3,7},{7,3},{8,12},{12,8},{9,1... | collective-permute-start | bytes 98312 | tf_op jit(solution)/shard_map/ppermute | solution.py:564
  19.9 5.7 %collective-permute-start.8 = (bf16[128,128]{1,0:T(8,128)(2,1)S(1)}, bf16[128,128]{1,0:T(8,128)(2,1)S(1)}, u32[]{:S(2)}, u32[]{:S(2)}) collective-permute-start(bf16[128,128]{1,0:T(8,128)(2,1)S(1)} %get-tuple-element.118), channel_id=1, source_target_pairs={{0,2},{2,0},{1,3},{3,1},{4,6},{6,4},{5,7},{7,5},{8,10},{10,8},{9,1... | collective-permute-start | bytes 98312 | tf_op jit(solution)/shard_map/ppermute | solution.py:564
  21.8 3.8 %collective-permute-start.9 = (bf16[128,128]{1,0:T(8,128)(2,1)S(1)}, bf16[128,128]{1,0:T(8,128)(2,1)S(1)}, u32[]{:S(2)}, u32[]{:S(2)}) collective-permute-start(bf16[128,128]{1,0:T(8,128)(2,1)S(1)} %get-tuple-element.119), channel_id=1, source_target_pairs={{0,1},{1,0},{2,3},{3,2},{4,5},{5,4},{6,7},{7,6},{8,9},{9,8},{10,11... | collective-permute-start | bytes 98312 | tf_op jit(solution)/shard_map/ppermute | solution.py:564
  26.0 7.0 %collective-permute-start.10 = (bf16[128,128]{1,0:T(8,128)(2,1)S(1)}, bf16[128,128]{1,0:T(8,128)(2,1)S(1)}, u32[]{:S(2)}, u32[]{:S(2)}) collective-permute-start(bf16[128,128]{1,0:T(8,128)(2,1)S(1)} %get-tuple-element.124), channel_id=1, source_target_pairs={{4,8},{8,4},{5,9},{9,5},{6,10},{10,6},{7,11},{11,7},{12,16},{16,12... | collective-permute-start | bytes 98312 | tf_op jit(solution)/shard_map/ppermute | solution.py:564
  26.2 8.0 %collective-permute-start.11 = (bf16[128,128]{1,0:T(8,128)(2,1)S(1)}, bf16[128,128]{1,0:T(8,128)(2,1)S(1)}, u32[]{:S(2)}, u32[]{:S(2)}) collective-permute-start(bf16[128,128]{1,0:T(8,128)(2,1)S(1)} %get-tuple-element.125), channel_id=1, source_target_pairs={{2,4},{4,2},{3,5},{5,3},{6,8},{8,6},{7,9},{9,7},{10,12},{12,10},{1... | collective-permute-start | bytes 98312 | tf_op jit(solution)/shard_map/ppermute | solution.py:564
  28.8 6.9 %collective-permute-start.12 = (bf16[128,128]{1,0:T(8,128)(2,1)S(1)}, bf16[128,128]{1,0:T(8,128)(2,1)S(1)}, u32[]{:S(2)}, u32[]{:S(2)}) collective-permute-start(bf16[128,128]{1,0:T(8,128)(2,1)S(1)} %get-tuple-element.126), channel_id=1, source_target_pairs={{1,2},{2,1},{3,4},{4,3},{5,6},{6,5},{7,8},{8,7},{9,10},{10,9},{11,... | collective-permute-start | bytes 98312 | tf_op jit(solution)/shard_map/ppermute | solution.py:564
  31.1 4.6 %collective-permute-start.13 = (bf16[128,128]{1,0:T(8,128)(2,1)S(1)}, bf16[128,128]{1,0:T(8,128)(2,1)S(1)}, u32[]{:S(2)}, u32[]{:S(2)}) collective-permute-start(bf16[128,128]{1,0:T(8,128)(2,1)S(1)} %get-tuple-element.127), channel_id=1, source_target_pairs={{0,4},{4,0},{1,5},{5,1},{2,6},{6,2},{3,7},{7,3},{8,12},{12,8},{9,1... | collective-permute-start | bytes 98312 | tf_op jit(solution)/shard_map/ppermute | solution.py:564
  31.1 4.6 %collective-permute-start.14 = (bf16[128,128]{1,0:T(8,128)(2,1)S(1)}, bf16[128,128]{1,0:T(8,128)(2,1)S(1)}, u32[]{:S(2)}, u32[]{:S(2)}) collective-permute-start(bf16[128,128]{1,0:T(8,128)(2,1)S(1)} %get-tuple-element.128), channel_id=1, source_target_pairs={{0,2},{2,0},{1,3},{3,1},{4,6},{6,4},{5,7},{7,5},{8,10},{10,8},{9,1... | collective-permute-start | bytes 98312 | tf_op jit(solution)/shard_map/ppermute | solution.py:564
  33.1 2.6 %collective-permute-start.15 = (bf16[128,128]{1,0:T(8,128)(2,1)S(1)}, bf16[128,128]{1,0:T(8,128)(2,1)S(1)}, u32[]{:S(2)}, u32[]{:S(2)}) collective-permute-start(bf16[128,128]{1,0:T(8,128)(2,1)S(1)} %get-tuple-element.129), channel_id=1, source_target_pairs={{0,1},{1,0},{2,3},{3,2},{4,5},{5,4},{6,7},{7,6},{8,9},{9,8},{10,11... | collective-permute-start | bytes 98312 | tf_op jit(solution)/shard_map/ppermute | solution.py:564
  36.1 6.7 %collective-permute-start.16 = (bf16[128,128]{1,0:T(8,128)(2,1)S(1)}, bf16[128,128]{1,0:T(8,128)(2,1)S(1)}, u32[]{:S(2)}, u32[]{:S(2)}) collective-permute-start(bf16[128,128]{1,0:T(8,128)(2,1)S(1)} %get-tuple-element.135), channel_id=1, source_target_pairs={{4,8},{8,4},{5,9},{9,5},{6,10},{10,6},{7,11},{11,7},{12,16},{16,12... | collective-permute-start | bytes 98312 | tf_op jit(solution)/shard_map/ppermute | solution.py:564
  36.7 7.5 %collective-permute-start.17 = (bf16[128,128]{1,0:T(8,128)(2,1)S(1)}, bf16[128,128]{1,0:T(8,128)(2,1)S(1)}, u32[]{:S(2)}, u32[]{:S(2)}) collective-permute-start(bf16[128,128]{1,0:T(8,128)(2,1)S(1)} %get-tuple-element.136), channel_id=1, source_target_pairs={{2,4},{4,2},{3,5},{5,3},{6,8},{8,6},{7,9},{9,7},{10,12},{12,10},{1... | collective-permute-start | bytes 98312 | tf_op jit(solution)/shard_map/ppermute | solution.py:564
  39.6 6.9 %collective-permute-start.18 = (bf16[128,128]{1,0:T(8,128)(2,1)S(1)}, bf16[128,128]{1,0:T(8,128)(2,1)S(1)}, u32[]{:S(2)}, u32[]{:S(2)}) collective-permute-start(bf16[128,128]{1,0:T(8,128)(2,1)S(1)} %get-tuple-element.137), channel_id=1, source_target_pairs={{1,2},{2,1},{3,4},{4,3},{5,6},{6,5},{7,8},{8,7},{9,10},{10,9},{11,... | collective-permute-start | bytes 98312 | tf_op jit(solution)/shard_map/ppermute | solution.py:564
  42.1 4.5 %collective-permute-start.19 = (bf16[128,128]{1,0:T(8,128)(2,1)S(1)}, bf16[128,128]{1,0:T(8,128)(2,1)S(1)}, u32[]{:S(2)}, u32[]{:S(2)}) collective-permute-start(bf16[128,128]{1,0:T(8,128)(2,1)S(1)} %get-tuple-element.138), channel_id=1, source_target_pairs={{0,4},{4,0},{1,5},{5,1},{2,6},{6,2},{3,7},{7,3},{8,12},{12,8},{9,1... | collective-permute-start | bytes 98312 | tf_op jit(solution)/shard_map/ppermute | solution.py:564
  42.1 4.5 %collective-permute-start.20 = (bf16[128,128]{1,0:T(8,128)(2,1)S(1)}, bf16[128,128]{1,0:T(8,128)(2,1)S(1)}, u32[]{:S(2)}, u32[]{:S(2)}) collective-permute-start(bf16[128,128]{1,0:T(8,128)(2,1)S(1)} %get-tuple-element.139), channel_id=1, source_target_pairs={{0,2},{2,0},{1,3},{3,1},{4,6},{6,4},{5,7},{7,5},{8,10},{10,8},{9,1... | collective-permute-start | bytes 98312 | tf_op jit(solution)/shard_map/ppermute | solution.py:564
  42.8 3.8 %collective-permute-start.21 = (bf16[128,128]{1,0:T(8,128)(2,1)S(1)}, bf16[128,128]{1,0:T(8,128)(2,1)S(1)}, u32[]{:S(2)}, u32[]{:S(2)}) collective-permute-start(bf16[128,128]{1,0:T(8,128)(2,1)S(1)} %get-tuple-element.140), channel_id=1, source_target_pairs={{0,1},{1,0},{2,3},{3,2},{4,5},{5,4},{6,7},{7,6},{8,9},{9,8},{10,11... | collective-permute-start | bytes 98312 | tf_op jit(solution)/shard_map/ppermute | solution.py:564
  47.0 7.0 %collective-permute-start.22 = (bf16[128,128]{1,0:T(8,128)(2,1)S(1)}, bf16[128,128]{1,0:T(8,128)(2,1)S(1)}, u32[]{:S(2)}, u32[]{:S(2)}) collective-permute-start(bf16[128,128]{1,0:T(8,128)(2,1)S(1)} %get-tuple-element.146), channel_id=1, source_target_pairs={{4,8},{8,4},{5,9},{9,5},{6,10},{10,6},{7,11},{11,7},{12,16},{16,12... | collective-permute-start | bytes 98312 | tf_op jit(solution)/shard_map/ppermute | solution.py:564
  47.3 7.8 %collective-permute-start.23 = (bf16[128,128]{1,0:T(8,128)(2,1)S(1)}, bf16[128,128]{1,0:T(8,128)(2,1)S(1)}, u32[]{:S(2)}, u32[]{:S(2)}) collective-permute-start(bf16[128,128]{1,0:T(8,128)(2,1)S(1)} %get-tuple-element.147), channel_id=1, source_target_pairs={{2,4},{4,2},{3,5},{5,3},{6,8},{8,6},{7,9},{9,7},{10,12},{12,10},{1... | collective-permute-start | bytes 98312 | tf_op jit(solution)/shard_map/ppermute | solution.py:564
  50.6 7.0 %collective-permute-start.24 = (bf16[128,128]{1,0:T(8,128)(2,1)S(1)}, bf16[128,128]{1,0:T(8,128)(2,1)S(1)}, u32[]{:S(2)}, u32[]{:S(2)}) collective-permute-start(bf16[128,128]{1,0:T(8,128)(2,1)S(1)} %get-tuple-element.148), channel_id=1, source_target_pairs={{1,2},{2,1},{3,4},{4,3},{5,6},{6,5},{7,8},{8,7},{9,10},{10,9},{11,... | collective-permute-start | bytes 98312 | tf_op jit(solution)/shard_map/ppermute | solution.py:564
  52.1 5.5 %collective-permute-start.25 = (bf16[128,128]{1,0:T(8,128)(2,1)S(1)}, bf16[128,128]{1,0:T(8,128)(2,1)S(1)}, u32[]{:S(2)}, u32[]{:S(2)}) collective-permute-start(bf16[128,128]{1,0:T(8,128)(2,1)S(1)} %get-tuple-element.149), channel_id=1, source_target_pairs={{0,4},{4,0},{1,5},{5,1},{2,6},{6,2},{3,7},{7,3},{8,12},{12,8},{9,1... | collective-permute-start | bytes 98312 | tf_op jit(solution)/shard_map/ppermute | solution.py:564
  52.1 5.5 %collective-permute-start.26 = (bf16[128,128]{1,0:T(8,128)(2,1)S(1)}, bf16[128,128]{1,0:T(8,128)(2,1)S(1)}, u32[]{:S(2)}, u32[]{:S(2)}) collective-permute-start(bf16[128,128]{1,0:T(8,128)(2,1)S(1)} %get-tuple-element.150), channel_id=1, source_target_pairs={{0,2},{2,0},{1,3},{3,1},{4,6},{6,4},{5,7},{7,5},{8,10},{10,8},{9,1... | collective-permute-start | bytes 98312 | tf_op jit(solution)/shard_map/ppermute | solution.py:564
  53.9 3.7 %collective-permute-start.27 = (bf16[128,128]{1,0:T(8,128)(2,1)S(1)}, bf16[128,128]{1,0:T(8,128)(2,1)S(1)}, u32[]{:S(2)}, u32[]{:S(2)}) collective-permute-start(bf16[128,128]{1,0:T(8,128)(2,1)S(1)} %get-tuple-element.151), channel_id=1, source_target_pairs={{0,1},{1,0},{2,3},{3,2},{4,5},{5,4},{6,7},{7,6},{8,9},{9,8},{10,11... | collective-permute-start | bytes 98312 | tf_op jit(solution)/shard_map/ppermute | solution.py:564
  58.1 7.1 %collective-permute-start.28 = (bf16[128,128]{1,0:T(8,128)(2,1)S(1)}, bf16[128,128]{1,0:T(8,128)(2,1)S(1)}, u32[]{:S(2)}, u32[]{:S(2)}) collective-permute-start(bf16[128,128]{1,0:T(8,128)(2,1)S(1)} %get-tuple-element.157), channel_id=1, source_target_pairs={{4,8},{8,4},{5,9},{9,5},{6,10},{10,6},{7,11},{11,7},{12,16},{16,12... | collective-permute-start | bytes 98312 | tf_op jit(solution)/shard_map/ppermute | solution.py:564
  58.3 8.0 %collective-permute-start.29 = (bf16[128,128]{1,0:T(8,128)(2,1)S(1)}, bf16[128,128]{1,0:T(8,128)(2,1)S(1)}, u32[]{:S(2)}, u32[]{:S(2)}) collective-permute-start(bf16[128,128]{1,0:T(8,128)(2,1)S(1)} %get-tuple-element.158), channel_id=1, source_target_pairs={{2,4},{4,2},{3,5},{5,3},{6,8},{8,6},{7,9},{9,7},{10,12},{12,10},{1... | collective-permute-start | bytes 98312 | tf_op jit(solution)/shard_map/ppermute | solution.py:564
  61.6 7.0 %collective-permute-start.30 = (bf16[128,128]{1,0:T(8,128)(2,1)S(1)}, bf16[128,128]{1,0:T(8,128)(2,1)S(1)}, u32[]{:S(2)}, u32[]{:S(2)}) collective-permute-start(bf16[128,128]{1,0:T(8,128)(2,1)S(1)} %get-tuple-element.159), channel_id=1, source_target_pairs={{1,2},{2,1},{3,4},{4,3},{5,6},{6,5},{7,8},{8,7},{9,10},{10,9},{11,... | collective-permute-start | bytes 98312 | tf_op jit(solution)/shard_map/ppermute | solution.py:564
  63.1 5.6 %collective-permute-start.31 = (bf16[128,128]{1,0:T(8,128)(2,1)S(1)}, bf16[128,128]{1,0:T(8,128)(2,1)S(1)}, u32[]{:S(2)}, u32[]{:S(2)}) collective-permute-start(bf16[128,128]{1,0:T(8,128)(2,1)S(1)} %get-tuple-element.160), channel_id=1, source_target_pairs={{0,4},{4,0},{1,5},{5,1},{2,6},{6,2},{3,7},{7,3},{8,12},{12,8},{9,1... | collective-permute-start | bytes 98312 | tf_op jit(solution)/shard_map/ppermute | solution.py:564
  63.1 5.6 %collective-permute-start.32 = (bf16[128,128]{1,0:T(8,128)(2,1)S(1)}, bf16[128,128]{1,0:T(8,128)(2,1)S(1)}, u32[]{:S(2)}, u32[]{:S(2)}) collective-permute-start(bf16[128,128]{1,0:T(8,128)(2,1)S(1)} %get-tuple-element.161), channel_id=1, source_target_pairs={{0,2},{2,0},{1,3},{3,1},{4,6},{6,4},{5,7},{7,5},{8,10},{10,8},{9,1... | collective-permute-start | bytes 98312 | tf_op jit(solution)/shard_map/ppermute | solution.py:564
  65.1 3.5 %collective-permute-start.33 = (bf16[128,128]{1,0:T(8,128)(2,1)S(1)}, bf16[128,128]{1,0:T(8,128)(2,1)S(1)}, u32[]{:S(2)}, u32[]{:S(2)}) collective-permute-start(bf16[128,128]{1,0:T(8,128)(2,1)S(1)} %get-tuple-element.162), channel_id=1, source_target_pairs={{0,1},{1,0},{2,3},{3,2},{4,5},{5,4},{6,7},{7,6},{8,9},{9,8},{10,11... | collective-permute-start | bytes 98312 | tf_op jit(solution)/shard_map/ppermute | solution.py:564
  69.1 7.1 %collective-permute-start.34 = (bf16[128,128]{1,0:T(8,128)(2,1)S(1)}, bf16[128,128]{1,0:T(8,128)(2,1)S(1)}, u32[]{:S(2)}, u32[]{:S(2)}) collective-permute-start(bf16[128,128]{1,0:T(8,128)(2,1)S(1)} %get-tuple-element.168), channel_id=1, source_target_pairs={{4,8},{8,4},{5,9},{9,5},{6,10},{10,6},{7,11},{11,7},{12,16},{16,12... | collective-permute-start | bytes 98312 | tf_op jit(solution)/shard_map/ppermute | solution.py:564
  69.3 8.2 %collective-permute-start.35 = (bf16[128,128]{1,0:T(8,128)(2,1)S(1)}, bf16[128,128]{1,0:T(8,128)(2,1)S(1)}, u32[]{:S(2)}, u32[]{:S(2)}) collective-permute-start(bf16[128,128]{1,0:T(8,128)(2,1)S(1)} %get-tuple-element.169), channel_id=1, source_target_pairs={{2,4},{4,2},{3,5},{5,3},{6,8},{8,6},{7,9},{9,7},{10,12},{12,10},{1... | collective-permute-start | bytes 98312 | tf_op jit(solution)/shard_map/ppermute | solution.py:564
  71.8 6.9 %collective-permute-start.36 = (bf16[128,128]{1,0:T(8,128)(2,1)S(1)}, bf16[128,128]{1,0:T(8,128)(2,1)S(1)}, u32[]{:S(2)}, u32[]{:S(2)}) collective-permute-start(bf16[128,128]{1,0:T(8,128)(2,1)S(1)} %get-tuple-element.170), channel_id=1, source_target_pairs={{1,2},{2,1},{3,4},{4,3},{5,6},{6,5},{7,8},{8,7},{9,10},{10,9},{11,... | collective-permute-start | bytes 98312 | tf_op jit(solution)/shard_map/ppermute | solution.py:564
  74.1 4.7 %collective-permute-start.37 = (bf16[128,128]{1,0:T(8,128)(2,1)S(1)}, bf16[128,128]{1,0:T(8,128)(2,1)S(1)}, u32[]{:S(2)}, u32[]{:S(2)}) collective-permute-start(bf16[128,128]{1,0:T(8,128)(2,1)S(1)} %get-tuple-element.171), channel_id=1, source_target_pairs={{0,4},{4,0},{1,5},{5,1},{2,6},{6,2},{3,7},{7,3},{8,12},{12,8},{9,1... | collective-permute-start | bytes 98312 | tf_op jit(solution)/shard_map/ppermute | solution.py:564
  74.1 4.7 %collective-permute-start.38 = (bf16[128,128]{1,0:T(8,128)(2,1)S(1)}, bf16[128,128]{1,0:T(8,128)(2,1)S(1)}, u32[]{:S(2)}, u32[]{:S(2)}) collective-permute-start(bf16[128,128]{1,0:T(8,128)(2,1)S(1)} %get-tuple-element.172), channel_id=1, source_target_pairs={{0,2},{2,0},{1,3},{3,1},{4,6},{6,4},{5,7},{7,5},{8,10},{10,8},{9,1... | collective-permute-start | bytes 98312 | tf_op jit(solution)/shard_map/ppermute | solution.py:564
  76.1 2.6 %collective-permute-start.39 = (bf16[128,128]{1,0:T(8,128)(2,1)S(1)}, bf16[128,128]{1,0:T(8,128)(2,1)S(1)}, u32[]{:S(2)}, u32[]{:S(2)}) collective-permute-start(bf16[128,128]{1,0:T(8,128)(2,1)S(1)} %get-tuple-element.173), channel_id=1, source_target_pairs={{0,1},{1,0},{2,3},{3,2},{4,5},{5,4},{6,7},{7,6},{8,9},{9,8},{10,11... | collective-permute-start | bytes 98312 | tf_op jit(solution)/shard_map/ppermute | solution.py:564
  79.2 6.7 %collective-permute-start.40 = (bf16[128,128]{1,0:T(8,128)(2,1)S(1)}, bf16[128,128]{1,0:T(8,128)(2,1)S(1)}, u32[]{:S(2)}, u32[]{:S(2)}) collective-permute-start(bf16[128,128]{1,0:T(8,128)(2,1)S(1)} %get-tuple-element.179), channel_id=1, source_target_pairs={{4,8},{8,4},{5,9},{9,5},{6,10},{10,6},{7,11},{11,7},{12,16},{16,12... | collective-permute-start | bytes 98312 | tf_op jit(solution)/shard_map/ppermute | solution.py:564
  79.7 7.5 %collective-permute-start.41 = (bf16[128,128]{1,0:T(8,128)(2,1)S(1)}, bf16[128,128]{1,0:T(8,128)(2,1)S(1)}, u32[]{:S(2)}, u32[]{:S(2)}) collective-permute-start(bf16[128,128]{1,0:T(8,128)(2,1)S(1)} %get-tuple-element.180), channel_id=1, source_target_pairs={{2,4},{4,2},{3,5},{5,3},{6,8},{8,6},{7,9},{9,7},{10,12},{12,10},{1... | collective-permute-start | bytes 98312 | tf_op jit(solution)/shard_map/ppermute | solution.py:564
  82.8 6.9 %collective-permute-start.42 = (bf16[128,128]{1,0:T(8,128)(2,1)S(1)}, bf16[128,128]{1,0:T(8,128)(2,1)S(1)}, u32[]{:S(2)}, u32[]{:S(2)}) collective-permute-start(bf16[128,128]{1,0:T(8,128)(2,1)S(1)} %get-tuple-element.181), channel_id=1, source_target_pairs={{1,2},{2,1},{3,4},{4,3},{5,6},{6,5},{7,8},{8,7},{9,10},{10,9},{11,... | collective-permute-start | bytes 98312 | tf_op jit(solution)/shard_map/ppermute | solution.py:564
  85.1 4.6 %collective-permute-start.43 = (bf16[128,128]{1,0:T(8,128)(2,1)S(1)}, bf16[128,128]{1,0:T(8,128)(2,1)S(1)}, u32[]{:S(2)}, u32[]{:S(2)}) collective-permute-start(bf16[128,128]{1,0:T(8,128)(2,1)S(1)} %get-tuple-element.182), channel_id=1, source_target_pairs={{0,4},{4,0},{1,5},{5,1},{2,6},{6,2},{3,7},{7,3},{8,12},{12,8},{9,1... | collective-permute-start | bytes 98312 | tf_op jit(solution)/shard_map/ppermute | solution.py:564
  85.1 4.6 %collective-permute-start.44 = (bf16[128,128]{1,0:T(8,128)(2,1)S(1)}, bf16[128,128]{1,0:T(8,128)(2,1)S(1)}, u32[]{:S(2)}, u32[]{:S(2)}) collective-permute-start(bf16[128,128]{1,0:T(8,128)(2,1)S(1)} %get-tuple-element.183), channel_id=1, source_target_pairs={{0,2},{2,0},{1,3},{3,1},{4,6},{6,4},{5,7},{7,5},{8,10},{10,8},{9,1... | collective-permute-start | bytes 98312 | tf_op jit(solution)/shard_map/ppermute | solution.py:564
  85.8 3.9 %collective-permute-start.45 = (bf16[128,128]{1,0:T(8,128)(2,1)S(1)}, bf16[128,128]{1,0:T(8,128)(2,1)S(1)}, u32[]{:S(2)}, u32[]{:S(2)}) collective-permute-start(bf16[128,128]{1,0:T(8,128)(2,1)S(1)} %get-tuple-element.184), channel_id=1, source_target_pairs={{0,1},{1,0},{2,3},{3,2},{4,5},{5,4},{6,7},{7,6},{8,9},{9,8},{10,11... | collective-permute-start | bytes 98312 | tf_op jit(solution)/shard_map/ppermute | solution.py:564
  90.1 7.0 %collective-permute-start.46 = (bf16[128,128]{1,0:T(8,128)(2,1)S(1)}, bf16[128,128]{1,0:T(8,128)(2,1)S(1)}, u32[]{:S(2)}, u32[]{:S(2)}) collective-permute-start(bf16[128,128]{1,0:T(8,128)(2,1)S(1)} %get-tuple-element.188), channel_id=1, source_target_pairs={{4,8},{8,4},{5,9},{9,5},{6,10},{10,6},{7,11},{11,7},{12,16},{16,12... | collective-permute-start | bytes 98312 | tf_op jit(solution)/shard_map/ppermute | solution.py:564
  90.4 7.6 %collective-permute-start.47 = (bf16[128,128]{1,0:T(8,128)(2,1)S(1)}, bf16[128,128]{1,0:T(8,128)(2,1)S(1)}, u32[]{:S(2)}, u32[]{:S(2)}) collective-permute-start(bf16[128,128]{1,0:T(8,128)(2,1)S(1)} %get-tuple-element.189), channel_id=1, source_target_pairs={{2,4},{4,2},{3,5},{5,3},{6,8},{8,6},{7,9},{9,7},{10,12},{12,10},{1... | collective-permute-start | bytes 98312 | tf_op jit(solution)/shard_map/ppermute | solution.py:564
  93.7 7.0 %collective-permute-start.48 = (bf16[128,128]{1,0:T(8,128)(2,1)S(1)}, bf16[128,128]{1,0:T(8,128)(2,1)S(1)}, u32[]{:S(2)}, u32[]{:S(2)}) collective-permute-start(bf16[128,128]{1,0:T(8,128)(2,1)S(1)} %get-tuple-element.190), channel_id=1, source_target_pairs={{1,2},{2,1},{3,4},{4,3},{5,6},{6,5},{7,8},{8,7},{9,10},{10,9},{11,... | collective-permute-start | bytes 98312 | tf_op jit(solution)/shard_map/ppermute | solution.py:564
  95.2 5.4 %collective-permute-start.49 = (bf16[128,128]{1,0:T(8,128)(2,1)S(1)}, bf16[128,128]{1,0:T(8,128)(2,1)S(1)}, u32[]{:S(2)}, u32[]{:S(2)}) collective-permute-start(bf16[128,128]{1,0:T(8,128)(2,1)S(1)} %get-tuple-element.191), channel_id=1, source_target_pairs={{0,4},{4,0},{1,5},{5,1},{2,6},{6,2},{3,7},{7,3},{8,12},{12,8},{9,1... | collective-permute-start | bytes 98312 | tf_op jit(solution)/shard_map/ppermute | solution.py:564
  95.2 5.4 %collective-permute-start.50 = (bf16[128,128]{1,0:T(8,128)(2,1)S(1)}, bf16[128,128]{1,0:T(8,128)(2,1)S(1)}, u32[]{:S(2)}, u32[]{:S(2)}) collective-permute-start(bf16[128,128]{1,0:T(8,128)(2,1)S(1)} %get-tuple-element.192), channel_id=1, source_target_pairs={{0,2},{2,0},{1,3},{3,1},{4,6},{6,4},{5,7},{7,5},{8,10},{10,8},{9,1... | collective-permute-start | bytes 98312 | tf_op jit(solution)/shard_map/ppermute | solution.py:564
  97.1 3.5 %collective-permute-start.51 = (bf16[128,128]{1,0:T(8,128)(2,1)S(1)}, bf16[128,128]{1,0:T(8,128)(2,1)S(1)}, u32[]{:S(2)}, u32[]{:S(2)}) collective-permute-start(bf16[128,128]{1,0:T(8,128)(2,1)S(1)} %get-tuple-element.193), channel_id=1, source_target_pairs={{0,1},{1,0},{2,3},{3,2},{4,5},{5,4},{6,7},{7,6},{8,9},{9,8},{10,11... | collective-permute-start | bytes 98312 | tf_op jit(solution)/shard_map/ppermute | solution.py:564
  101.4 1.3 %collective-permute-start.52 = (f32[64,128]{1,0:T(8,128)S(1)}, f32[64,128]{1,0:T(8,128)S(1)}, u32[]{:S(2)}, u32[]{:S(2)}) collective-permute-start(f32[64,128]{1,0:T(8,128)S(1)} %get-tuple-element.195), channel_id=1, source_target_pairs={{0,1},{1,0},{2,3},{3,2},{4,5},{5,4},{6,7},{7,6},{8,9},{9,8},{10,11... | collective-permute-start | bytes 98312 | tf_op jit(solution)/shard_map/ppermute | solution.py:547
  102.7 4.9 %collective-permute-start.55 = (f32[64,128]{1,0:T(8,128)S(1)}, f32[64,128]{1,0:T(8,128)S(1)}, u32[]{:S(2)}, u32[]{:S(2)}) collective-permute-start(f32[64,128]{1,0:T(8,128)S(1)} %add.25), channel_id=1, source_target_pairs={{0,6},{1,7},{2,4},{3,5},{4,2},{5,3},{6,0},{7,1},{8,14},{9,15},{10,... | collective-permute-start | bytes 98312 | tf_op jit(solution)/shard_map/ppermute | solution.py:547
  102.7 4.9 %collective-permute-start.54 = (f32[64,128]{1,0:T(8,128)S(1)}, f32[64,128]{1,0:T(8,128)S(1)}, u32[]{:S(2)}, u32[]{:S(2)}) collective-permute-start(f32[64,128]{1,0:T(8,128)S(1)} %add.25), channel_id=1, source_target_pairs={{0,4},{1,5},{2,6},{3,7},{4,0},{5,1},{6,2},{7,3},{8,12},{9,13},{10,... | collective-permute-start | bytes 98312 | tf_op jit(solution)/shard_map/ppermute | solution.py:547
  103.7 4.4 %collective-permute-start.53 = (f32[64,128]{1,0:T(8,128)S(1)}, f32[64,128]{1,0:T(8,128)S(1)}, u32[]{:S(2)}, u32[]{:S(2)}) collective-permute-start(f32[64,128]{1,0:T(8,128)S(1)} %add.25), channel_id=1, source_target_pairs={{0,2},{1,3},{2,0},{3,1},{4,6},{5,7},{6,4},{7,5},{8,10},{9,11},{10,... | collective-permute-start | bytes 98312 | tf_op jit(solution)/shard_map/ppermute | solution.py:547
  108.1 6.0 %collective-permute-start.58 = (f32[64,128]{1,0:T(8,128)S(1)}, f32[64,128]{1,0:T(8,128)S(1)}, u32[]{:S(2)}, u32[]{:S(2)}) collective-permute-start(f32[64,128]{1,0:T(8,128)S(1)} %add_add_fusion.1), channel_id=1, source_target_pairs={{0,24},{1,25},{2,26},{3,27},{4,28},{5,29},{6,30},{7,31},{8,16},{9,... | collective-permute-start | bytes 98312 | tf_op jit(solution)/shard_map/ppermute | solution.py:547
  110.2 4.8 %collective-permute-start.57 = (f32[64,128]{1,0:T(8,128)S(1)}, f32[64,128]{1,0:T(8,128)S(1)}, u32[]{:S(2)}, u32[]{:S(2)}) collective-permute-start(f32[64,128]{1,0:T(8,128)S(1)} %add_add_fusion.1), channel_id=1, source_target_pairs={{0,16},{1,17},{2,18},{3,19},{4,20},{5,21},{6,22},{7,23},{8,24},{9,... | collective-permute-start | bytes 98312 | tf_op jit(solution)/shard_map/ppermute | solution.py:547
  110.2 4.8 %collective-permute-start.56 = (f32[64,128]{1,0:T(8,128)S(1)}, f32[64,128]{1,0:T(8,128)S(1)}, u32[]{:S(2)}, u32[]{:S(2)}) collective-permute-start(f32[64,128]{1,0:T(8,128)S(1)} %add_add_fusion.1), channel_id=1, source_target_pairs={{0,8},{1,9},{2,10},{3,11},{4,12},{5,13},{6,14},{7,15},{8,0},{9,1},... | collective-permute-start | bytes 98312 | tf_op jit(solution)/shard_map/ppermute | solution.py:547
  115.0 1.3 %collective-permute-start.59 = (f32[64,128]{1,0:T(8,128)S(1)}, f32[64,128]{1,0:T(8,128)S(1)}, u32[]{:S(2)}, u32[]{:S(2)}) collective-permute-start(f32[64,128]{1,0:T(8,128)S(1)} %add_add_fusion.refs_1_), channel_id=1, source_target_pairs={{0,1},{1,0},{2,3},{3,2},{4,5},{5,4},{6,7},{7,6},{8,9},{9,8},{10,11... | collective-permute-start | bytes 98312 | tf_op jit(solution)/shard_map/ppermute | solution.py:547
